TPU v7x, 32 devices: a whole 2x2x4 slice. The times are simulated.
32 devices in a mesh: leaf: 8 (over z, x), group: 4 (over y, core).
Axes of the slice: x: 2, y: 2, z: 4, core: 2. Of those that a mesh axis runs over, the one named last changes fastest.
Arguments:
- q_two: float32 [65536, 256], P(('group', 'leaf'))
- q_one: float32 [65536, 256], P(('group', 'leaf'))
- sources: float32 [65536, 256], P(('group', 'leaf'))
- coupling_two: float32 [2, 256, 256], replicated, as said below
- coupling_one: float32 [256, 256], replicated, as said below
Outputs:
- panel_one: float32 [65536, 256], P(('group', 'leaf'))
- solution: float32 [65536, 256], P(('group', 'leaf'))
Inputs may be any that keep to these rules, and one draw needn't show every extreme that they name: coupling_two[0], coupling_two[1] and coupling_one are symmetric and positive definite. `coupling_one`: symmetric and positive definite.
All inputs are finite; a program needn't handle non-finite values.
Results may differ from a plain program's by a relative error of at most 0.00019.
Values sent between devices are 32-bit elements; how exact they have to be, the bound alone decides.
No kernel may reach another device: no remote copies, remote signals or barrier semaphores. Data moves between devices by JAX's collectives and lax.ppermute only.
A program may use at most 64 MiB of HBM per device.

v0:
```python
import functools

import jax
import jax.numpy as jnp
from jax import lax
from jax.experimental import pallas as pl
from jax.experimental.pallas import tpu as pltpu
from jax.sharding import PartitionSpec as P

HIGH = lax.Precision.HIGHEST
AXES = ("leaf", "group")
F32 = jnp.float32
BF16 = jnp.bfloat16
R = 256
LANES = 128
PANEL = 32
TILE = 512
VMEM_LIMIT = 40 * 1024 * 1024
TERMS = 2304
TOP = 896


def split2(x):
    high = x.astype(BF16)
    return high, (x - high.astype(F32)).astype(BF16)


def split3(x):
    high = x.astype(BF16)
    rest = x - high.astype(F32)
    mid = rest.astype(BF16)
    return high, mid, (rest - mid.astype(F32)).astype(BF16)


def dot(left, right):
    return jnp.dot(left, right, preferred_element_type=F32)


def dot_t(left, right):
    return lax.dot_general(left, right, (((0,), (0,)), ((), ())), preferred_element_type=F32)


def dot_full(left, right):
    return jnp.dot(left, right, precision=HIGH, preferred_element_type=F32)


def dot_t_full(left, right):
    return lax.dot_general(
        left, right, (((0,), (0,)), ((), ())), precision=HIGH, preferred_element_type=F32
    )


def store_symmetric(ref, row, block):
    ref[row : row + 128, :] = block[:128, :128]
    ref[row + 128 : row + 256, :] = block[128:, :128]
    ref[row + 256 : row + 384, :] = block[128:, 128:]


def store_square(ref, row, block):
    ref[row : row + 256, :] = block[:, :128]
    ref[row + 256 : row + 512, :] = block[:, 128:]


def load_symmetric(ref, row):
    lower = ref[row + 128 : row + 256, :]
    top = jnp.concatenate([ref[row : row + 128, :], lower.T], axis=1)
    bottom = jnp.concatenate([lower, ref[row + 256 : row + 384, :]], axis=1)
    return jnp.concatenate([top, bottom], axis=0)


def load_square(ref, row):
    return jnp.concatenate([ref[row : row + 256, :], ref[row + 256 : row + 512, :]], axis=1)


def gram_kernel(q_two, q_one, sources, out, acc):
    step = pl.program_id(0)

    @pl.when(step == 0)
    def _():
        acc[...] = jnp.zeros_like(acc)

    h2, l2 = split2(q_two[...])
    h1, l1 = split2(q_one[...])
    hs, ls = split2(sources[...])
    acc[0] += dot_t(h2, h2)
    acc[1] += dot_t(h2, l2)
    acc[2] += dot_t(h2, h1) + dot_t(h2, l1) + dot_t(l2, h1)
    acc[3] += dot_t(h2, hs) + dot_t(h2, ls) + dot_t(l2, hs)
    acc[4] += dot_t(h1, h1)
    acc[5] += dot_t(h1, l1)
    acc[6] += dot_t(h1, hs) + dot_t(h1, ls) + dot_t(l1, hs)

    @pl.when(step == pl.num_programs(0) - 1)
    def _():
        cross2 = acc[1]
        store_symmetric(out, 0, acc[0] + cross2 + cross2.T)
        store_square(out, 384, acc[2])
        store_square(out, 896, acc[3])
        cross1 = acc[5]
        store_symmetric(out, 1408, acc[4] + cross1 + cross1.T)
        store_square(out, 1792, acc[6])


def gram_terms(q_two, q_one, sources):
    rows = q_two.shape[0]
    spec = pl.BlockSpec((TILE, R), lambda i: (i, 0))
    return pl.pallas_call(
        gram_kernel,
        grid=(rows // TILE,),
        in_specs=[spec, spec, spec],
        out_specs=pl.BlockSpec((TERMS, LANES), lambda i: (0, 0)),
        out_shape=jax.ShapeDtypeStruct((TERMS, LANES), F32),
        scratch_shapes=[pltpu.VMEM((7, R, R), F32)],
        compiler_params=pltpu.CompilerParams(vmem_limit_bytes=60 * 1024 * 1024),
        name="gram",
    )(q_two, q_one, sources)


def spread_lane(x, lane):
    return jnp.broadcast_to(x[:, lane : lane + 1], (8, LANES))


def eliminate(block, cols, rows):
    lane = lax.broadcasted_iota(jnp.int32, (8, LANES), 1)
    sub = lax.broadcasted_iota(jnp.int32, (8, LANES), 0)
    count = len(block)
    for t in range(count):
        own = [spread_lane(block[t], 8 * t + j) for j in range(8)]
        for j in range(8):
            cols[64 * t + 8 * j : 64 * t + 8 * j + 8, :] = own[j]
        rows[8 * t : 8 * t + 8, :] = block[t]
        entry = {}
        for i in range(8):
            for j in range(i + 1):
                at = 64 * t + 8 * j + i
                entry[i, j] = jnp.broadcast_to(cols[at : at + 1, :], (8, LANES))
        entry = sweep_small(entry)
        inverse = lambda i, j: entry[max(i, j), min(i, j)]
        inside = (lane >= 8 * t) & (lane < 8 * t + 8)
        old = []
        for j in range(8):
            row = jnp.broadcast_to(rows[8 * t + j : 8 * t + j + 1, :], (8, LANES))
            old.append(jnp.where(inside, jnp.where(lane == 8 * t + j, 1.0, 0.0), row))
        new = [tree_sum([inverse(i, j) * old[j] for j in range(8)]) for i in range(8)]
        for g in range(count):
            if g == t:
                continue
            base = jnp.where(inside, 0.0, block[g])
            terms = [spread_lane(block[g], 8 * t + j) * new[j] for j in range(8)]
            block[g] = base - tree_sum(terms)
        merged = new[0]
        for j in range(1, 8):
            merged = jnp.where(sub == j, new[j], merged)
        block[t] = merged
    return block


def tree_sum(terms):
    while len(terms) > 1:
        terms = [
            terms[i] + terms[i + 1] if i + 1 < len(terms) else terms[i]
            for i in range(0, len(terms), 2)
        ]
    return terms[0]


def sweep_small(entry):
    entry = dict(entry)
    get = lambda i, j: entry[max(i, j), min(i, j)]
    for k in range(0, 8, 2):
        a, b, c = get(k, k), get(k + 1, k), get(k + 1, k + 1)
        inv = pl.reciprocal(a * c - b * b, approx=True)
        e, f, g = c * inv, b * inv, a * inv
        others = [i for i in range(8) if i not in (k, k + 1)]
        left = {i: (get(i, k), get(i, k + 1)) for i in others}
        swept = {i: (e * u - f * v, g * v - f * u) for i, (u, v) in left.items()}
        for i in others:
            for j in others:
                if j <= i:
                    u, v = left[i]
                    m, n = swept[j]
                    entry[i, j] = entry[i, j] - (u * m + v * n)
        for i in others:
            entry[max(i, k), min(i, k)] = swept[i][0]
            entry[max(i, k + 1), min(i, k + 1)] = swept[i][1]
        entry[k, k], entry[k + 1, k], entry[k + 1, k + 1] = -e, f, -g
    return {key: -value for key, value in entry.items()}


def invert_half(matrix, cols, rows):
    block = eliminate([matrix[8 * i : 8 * i + 8, :] for i in range(LANES // 8)], cols, rows)
    return jnp.concatenate(block, axis=0)


def invert(matrix, cols, rows):
    eye = lax.broadcasted_iota(jnp.int32, (R, R), 0) == lax.broadcasted_iota(jnp.int32, (R, R), 1)
    diagonal = jnp.where(eye, matrix, 0.0)
    scale_row = lax.rsqrt(jnp.sum(diagonal, axis=0, keepdims=True))
    scale_col = lax.rsqrt(jnp.sum(diagonal, axis=1, keepdims=True))
    matrix = matrix * scale_col * scale_row
    side = matrix[:LANES, LANES:]
    first = invert_half(matrix[:LANES, :LANES], cols, rows)
    across = dot_full(first, side)
    second = invert_half(matrix[LANES:, LANES:] - dot_t_full(side, across), cols, rows)
    corner = -dot_full(across, second)
    first = first - dot_full(corner, across.T)
    top = jnp.concatenate([first, corner], axis=1)
    bottom = jnp.concatenate([corner.T, second], axis=1)
    return jnp.concatenate([top, bottom], axis=0) * scale_col * scale_row


SCRATCH = [pltpu.VMEM((1024, LANES), F32), pltpu.VMEM((LANES, LANES), F32)]


def level_kernel(terms, coupling, x_out, y_out, top_out, cols, rows):
    half = lax.axis_index("group") // 2
    inverse = invert(coupling[half] + load_symmetric(terms, 0), cols, rows)
    cross = load_square(terms, 384)
    x = dot_full(inverse, cross)
    y = dot_full(inverse, load_square(terms, 896))
    x_out[...] = x
    y_out[...] = y
    store_symmetric(top_out, 0, load_symmetric(terms, 1408) - dot_t_full(cross, x))
    store_square(top_out, 384, load_square(terms, 1792) - dot_t_full(cross, y))


def level_solve(terms, coupling):
    square = jax.ShapeDtypeStruct((R, R), F32)
    return pl.pallas_call(
        level_kernel,
        out_shape=(square, square, jax.ShapeDtypeStruct((TOP, LANES), F32)),
        scratch_shapes=SCRATCH,
        compiler_params=pltpu.CompilerParams(vmem_limit_bytes=VMEM_LIMIT),
        name="level_solve",
    )(terms, coupling)


def root_kernel(top, coupling, x, y, w_out, z_out, cols, rows):
    inverse = invert(coupling[...] + load_symmetric(top, 0), cols, rows)
    w = dot_full(inverse, load_square(top, 384))
    w_out[...] = w
    z_out[...] = y[...] - dot_full(x[...], w)


def root_solve(top, coupling, x, y):
    square = jax.ShapeDtypeStruct((R, R), F32)
    return pl.pallas_call(
        root_kernel,
        out_shape=(square, square),
        scratch_shapes=SCRATCH,
        compiler_params=pltpu.CompilerParams(vmem_limit_bytes=VMEM_LIMIT),
        name="root_solve",
    )(top, coupling, x, y)


def dot_three(lh, ll, rh, rl):
    return dot(lh, rh) + (dot(lh, rl) + dot(ll, rh))


def panel_kernel(q_two, q_one, x, out):
    out[...] = q_one[...] - dot_three(*split2(q_two[...]), *split2(x[...]))


def field_kernel(q_two, q_one, sources, w, z, out):
    change = dot_three(*split2(q_one[...]), *split2(w[...]))
    change += dot_three(*split2(q_two[...]), *split2(z[...]))
    out[...] = sources[...] - change


def update(kernel, tall, square, name):
    rows = tall[0].shape[0]
    spec = pl.BlockSpec((TILE, R), lambda i: (i, 0))
    whole = pl.BlockSpec((R, R), lambda i: (0, 0))
    return pl.pallas_call(
        kernel,
        grid=(rows // TILE,),
        in_specs=[spec] * len(tall) + [whole] * len(square),
        out_specs=spec,
        out_shape=jax.ShapeDtypeStruct((rows, R), F32),
        compiler_params=pltpu.CompilerParams(vmem_limit_bytes=VMEM_LIMIT),
        name=name,
    )(*tall, *square)


def exchange(x, mask):
    count = lax.axis_size(AXES)
    return lax.ppermute(x, AXES, [(i, i ^ mask) for i in range(count)])


def code_of(index, bits):
    code = 0
    for place, bit in enumerate(bits):
        code = code | ((index >> bit) & 1) << place
    return code


def mask_of(code, bits):
    return sum(1 << bit for place, bit in enumerate(bits) if code >> place & 1)


def reduce_scatter(x, index, bits):
    count = 1 << len(bits)
    mine = code_of(index, bits)
    parts = x.reshape(count, x.shape[0] // count, x.shape[1])
    got = lax.dynamic_index_in_dim(parts, mine, 0, keepdims=False)
    arrived = []
    for other in range(1, count):
        part = lax.dynamic_index_in_dim(parts, mine ^ other, 0, keepdims=False)
        arrived.append(exchange(part, mask_of(other, bits)))
    for part in arrived:
        got = got + part
    return got


def all_gather(x, index, bits):
    count = 1 << len(bits)
    mine = code_of(index, bits)
    pieces = [x] + [exchange(x, mask_of(other, bits)) for other in range(1, count)]
    out = jnp.zeros((count,) + x.shape, x.dtype)
    for other, piece in enumerate(pieces):
        out = lax.dynamic_update_index_in_dim(out, piece, mine ^ other, 0)
    return out.reshape(count * x.shape[0], x.shape[1])


def scatter_leaf(x):
    count = lax.axis_size("leaf")
    parts = x.reshape(count, x.shape[0] // count, x.shape[1])
    return jnp.sum(lax.all_to_all(parts, "leaf", 0, 0), axis=0)


def gather_leaf(x):
    count = lax.axis_size("leaf")
    parts = jnp.broadcast_to(x[None], (count,) + x.shape)
    return lax.all_to_all(parts, "leaf", 0, 0).reshape(count * x.shape[0], x.shape[1])


def per_device(q_two, q_one, sources, coupling_two, coupling_one):
    index = lax.axis_index(AXES)
    terms = gram_terms(q_two, q_one, sources)
    terms = reduce_scatter(terms, index, [0])
    terms = gather_leaf(scatter_leaf(terms))
    terms = all_gather(terms, index, [0])
    x, y, top = level_solve(terms, coupling_two)
    mine = index & 1
    parts = top.reshape(2, TOP // 2, LANES)
    part = lax.dynamic_index_in_dim(parts, mine, 0, keepdims=False)
    part = part + exchange(part, 2)
    top = all_gather(part, index, [0])
    panel_one = update(panel_kernel, [q_two, q_one], [x], "panel")
    w, z = root_solve(top, coupling_one, x, y)
    solution = update(field_kernel, [q_two, q_one, sources], [w, z], "field")
    return (panel_one, solution)


def solution(mesh):
    placed = P(("group", "leaf"), None)
    return jax.shard_map(
        per_device,
        mesh=mesh,
        in_specs=(placed, placed, placed, P(), P()),
        out_specs=(placed, placed),
        check_vma=False,
    )
```

profile of v0, /device:TPU:0, one launch (start us, length us, event | category | flops | bytes accessed | tf_op | source)
XLA Modules:
  0.0 93.7 jit_solution(4851927344183708261)
XLA Ops:
  0.6 7.4 %gram.1 = f32[2304,128]{1,0:T(8,128)} custom-call(f32[2048,256]{1,0:T(8,128)} %q_two.5, f32[2048,256]{1,0:T(8,128)} %q_one.5, f32[2048,256]{1,0:T(8,128)} %sources.3), custom_call_target="tpu_custom_call" | custom-call | tf_op jit(solution)/shard_map/gram/pallas_call | solution.py:107
  8.0 0.0 copy-start.5
  8.0 1.2 %dynamic-slice_bitcast_fusion = f32[1152,128]{1,0:T(8,128)S(1)} fusion(f32[2,1152,128]{2,1,0:T(8,128)} %bitcast.27, s32[]{:T(128)S(6)} %select_n.18), kind=kLoop, calls=%fused_computation.3 | loop fusion | bytes 1179652 | tf_op jit(solution)/shard_map/jit(dynamic_index_in_dim)/squeeze | solution.py:308
  9.3 0.5 collective-permute-start
  9.8 1.6 %collective-permute-done = f32[1152,128]{1,0:T(8,128)S(1)} collective-permute-done((f32[1152,128]{1,0:T(8,128)S(1)}, f32[1152,128]{1,0:T(8,128)S(1)}, u32[]{:S(2)}, u32[]{:S(2)}) %collective-permute-start) | collective-permute-done | bytes 589856 | tf_op jit(solution)/shard_map/ppermute | solution.py:287
  11.4 0.0 copy-done.5
  11.4 0.1 bitcast_add_fusion
  11.5 23.8 %all_to_all.10 = f32[8,144,128]{2,1,0:T(8,128)S(1)} all-to-all(f32[8,144,128]{2,1,0:T(8,128)S(1)} %bitcast.31), channel_id=1, replica_groups=mesh['leaf'=8,'group'=4] {'leaf'}, dimensions={0} | all-to-all | bytes 1179648 | tf_op jit(solution)/shard_map/all_to_all | solution.py:328
  35.4 19.3 %all_to_all.11 = f32[8,144,128]{2,1,0:T(8,128)S(1)} all-to-all(f32[8,144,128]{2,1,0:T(8,128)S(1)} %broadcast_in_dim.27), channel_id=1, replica_groups=mesh['leaf'=8,'group'=4] {'leaf'}, dimensions={0} | all-to-all | bytes 1179648 | tf_op jit(solution)/shard_map/all_to_all | solution.py:334
  54.6 0.0 collective-permute-start.1
  54.6 0.1 broadcast_in_dim.26
  54.7 0.0 copy-start.3
  54.8 1.9 %collective-permute-done.1 = f32[1152,128]{1,0:T(8,128)S(1)} collective-permute-done((f32[1152,128]{1,0:T(8,128)S(1)}, f32[1152,128]{1,0:T(8,128)S(1)}, u32[]{:S(2)}, u32[]{:S(2)}) %collective-permute-start.1) | collective-permute-done | bytes 589856 | tf_op jit(solution)/shard_map/ppermute | solution.py:287
  56.6 0.0 copy-start.1
  56.7 0.0 copy-done.3
  56.7 0.0 copy-start
  56.7 11.5 %level_solve.1 = (f32[256,256]{1,0:T(8,128)S(1)}, f32[256,256]{1,0:T(8,128)S(1)}, f32[896,128]{1,0:T(8,128)S(1)}) custom-call(f32[2304,128]{1,0:T(8,128)S(1)} %bitcast.23, f32[2,256,256]{2,1,0:T(8,128)S(1)} %copy-done.3), custom_call_target="tpu_custom_call" | custom-call | tf_op jit(solution)/shard_map/level_solve/pallas_call | solution.py:229
  68.2 1.6 %collective-permute-start.2 = (f32[448,128]{1,0:T(8,128)S(1)}, f32[448,128]{1,0:T(8,128)S(1)}, u32[]{:S(2)}, u32[]{:S(2)}) collective-permute-start(f32[448,128]{1,0:T(8,128)S(1)} %dynamic-slice_bitcast_fusion.1), channel_id=1, source_target_pairs={{0,2},{1,3},{2,0},{3,1},{4,6},{5,7},{6,4},{7,5},{8,10},{9,11},{10,... | collective-permute-start | bytes 688136 | tf_op jit(solution)/shard_map/ppermute | solution.py:287
  69.8 6.1 %collective-permute-done.2 = f32[448,128]{1,0:T(8,128)S(1)} collective-permute-done((f32[448,128]{1,0:T(8,128)S(1)}, f32[448,128]{1,0:T(8,128)S(1)}, u32[]{:S(2)}, u32[]{:S(2)}) %collective-permute-start.2) | collective-permute-done | bytes 229408 | tf_op jit(solution)/shard_map/ppermute | solution.py:287
  76.0 0.1 collective-permute-start.3
  76.1 0.0 copy-done.1
  76.1 0.0 copy-done
  76.1 0.0 copy-start.4
  76.1 0.0 copy-start.2
  76.1 2.8 %panel.1 = f32[2048,256]{1,0:T(8,128)} custom-call(f32[2048,256]{1,0:T(8,128)S(1)} %copy-done, f32[2048,256]{1,0:T(8,128)S(1)} %copy-done.1, f32[256,256]{1,0:T(8,128)S(1)} %get-tuple-element.7.x), custom_call_target="tpu_custom_call" | custom-call | tf_op jit(solution)/shard_map/panel/pallas_call | solution.py:274
  78.9 0.0 collective-permute-done.3
  78.9 0.0 copy-done.4
  78.9 11.4 %root_solve.1 = (f32[256,256]{1,0:T(8,128)S(1)}, f32[256,256]{1,0:T(8,128)S(1)}) custom-call(f32[896,128]{1,0:T(8,128)S(1)} %bitcast.24, f32[256,256]{1,0:T(8,128)S(1)} %copy-done.4, f32[256,256]{1,0:T(8,128)S(1)} %get-tuple-element.7.x, f32[256,256]{1,0:T(8,128)S(1)} %get-tuple-element.9.y), custom_call_target="tpu_custom_call" | custom-call | tf_op jit(solution)/shard_map/root_solve/pallas_call | solution.py:247
  90.3 0.0 copy-done.2
  90.3 3.4 %field.1 = f32[2048,256]{1,0:T(8,128)} custom-call(f32[2048,256]{1,0:T(8,128)S(1)} %copy-done, f32[2048,256]{1,0:T(8,128)S(1)} %copy-done.1, f32[2048,256]{1,0:T(8,128)S(1)} %copy-done.2, f32[256,256]{1,0:T(8,128)S(1)} %get-tuple-element.10.w, f32[256,256]{1,0:T(8,128)S(1)} %get-tuple-element.11.z), custom_call_target="tpu_custom_call" | custom-call | tf_op jit(solution)/shard_map/field/pallas_call | solution.py:274
  (8 shorter events, 0.3 us)
Async XLA Ops:
  8.0 3.4 %copy-start.5 = (f32[2304,128]{1,0:T(8,128)S(1)}, f32[2304,128]{1,0:T(8,128)}, u32[]{:S(2)}) copy-start(f32[2304,128]{1,0:T(8,128)} %gram.1) | copy-start | bytes 3538948
  9.3 2.1 %collective-permute-start = (f32[1152,128]{1,0:T(8,128)S(1)}, f32[1152,128]{1,0:T(8,128)S(1)}, u32[]{:S(2)}, u32[]{:S(2)}) collective-permute-start(f32[1152,128]{1,0:T(8,128)S(1)} %dynamic-slice_bitcast_fusion), channel_id=1, source_target_pairs={{0,1},{1,0},{2,3},{3,2},{4,5},{5,4},{6,7},{7,6},{8,9},{9,8},{10,11... | collective-permute-start | bytes 1769480 | tf_op jit(solution)/shard_map/ppermute | solution.py:287
  54.6 2.0 %collective-permute-start.1 = (f32[1152,128]{1,0:T(8,128)S(1)}, f32[1152,128]{1,0:T(8,128)S(1)}, u32[]{:S(2)}, u32[]{:S(2)}) collective-permute-start(f32[1152,128]{1,0:T(8,128)S(1)} %bitcast.29), channel_id=1, source_target_pairs={{0,1},{1,0},{2,3},{3,2},{4,5},{5,4},{6,7},{7,6},{8,9},{9,8},{10,11... | collective-permute-start | bytes 1769480 | tf_op jit(solution)/shard_map/ppermute | solution.py:287
  54.7 2.0 %copy-start.3 = (f32[2,256,256]{2,1,0:T(8,128)S(1)}, f32[2,256,256]{2,1,0:T(8,128)}, u32[]{:S(2)}) copy-start(f32[2,256,256]{2,1,0:T(8,128)} %coupling.2) | copy-start | bytes 1572868
  56.6 19.4 %copy-start.1 = (f32[2048,256]{1,0:T(8,128)S(1)}, f32[2048,256]{1,0:T(8,128)}, u32[]{:S(2)}) copy-start(f32[2048,256]{1,0:T(8,128)} %q_one.5) | copy-start | bytes 6291460
  56.7 19.4 %copy-start = (f32[2048,256]{1,0:T(8,128)S(1)}, f32[2048,256]{1,0:T(8,128)}, u32[]{:S(2)}) copy-start(f32[2048,256]{1,0:T(8,128)} %q_two.5) | copy-start | bytes 6291460
  68.2 7.7 %collective-permute-start.2 = (f32[448,128]{1,0:T(8,128)S(1)}, f32[448,128]{1,0:T(8,128)S(1)}, u32[]{:S(2)}, u32[]{:S(2)}) collective-permute-start(f32[448,128]{1,0:T(8,128)S(1)} %dynamic-slice_bitcast_fusion.1), channel_id=1, source_target_pairs={{0,2},{1,3},{2,0},{3,1},{4,6},{5,7},{6,4},{7,5},{8,10},{9,11},{10,... | collective-permute-start | bytes 688136 | tf_op jit(solution)/shard_map/ppermute | solution.py:287
  76.0 2.9 %collective-permute-start.3 = (f32[448,128]{1,0:T(8,128)S(1)}, f32[448,128]{1,0:T(8,128)S(1)}, u32[]{:S(2)}, u32[]{:S(2)}) collective-permute-start(f32[448,128]{1,0:T(8,128)S(1)} %get-tuple-element.13), channel_id=1, source_target_pairs={{0,1},{1,0},{2,3},{3,2},{4,5},{5,4},{6,7},{7,6},{8,9},{9,8},{10,11... | collective-permute-start | bytes 688136 | tf_op jit(solution)/shard_map/ppermute | solution.py:287
  76.1 2.8 %copy-start.4 = (f32[256,256]{1,0:T(8,128)S(1)}, f32[256,256]{1,0:T(8,128)}, u32[]{:S(2)}) copy-start(f32[256,256]{1,0:T(8,128)} %coupling.3) | copy-start | bytes 786436
  76.1 14.2 %copy-start.2 = (f32[2048,256]{1,0:T(8,128)S(1)}, f32[2048,256]{1,0:T(8,128)}, u32[]{:S(2)}) copy-start(f32[2048,256]{1,0:T(8,128)} %sources.3) | copy-start | bytes 6291460
where the time goes:
time: 94 us; the launch traced here: 93.7 us
  blocking collectives  43.1 us (46%)
  Pallas kernels  36.4 us (39%)
  waiting for transfers between devices  9.62 us (10%)
  starting transfers between devices  2.17 us (2%)
  local copies, waits for them, and re-layouts  1.51 us (2%)
    all_to_all x1, blocking collectives, scatter_leaf(): return jnp.sum(lax.all_to_all(parts, 'leaf', 0, 0), axis=0)  23.8 us
    all_to_all x1, blocking collectives, gather_leaf(): lax.all_to_all(parts, 'leaf', 0, 0).reshape(count * x.shape[0], x.shape[1])  19.3 us
    pallas_call x1, Pallas kernels, level_solve(): pl.pallas_call(level_kernel, out_shape=(square, square, jax.ShapeDtypeStr...  11.5 us
    pallas_call x1, Pallas kernels, root_solve(): pl.pallas_call(root_kernel, out_shape=(square, square), scratch_shapes=SC...  11.4 us
    ppermute x4, waiting for transfers between devices, exchange(): return lax.ppermute(x, AXES, [(i, i ^ mask) for i in range(count)])  9.62 us
    pallas_call x1, Pallas kernels, gram_terms(): pl.pallas_call(gram_kernel, grid=(rows // TILE,), in_specs=[spec, spec, s...  7.41 us
    pallas_call x2, Pallas kernels, update(): pl.pallas_call(kernel, grid=(rows // TILE,), in_specs=[spec] * len(tall)...  6.18 us
    ppermute x4, starting transfers between devices, exchange(): return lax.ppermute(x, AXES, [(i, i ^ mask) for i in range(count)])  2.17 us
  transfers between devices with their start and end apart: 4, of which 3 were waited for; matrix products, arithmetic and copies ran while one was open for 0% of the time, Pallas kernels for 3%

commit v1 on v0

--- a/solution.py
+++ b/solution.py
@@ -16,8 +16,6 @@
 PANEL = 32
 TILE = 512
 VMEM_LIMIT = 40 * 1024 * 1024
-TERMS = 2304
-TOP = 896
 
 
 def split2(x):
@@ -72,48 +70,77 @@
     return jnp.concatenate([ref[row : row + 256, :], ref[row + 256 : row + 512, :]], axis=1)
 
 
-def gram_kernel(q_two, q_one, sources, out, acc):
-    step = pl.program_id(0)
-
-    @pl.when(step == 0)
+def zero_first(acc):
+    @pl.when(pl.program_id(0) == 0)
     def _():
         acc[...] = jnp.zeros_like(acc)
 
+
+def at_last(body):
+    pl.when(pl.program_id(0) == pl.num_programs(0) - 1)(body)
+
+
+def own_gram_kernel(q_two, out, acc):
+    zero_first(acc)
+    h2, l2 = split2(q_two[...])
+    acc[0] += dot_t(h2, h2)
+    acc[1] += dot_t(h2, l2)
+
+    @at_last
+    def _():
+        low = acc[1]
+        store_symmetric(out, 0, acc[0] + low + low.T)
+
+
+def cross_gram_kernel(q_two, q_one, out, acc):
+    zero_first(acc)
+    h2, l2 = split2(q_two[...])
+    h1, l1 = split2(q_one[...])
+    acc[0] += dot_t(h2, h1) + dot_t(h2, l1) + dot_t(l2, h1)
+    acc[1] += dot_t(h1, h1)
+    acc[2] += dot_t(h1, l1)
+
+    @at_last
+    def _():
+        store_square(out, 0, acc[0])
+        low = acc[2]
+        store_symmetric(out, 512, acc[1] + low + low.T)
+
+
+def source_gram_kernel(q_two, q_one, sources, out, acc):
+    zero_first(acc)
     h2, l2 = split2(q_two[...])
     h1, l1 = split2(q_one[...])
     hs, ls = split2(sources[...])
-    acc[0] += dot_t(h2, h2)
-    acc[1] += dot_t(h2, l2)
-    acc[2] += dot_t(h2, h1) + dot_t(h2, l1) + dot_t(l2, h1)
-    acc[3] += dot_t(h2, hs) + dot_t(h2, ls) + dot_t(l2, hs)
-    acc[4] += dot_t(h1, h1)
-    acc[5] += dot_t(h1, l1)
-    acc[6] += dot_t(h1, hs) + dot_t(h1, ls) + dot_t(l1, hs)
-
-    @pl.when(step == pl.num_programs(0) - 1)
+    acc[0] += dot_t(h2, hs) + dot_t(h2, ls) + dot_t(l2, hs)
+    acc[1] += dot_t(h1, hs) + dot_t(h1, ls) + dot_t(l1, hs)
+
+    @at_last
     def _():
-        cross2 = acc[1]
-        store_symmetric(out, 0, acc[0] + cross2 + cross2.T)
-        store_square(out, 384, acc[2])
-        store_square(out, 896, acc[3])
-        cross1 = acc[5]
-        store_symmetric(out, 1408, acc[4] + cross1 + cross1.T)
-        store_square(out, 1792, acc[6])
-
-
-def gram_terms(q_two, q_one, sources):
-    rows = q_two.shape[0]
+        store_square(out, 0, acc[0])
+        store_square(out, 512, acc[1])
+
+
+def estimate(passes, rows, arrays):
+    return pl.CostEstimate(
+        flops=2 * passes * rows * R * R, bytes_accessed=4 * arrays * rows * R, transcendentals=0
+    )
+
+
+def gram(kernel, tall, blocks, passes, packed, name):
+    rows = tall[0].shape[0]
     spec = pl.BlockSpec((TILE, R), lambda i: (i, 0))
     return pl.pallas_call(
-        gram_kernel,
+        kernel,
         grid=(rows // TILE,),
-        in_specs=[spec, spec, spec],
-        out_specs=pl.BlockSpec((TERMS, LANES), lambda i: (0, 0)),
-        out_shape=jax.ShapeDtypeStruct((TERMS, LANES), F32),
-        scratch_shapes=[pltpu.VMEM((7, R, R), F32)],
-        compiler_params=pltpu.CompilerParams(vmem_limit_bytes=60 * 1024 * 1024),
-        name="gram",
-    )(q_two, q_one, sources)
+        in_specs=[spec] * len(tall),
+        out_specs=pl.BlockSpec((packed, LANES), lambda i: (0, 0)),
+        out_shape=jax.ShapeDtypeStruct((packed, LANES), F32),
+        scratch_shapes=[pltpu.VMEM((blocks, R, R), F32)],
+        compiler_params=pltpu.CompilerParams(vmem_limit_bytes=VMEM_LIMIT),
+        cost_estimate=estimate(passes, rows, len(tall)),
+        name=name,
+    )(*tall)
 
 
 def spread_lane(x, lane):
@@ -192,7 +219,23 @@
     return jnp.concatenate(block, axis=0)
 
 
-def invert(matrix, cols, rows):
+SQUARE = jax.ShapeDtypeStruct((R, R), F32)
+CORNER = jax.ShapeDtypeStruct((LANES, LANES), F32)
+
+
+def call(kernel, out_shape, args, name, scratch=(), flops=0):
+    return pl.pallas_call(
+        kernel,
+        out_shape=out_shape,
+        scratch_shapes=list(scratch),
+        compiler_params=pltpu.CompilerParams(vmem_limit_bytes=VMEM_LIMIT),
+        cost_estimate=pl.CostEstimate(flops=flops, bytes_accessed=R * R * 4, transcendentals=0),
+        name=name,
+    )(*args)
+
+
+def first_kernel(which, gram_ref, coupling, first_out, across_out, rest_out, row_out, col_out, cols, rows):
+    matrix = coupling[which()] + load_symmetric(gram_ref, 0)
     eye = lax.broadcasted_iota(jnp.int32, (R, R), 0) == lax.broadcasted_iota(jnp.int32, (R, R), 1)
     diagonal = jnp.where(eye, matrix, 0.0)
     scale_row = lax.rsqrt(jnp.sum(diagonal, axis=0, keepdims=True))
@@ -201,56 +244,62 @@
     side = matrix[:LANES, LANES:]
     first = invert_half(matrix[:LANES, :LANES], cols, rows)
     across = dot_full(first, side)
-    second = invert_half(matrix[LANES:, LANES:] - dot_t_full(side, across), cols, rows)
-    corner = -dot_full(across, second)
-    first = first - dot_full(corner, across.T)
-    top = jnp.concatenate([first, corner], axis=1)
-    bottom = jnp.concatenate([corner.T, second], axis=1)
-    return jnp.concatenate([top, bottom], axis=0) * scale_col * scale_row
+    first_out[...] = first
+    across_out[...] = across
+    rest_out[...] = matrix[LANES:, LANES:] - dot_t_full(side, across)
+    row_out[...] = jnp.broadcast_to(scale_row, (8, R))
+    col_out[...] = jnp.broadcast_to(scale_col, (R, LANES))
+
+
+def second_kernel(first, across, rest, row, col, out, cols, rows):
+    second = invert_half(rest[...], cols, rows)
+    corner = -dot_full(across[...], second)
+    top = first[...] - dot_full(corner, across[...].T)
+    out[:LANES, :LANES] = top * col[:LANES, :] * row[:1, :LANES]
+    out[:LANES, LANES:] = corner * col[:LANES, :] * row[:1, LANES:]
+    out[LANES:, :LANES] = corner.T * col[LANES:, :] * row[:1, :LANES]
+    out[LANES:, LANES:] = second * col[LANES:, :] * row[:1, LANES:]
 
 
 SCRATCH = [pltpu.VMEM((1024, LANES), F32), pltpu.VMEM((LANES, LANES), F32)]
-
-
-def level_kernel(terms, coupling, x_out, y_out, top_out, cols, rows):
-    half = lax.axis_index("group") // 2
-    inverse = invert(coupling[half] + load_symmetric(terms, 0), cols, rows)
-    cross = load_square(terms, 384)
-    x = dot_full(inverse, cross)
-    y = dot_full(inverse, load_square(terms, 896))
+HALF_FLOPS = 5_000_000_000
+
+
+def invert_first(which, packed, coupling, name):
+    shapes = (
+        CORNER,
+        CORNER,
+        CORNER,
+        jax.ShapeDtypeStruct((8, R), F32),
+        jax.ShapeDtypeStruct((R, LANES), F32),
+    )
+    kernel = functools.partial(first_kernel, which)
+    return call(kernel, shapes, (packed, coupling), name, SCRATCH, HALF_FLOPS)
+
+
+def invert_second(parts, name):
+    return call(second_kernel, SQUARE, parts, name, SCRATCH, HALF_FLOPS)
+
+
+def half_index():
+    return lax.axis_index("group") // 2
+
+
+def no_index():
+    return 0
+
+
+def panel_solve_kernel(inverse, terms, x_out, root_out):
+    cross = load_square(terms, 0)
+    x = dot_full(inverse[...], cross)
     x_out[...] = x
-    y_out[...] = y
-    store_symmetric(top_out, 0, load_symmetric(terms, 1408) - dot_t_full(cross, x))
-    store_square(top_out, 384, load_square(terms, 1792) - dot_t_full(cross, y))
-
-
-def level_solve(terms, coupling):
-    square = jax.ShapeDtypeStruct((R, R), F32)
-    return pl.pallas_call(
-        level_kernel,
-        out_shape=(square, square, jax.ShapeDtypeStruct((TOP, LANES), F32)),
-        scratch_shapes=SCRATCH,
-        compiler_params=pltpu.CompilerParams(vmem_limit_bytes=VMEM_LIMIT),
-        name="level_solve",
-    )(terms, coupling)
-
-
-def root_kernel(top, coupling, x, y, w_out, z_out, cols, rows):
-    inverse = invert(coupling[...] + load_symmetric(top, 0), cols, rows)
-    w = dot_full(inverse, load_square(top, 384))
-    w_out[...] = w
-    z_out[...] = y[...] - dot_full(x[...], w)
-
-
-def root_solve(top, coupling, x, y):
-    square = jax.ShapeDtypeStruct((R, R), F32)
-    return pl.pallas_call(
-        root_kernel,
-        out_shape=(square, square),
-        scratch_shapes=SCRATCH,
-        compiler_params=pltpu.CompilerParams(vmem_limit_bytes=VMEM_LIMIT),
-        name="root_solve",
-    )(top, coupling, x, y)
+    store_symmetric(root_out, 0, load_symmetric(terms, 512) - dot_t_full(cross, x))
+
+
+def source_solve_kernel(inverse, x, terms, y_out, side_out):
+    projected = load_square(terms, 0)
+    y_out[...] = dot_full(inverse[...], projected)
+    store_square(side_out, 0, load_square(terms, 512) - dot_t_full(x[...], projected))
 
 
 def dot_three(lh, ll, rh, rl):
@@ -261,25 +310,32 @@
     out[...] = q_one[...] - dot_three(*split2(q_two[...]), *split2(x[...]))
 
 
-def field_kernel(q_two, q_one, sources, w, z, out):
-    change = dot_three(*split2(q_one[...]), *split2(w[...]))
-    change += dot_three(*split2(q_two[...]), *split2(z[...]))
+def field_kernel(q_two, q_one, sources, inverse, side, x, y, out, w_ref, z_ref):
+    @pl.when(pl.program_id(0) == 0)
+    def _():
+        w = dot_full(inverse[...], load_square(side, 0))
+        w_ref[...] = w
+        z_ref[...] = y[...] - dot_full(x[...], w)
+
+    change = dot_three(*split2(q_one[...]), *split2(w_ref[...]))
+    change += dot_three(*split2(q_two[...]), *split2(z_ref[...]))
     out[...] = sources[...] - change
 
 
-def update(kernel, tall, square, name):
+def update(kernel, tall, small, passes, name, scratch=()):
     rows = tall[0].shape[0]
     spec = pl.BlockSpec((TILE, R), lambda i: (i, 0))
-    whole = pl.BlockSpec((R, R), lambda i: (0, 0))
     return pl.pallas_call(
         kernel,
         grid=(rows // TILE,),
-        in_specs=[spec] * len(tall) + [whole] * len(square),
+        in_specs=[spec] * len(tall) + [pl.BlockSpec(x.shape, lambda i: (0, 0)) for x in small],
         out_specs=spec,
         out_shape=jax.ShapeDtypeStruct((rows, R), F32),
+        scratch_shapes=list(scratch),
         compiler_params=pltpu.CompilerParams(vmem_limit_bytes=VMEM_LIMIT),
+        cost_estimate=estimate(passes, rows, len(tall) + 1),
         name=name,
-    )(*tall, *square)
+    )(*tall, *small)
 
 
 def exchange(x, mask):
@@ -316,39 +372,76 @@
     count = 1 << len(bits)
     mine = code_of(index, bits)
     pieces = [x] + [exchange(x, mask_of(other, bits)) for other in range(1, count)]
+    if count == 2:
+        low = jnp.where(mine == 0, pieces[0], pieces[1])
+        high = jnp.where(mine == 0, pieces[1], pieces[0])
+        return jnp.concatenate([low, high], axis=0)
     out = jnp.zeros((count,) + x.shape, x.dtype)
     for other, piece in enumerate(pieces):
         out = lax.dynamic_update_index_in_dim(out, piece, mine ^ other, 0)
     return out.reshape(count * x.shape[0], x.shape[1])
 
 
-def scatter_leaf(x):
-    count = lax.axis_size("leaf")
-    parts = x.reshape(count, x.shape[0] // count, x.shape[1])
-    return jnp.sum(lax.all_to_all(parts, "leaf", 0, 0), axis=0)
-
-
-def gather_leaf(x):
-    count = lax.axis_size("leaf")
-    parts = jnp.broadcast_to(x[None], (count,) + x.shape)
-    return lax.all_to_all(parts, "leaf", 0, 0).reshape(count * x.shape[0], x.shape[1])
+def all_sum(x, bits):
+    count = 1 << len(bits)
+    arrived = [exchange(x, mask_of(other, bits)) for other in range(1, count)]
+    for part in arrived:
+        x = x + part
+    return x
 
 
 def per_device(q_two, q_one, sources, coupling_two, coupling_one):
     index = lax.axis_index(AXES)
-    terms = gram_terms(q_two, q_one, sources)
-    terms = reduce_scatter(terms, index, [0])
-    terms = gather_leaf(scatter_leaf(terms))
-    terms = all_gather(terms, index, [0])
-    x, y, top = level_solve(terms, coupling_two)
-    mine = index & 1
-    parts = top.reshape(2, TOP // 2, LANES)
-    part = lax.dynamic_index_in_dim(parts, mine, 0, keepdims=False)
-    part = part + exchange(part, 2)
-    top = all_gather(part, index, [0])
-    panel_one = update(panel_kernel, [q_two, q_one], [x], "panel")
-    w, z = root_solve(top, coupling_one, x, y)
-    solution = update(field_kernel, [q_two, q_one, sources], [w, z], "field")
+    leaf_end = lax.axis_size("leaf").bit_length() + 1
+    outer = [list(range(low, min(low + 2, leaf_end))) for low in range(3, leaf_end, 2)]
+    own = gram(own_gram_kernel, [q_two], 2, 2, 384, "own_gram")
+    crossing = gram(cross_gram_kernel, [q_two, q_one], 3, 5, 896, "cross_gram")
+    source = gram(source_gram_kernel, [q_two, q_one, sources], 2, 6, 1024, "source_gram")
+
+    own = reduce_scatter(reduce_scatter(own, index, [0]), index, [2])
+    for bits in outer:
+        own = all_sum(own, bits)
+    own = all_gather(all_gather(own, index, [2]), index, [0])
+
+    stages = [[0], [2]] + outer
+
+    def whole_sum(terms):
+        for bits in stages:
+            terms = reduce_scatter(terms, index, bits)
+        for bits in reversed(stages):
+            terms = all_gather(terms, index, bits)
+        return terms
+
+    crossing = whole_sum(crossing)
+    source = whole_sum(source)
+
+    def across_halves(terms):
+        mine = index & 1
+        parts = terms.reshape(2, terms.shape[0] // 2, LANES)
+        part = lax.dynamic_index_in_dim(parts, mine, 0, keepdims=False)
+        return all_gather(part + exchange(part, 2), index, [0])
+
+    parts = invert_first(half_index, own, coupling_two, "level_first")
+    inverse = invert_second(parts, "level_second")
+    x, root = call(
+        panel_solve_kernel, (SQUARE, jax.ShapeDtypeStruct((384, LANES), F32)), (inverse, crossing), "panel_solve"
+    )
+    root = across_halves(root)
+    panel_one = update(panel_kernel, [q_two, q_one], [x], 3, "panel")
+    y, side = call(
+        source_solve_kernel, (SQUARE, jax.ShapeDtypeStruct((512, LANES), F32)), (inverse, x, source), "source_solve"
+    )
+    side = across_halves(side)
+    parts = invert_first(no_index, root, coupling_one[None], "root_first")
+    inverse = invert_second(parts, "root_second")
+    solution = update(
+        field_kernel,
+        [q_two, q_one, sources],
+        [inverse, side, x, y],
+        6,
+        "field",
+        [pltpu.VMEM((R, R), F32), pltpu.VMEM((R, R), F32)],
+    )
     return (panel_one, solution)
 
 

time: 94 us -> 97.6 us (1.038)
  blocking collectives: 43.1 us -> 0 us
  starting transfers between devices: 2.17 us -> 33.4 us
  waiting for transfers between devices: 9.62 us -> 17.8 us
  local copies, waits for them, and re-layouts: 1.51 us -> 7.29 us
  other arithmetic: 0.14 us -> 2.43 us
  Pallas kernels: 36.4 us -> 35.1 us
    all_to_all x2 -> x0, blocking collectives: 43.1 us -> none  [the longest x1 23.8 us: scatter_leaf(): return jnp.sum(lax.all_to_all(parts, 'leaf', 0, 0), axis=0)]
    ppermute x4 -> x31, starting transfers between devices: 2.17 us -> 33.4 us  [exchange(): return lax.ppermute(x, AXES, [(i, i ^ mask) for i in range(count)])]
    ppermute x4 -> x31, waiting for transfers between devices: 9.62 us -> 17.8 us  [exchange(): return lax.ppermute(x, AXES, [(i, i ^ mask) for i in range(count)])]
    unnamed x12 -> x18, local copies, waits for them, and re-layouts: 0.03 us -> 6.38 us
    pallas_call x3 -> x9, Pallas kernels: 30.2 us -> 27.8 us  [the longest x6 21.4 us: call(): pl.pallas_call(kernel, out_shape=out_shape, scratch_shapes=list(scratch),...]
    add x1 -> x6, other arithmetic: 0.06 us -> 2.01 us  [reduce_scatter(): got = got + part]
    pallas_call x2, Pallas kernels: 6.18 us -> 7.3 us  [update(): pl.pallas_call(kernel, grid=(rows // TILE,), in_specs=[spec] * len(tall)...]
  transfers between devices with their start and end apart: 4 -> 31, of which waited for: 3 -> 11; matrix products, arithmetic and copies ran while one was open for 0% -> 3% of each run, Pallas kernels for 3% -> 29%
where the time goes in v1:
time: 97.6 us; the launch traced here: 97.3 us
  Pallas kernels  35.1 us (36%)
  starting transfers between devices  33.4 us (34%)
  waiting for transfers between devices  17.8 us (18%)
  local copies, waits for them, and re-layouts  7.29 us (7%)
  other arithmetic  2.43 us (2%)
  between operations  1.21 us (1%)
    ppermute x31, starting transfers between devices, exchange(): return lax.ppermute(x, AXES, [(i, i ^ mask) for i in range(count)])  33.4 us
    pallas_call x6, Pallas kernels, call(): pl.pallas_call(kernel, out_shape=out_shape, scratch_shapes=list(scratch),...  21.4 us
    ppermute x31, waiting for transfers between devices, exchange(): return lax.ppermute(x, AXES, [(i, i ^ mask) for i in range(count)])  17.8 us
    pallas_call x2, Pallas kernels, update(): pl.pallas_call(kernel, grid=(rows // TILE,), in_specs=[spec] * len(tall)...  7.3 us
    pallas_call x3, Pallas kernels, gram(): pl.pallas_call(kernel, grid=(rows // TILE,), in_specs=[spec] * len(tall),...  6.45 us
    unnamed x18, local copies, waits for them, and re-layouts  6.38 us
    add x6, other arithmetic, reduce_scatter(): got = got + part  2.01 us
  transfers between devices with their start and end apart: 31, of which 11 were waited for; matrix products, arithmetic and copies ran while one was open for 3% of the time, Pallas kernels for 29%

profile of v1, /device:TPU:0, one launch (start us, length us, event | category | flops | bytes accessed | tf_op | source)
XLA Modules:
  0.0 97.3 jit_solution(14106668651289469088)
XLA Ops:
  0.7 1.6 %copy-done = f32[2048,256]{1,0:T(8,128)S(1)} copy-done((f32[2048,256]{1,0:T(8,128)S(1)}, f32[2048,256]{1,0:T(8,128)}, u32[]{:S(2)}) %copy-start) | copy-done | bytes 2097176
  2.2 1.5 %own_gram.1 = f32[384,128]{1,0:T(8,128)S(1)} custom-call(f32[2048,256]{1,0:T(8,128)S(1)} %copy-done), custom_call_target="tpu_custom_call" | custom-call | flops 536870912 | bytes 2097152 | tf_op jit(solution)/shard_map/own_gram/pallas_call | solution.py:133
  3.8 0.5 collective-permute-start
  4.3 1.6 %copy-done.2 = f32[2048,256]{1,0:T(8,128)S(1)} copy-done((f32[2048,256]{1,0:T(8,128)S(1)}, f32[2048,256]{1,0:T(8,128)}, u32[]{:S(2)}) %copy-start.2) | copy-done | bytes 2097176
  5.9 2.4 %cross_gram.1 = f32[896,128]{1,0:T(8,128)S(1)} custom-call(f32[2048,256]{1,0:T(8,128)S(1)} %copy-done.1, f32[2048,256]{1,0:T(8,128)S(1)} %copy-done.2), custom_call_target="tpu_custom_call" | custom-call | flops 1342177280 | bytes 4194304 | tf_op jit(solution)/shard_map/cross_gram/pallas_call | solution.py:133
  8.3 0.7 dynamic-slice_bitcast_fusion.1
  9.0 0.1 collective-permute-start.7
  9.0 0.0 collective-permute-done
  9.1 3.0 %collective-permute-start.1 = (f32[96,128]{1,0:T(8,128)S(1)}, f32[96,128]{1,0:T(8,128)S(1)}, u32[]{:S(2)}, u32[]{:S(2)}) collective-permute-start(f32[96,128]{1,0:T(8,128)S(1)} %dynamic-slice_bitcast_fusion.7), channel_id=1, source_target_pairs={{0,4},{1,5},{2,6},{3,7},{4,0},{5,1},{6,2},{7,3},{8,12},{9,13},{10,... | collective-permute-start | bytes 147464 | tf_op jit(solution)/shard_map/ppermute | solution.py:343
  12.1 1.6 %copy-done.3 = f32[2048,256]{1,0:T(8,128)S(1)} copy-done((f32[2048,256]{1,0:T(8,128)S(1)}, f32[2048,256]{1,0:T(8,128)}, u32[]{:S(2)}) %copy-start.3) | copy-done | bytes 2097176
  13.7 1.6 %copy-done.5 = f32[2048,256]{1,0:T(8,128)S(1)} copy-done((f32[2048,256]{1,0:T(8,128)S(1)}, f32[2048,256]{1,0:T(8,128)}, u32[]{:S(2)}) %copy-start.5) | copy-done | bytes 2097176
  15.3 2.6 %source_gram.1 = f32[1024,128]{1,0:T(8,128)S(1)} custom-call(f32[2048,256]{1,0:T(8,128)S(1)} %copy-done.1, f32[2048,256]{1,0:T(8,128)S(1)} %copy-done.3, f32[2048,256]{1,0:T(8,128)S(1)} %copy-done.5), custom_call_target="tpu_custom_call" | custom-call | flops 1610612736 | bytes 6291456 | tf_op jit(solution)/shard_map/source_gram/pallas_call | solution.py:133
  17.9 3.7 %collective-permute-start.4 = (f32[96,128]{1,0:T(8,128)S(1)}, f32[96,128]{1,0:T(8,128)S(1)}, u32[]{:S(2)}, u32[]{:S(2)}) collective-permute-start(f32[96,128]{1,0:T(8,128)S(1)} %bitcast_add_fusion.5), channel_id=1, source_target_pairs={{0,24},{1,25},{2,26},{3,27},{4,28},{5,29},{6,30},{7,31},{8,16},{9,... | collective-permute-start | bytes 147464 | tf_op jit(solution)/shard_map/ppermute | solution.py:343
  21.6 0.8 collective-permute-start.2
  22.4 0.1 collective-permute-start.19
  22.5 0.0 copy-start.7
  22.5 1.7 %collective-permute-done.4 = f32[96,128]{1,0:T(8,128)S(1)} collective-permute-done((f32[96,128]{1,0:T(8,128)S(1)}, f32[96,128]{1,0:T(8,128)S(1)}, u32[]{:S(2)}, u32[]{:S(2)}) %collective-permute-start.4) | collective-permute-done | bytes 49184 | tf_op jit(solution)/shard_map/ppermute | solution.py:343
  24.2 2.4 %collective-permute-done.3 = f32[96,128]{1,0:T(8,128)S(1)} collective-permute-done((f32[96,128]{1,0:T(8,128)S(1)}, f32[96,128]{1,0:T(8,128)S(1)}, u32[]{:S(2)}, u32[]{:S(2)}) %collective-permute-start.3) | collective-permute-done | bytes 49184 | tf_op jit(solution)/shard_map/ppermute | solution.py:343
  26.5 0.0 collective-permute-done.2
  26.6 0.6 collective-permute-start.5
  27.2 0.0 collective-permute-done.7
  27.2 1.0 bitcast_add_fusion.1
  28.2 1.5 %collective-permute-start.8 = (f32[224,128]{1,0:T(8,128)S(1)}, f32[224,128]{1,0:T(8,128)S(1)}, u32[]{:S(2)}, u32[]{:S(2)}) collective-permute-start(f32[224,128]{1,0:T(8,128)S(1)} %dynamic-slice_bitcast_fusion.4), channel_id=1, source_target_pairs={{0,4},{1,5},{2,6},{3,7},{4,0},{5,1},{6,2},{7,3},{8,12},{9,13},{10,... | collective-permute-start | bytes 344072 | tf_op jit(solution)/shard_map/ppermute | solution.py:343
  29.7 1.0 %collective-permute-done.5 = f32[96,128]{1,0:T(8,128)S(1)} collective-permute-done((f32[96,128]{1,0:T(8,128)S(1)}, f32[96,128]{1,0:T(8,128)S(1)}, u32[]{:S(2)}, u32[]{:S(2)}) %collective-permute-start.5) | collective-permute-done | bytes 49184 | tf_op jit(solution)/shard_map/ppermute | solution.py:343
  30.8 0.1 collective-permute-start.6
  30.8 1.0 %bitcast_add_fusion = f32[512,128]{1,0:T(8,128)S(1)} fusion(f32[512,128]{1,0:T(8,128)} %collective-permute-done.19, f32[2,512,128]{2,1,0:T(8,128)S(1)} %bitcast.92, s32[]{:T(128)S(6)} %select_n.150), kind=kLoop, calls=%fused_computation.4 | loop fusion | flops 65536 | bytes 786436 | tf_op jit(solution)/shard_map/add | solution.py:367
  31.9 1.0 %collective-permute-start.20 = (f32[256,128]{1,0:T(8,128)S(1)}, f32[256,128]{1,0:T(8,128)S(1)}, u32[]{:S(2)}, u32[]{:S(2)}) collective-permute-start(f32[256,128]{1,0:T(8,128)S(1)} %dynamic-slice_bitcast_fusion.3), channel_id=1, source_target_pairs={{0,4},{1,5},{2,6},{3,7},{4,0},{5,1},{6,2},{7,3},{8,12},{9,13},{10,... | collective-permute-start | bytes 393224 | tf_op jit(solution)/shard_map/ppermute | solution.py:343
  32.9 0.1 collective-permute-done.8
  33.1 0.6 collective-permute-start.9
  33.7 2.9 %collective-permute-start.11 = (f32[56,128]{1,0:T(8,128)S(1)}, f32[56,128]{1,0:T(8,128)S(1)}, u32[]{:S(2)}, u32[]{:S(2)}) collective-permute-start(f32[56,128]{1,0:T(8,128)S(1)} %get-tuple-element.52), channel_id=1, source_target_pairs={{0,24},{1,25},{2,26},{3,27},{4,28},{5,29},{6,30},{7,31},{8,16},{9,... | collective-permute-start | bytes 86024 | tf_op jit(solution)/shard_map/ppermute | solution.py:343
  36.6 0.0 collective-permute-start.10
  36.7 5.0 %level_first.1 = (f32[128,128]{1,0:T(8,128)S(1)}, f32[128,128]{1,0:T(8,128)S(1)}, f32[128,128]{1,0:T(8,128)S(1)}, f32[8,256]{1,0:T(8,128)S(1)}, f32[256,128]{1,0:T(8,128)S(1)}) custom-call(f32[384,128]{1,0:T(8,128)S(1)} %pad_maximum_fusion.5.gram_ref, f32[2,256,256]{2,1,0:T(8,128)S(1)} %copy-done.7), custom_call_target="tpu_custom_call" | custom-call | flops 5000000000 | bytes 262144 | tf_op jit(solution)/shard_map/level_first/pallas_call | solution.py:227
  41.7 4.9 %level_second.1.inverse = f32[256,256]{1,0:T(8,128)S(1)} custom-call(f32[128,128]{1,0:T(8,128)S(1)} %get-tuple-element.16.first, f32[128,128]{1,0:T(8,128)S(1)} %get-tuple-element.17.across, f32[128,128]{1,0:T(8,128)S(1)} %get-tuple-element.18.rest, f32[8,256]{1,0:T(8,128)S(1)} %get-tuple-element.19.row, f32[256,128]{1,0:T(8,128)S(1)} %get-tuple-element.20.col), custom_call_target="tpu_custom_call" | custom-call | flops 5000000000 | bytes 262144 | tf_op jit(solution)/shard_map/level_second/pallas_call | solution.py:227
  46.6 3.0 %collective-permute-start.13 = (f32[56,128]{1,0:T(8,128)S(1)}, f32[56,128]{1,0:T(8,128)S(1)}, u32[]{:S(2)}, u32[]{:S(2)}) collective-permute-start(f32[56,128]{1,0:T(8,128)S(1)} %get-tuple-element.33), channel_id=1, source_target_pairs={{0,16},{1,17},{2,18},{3,19},{4,20},{5,21},{6,22},{7,23},{8,24},{9,... | collective-permute-start | bytes 86024 | tf_op jit(solution)/shard_map/ppermute | solution.py:343
  49.6 1.5 %collective-permute-start.14 = (f32[56,128]{1,0:T(8,128)S(1)}, f32[56,128]{1,0:T(8,128)S(1)}, u32[]{:S(2)}, u32[]{:S(2)}) collective-permute-start(f32[56,128]{1,0:T(8,128)S(1)} %get-tuple-element.33), channel_id=1, source_target_pairs={{0,24},{1,25},{2,26},{3,27},{4,28},{5,29},{6,30},{7,31},{8,16},{9,... | collective-permute-start | bytes 86024 | tf_op jit(solution)/shard_map/ppermute | solution.py:343
  51.2 0.6 collective-permute-start.21
  51.7 2.9 %collective-permute-start.23 = (f32[64,128]{1,0:T(8,128)S(1)}, f32[64,128]{1,0:T(8,128)S(1)}, u32[]{:S(2)}, u32[]{:S(2)}) collective-permute-start(f32[64,128]{1,0:T(8,128)S(1)} %get-tuple-element.49), channel_id=1, source_target_pairs={{0,24},{1,25},{2,26},{3,27},{4,28},{5,29},{6,30},{7,31},{8,16},{9,... | collective-permute-start | bytes 98312 | tf_op jit(solution)/shard_map/ppermute | solution.py:343
  54.7 0.1 collective-permute-start.22
  54.8 0.8 collective-permute-done.21
  55.6 1.9 %collective-permute-done.23 = f32[64,128]{1,0:T(8,128)S(1)} collective-permute-done((f32[64,128]{1,0:T(8,128)S(1)}, f32[64,128]{1,0:T(8,128)S(1)}, u32[]{:S(2)}, u32[]{:S(2)}) %collective-permute-start.23) | collective-permute-done | bytes 32800 | tf_op jit(solution)/shard_map/ppermute | solution.py:343
  57.5 2.1 %collective-permute-done.22 = f32[64,128]{1,0:T(8,128)S(1)} collective-permute-done((f32[64,128]{1,0:T(8,128)S(1)}, f32[64,128]{1,0:T(8,128)S(1)}, u32[]{:S(2)}, u32[]{:S(2)}) %collective-permute-start.22) | collective-permute-done | bytes 32800 | tf_op jit(solution)/shard_map/ppermute | solution.py:343
  59.6 0.1 collective-permute-start.24
  59.7 1.5 %collective-permute-start.15 = (f32[224,128]{1,0:T(8,128)S(1)}, f32[224,128]{1,0:T(8,128)S(1)}, u32[]{:S(2)}, u32[]{:S(2)}) collective-permute-start(f32[224,128]{1,0:T(8,128)S(1)} %bitcast.109), channel_id=1, source_target_pairs={{0,4},{1,5},{2,6},{3,7},{4,0},{5,1},{6,2},{7,3},{8,12},{9,13},{10,... | collective-permute-start | bytes 344072 | tf_op jit(solution)/shard_map/ppermute | solution.py:343
  61.2 2.1 %collective-permute-start.25 = (f32[64,128]{1,0:T(8,128)S(1)}, f32[64,128]{1,0:T(8,128)S(1)}, u32[]{:S(2)}, u32[]{:S(2)}) collective-permute-start(f32[64,128]{1,0:T(8,128)S(1)} %get-tuple-element.31), channel_id=1, source_target_pairs={{0,16},{1,17},{2,18},{3,19},{4,20},{5,21},{6,22},{7,23},{8,24},{9,... | collective-permute-start | bytes 98312 | tf_op jit(solution)/shard_map/ppermute | solution.py:343
  63.3 2.2 %collective-permute-start.26 = (f32[64,128]{1,0:T(8,128)S(1)}, f32[64,128]{1,0:T(8,128)S(1)}, u32[]{:S(2)}, u32[]{:S(2)}) collective-permute-start(f32[64,128]{1,0:T(8,128)S(1)} %get-tuple-element.31), channel_id=1, source_target_pairs={{0,24},{1,25},{2,26},{3,27},{4,28},{5,29},{6,30},{7,31},{8,16},{9,... | collective-permute-start | bytes 98312 | tf_op jit(solution)/shard_map/ppermute | solution.py:343
  65.5 0.5 collective-permute-done.25
  66.0 3.0 %collective-permute-done.26 = f32[64,128]{1,0:T(8,128)S(1)} collective-permute-done((f32[64,128]{1,0:T(8,128)S(1)}, f32[64,128]{1,0:T(8,128)S(1)}, u32[]{:S(2)}, u32[]{:S(2)}) %collective-permute-start.26) | collective-permute-done | bytes 32800 | tf_op jit(solution)/shard_map/ppermute | solution.py:343
  69.0 0.7 collective-permute-start.27
  69.7 0.0 copy-start.4
  69.7 0.1 collective-permute-start.16
  69.8 4.2 %collective-permute-done.27 = f32[256,128]{1,0:T(8,128)S(1)} collective-permute-done((f32[256,128]{1,0:T(8,128)S(1)}, f32[256,128]{1,0:T(8,128)S(1)}, u32[]{:S(2)}, u32[]{:S(2)}) %collective-permute-start.27) | collective-permute-done | bytes 131104 | tf_op jit(solution)/shard_map/ppermute | solution.py:343
  74.1 1.1 %panel_solve.1 = (f32[256,256]{1,0:T(8,128)S(1)}, f32[384,128]{1,0:T(8,128)S(1)}) custom-call(f32[256,256]{1,0:T(8,128)S(1)} %level_second.1.inverse, f32[896,128]{1,0:T(8,128)S(1)} %pad_maximum_fusion.1.terms), custom_call_target="tpu_custom_call" | custom-call | bytes 262144 | tf_op jit(solution)/shard_map/panel_solve/pallas_call | solution.py:227
  75.2 1.8 %collective-permute-start.17 = (f32[192,128]{1,0:T(8,128)S(1)}, f32[192,128]{1,0:T(8,128)S(1)}, u32[]{:S(2)}, u32[]{:S(2)}) collective-permute-start(f32[192,128]{1,0:T(8,128)S(1)} %dynamic-slice_bitcast_fusion.5), channel_id=1, source_target_pairs={{0,2},{1,3},{2,0},{3,1},{4,6},{5,7},{6,4},{7,5},{8,10},{9,11},{10,... | collective-permute-start | bytes 294920 | tf_op jit(solution)/shard_map/ppermute | solution.py:343
  77.0 0.1 collective-permute-start.28
  77.1 2.8 %panel.1 = f32[2048,256]{1,0:T(8,128)} custom-call(f32[2048,256]{1,0:T(8,128)S(1)} %copy-done.1, f32[2048,256]{1,0:T(8,128)S(1)} %copy-done.4, f32[256,256]{1,0:T(8,128)S(1)} %get-tuple-element.21.x), custom_call_target="tpu_custom_call" | custom-call | flops 805306368 | bytes 6291456 | tf_op jit(solution)/shard_map/panel/pallas_call | solution.py:328
  79.8 0.2 collective-permute-done.17
  80.1 0.0 copy-start.8
  80.1 0.3 collective-permute-start.18
  80.5 0.6 source_solve.1
  81.2 1.4 %collective-permute-start.29 = (f32[256,128]{1,0:T(8,128)S(1)}, f32[256,128]{1,0:T(8,128)S(1)}, u32[]{:S(2)}, u32[]{:S(2)}) collective-permute-start(f32[256,128]{1,0:T(8,128)S(1)} %dynamic-slice_bitcast_fusion.2), channel_id=1, source_target_pairs={{0,2},{1,3},{2,0},{3,1},{4,6},{5,7},{6,4},{7,5},{8,10},{9,11},{10,... | collective-permute-start | bytes 393224 | tf_op jit(solution)/shard_map/ppermute | solution.py:343
  82.6 5.0 %root_first.1 = (f32[128,128]{1,0:T(8,128)S(1)}, f32[128,128]{1,0:T(8,128)S(1)}, f32[128,128]{1,0:T(8,128)S(1)}, f32[8,256]{1,0:T(8,128)S(1)}, f32[256,128]{1,0:T(8,128)S(1)}) custom-call(f32[384,128]{1,0:T(8,128)S(1)} %pad_maximum_fusion.6.gram_ref, f32[1,256,256]{2,1,0:T(8,128)S(1)} %bitcast.101), custom_call_target="tpu_custom_call" | custom-call | flops 5000000000 | bytes 262144 | tf_op jit(solution)/shard_map/root_first/pallas_call | solution.py:227
  87.6 0.3 collective-permute-start.30
  87.9 4.9 %root_second.1.inverse = f32[256,256]{1,0:T(8,128)S(1)} custom-call(f32[128,128]{1,0:T(8,128)S(1)} %get-tuple-element.23.first, f32[128,128]{1,0:T(8,128)S(1)} %get-tuple-element.24.across, f32[128,128]{1,0:T(8,128)S(1)} %get-tuple-element.25.rest, f32[8,256]{1,0:T(8,128)S(1)} %get-tuple-element.26.row, f32[256,128]{1,0:T(8,128)S(1)} %get-tuple-element.27.col), custom_call_target="tpu_custom_call" | custom-call | flops 5000000000 | bytes 262144 | tf_op jit(solution)/shard_map/root_second/pallas_call | solution.py:227
  92.8 4.5 %field.1 = f32[2048,256]{1,0:T(8,128)} custom-call(f32[2048,256]{1,0:T(8,128)S(1)} %copy-done.1, f32[2048,256]{1,0:T(8,128)S(1)} %copy-done.4, f32[2048,256]{1,0:T(8,128)S(1)} %copy-done.6, f32[256,256]{1,0:T(8,128)S(1)} %root_second.1.inverse, f32[512,128]{1,0:T(8,128)S(1)} %pad_maximum_fusion.3.side, f32[256,256]{1,0:T(8,128)S(1)} %get-tuple-element.21.x, ...), custom_call_target="tpu_custom_call" | custom-call | flops 1610612736 | bytes 8388608 | tf_op jit(solution)/shard_map/field/pallas_call | solution.py:328
  (72 shorter events, 0.7 us)
Async XLA Ops:
  0.6 1.6 %copy-start = (f32[2048,256]{1,0:T(8,128)S(1)}, f32[2048,256]{1,0:T(8,128)}, u32[]{:S(2)}) copy-start(f32[2048,256]{1,0:T(8,128)} %q_two.9) | copy-start | bytes 6291460
  2.2 2.1 %copy-start.1 = (f32[2048,256]{1,0:T(8,128)S(1)}, f32[2048,256]{1,0:T(8,128)}, u32[]{:S(2)}) copy-start(f32[2048,256]{1,0:T(8,128)} %q_two.9) | copy-start | bytes 6291460
  3.8 5.3 %collective-permute-start = (f32[192,128]{1,0:T(8,128)S(1)}, f32[192,128]{1,0:T(8,128)S(1)}, u32[]{:S(2)}, u32[]{:S(2)}) collective-permute-start(f32[192,128]{1,0:T(8,128)S(1)} %dynamic-slice_bitcast_fusion.6), channel_id=1, source_target_pairs={{0,1},{1,0},{2,3},{3,2},{4,5},{5,4},{6,7},{7,6},{8,9},{9,8},{10,11... | collective-permute-start | bytes 294920 | tf_op jit(solution)/shard_map/ppermute | solution.py:343
  4.3 1.6 %copy-start.2 = (f32[2048,256]{1,0:T(8,128)S(1)}, f32[2048,256]{1,0:T(8,128)}, u32[]{:S(2)}) copy-start(f32[2048,256]{1,0:T(8,128)} %q_one.7) | copy-start | bytes 6291460
  9.0 18.2 %collective-permute-start.7 = (f32[448,128]{1,0:T(8,128)}, f32[448,128]{1,0:T(8,128)}, u32[]{:S(2)}, u32[]{:S(2)}) collective-permute-start(f32[448,128]{1,0:T(8,128)} %dynamic-slice_bitcast_fusion.1), channel_id=1, source_target_pairs={{0,1},{1,0},{2,3},{3,2},{4,5},{5,4},{6,7},{7,6},{8,9},{9,8},{10,11... | collective-permute-start | bytes 688136 | tf_op jit(solution)/shard_map/ppermute | solution.py:343
  9.1 8.8 %collective-permute-start.1 = (f32[96,128]{1,0:T(8,128)S(1)}, f32[96,128]{1,0:T(8,128)S(1)}, u32[]{:S(2)}, u32[]{:S(2)}) collective-permute-start(f32[96,128]{1,0:T(8,128)S(1)} %dynamic-slice_bitcast_fusion.7), channel_id=1, source_target_pairs={{0,4},{1,5},{2,6},{3,7},{4,0},{5,1},{6,2},{7,3},{8,12},{9,13},{10,... | collective-permute-start | bytes 147464 | tf_op jit(solution)/shard_map/ppermute | solution.py:343
  12.1 1.6 %copy-start.3 = (f32[2048,256]{1,0:T(8,128)S(1)}, f32[2048,256]{1,0:T(8,128)}, u32[]{:S(2)}) copy-start(f32[2048,256]{1,0:T(8,128)} %q_one.7) | copy-start | bytes 6291460
  13.7 1.6 %copy-start.5 = (f32[2048,256]{1,0:T(8,128)S(1)}, f32[2048,256]{1,0:T(8,128)}, u32[]{:S(2)}) copy-start(f32[2048,256]{1,0:T(8,128)} %sources.3) | copy-start | bytes 6291460
  17.9 6.3 %collective-permute-start.4 = (f32[96,128]{1,0:T(8,128)S(1)}, f32[96,128]{1,0:T(8,128)S(1)}, u32[]{:S(2)}, u32[]{:S(2)}) collective-permute-start(f32[96,128]{1,0:T(8,128)S(1)} %bitcast_add_fusion.5), channel_id=1, source_target_pairs={{0,24},{1,25},{2,26},{3,27},{4,28},{5,29},{6,30},{7,31},{8,16},{9,... | collective-permute-start | bytes 147464 | tf_op jit(solution)/shard_map/ppermute | solution.py:343
  21.6 5.0 %collective-permute-start.3 = (f32[96,128]{1,0:T(8,128)S(1)}, f32[96,128]{1,0:T(8,128)S(1)}, u32[]{:S(2)}, u32[]{:S(2)}) collective-permute-start(f32[96,128]{1,0:T(8,128)S(1)} %bitcast_add_fusion.5), channel_id=1, source_target_pairs={{0,16},{1,17},{2,18},{3,19},{4,20},{5,21},{6,22},{7,23},{8,24},{9,... | collective-permute-start | bytes 147464 | tf_op jit(solution)/shard_map/ppermute | solution.py:343
  21.6 5.0 %collective-permute-start.2 = (f32[96,128]{1,0:T(8,128)S(1)}, f32[96,128]{1,0:T(8,128)S(1)}, u32[]{:S(2)}, u32[]{:S(2)}) collective-permute-start(f32[96,128]{1,0:T(8,128)S(1)} %bitcast_add_fusion.5), channel_id=1, source_target_pairs={{0,8},{1,9},{2,10},{3,11},{4,12},{5,13},{6,14},{7,15},{8,0},{9,1},... | collective-permute-start | bytes 147464 | tf_op jit(solution)/shard_map/ppermute | solution.py:343
  22.4 8.5 %collective-permute-start.19 = (f32[512,128]{1,0:T(8,128)S(1)}, f32[512,128]{1,0:T(8,128)}, u32[]{:S(2)}, u32[]{:S(2)}) collective-permute-start(f32[512,128]{1,0:T(8,128)S(1)} %dynamic-slice_bitcast_fusion), channel_id=1, source_target_pairs={{0,1},{1,0},{2,3},{3,2},{4,5},{5,4},{6,7},{7,6},{8,9},{9,8},{10,11... | collective-permute-start | bytes 786440 | tf_op jit(solution)/shard_map/ppermute | solution.py:343
  22.5 14.2 %copy-start.7 = (f32[2,256,256]{2,1,0:T(8,128)S(1)}, f32[2,256,256]{2,1,0:T(8,128)}, u32[]{:S(2)}) copy-start(f32[2,256,256]{2,1,0:T(8,128)} %coupling.1) | copy-start | bytes 1572868
  26.6 4.2 %collective-permute-start.5 = (f32[96,128]{1,0:T(8,128)S(1)}, f32[96,128]{1,0:T(8,128)S(1)}, u32[]{:S(2)}, u32[]{:S(2)}) collective-permute-start(f32[96,128]{1,0:T(8,128)S(1)} %add_add_fusion), channel_id=1, source_target_pairs={{0,4},{1,5},{2,6},{3,7},{4,0},{5,1},{6,2},{7,3},{8,12},{9,13},{10,... | collective-permute-start | bytes 147464 | tf_op jit(solution)/shard_map/ppermute | solution.py:343
  28.2 4.9 %collective-permute-start.8 = (f32[224,128]{1,0:T(8,128)S(1)}, f32[224,128]{1,0:T(8,128)S(1)}, u32[]{:S(2)}, u32[]{:S(2)}) collective-permute-start(f32[224,128]{1,0:T(8,128)S(1)} %dynamic-slice_bitcast_fusion.4), channel_id=1, source_target_pairs={{0,4},{1,5},{2,6},{3,7},{4,0},{5,1},{6,2},{7,3},{8,12},{9,13},{10,... | collective-permute-start | bytes 344072 | tf_op jit(solution)/shard_map/ppermute | solution.py:343
  30.8 5.9 %collective-permute-start.6 = (f32[192,128]{1,0:T(8,128)S(1)}, f32[192,128]{1,0:T(8,128)S(1)}, u32[]{:S(2)}, u32[]{:S(2)}) collective-permute-start(f32[192,128]{1,0:T(8,128)S(1)} %pad_maximum_fusion.7), channel_id=1, source_target_pairs={{0,1},{1,0},{2,3},{3,2},{4,5},{5,4},{6,7},{7,6},{8,9},{9,8},{10,11... | collective-permute-start | bytes 294920 | tf_op jit(solution)/shard_map/ppermute | solution.py:343
  31.9 19.3 %collective-permute-start.20 = (f32[256,128]{1,0:T(8,128)S(1)}, f32[256,128]{1,0:T(8,128)S(1)}, u32[]{:S(2)}, u32[]{:S(2)}) collective-permute-start(f32[256,128]{1,0:T(8,128)S(1)} %dynamic-slice_bitcast_fusion.3), channel_id=1, source_target_pairs={{0,4},{1,5},{2,6},{3,7},{4,0},{5,1},{6,2},{7,3},{8,12},{9,13},{10,... | collective-permute-start | bytes 393224 | tf_op jit(solution)/shard_map/ppermute | solution.py:343
  33.1 13.5 %collective-permute-start.9 = (f32[56,128]{1,0:T(8,128)S(1)}, f32[56,128]{1,0:T(8,128)S(1)}, u32[]{:S(2)}, u32[]{:S(2)}) collective-permute-start(f32[56,128]{1,0:T(8,128)S(1)} %get-tuple-element.51), channel_id=1, source_target_pairs={{0,8},{1,9},{2,10},{3,11},{4,12},{5,13},{6,14},{7,15},{8,0},{9,1},... | collective-permute-start | bytes 86024 | tf_op jit(solution)/shard_map/ppermute | solution.py:343
  33.7 12.9 %collective-permute-start.11 = (f32[56,128]{1,0:T(8,128)S(1)}, f32[56,128]{1,0:T(8,128)S(1)}, u32[]{:S(2)}, u32[]{:S(2)}) collective-permute-start(f32[56,128]{1,0:T(8,128)S(1)} %get-tuple-element.52), channel_id=1, source_target_pairs={{0,24},{1,25},{2,26},{3,27},{4,28},{5,29},{6,30},{7,31},{8,16},{9,... | collective-permute-start | bytes 86024 | tf_op jit(solution)/shard_map/ppermute | solution.py:343
  36.6 9.9 %collective-permute-start.10 = (f32[56,128]{1,0:T(8,128)S(1)}, f32[56,128]{1,0:T(8,128)S(1)}, u32[]{:S(2)}, u32[]{:S(2)}) collective-permute-start(f32[56,128]{1,0:T(8,128)S(1)} %get-tuple-element.53), channel_id=1, source_target_pairs={{0,16},{1,17},{2,18},{3,19},{4,20},{5,21},{6,22},{7,23},{8,24},{9,... | collective-permute-start | bytes 86024 | tf_op jit(solution)/shard_map/ppermute | solution.py:343
  46.6 8.1 %collective-permute-start.13 = (f32[56,128]{1,0:T(8,128)S(1)}, f32[56,128]{1,0:T(8,128)S(1)}, u32[]{:S(2)}, u32[]{:S(2)}) collective-permute-start(f32[56,128]{1,0:T(8,128)S(1)} %get-tuple-element.33), channel_id=1, source_target_pairs={{0,16},{1,17},{2,18},{3,19},{4,20},{5,21},{6,22},{7,23},{8,24},{9,... | collective-permute-start | bytes 86024 | tf_op jit(solution)/shard_map/ppermute | solution.py:343
  49.6 5.1 %collective-permute-start.12 = (f32[56,128]{1,0:T(8,128)S(1)}, f32[56,128]{1,0:T(8,128)S(1)}, u32[]{:S(2)}, u32[]{:S(2)}) collective-permute-start(f32[56,128]{1,0:T(8,128)S(1)} %get-tuple-element.33), channel_id=1, source_target_pairs={{0,8},{1,9},{2,10},{3,11},{4,12},{5,13},{6,14},{7,15},{8,0},{9,1},... | collective-permute-start | bytes 86024 | tf_op jit(solution)/shard_map/ppermute | solution.py:343
  49.6 10.0 %collective-permute-start.14 = (f32[56,128]{1,0:T(8,128)S(1)}, f32[56,128]{1,0:T(8,128)S(1)}, u32[]{:S(2)}, u32[]{:S(2)}) collective-permute-start(f32[56,128]{1,0:T(8,128)S(1)} %get-tuple-element.33), channel_id=1, source_target_pairs={{0,24},{1,25},{2,26},{3,27},{4,28},{5,29},{6,30},{7,31},{8,16},{9,... | collective-permute-start | bytes 86024 | tf_op jit(solution)/shard_map/ppermute | solution.py:343
  51.2 4.4 %collective-permute-start.21 = (f32[64,128]{1,0:T(8,128)S(1)}, f32[64,128]{1,0:T(8,128)S(1)}, u32[]{:S(2)}, u32[]{:S(2)}) collective-permute-start(f32[64,128]{1,0:T(8,128)S(1)} %get-tuple-element.48), channel_id=1, source_target_pairs={{0,8},{1,9},{2,10},{3,11},{4,12},{5,13},{6,14},{7,15},{8,0},{9,1},... | collective-permute-start | bytes 98312 | tf_op jit(solution)/shard_map/ppermute | solution.py:343
  51.7 5.7 %collective-permute-start.23 = (f32[64,128]{1,0:T(8,128)S(1)}, f32[64,128]{1,0:T(8,128)S(1)}, u32[]{:S(2)}, u32[]{:S(2)}) collective-permute-start(f32[64,128]{1,0:T(8,128)S(1)} %get-tuple-element.49), channel_id=1, source_target_pairs={{0,24},{1,25},{2,26},{3,27},{4,28},{5,29},{6,30},{7,31},{8,16},{9,... | collective-permute-start | bytes 98312 | tf_op jit(solution)/shard_map/ppermute | solution.py:343
  54.7 4.8 %collective-permute-start.22 = (f32[64,128]{1,0:T(8,128)S(1)}, f32[64,128]{1,0:T(8,128)S(1)}, u32[]{:S(2)}, u32[]{:S(2)}) collective-permute-start(f32[64,128]{1,0:T(8,128)S(1)} %get-tuple-element.50), channel_id=1, source_target_pairs={{0,16},{1,17},{2,18},{3,19},{4,20},{5,21},{6,22},{7,23},{8,24},{9,... | collective-permute-start | bytes 98312 | tf_op jit(solution)/shard_map/ppermute | solution.py:343
  59.6 6.0 %collective-permute-start.24 = (f32[64,128]{1,0:T(8,128)S(1)}, f32[64,128]{1,0:T(8,128)S(1)}, u32[]{:S(2)}, u32[]{:S(2)}) collective-permute-start(f32[64,128]{1,0:T(8,128)S(1)} %get-tuple-element.31), channel_id=1, source_target_pairs={{0,8},{1,9},{2,10},{3,11},{4,12},{5,13},{6,14},{7,15},{8,0},{9,1},... | collective-permute-start | bytes 98312 | tf_op jit(solution)/shard_map/ppermute | solution.py:343
  59.7 10.0 %collective-permute-start.15 = (f32[224,128]{1,0:T(8,128)S(1)}, f32[224,128]{1,0:T(8,128)S(1)}, u32[]{:S(2)}, u32[]{:S(2)}) collective-permute-start(f32[224,128]{1,0:T(8,128)S(1)} %bitcast.109), channel_id=1, source_target_pairs={{0,4},{1,5},{2,6},{3,7},{4,0},{5,1},{6,2},{7,3},{8,12},{9,13},{10,... | collective-permute-start | bytes 344072 | tf_op jit(solution)/shard_map/ppermute | solution.py:343
  61.2 4.8 %collective-permute-start.25 = (f32[64,128]{1,0:T(8,128)S(1)}, f32[64,128]{1,0:T(8,128)S(1)}, u32[]{:S(2)}, u32[]{:S(2)}) collective-permute-start(f32[64,128]{1,0:T(8,128)S(1)} %get-tuple-element.31), channel_id=1, source_target_pairs={{0,16},{1,17},{2,18},{3,19},{4,20},{5,21},{6,22},{7,23},{8,24},{9,... | collective-permute-start | bytes 98312 | tf_op jit(solution)/shard_map/ppermute | solution.py:343
  63.3 5.7 %collective-permute-start.26 = (f32[64,128]{1,0:T(8,128)S(1)}, f32[64,128]{1,0:T(8,128)S(1)}, u32[]{:S(2)}, u32[]{:S(2)}) collective-permute-start(f32[64,128]{1,0:T(8,128)S(1)} %get-tuple-element.31), channel_id=1, source_target_pairs={{0,24},{1,25},{2,26},{3,27},{4,28},{5,29},{6,30},{7,31},{8,16},{9,... | collective-permute-start | bytes 98312 | tf_op jit(solution)/shard_map/ppermute | solution.py:343
  69.0 5.0 %collective-permute-start.27 = (f32[256,128]{1,0:T(8,128)S(1)}, f32[256,128]{1,0:T(8,128)S(1)}, u32[]{:S(2)}, u32[]{:S(2)}) collective-permute-start(f32[256,128]{1,0:T(8,128)S(1)} %bitcast.106), channel_id=1, source_target_pairs={{0,4},{1,5},{2,6},{3,7},{4,0},{5,1},{6,2},{7,3},{8,12},{9,13},{10,... | collective-permute-start | bytes 393224 | tf_op jit(solution)/shard_map/ppermute | solution.py:343
  69.7 7.4 %copy-start.4 = (f32[2048,256]{1,0:T(8,128)S(1)}, f32[2048,256]{1,0:T(8,128)}, u32[]{:S(2)}) copy-start(f32[2048,256]{1,0:T(8,128)} %q_one.7) | copy-start | bytes 6291460
  69.7 4.3 %collective-permute-start.16 = (f32[448,128]{1,0:T(8,128)S(1)}, f32[448,128]{1,0:T(8,128)S(1)}, u32[]{:S(2)}, u32[]{:S(2)}) collective-permute-start(f32[448,128]{1,0:T(8,128)S(1)} %pad_maximum_fusion.4), channel_id=1, source_target_pairs={{0,1},{1,0},{2,3},{3,2},{4,5},{5,4},{6,7},{7,6},{8,9},{9,8},{10,11... | collective-permute-start | bytes 688136 | tf_op jit(solution)/shard_map/ppermute | solution.py:343
  75.2 4.9 %collective-permute-start.17 = (f32[192,128]{1,0:T(8,128)S(1)}, f32[192,128]{1,0:T(8,128)S(1)}, u32[]{:S(2)}, u32[]{:S(2)}) collective-permute-start(f32[192,128]{1,0:T(8,128)S(1)} %dynamic-slice_bitcast_fusion.5), channel_id=1, source_target_pairs={{0,2},{1,3},{2,0},{3,1},{4,6},{5,7},{6,4},{7,5},{8,10},{9,11},{10,... | collective-permute-start | bytes 294920 | tf_op jit(solution)/shard_map/ppermute | solution.py:343
  77.0 3.4 %collective-permute-start.28 = (f32[512,128]{1,0:T(8,128)S(1)}, f32[512,128]{1,0:T(8,128)S(1)}, u32[]{:S(2)}, u32[]{:S(2)}) collective-permute-start(f32[512,128]{1,0:T(8,128)S(1)} %pad_maximum_fusion.2), channel_id=1, source_target_pairs={{0,1},{1,0},{2,3},{3,2},{4,5},{5,4},{6,7},{7,6},{8,9},{9,8},{10,11... | collective-permute-start | bytes 786440 | tf_op jit(solution)/shard_map/ppermute | solution.py:343
  80.1 2.5 %copy-start.8 = (f32[256,256]{1,0:T(8,128)S(1)}, f32[256,256]{1,0:T(8,128)}, u32[]{:S(2)}) copy-start(f32[256,256]{1,0:T(8,128)} %param.9) | copy-start | bytes 786436
  80.1 2.4 %collective-permute-start.18 = (f32[192,128]{1,0:T(8,128)S(1)}, f32[192,128]{1,0:T(8,128)S(1)}, u32[]{:S(2)}, u32[]{:S(2)}) collective-permute-start(f32[192,128]{1,0:T(8,128)S(1)} %fusion.7), channel_id=1, source_target_pairs={{0,1},{1,0},{2,3},{3,2},{4,5},{5,4},{6,7},{7,6},{8,9},{9,8},{10,11... | collective-permute-start | bytes 294920 | tf_op jit(solution)/shard_map/ppermute | solution.py:343
  81.2 6.4 %collective-permute-start.29 = (f32[256,128]{1,0:T(8,128)S(1)}, f32[256,128]{1,0:T(8,128)S(1)}, u32[]{:S(2)}, u32[]{:S(2)}) collective-permute-start(f32[256,128]{1,0:T(8,128)S(1)} %dynamic-slice_bitcast_fusion.2), channel_id=1, source_target_pairs={{0,2},{1,3},{2,0},{3,1},{4,6},{5,7},{6,4},{7,5},{8,10},{9,11},{10,... | collective-permute-start | bytes 393224 | tf_op jit(solution)/shard_map/ppermute | solution.py:343
  87.6 5.1 %collective-permute-start.30 = (f32[256,128]{1,0:T(8,128)S(1)}, f32[256,128]{1,0:T(8,128)S(1)}, u32[]{:S(2)}, u32[]{:S(2)}) collective-permute-start(f32[256,128]{1,0:T(8,128)S(1)} %fusion.6), channel_id=1, source_target_pairs={{0,1},{1,0},{2,3},{3,2},{4,5},{5,4},{6,7},{7,6},{8,9},{9,8},{10,11... | collective-permute-start | bytes 393224 | tf_op jit(solution)/shard_map/ppermute | solution.py:343
  87.9 4.9 %copy-start.6 = (f32[2048,256]{1,0:T(8,128)S(1)}, f32[2048,256]{1,0:T(8,128)}, u32[]{:S(2)}) copy-start(f32[2048,256]{1,0:T(8,128)} %sources.3) | copy-start | bytes 6291460

commit v2 on v1

--- a/solution.py
+++ b/solution.py
@@ -13,9 +13,9 @@
 BF16 = jnp.bfloat16
 R = 256
 LANES = 128
-PANEL = 32
 TILE = 512
 VMEM_LIMIT = 40 * 1024 * 1024
+OWN, CROSS, PROJECTED, ROOT, SIDE, TERMS = 0, 384, 896, 1408, 1792, 2304
 
 
 def split2(x):
@@ -70,77 +70,75 @@
     return jnp.concatenate([ref[row : row + 256, :], ref[row + 256 : row + 512, :]], axis=1)
 
 
-def zero_first(acc):
-    @pl.when(pl.program_id(0) == 0)
-    def _():
-        acc[...] = jnp.zeros_like(acc)
-
-
-def at_last(body):
-    pl.when(pl.program_id(0) == pl.num_programs(0) - 1)(body)
-
-
-def own_gram_kernel(q_two, out, acc):
-    zero_first(acc)
-    h2, l2 = split2(q_two[...])
-    acc[0] += dot_t(h2, h2)
-    acc[1] += dot_t(h2, l2)
-
-    @at_last
-    def _():
-        low = acc[1]
-        store_symmetric(out, 0, acc[0] + low + low.T)
-
-
-def cross_gram_kernel(q_two, q_one, out, acc):
-    zero_first(acc)
-    h2, l2 = split2(q_two[...])
-    h1, l1 = split2(q_one[...])
-    acc[0] += dot_t(h2, h1) + dot_t(h2, l1) + dot_t(l2, h1)
-    acc[1] += dot_t(h1, h1)
-    acc[2] += dot_t(h1, l1)
-
-    @at_last
-    def _():
-        store_square(out, 0, acc[0])
-        low = acc[2]
-        store_symmetric(out, 512, acc[1] + low + low.T)
-
-
-def source_gram_kernel(q_two, q_one, sources, out, acc):
-    zero_first(acc)
-    h2, l2 = split2(q_two[...])
-    h1, l1 = split2(q_one[...])
-    hs, ls = split2(sources[...])
-    acc[0] += dot_t(h2, hs) + dot_t(h2, ls) + dot_t(l2, hs)
-    acc[1] += dot_t(h1, hs) + dot_t(h1, ls) + dot_t(l1, hs)
-
-    @at_last
-    def _():
-        store_square(out, 0, acc[0])
-        store_square(out, 512, acc[1])
+def gram_kernel(q_two, q_one, sources, keep, send, b2, b1, bs, acc, packed, sems):
+    tiles = b2.shape[0] // TILE
+    pairs = ((q_two, b2), (q_one, b1), (sources, bs))
+
+    def copy(tile, which):
+        here = pl.ds(tile * TILE, TILE)
+        source, target = pairs[which]
+        return pltpu.make_async_copy(source.at[here], target.at[here], sems.at[which, tile])
+
+    for tile in range(tiles):
+        for which in range(3):
+            copy(tile, which).start()
+    acc[...] = jnp.zeros_like(acc)
+
+    def step(tile, carry):
+        for which in range(3):
+            copy(tile, which).wait()
+        here = pl.ds(pl.multiple_of(tile * TILE, TILE), TILE)
+        h2, l2 = split2(b2[here, :])
+        h1, l1 = split2(b1[here, :])
+        hs, ls = split2(bs[here, :])
+        acc[0] += dot_t(h2, h2)
+        acc[1] += dot_t(h2, l2)
+        acc[2] += dot_t(h2, h1) + dot_t(h2, l1) + dot_t(l2, h1)
+        acc[3] += dot_t(h2, hs) + dot_t(h2, ls) + dot_t(l2, hs)
+        acc[4] += dot_t(h1, h1)
+        acc[5] += dot_t(h1, l1)
+        acc[6] += dot_t(h1, hs) + dot_t(h1, ls) + dot_t(l1, hs)
+        return carry
+
+    lax.fori_loop(0, tiles, step, 0)
+    low = acc[1]
+    store_symmetric(packed, OWN, acc[0] + low + low.T)
+    store_square(packed, CROSS, acc[2])
+    store_square(packed, PROJECTED, acc[3])
+    low = acc[5]
+    store_symmetric(packed, ROOT, acc[4] + low + low.T)
+    store_square(packed, SIDE, acc[6])
+    mine = lax.rem(lax.axis_index("group"), 2)
+    half = TERMS // 2
+    keep[...] = packed[pl.ds(pl.multiple_of(mine * half, 8), half), :]
+    send[...] = packed[pl.ds(pl.multiple_of((1 - mine) * half, 8), half), :]
+
+
+def gram(q_two, q_one, sources):
+    rows = q_two.shape[0]
+    part = jax.ShapeDtypeStruct((TERMS // 2, LANES), F32)
+    return pl.pallas_call(
+        gram_kernel,
+        in_specs=[pl.BlockSpec(memory_space=pl.ANY)] * 3,
+        out_shape=(part, part),
+        scratch_shapes=[
+            pltpu.VMEM((rows, R), F32),
+            pltpu.VMEM((rows, R), F32),
+            pltpu.VMEM((rows, R), F32),
+            pltpu.VMEM((7, R, R), F32),
+            pltpu.VMEM((TERMS, LANES), F32),
+            pltpu.SemaphoreType.DMA((3, rows // TILE)),
+        ],
+        compiler_params=pltpu.CompilerParams(vmem_limit_bytes=60 * 1024 * 1024),
+        cost_estimate=estimate(13, rows, 3),
+        name="gram",
+    )(q_two, q_one, sources)
 
 
 def estimate(passes, rows, arrays):
     return pl.CostEstimate(
         flops=2 * passes * rows * R * R, bytes_accessed=4 * arrays * rows * R, transcendentals=0
     )
-
-
-def gram(kernel, tall, blocks, passes, packed, name):
-    rows = tall[0].shape[0]
-    spec = pl.BlockSpec((TILE, R), lambda i: (i, 0))
-    return pl.pallas_call(
-        kernel,
-        grid=(rows // TILE,),
-        in_specs=[spec] * len(tall),
-        out_specs=pl.BlockSpec((packed, LANES), lambda i: (0, 0)),
-        out_shape=jax.ShapeDtypeStruct((packed, LANES), F32),
-        scratch_shapes=[pltpu.VMEM((blocks, R, R), F32)],
-        compiler_params=pltpu.CompilerParams(vmem_limit_bytes=VMEM_LIMIT),
-        cost_estimate=estimate(passes, rows, len(tall)),
-        name=name,
-    )(*tall)
 
 
 def spread_lane(x, lane):
@@ -235,7 +233,7 @@
 
 
 def first_kernel(which, gram_ref, coupling, first_out, across_out, rest_out, row_out, col_out, cols, rows):
-    matrix = coupling[which()] + load_symmetric(gram_ref, 0)
+    matrix = coupling[which()] + load_symmetric(gram_ref, OWN)
     eye = lax.broadcasted_iota(jnp.int32, (R, R), 0) == lax.broadcasted_iota(jnp.int32, (R, R), 1)
     diagonal = jnp.where(eye, matrix, 0.0)
     scale_row = lax.rsqrt(jnp.sum(diagonal, axis=0, keepdims=True))
@@ -290,16 +288,16 @@
 
 
 def panel_solve_kernel(inverse, terms, x_out, root_out):
-    cross = load_square(terms, 0)
+    cross = load_square(terms, CROSS)
     x = dot_full(inverse[...], cross)
     x_out[...] = x
-    store_symmetric(root_out, 0, load_symmetric(terms, 512) - dot_t_full(cross, x))
+    store_symmetric(root_out, 0, load_symmetric(terms, ROOT) - dot_t_full(cross, x))
 
 
 def source_solve_kernel(inverse, x, terms, y_out, side_out):
-    projected = load_square(terms, 0)
+    projected = load_square(terms, PROJECTED)
     y_out[...] = dot_full(inverse[...], projected)
-    store_square(side_out, 0, load_square(terms, 512) - dot_t_full(x[...], projected))
+    store_square(side_out, 0, load_square(terms, SIDE) - dot_t_full(x[...], projected))
 
 
 def dot_three(lh, ll, rh, rl):
@@ -343,93 +341,50 @@
     return lax.ppermute(x, AXES, [(i, i ^ mask) for i in range(count)])
 
 
-def code_of(index, bits):
-    code = 0
-    for place, bit in enumerate(bits):
-        code = code | ((index >> bit) & 1) << place
-    return code
-
-
-def mask_of(code, bits):
-    return sum(1 << bit for place, bit in enumerate(bits) if code >> place & 1)
-
-
-def reduce_scatter(x, index, bits):
-    count = 1 << len(bits)
-    mine = code_of(index, bits)
-    parts = x.reshape(count, x.shape[0] // count, x.shape[1])
-    got = lax.dynamic_index_in_dim(parts, mine, 0, keepdims=False)
-    arrived = []
-    for other in range(1, count):
-        part = lax.dynamic_index_in_dim(parts, mine ^ other, 0, keepdims=False)
-        arrived.append(exchange(part, mask_of(other, bits)))
-    for part in arrived:
-        got = got + part
-    return got
-
-
-def all_gather(x, index, bits):
-    count = 1 << len(bits)
-    mine = code_of(index, bits)
-    pieces = [x] + [exchange(x, mask_of(other, bits)) for other in range(1, count)]
-    if count == 2:
-        low = jnp.where(mine == 0, pieces[0], pieces[1])
-        high = jnp.where(mine == 0, pieces[1], pieces[0])
-        return jnp.concatenate([low, high], axis=0)
-    out = jnp.zeros((count,) + x.shape, x.dtype)
-    for other, piece in enumerate(pieces):
-        out = lax.dynamic_update_index_in_dim(out, piece, mine ^ other, 0)
-    return out.reshape(count * x.shape[0], x.shape[1])
-
-
-def all_sum(x, bits):
-    count = 1 << len(bits)
-    arrived = [exchange(x, mask_of(other, bits)) for other in range(1, count)]
-    for part in arrived:
-        x = x + part
-    return x
+def scatter_sum(x, index, bit):
+    mine = (index >> bit) & 1
+    parts = x.reshape(2, x.shape[0] // 2, x.shape[1])
+    sent = lax.dynamic_index_in_dim(parts, 1 - mine, 0, keepdims=False)
+    kept = lax.dynamic_index_in_dim(parts, mine, 0, keepdims=False)
+    return kept + exchange(sent, 1 << bit)
+
+
+def gather(x, index, bit):
+    mine = (index >> bit) & 1
+    other = exchange(x, 1 << bit)
+    low = jnp.where(mine == 0, x, other)
+    high = jnp.where(mine == 0, other, x)
+    return jnp.concatenate([low, high], axis=0)
 
 
 def per_device(q_two, q_one, sources, coupling_two, coupling_one):
     index = lax.axis_index(AXES)
-    leaf_end = lax.axis_size("leaf").bit_length() + 1
-    outer = [list(range(low, min(low + 2, leaf_end))) for low in range(3, leaf_end, 2)]
-    own = gram(own_gram_kernel, [q_two], 2, 2, 384, "own_gram")
-    crossing = gram(cross_gram_kernel, [q_two, q_one], 3, 5, 896, "cross_gram")
-    source = gram(source_gram_kernel, [q_two, q_one, sources], 2, 6, 1024, "source_gram")
-
-    own = reduce_scatter(reduce_scatter(own, index, [0]), index, [2])
-    for bits in outer:
-        own = all_sum(own, bits)
-    own = all_gather(all_gather(own, index, [2]), index, [0])
-
-    stages = [[0], [2]] + outer
-
-    def whole_sum(terms):
-        for bits in stages:
-            terms = reduce_scatter(terms, index, bits)
-        for bits in reversed(stages):
-            terms = all_gather(terms, index, bits)
-        return terms
-
-    crossing = whole_sum(crossing)
-    source = whole_sum(source)
+    leaf_bits = list(range(2, lax.axis_size("leaf").bit_length() + 1))
+    orders = (leaf_bits, leaf_bits[1:] + leaf_bits[:1])
+    keep, send = gram(q_two, q_one, sources)
+    terms = keep + exchange(send, 1)
+    parts = [terms[: TERMS // 4], terms[TERMS // 4 :]]
+    for step in range(len(leaf_bits)):
+        parts = [scatter_sum(x, index, order[step]) for x, order in zip(parts, orders)]
+    for step in reversed(range(len(leaf_bits))):
+        parts = [gather(x, index, order[step]) for x, order in zip(parts, orders)]
+    terms = gather(jnp.concatenate(parts, axis=0), index, 0)
 
     def across_halves(terms):
         mine = index & 1
         parts = terms.reshape(2, terms.shape[0] // 2, LANES)
         part = lax.dynamic_index_in_dim(parts, mine, 0, keepdims=False)
-        return all_gather(part + exchange(part, 2), index, [0])
-
-    parts = invert_first(half_index, own, coupling_two, "level_first")
+        return gather(part + exchange(part, 2), index, 0)
+
+    parts = invert_first(half_index, terms, coupling_two, "level_first")
     inverse = invert_second(parts, "level_second")
     x, root = call(
-        panel_solve_kernel, (SQUARE, jax.ShapeDtypeStruct((384, LANES), F32)), (inverse, crossing), "panel_solve"
+        panel_solve_kernel, (SQUARE, jax.ShapeDtypeStruct((384, LANES), F32)), (inverse, terms), "panel_solve"
     )
     root = across_halves(root)
     panel_one = update(panel_kernel, [q_two, q_one], [x], 3, "panel")
     y, side = call(
-        source_solve_kernel, (SQUARE, jax.ShapeDtypeStruct((512, LANES), F32)), (inverse, x, source), "source_solve"
+        source_solve_kernel, (SQUARE, jax.ShapeDtypeStruct((512, LANES), F32)), (inverse, x, terms), "source_solve"
     )
     side = across_halves(side)
     parts = invert_first(no_index, root, coupling_one[None], "root_first")

time: 97.6 us -> 82.9 us (0.85)
  starting transfers between devices: 33.4 us -> 24.8 us
  local copies, waits for them, and re-layouts: 7.29 us -> 0.19 us
  waiting for transfers between devices: 17.8 us -> 19.1 us
    ppermute x31 -> x18, starting transfers between devices: 33.4 us -> 24.8 us  [exchange(): return lax.ppermute(x, AXES, [(i, i ^ mask) for i in range(count)])]
    unnamed x18 -> x10, local copies, waits for them, and re-layouts: 6.38 us -> 0.03 us
    ppermute x31 -> x18, waiting for transfers between devices: 17.8 us -> 19.1 us  [exchange(): return lax.ppermute(x, AXES, [(i, i ^ mask) for i in range(count)])]
    pallas_call x3 -> x1, Pallas kernels: 6.45 us -> 7.2 us  [gram(): pl.pallas_call(gram_kernel, in_specs=[pl.BlockSpec(memory_space=pl.ANY)]...]
  transfers between devices with their start and end apart: 31 -> 18, of which waited for: 11 -> 13; matrix products, arithmetic and copies ran while one was open for 3% -> 0% of each run, Pallas kernels for 29% -> 15%
where the time goes in v2:
time: 82.9 us; the launch traced here: 82.7 us
  Pallas kernels  36 us (43%)
  starting transfers between devices  24.8 us (30%)
  waiting for transfers between devices  19.1 us (23%)
  other arithmetic  1.62 us (2%)
  between operations  1.01 us (1%)
    ppermute x18, starting transfers between devices, exchange(): return lax.ppermute(x, AXES, [(i, i ^ mask) for i in range(count)])  24.8 us
    pallas_call x6, Pallas kernels, call(): pl.pallas_call(kernel, out_shape=out_shape, scratch_shapes=list(scratch),...  21.6 us
    ppermute x18, waiting for transfers between devices, exchange(): return lax.ppermute(x, AXES, [(i, i ^ mask) for i in range(count)])  19.1 us
    pallas_call x2, Pallas kernels, update(): pl.pallas_call(kernel, grid=(rows // TILE,), in_specs=[spec] * len(tall)...  7.29 us
    pallas_call x1, Pallas kernels, gram(): pl.pallas_call(gram_kernel, in_specs=[pl.BlockSpec(memory_space=pl.ANY)]...  7.2 us
  transfers between devices with their start and end apart: 18, of which 13 were waited for; matrix products, arithmetic and copies ran while one was open for 0% of the time, Pallas kernels for 15%

profile of v2, /device:TPU:0, one launch (start us, length us, event | category | flops | bytes accessed | tf_op | source)
XLA Modules:
  0.0 82.7 jit_solution(12413097732182400120)
XLA Ops:
  0.6 7.2 %gram.1 = (f32[1152,128]{1,0:T(8,128)}, f32[1152,128]{1,0:T(8,128)}) custom-call(f32[2048,256]{1,0:T(8,128)} %q_two.5, f32[2048,256]{1,0:T(8,128)} %q_one.5, f32[2048,256]{1,0:T(8,128)} %sources.3), custom_call_target="tpu_custom_call" | custom-call | flops 3489660928 | bytes 6291456 | tf_op jit(solution)/shard_map/gram/pallas_call | solution.py:120
  7.8 0.5 collective-permute-start
  8.3 1.8 %collective-permute-done = f32[1152,128]{1,0:T(8,128)S(1)} collective-permute-done((f32[1152,128]{1,0:T(8,128)}, f32[1152,128]{1,0:T(8,128)S(1)}, u32[]{:S(2)}, u32[]{:S(2)}) %collective-permute-start) | collective-permute-done | bytes 589856 | tf_op jit(solution)/shard_map/ppermute | solution.py:341
  10.2 1.1 %add.67 = f32[1152,128]{1,0:T(8,128)S(1)} add(f32[1152,128]{1,0:T(8,128)} %get-tuple-element.18, f32[1152,128]{1,0:T(8,128)S(1)} %collective-permute-done) | non-fusion elementwise | flops 147456 | bytes 1769472 | tf_op jit(solution)/shard_map/add | solution.py:365
  11.4 2.9 %collective-permute-start.1 = (f32[288,128]{1,0:T(8,128)S(1)}, f32[288,128]{1,0:T(8,128)S(1)}, u32[]{:S(2)}, u32[]{:S(2)}) collective-permute-start(f32[288,128]{1,0:T(8,128)S(1)} %dynamic-slice_bitcast_fusion.1), channel_id=1, source_target_pairs={{0,4},{1,5},{2,6},{3,7},{4,0},{5,1},{6,2},{7,3},{8,12},{9,13},{10,... | collective-permute-start | bytes 442376 | tf_op jit(solution)/shard_map/ppermute | solution.py:341
  14.3 1.6 %collective-permute-start.7 = (f32[288,128]{1,0:T(8,128)S(1)}, f32[288,128]{1,0:T(8,128)S(1)}, u32[]{:S(2)}, u32[]{:S(2)}) collective-permute-start(f32[288,128]{1,0:T(8,128)S(1)} %dynamic-slice_bitcast_fusion), channel_id=1, source_target_pairs={{0,8},{1,9},{2,10},{3,11},{4,12},{5,13},{6,14},{7,15},{8,0},{9,1},... | collective-permute-start | bytes 442376 | tf_op jit(solution)/shard_map/ppermute | solution.py:341
  16.0 2.5 %collective-permute-done.1 = f32[288,128]{1,0:T(8,128)S(1)} collective-permute-done((f32[288,128]{1,0:T(8,128)S(1)}, f32[288,128]{1,0:T(8,128)S(1)}, u32[]{:S(2)}, u32[]{:S(2)}) %collective-permute-start.1) | collective-permute-done | bytes 147488 | tf_op jit(solution)/shard_map/ppermute | solution.py:341
  18.5 1.9 %collective-permute-start.2 = (f32[144,128]{1,0:T(8,128)S(1)}, f32[144,128]{1,0:T(8,128)S(1)}, u32[]{:S(2)}, u32[]{:S(2)}) collective-permute-start(f32[144,128]{1,0:T(8,128)S(1)} %dynamic-slice_bitcast_fusion.5), channel_id=1, source_target_pairs={{0,8},{1,9},{2,10},{3,11},{4,12},{5,13},{6,14},{7,15},{8,0},{9,1},... | collective-permute-start | bytes 221192 | tf_op jit(solution)/shard_map/ppermute | solution.py:341
  20.4 0.0 collective-permute-done.7
  20.5 2.7 %collective-permute-start.8 = (f32[144,128]{1,0:T(8,128)S(1)}, f32[144,128]{1,0:T(8,128)S(1)}, u32[]{:S(2)}, u32[]{:S(2)}) collective-permute-start(f32[144,128]{1,0:T(8,128)S(1)} %dynamic-slice_bitcast_fusion.4), channel_id=1, source_target_pairs={{0,16},{1,17},{2,18},{3,19},{4,20},{5,21},{6,22},{7,23},{8,24},{9,... | collective-permute-start | bytes 221192 | tf_op jit(solution)/shard_map/ppermute | solution.py:341
  23.1 0.0 collective-permute-done.2
  23.1 2.7 %collective-permute-start.3 = (f32[72,128]{1,0:T(8,128)S(1)}, f32[72,128]{1,0:T(8,128)S(1)}, u32[]{:S(2)}, u32[]{:S(2)}) collective-permute-start(f32[72,128]{1,0:T(8,128)S(1)} %dynamic-slice_bitcast_fusion.7), channel_id=1, source_target_pairs={{0,16},{1,17},{2,18},{3,19},{4,20},{5,21},{6,22},{7,23},{8,24},{9,... | collective-permute-start | bytes 110600 | tf_op jit(solution)/shard_map/ppermute | solution.py:341
  25.9 1.5 %collective-permute-done.8 = f32[144,128]{1,0:T(8,128)S(1)} collective-permute-done((f32[144,128]{1,0:T(8,128)S(1)}, f32[144,128]{1,0:T(8,128)S(1)}, u32[]{:S(2)}, u32[]{:S(2)}) %collective-permute-start.8) | collective-permute-done | bytes 73760 | tf_op jit(solution)/shard_map/ppermute | solution.py:341
  27.4 1.6 %collective-permute-start.9 = (f32[72,128]{1,0:T(8,128)S(1)}, f32[72,128]{1,0:T(8,128)S(1)}, u32[]{:S(2)}, u32[]{:S(2)}) collective-permute-start(f32[72,128]{1,0:T(8,128)S(1)} %dynamic-slice_bitcast_fusion.6), channel_id=1, source_target_pairs={{0,4},{1,5},{2,6},{3,7},{4,0},{5,1},{6,2},{7,3},{8,12},{9,13},{10,... | collective-permute-start | bytes 110600 | tf_op jit(solution)/shard_map/ppermute | solution.py:341
  28.9 0.0 collective-permute-done.3
  29.0 1.8 %collective-permute-start.4 = (f32[72,128]{1,0:T(8,128)S(1)}, f32[72,128]{1,0:T(8,128)S(1)}, u32[]{:S(2)}, u32[]{:S(2)}) collective-permute-start(f32[72,128]{1,0:T(8,128)S(1)} %bitcast_add_fusion.5), channel_id=1, source_target_pairs={{0,16},{1,17},{2,18},{3,19},{4,20},{5,21},{6,22},{7,23},{8,24},{9,... | collective-permute-start | bytes 110600 | tf_op jit(solution)/shard_map/ppermute | solution.py:341
  30.7 0.8 %collective-permute-done.9 = f32[72,128]{1,0:T(8,128)S(1)} collective-permute-done((f32[72,128]{1,0:T(8,128)S(1)}, f32[72,128]{1,0:T(8,128)S(1)}, u32[]{:S(2)}, u32[]{:S(2)}) %collective-permute-start.9) | collective-permute-done | bytes 36896 | tf_op jit(solution)/shard_map/ppermute | solution.py:341
  31.6 1.5 %collective-permute-start.10 = (f32[72,128]{1,0:T(8,128)S(1)}, f32[72,128]{1,0:T(8,128)S(1)}, u32[]{:S(2)}, u32[]{:S(2)}) collective-permute-start(f32[72,128]{1,0:T(8,128)S(1)} %bitcast_add_fusion.4), channel_id=1, source_target_pairs={{0,4},{1,5},{2,6},{3,7},{4,0},{5,1},{6,2},{7,3},{8,12},{9,13},{10,... | collective-permute-start | bytes 110600 | tf_op jit(solution)/shard_map/ppermute | solution.py:341
  33.1 1.3 %collective-permute-done.4 = f32[72,128]{1,0:T(8,128)S(1)} collective-permute-done((f32[72,128]{1,0:T(8,128)S(1)}, f32[72,128]{1,0:T(8,128)S(1)}, u32[]{:S(2)}, u32[]{:S(2)}) %collective-permute-start.4) | collective-permute-done | bytes 36896 | tf_op jit(solution)/shard_map/ppermute | solution.py:341
  34.4 0.5 collective-permute-start.5
  34.9 0.7 collective-permute-done.10
  35.6 2.2 %collective-permute-start.11 = (f32[144,128]{1,0:T(8,128)S(1)}, f32[144,128]{1,0:T(8,128)S(1)}, u32[]{:S(2)}, u32[]{:S(2)}) collective-permute-start(f32[144,128]{1,0:T(8,128)S(1)} %pad_maximum_fusion.7), channel_id=1, source_target_pairs={{0,16},{1,17},{2,18},{3,19},{4,20},{5,21},{6,22},{7,23},{8,24},{9,... | collective-permute-start | bytes 221192 | tf_op jit(solution)/shard_map/ppermute | solution.py:341
  37.8 1.0 %collective-permute-done.5 = f32[144,128]{1,0:T(8,128)S(1)} collective-permute-done((f32[144,128]{1,0:T(8,128)S(1)}, f32[144,128]{1,0:T(8,128)S(1)}, u32[]{:S(2)}, u32[]{:S(2)}) %collective-permute-start.5) | collective-permute-done | bytes 73760 | tf_op jit(solution)/shard_map/ppermute | solution.py:341
  38.9 0.8 collective-permute-start.6
  39.7 1.3 %collective-permute-done.11 = f32[144,128]{1,0:T(8,128)S(1)} collective-permute-done((f32[144,128]{1,0:T(8,128)S(1)}, f32[144,128]{1,0:T(8,128)S(1)}, u32[]{:S(2)}, u32[]{:S(2)}) %collective-permute-start.11) | collective-permute-done | bytes 73760 | tf_op jit(solution)/shard_map/ppermute | solution.py:341
  41.0 1.8 %collective-permute-start.12 = (f32[288,128]{1,0:T(8,128)S(1)}, f32[288,128]{1,0:T(8,128)S(1)}, u32[]{:S(2)}, u32[]{:S(2)}) collective-permute-start(f32[288,128]{1,0:T(8,128)S(1)} %pad_maximum_fusion.5), channel_id=1, source_target_pairs={{0,8},{1,9},{2,10},{3,11},{4,12},{5,13},{6,14},{7,15},{8,0},{9,1},... | collective-permute-start | bytes 442376 | tf_op jit(solution)/shard_map/ppermute | solution.py:341
  42.8 1.3 %collective-permute-done.6 = f32[288,128]{1,0:T(8,128)S(1)} collective-permute-done((f32[288,128]{1,0:T(8,128)S(1)}, f32[288,128]{1,0:T(8,128)S(1)}, u32[]{:S(2)}, u32[]{:S(2)}) %collective-permute-start.6) | collective-permute-done | bytes 147488 | tf_op jit(solution)/shard_map/ppermute | solution.py:341
  44.1 2.1 %collective-permute-done.12 = f32[288,128]{1,0:T(8,128)S(1)} collective-permute-done((f32[288,128]{1,0:T(8,128)S(1)}, f32[288,128]{1,0:T(8,128)S(1)}, u32[]{:S(2)}, u32[]{:S(2)}) %collective-permute-start.12) | collective-permute-done | bytes 147488 | tf_op jit(solution)/shard_map/ppermute | solution.py:341
  46.3 0.1 collective-permute-start.13
  46.4 0.0 copy-start.3
  46.4 2.0 %collective-permute-done.13 = f32[1152,128]{1,0:T(8,128)S(1)} collective-permute-done((f32[1152,128]{1,0:T(8,128)S(1)}, f32[1152,128]{1,0:T(8,128)S(1)}, u32[]{:S(2)}, u32[]{:S(2)}) %collective-permute-start.13) | collective-permute-done | bytes 589856 | tf_op jit(solution)/shard_map/ppermute | solution.py:341
  48.4 0.1 broadcast_select_fusion.1
  48.5 0.1 pad_maximum_fusion.gram_ref.terms
  48.5 0.0 copy-done.3
  48.6 5.0 %level_first.1 = (f32[128,128]{1,0:T(8,128)S(1)}, f32[128,128]{1,0:T(8,128)S(1)}, f32[128,128]{1,0:T(8,128)S(1)}, f32[8,256]{1,0:T(8,128)S(1)}, f32[256,128]{1,0:T(8,128)S(1)}) custom-call(f32[2304,128]{1,0:T(8,128)S(1)} %pad_maximum_fusion.gram_ref.terms, f32[2,256,256]{2,1,0:T(8,128)S(1)} %copy-done.3), custom_call_target="tpu_custom_call" | custom-call | flops 5000000000 | bytes 262144 | tf_op jit(solution)/shard_map/level_first/pallas_call | solution.py:225
  53.5 0.0 copy-start.1
  53.5 4.9 %level_second.1.inverse = f32[256,256]{1,0:T(8,128)S(1)} custom-call(f32[128,128]{1,0:T(8,128)S(1)} %get-tuple-element.20.first, f32[128,128]{1,0:T(8,128)S(1)} %get-tuple-element.21.across, f32[128,128]{1,0:T(8,128)S(1)} %get-tuple-element.22.rest, f32[8,256]{1,0:T(8,128)S(1)} %get-tuple-element.23.row, f32[256,128]{1,0:T(8,128)S(1)} %get-tuple-element.24.col), custom_call_target="tpu_custom_call" | custom-call | flops 5000000000 | bytes 262144 | tf_op jit(solution)/shard_map/level_second/pallas_call | solution.py:225
  58.4 0.0 copy-start
  58.4 1.1 %panel_solve.1 = (f32[256,256]{1,0:T(8,128)S(1)}, f32[384,128]{1,0:T(8,128)S(1)}) custom-call(f32[256,256]{1,0:T(8,128)S(1)} %level_second.1.inverse, f32[2304,128]{1,0:T(8,128)S(1)} %pad_maximum_fusion.gram_ref.terms), custom_call_target="tpu_custom_call" | custom-call | bytes 262144 | tf_op jit(solution)/shard_map/panel_solve/pallas_call | solution.py:225
  59.5 0.8 %source_solve.1 = (f32[256,256]{1,0:T(8,128)S(1)}, f32[512,128]{1,0:T(8,128)S(1)}) custom-call(f32[256,256]{1,0:T(8,128)S(1)} %level_second.1.inverse, f32[256,256]{1,0:T(8,128)S(1)} %get-tuple-element.25.x, f32[2304,128]{1,0:T(8,128)S(1)} %pad_maximum_fusion.gram_ref.terms), custom_call_target="tpu_custom_call" | custom-call | bytes 262144 | tf_op jit(solution)/shard_map/source_solve/pallas_call | solution.py:225
  60.4 1.8 %collective-permute-start.14 = (f32[192,128]{1,0:T(8,128)S(1)}, f32[192,128]{1,0:T(8,128)S(1)}, u32[]{:S(2)}, u32[]{:S(2)}) collective-permute-start(f32[192,128]{1,0:T(8,128)S(1)} %dynamic-slice_bitcast_fusion.3), channel_id=1, source_target_pairs={{0,2},{1,3},{2,0},{3,1},{4,6},{5,7},{6,4},{7,5},{8,10},{9,11},{10,... | collective-permute-start | bytes 294920 | tf_op jit(solution)/shard_map/ppermute | solution.py:341
  62.2 0.0 copy-start.4
  62.3 0.3 collective-permute-start.16
  62.6 0.0 copy-done.1
  62.6 0.0 copy-done
  62.6 2.8 %panel.1 = f32[2048,256]{1,0:T(8,128)} custom-call(f32[2048,256]{1,0:T(8,128)S(1)} %copy-done, f32[2048,256]{1,0:T(8,128)S(1)} %copy-done.1, f32[256,256]{1,0:T(8,128)S(1)} %get-tuple-element.25.x), custom_call_target="tpu_custom_call" | custom-call | flops 805306368 | bytes 6291456 | tf_op jit(solution)/shard_map/panel/pallas_call | solution.py:326
  65.3 0.6 collective-permute-done.14
  65.9 0.1 collective-permute-start.15
  66.0 2.1 %collective-permute-done.16 = f32[256,128]{1,0:T(8,128)S(1)} collective-permute-done((f32[256,128]{1,0:T(8,128)S(1)}, f32[256,128]{1,0:T(8,128)S(1)}, u32[]{:S(2)}, u32[]{:S(2)}) %collective-permute-start.16) | collective-permute-done | bytes 131104 | tf_op jit(solution)/shard_map/ppermute | solution.py:341
  68.1 0.1 collective-permute-start.17
  68.2 0.0 collective-permute-done.15
  68.3 0.0 copy-done.4
  68.3 5.0 %root_first.1 = (f32[128,128]{1,0:T(8,128)S(1)}, f32[128,128]{1,0:T(8,128)S(1)}, f32[128,128]{1,0:T(8,128)S(1)}, f32[8,256]{1,0:T(8,128)S(1)}, f32[256,128]{1,0:T(8,128)S(1)}) custom-call(f32[384,128]{1,0:T(8,128)S(1)} %pad_maximum_fusion.3.gram_ref, f32[1,256,256]{2,1,0:T(8,128)S(1)} %bitcast.45), custom_call_target="tpu_custom_call" | custom-call | flops 5000000000 | bytes 262144 | tf_op jit(solution)/shard_map/root_first/pallas_call | solution.py:225
  73.3 0.0 copy-start.2
  73.3 4.9 %root_second.1.inverse = f32[256,256]{1,0:T(8,128)S(1)} custom-call(f32[128,128]{1,0:T(8,128)S(1)} %get-tuple-element.27.first, f32[128,128]{1,0:T(8,128)S(1)} %get-tuple-element.28.across, f32[128,128]{1,0:T(8,128)S(1)} %get-tuple-element.29.rest, f32[8,256]{1,0:T(8,128)S(1)} %get-tuple-element.30.row, f32[256,128]{1,0:T(8,128)S(1)} %get-tuple-element.31.col), custom_call_target="tpu_custom_call" | custom-call | flops 5000000000 | bytes 262144 | tf_op jit(solution)/shard_map/root_second/pallas_call | solution.py:225
  78.1 0.0 collective-permute-done.17
  78.2 0.0 copy-done.2
  78.2 4.5 %field.1 = f32[2048,256]{1,0:T(8,128)} custom-call(f32[2048,256]{1,0:T(8,128)S(1)} %copy-done, f32[2048,256]{1,0:T(8,128)S(1)} %copy-done.1, f32[2048,256]{1,0:T(8,128)S(1)} %copy-done.2, f32[256,256]{1,0:T(8,128)S(1)} %root_second.1.inverse, f32[512,128]{1,0:T(8,128)S(1)} %pad_maximum_fusion.2.side, f32[256,256]{1,0:T(8,128)S(1)} %get-tuple-element.25.x, ...), custom_call_target="tpu_custom_call" | custom-call | flops 1610612736 | bytes 8388608 | tf_op jit(solution)/shard_map/field/pallas_call | solution.py:326
  (32 shorter events, 0.5 us)
Async XLA Ops:
  7.8 2.4 %collective-permute-start = (f32[1152,128]{1,0:T(8,128)}, f32[1152,128]{1,0:T(8,128)S(1)}, u32[]{:S(2)}, u32[]{:S(2)}) collective-permute-start(f32[1152,128]{1,0:T(8,128)} %get-tuple-element.19), channel_id=1, source_target_pairs={{0,1},{1,0},{2,3},{3,2},{4,5},{5,4},{6,7},{7,6},{8,9},{9,8},{10,11... | collective-permute-start | bytes 1769480 | tf_op jit(solution)/shard_map/ppermute | solution.py:341
  11.4 7.1 %collective-permute-start.1 = (f32[288,128]{1,0:T(8,128)S(1)}, f32[288,128]{1,0:T(8,128)S(1)}, u32[]{:S(2)}, u32[]{:S(2)}) collective-permute-start(f32[288,128]{1,0:T(8,128)S(1)} %dynamic-slice_bitcast_fusion.1), channel_id=1, source_target_pairs={{0,4},{1,5},{2,6},{3,7},{4,0},{5,1},{6,2},{7,3},{8,12},{9,13},{10,... | collective-permute-start | bytes 442376 | tf_op jit(solution)/shard_map/ppermute | solution.py:341
  14.3 6.1 %collective-permute-start.7 = (f32[288,128]{1,0:T(8,128)S(1)}, f32[288,128]{1,0:T(8,128)S(1)}, u32[]{:S(2)}, u32[]{:S(2)}) collective-permute-start(f32[288,128]{1,0:T(8,128)S(1)} %dynamic-slice_bitcast_fusion), channel_id=1, source_target_pairs={{0,8},{1,9},{2,10},{3,11},{4,12},{5,13},{6,14},{7,15},{8,0},{9,1},... | collective-permute-start | bytes 442376 | tf_op jit(solution)/shard_map/ppermute | solution.py:341
  18.5 4.6 %collective-permute-start.2 = (f32[144,128]{1,0:T(8,128)S(1)}, f32[144,128]{1,0:T(8,128)S(1)}, u32[]{:S(2)}, u32[]{:S(2)}) collective-permute-start(f32[144,128]{1,0:T(8,128)S(1)} %dynamic-slice_bitcast_fusion.5), channel_id=1, source_target_pairs={{0,8},{1,9},{2,10},{3,11},{4,12},{5,13},{6,14},{7,15},{8,0},{9,1},... | collective-permute-start | bytes 221192 | tf_op jit(solution)/shard_map/ppermute | solution.py:341
  20.5 6.9 %collective-permute-start.8 = (f32[144,128]{1,0:T(8,128)S(1)}, f32[144,128]{1,0:T(8,128)S(1)}, u32[]{:S(2)}, u32[]{:S(2)}) collective-permute-start(f32[144,128]{1,0:T(8,128)S(1)} %dynamic-slice_bitcast_fusion.4), channel_id=1, source_target_pairs={{0,16},{1,17},{2,18},{3,19},{4,20},{5,21},{6,22},{7,23},{8,24},{9,... | collective-permute-start | bytes 221192 | tf_op jit(solution)/shard_map/ppermute | solution.py:341
  23.1 5.8 %collective-permute-start.3 = (f32[72,128]{1,0:T(8,128)S(1)}, f32[72,128]{1,0:T(8,128)S(1)}, u32[]{:S(2)}, u32[]{:S(2)}) collective-permute-start(f32[72,128]{1,0:T(8,128)S(1)} %dynamic-slice_bitcast_fusion.7), channel_id=1, source_target_pairs={{0,16},{1,17},{2,18},{3,19},{4,20},{5,21},{6,22},{7,23},{8,24},{9,... | collective-permute-start | bytes 110600 | tf_op jit(solution)/shard_map/ppermute | solution.py:341
  27.4 4.2 %collective-permute-start.9 = (f32[72,128]{1,0:T(8,128)S(1)}, f32[72,128]{1,0:T(8,128)S(1)}, u32[]{:S(2)}, u32[]{:S(2)}) collective-permute-start(f32[72,128]{1,0:T(8,128)S(1)} %dynamic-slice_bitcast_fusion.6), channel_id=1, source_target_pairs={{0,4},{1,5},{2,6},{3,7},{4,0},{5,1},{6,2},{7,3},{8,12},{9,13},{10,... | collective-permute-start | bytes 110600 | tf_op jit(solution)/shard_map/ppermute | solution.py:341
  29.0 5.4 %collective-permute-start.4 = (f32[72,128]{1,0:T(8,128)S(1)}, f32[72,128]{1,0:T(8,128)S(1)}, u32[]{:S(2)}, u32[]{:S(2)}) collective-permute-start(f32[72,128]{1,0:T(8,128)S(1)} %bitcast_add_fusion.5), channel_id=1, source_target_pairs={{0,16},{1,17},{2,18},{3,19},{4,20},{5,21},{6,22},{7,23},{8,24},{9,... | collective-permute-start | bytes 110600 | tf_op jit(solution)/shard_map/ppermute | solution.py:341
  31.6 4.0 %collective-permute-start.10 = (f32[72,128]{1,0:T(8,128)S(1)}, f32[72,128]{1,0:T(8,128)S(1)}, u32[]{:S(2)}, u32[]{:S(2)}) collective-permute-start(f32[72,128]{1,0:T(8,128)S(1)} %bitcast_add_fusion.4), channel_id=1, source_target_pairs={{0,4},{1,5},{2,6},{3,7},{4,0},{5,1},{6,2},{7,3},{8,12},{9,13},{10,... | collective-permute-start | bytes 110600 | tf_op jit(solution)/shard_map/ppermute | solution.py:341
  34.4 4.4 %collective-permute-start.5 = (f32[144,128]{1,0:T(8,128)S(1)}, f32[144,128]{1,0:T(8,128)S(1)}, u32[]{:S(2)}, u32[]{:S(2)}) collective-permute-start(f32[144,128]{1,0:T(8,128)S(1)} %pad_maximum_fusion.6), channel_id=1, source_target_pairs={{0,8},{1,9},{2,10},{3,11},{4,12},{5,13},{6,14},{7,15},{8,0},{9,1},... | collective-permute-start | bytes 221192 | tf_op jit(solution)/shard_map/ppermute | solution.py:341
  35.6 5.4 %collective-permute-start.11 = (f32[144,128]{1,0:T(8,128)S(1)}, f32[144,128]{1,0:T(8,128)S(1)}, u32[]{:S(2)}, u32[]{:S(2)}) collective-permute-start(f32[144,128]{1,0:T(8,128)S(1)} %pad_maximum_fusion.7), channel_id=1, source_target_pairs={{0,16},{1,17},{2,18},{3,19},{4,20},{5,21},{6,22},{7,23},{8,24},{9,... | collective-permute-start | bytes 221192 | tf_op jit(solution)/shard_map/ppermute | solution.py:341
  38.9 5.2 %collective-permute-start.6 = (f32[288,128]{1,0:T(8,128)S(1)}, f32[288,128]{1,0:T(8,128)S(1)}, u32[]{:S(2)}, u32[]{:S(2)}) collective-permute-start(f32[288,128]{1,0:T(8,128)S(1)} %pad_maximum_fusion.4), channel_id=1, source_target_pairs={{0,4},{1,5},{2,6},{3,7},{4,0},{5,1},{6,2},{7,3},{8,12},{9,13},{10,... | collective-permute-start | bytes 442376 | tf_op jit(solution)/shard_map/ppermute | solution.py:341
  41.0 5.2 %collective-permute-start.12 = (f32[288,128]{1,0:T(8,128)S(1)}, f32[288,128]{1,0:T(8,128)S(1)}, u32[]{:S(2)}, u32[]{:S(2)}) collective-permute-start(f32[288,128]{1,0:T(8,128)S(1)} %pad_maximum_fusion.5), channel_id=1, source_target_pairs={{0,8},{1,9},{2,10},{3,11},{4,12},{5,13},{6,14},{7,15},{8,0},{9,1},... | collective-permute-start | bytes 442376 | tf_op jit(solution)/shard_map/ppermute | solution.py:341
  46.3 2.1 %collective-permute-start.13 = (f32[1152,128]{1,0:T(8,128)S(1)}, f32[1152,128]{1,0:T(8,128)S(1)}, u32[]{:S(2)}, u32[]{:S(2)}) collective-permute-start(f32[1152,128]{1,0:T(8,128)S(1)} %pad_maximum_fusion.1), channel_id=1, source_target_pairs={{0,1},{1,0},{2,3},{3,2},{4,5},{5,4},{6,7},{7,6},{8,9},{9,8},{10,11... | collective-permute-start | bytes 1769480 | tf_op jit(solution)/shard_map/ppermute | solution.py:341
  46.4 2.2 %copy-start.3 = (f32[2,256,256]{2,1,0:T(8,128)S(1)}, f32[2,256,256]{2,1,0:T(8,128)}, u32[]{:S(2)}) copy-start(f32[2,256,256]{2,1,0:T(8,128)} %coupling.1) | copy-start | bytes 1572868
  53.5 9.0 %copy-start.1 = (f32[2048,256]{1,0:T(8,128)S(1)}, f32[2048,256]{1,0:T(8,128)}, u32[]{:S(2)}) copy-start(f32[2048,256]{1,0:T(8,128)} %q_one.5) | copy-start | bytes 6291460
  58.4 4.2 %copy-start = (f32[2048,256]{1,0:T(8,128)S(1)}, f32[2048,256]{1,0:T(8,128)}, u32[]{:S(2)}) copy-start(f32[2048,256]{1,0:T(8,128)} %q_two.5) | copy-start | bytes 6291460
  60.4 5.5 %collective-permute-start.14 = (f32[192,128]{1,0:T(8,128)S(1)}, f32[192,128]{1,0:T(8,128)S(1)}, u32[]{:S(2)}, u32[]{:S(2)}) collective-permute-start(f32[192,128]{1,0:T(8,128)S(1)} %dynamic-slice_bitcast_fusion.3), channel_id=1, source_target_pairs={{0,2},{1,3},{2,0},{3,1},{4,6},{5,7},{6,4},{7,5},{8,10},{9,11},{10,... | collective-permute-start | bytes 294920 | tf_op jit(solution)/shard_map/ppermute | solution.py:341
  62.2 6.0 %copy-start.4 = (f32[256,256]{1,0:T(8,128)S(1)}, f32[256,256]{1,0:T(8,128)}, u32[]{:S(2)}) copy-start(f32[256,256]{1,0:T(8,128)} %param.9) | copy-start | bytes 786436
  62.3 5.9 %collective-permute-start.16 = (f32[256,128]{1,0:T(8,128)S(1)}, f32[256,128]{1,0:T(8,128)S(1)}, u32[]{:S(2)}, u32[]{:S(2)}) collective-permute-start(f32[256,128]{1,0:T(8,128)S(1)} %dynamic-slice_bitcast_fusion.2), channel_id=1, source_target_pairs={{0,2},{1,3},{2,0},{3,1},{4,6},{5,7},{6,4},{7,5},{8,10},{9,11},{10,... | collective-permute-start | bytes 393224 | tf_op jit(solution)/shard_map/ppermute | solution.py:341
  65.9 2.3 %collective-permute-start.15 = (f32[192,128]{1,0:T(8,128)S(1)}, f32[192,128]{1,0:T(8,128)S(1)}, u32[]{:S(2)}, u32[]{:S(2)}) collective-permute-start(f32[192,128]{1,0:T(8,128)S(1)} %fusion.2), channel_id=1, source_target_pairs={{0,1},{1,0},{2,3},{3,2},{4,5},{5,4},{6,7},{7,6},{8,9},{9,8},{10,11... | collective-permute-start | bytes 294920 | tf_op jit(solution)/shard_map/ppermute | solution.py:341
  68.1 10.0 %collective-permute-start.17 = (f32[256,128]{1,0:T(8,128)S(1)}, f32[256,128]{1,0:T(8,128)S(1)}, u32[]{:S(2)}, u32[]{:S(2)}) collective-permute-start(f32[256,128]{1,0:T(8,128)S(1)} %fusion.1), channel_id=1, source_target_pairs={{0,1},{1,0},{2,3},{3,2},{4,5},{5,4},{6,7},{7,6},{8,9},{9,8},{10,11... | collective-permute-start | bytes 393224 | tf_op jit(solution)/shard_map/ppermute | solution.py:341
  73.3 5.0 %copy-start.2 = (f32[2048,256]{1,0:T(8,128)S(1)}, f32[2048,256]{1,0:T(8,128)}, u32[]{:S(2)}) copy-start(f32[2048,256]{1,0:T(8,128)} %sources.3) | copy-start | bytes 6291460

commit v3 on v2

--- a/solution.py
+++ b/solution.py
@@ -14,6 +14,7 @@
 R = 256
 LANES = 128
 TILE = 512
+AHEAD = 2
 VMEM_LIMIT = 40 * 1024 * 1024
 OWN, CROSS, PROJECTED, ROOT, SIDE, TERMS = 0, 384, 896, 1408, 1792, 2304
 
@@ -75,29 +76,42 @@
     pairs = ((q_two, b2), (q_one, b1), (sources, bs))
 
     def copy(tile, which):
-        here = pl.ds(tile * TILE, TILE)
+        here = pl.ds(pl.multiple_of(tile * TILE, TILE), TILE)
         source, target = pairs[which]
         return pltpu.make_async_copy(source.at[here], target.at[here], sems.at[which, tile])
 
-    for tile in range(tiles):
+    def start(tile):
         for which in range(3):
             copy(tile, which).start()
+
+    for tile in range(AHEAD):
+        start(tile)
     acc[...] = jnp.zeros_like(acc)
 
     def step(tile, carry):
         for which in range(3):
             copy(tile, which).wait()
+
+        @pl.when(tile + AHEAD < tiles)
+        def _():
+            start(tile + AHEAD)
+
         here = pl.ds(pl.multiple_of(tile * TILE, TILE), TILE)
         h2, l2 = split2(b2[here, :])
         h1, l1 = split2(b1[here, :])
         hs, ls = split2(bs[here, :])
-        acc[0] += dot_t(h2, h2)
-        acc[1] += dot_t(h2, l2)
-        acc[2] += dot_t(h2, h1) + dot_t(h2, l1) + dot_t(l2, h1)
-        acc[3] += dot_t(h2, hs) + dot_t(h2, ls) + dot_t(l2, hs)
-        acc[4] += dot_t(h1, h1)
-        acc[5] += dot_t(h1, l1)
-        acc[6] += dot_t(h1, hs) + dot_t(h1, ls) + dot_t(l1, hs)
+        h2t, l2t, h1t, l1t = h2.T, l2.T, h1.T, l1.T
+        left2 = jnp.concatenate([h2t, h2t, l2t], axis=1)
+        left1 = jnp.concatenate([h1t, h1t, l1t], axis=1)
+        right1 = jnp.concatenate([h1, l1, h1], axis=0)
+        rights = jnp.concatenate([hs, ls, hs], axis=0)
+        acc[0] += dot(h2t, h2)
+        acc[1] += dot(h2t, l2)
+        acc[2] += dot(left2, right1)
+        acc[3] += dot(left2, rights)
+        acc[4] += dot(h1t, h1)
+        acc[5] += dot(h1t, l1)
+        acc[6] += dot(left1, rights)
         return carry
 
     lax.fori_loop(0, tiles, step, 0)
@@ -146,38 +160,50 @@
 
 
 def eliminate(block, cols, rows):
+    count = len(block)
+    lane = lax.broadcasted_iota(jnp.int32, (8, LANES), 1)
+    for start in range(0, count, 4):
+        panel = block[start : start + 4]
+        left = stack_left(jnp.concatenate(panel, axis=0))
+        for t in range(4):
+            panel = eliminate_group(panel, t, start + t, cols, rows)
+        inside = (lane >= 8 * start) & (lane < 8 * start + 32)
+        panel = [jnp.where(inside, -x, x) for x in panel]
+        change = dot_t(left, stack_right(jnp.concatenate(panel, axis=0)))
+        for g in range(count):
+            if start <= g < start + 4:
+                block[g] = panel[g - start]
+            else:
+                block[g] = jnp.where(inside, 0.0, block[g]) - change[8 * g : 8 * g + 8, :]
+    return [-x for x in block]
+
+
+def eliminate_group(panel, t, at, cols, rows):
     lane = lax.broadcasted_iota(jnp.int32, (8, LANES), 1)
     sub = lax.broadcasted_iota(jnp.int32, (8, LANES), 0)
-    count = len(block)
-    for t in range(count):
-        own = [spread_lane(block[t], 8 * t + j) for j in range(8)]
-        for j in range(8):
-            cols[64 * t + 8 * j : 64 * t + 8 * j + 8, :] = own[j]
-        rows[8 * t : 8 * t + 8, :] = block[t]
-        entry = {}
-        for i in range(8):
-            for j in range(i + 1):
-                at = 64 * t + 8 * j + i
-                entry[i, j] = jnp.broadcast_to(cols[at : at + 1, :], (8, LANES))
-        entry = sweep_small(entry)
-        inverse = lambda i, j: entry[max(i, j), min(i, j)]
-        inside = (lane >= 8 * t) & (lane < 8 * t + 8)
-        old = []
-        for j in range(8):
-            row = jnp.broadcast_to(rows[8 * t + j : 8 * t + j + 1, :], (8, LANES))
-            old.append(jnp.where(inside, jnp.where(lane == 8 * t + j, 1.0, 0.0), row))
-        new = [tree_sum([inverse(i, j) * old[j] for j in range(8)]) for i in range(8)]
-        for g in range(count):
-            if g == t:
-                continue
-            base = jnp.where(inside, 0.0, block[g])
-            terms = [spread_lane(block[g], 8 * t + j) * new[j] for j in range(8)]
-            block[g] = base - tree_sum(terms)
-        merged = new[0]
-        for j in range(1, 8):
-            merged = jnp.where(sub == j, new[j], merged)
-        block[t] = merged
-    return block
+    for j in range(8):
+        cols[64 * at + 8 * j : 64 * at + 8 * j + 8, :] = spread_lane(panel[t], 8 * at + j)
+    rows[8 * at : 8 * at + 8, :] = panel[t]
+    entry = {}
+    for i in range(8):
+        for j in range(i + 1):
+            row = 64 * at + 8 * j + i
+            entry[i, j] = jnp.broadcast_to(cols[row : row + 1, :], (8, LANES))
+    inside = (lane >= 8 * at) & (lane < 8 * at + 8)
+    line = []
+    for j in range(8):
+        row = jnp.broadcast_to(rows[8 * at + j : 8 * at + j + 1, :], (8, LANES))
+        line.append(jnp.where(inside, jnp.where(lane == 8 * at + j, 1.0, 0.0), row))
+    line = solve_small(entry, line)
+    for g in range(4):
+        if g != t:
+            terms = [spread_lane(panel[g], 8 * at + j) * line[j] for j in range(8)]
+            panel[g] = jnp.where(inside, 0.0, panel[g]) - tree_sum(terms)
+    merged = line[0]
+    for j in range(1, 8):
+        merged = jnp.where(sub == j, line[j], merged)
+    panel[t] = merged
+    return panel
 
 
 def tree_sum(terms):
@@ -189,27 +215,42 @@
     return terms[0]
 
 
-def sweep_small(entry):
-    entry = dict(entry)
-    get = lambda i, j: entry[max(i, j), min(i, j)]
+def solve_small(entry, line):
+    factors, pivots = {}, {}
     for k in range(0, 8, 2):
-        a, b, c = get(k, k), get(k + 1, k), get(k + 1, k + 1)
+        a, b, c = entry[k, k], entry[k + 1, k], entry[k + 1, k + 1]
         inv = pl.reciprocal(a * c - b * b, approx=True)
         e, f, g = c * inv, b * inv, a * inv
-        others = [i for i in range(8) if i not in (k, k + 1)]
-        left = {i: (get(i, k), get(i, k + 1)) for i in others}
-        swept = {i: (e * u - f * v, g * v - f * u) for i, (u, v) in left.items()}
-        for i in others:
-            for j in others:
-                if j <= i:
-                    u, v = left[i]
-                    m, n = swept[j]
-                    entry[i, j] = entry[i, j] - (u * m + v * n)
-        for i in others:
-            entry[max(i, k), min(i, k)] = swept[i][0]
-            entry[max(i, k + 1), min(i, k + 1)] = swept[i][1]
-        entry[k, k], entry[k + 1, k], entry[k + 1, k + 1] = -e, f, -g
-    return {key: -value for key, value in entry.items()}
+        pivots[k] = (e, f, g)
+        for i in range(k + 2, 8):
+            u, v = entry[i, k], entry[i, k + 1]
+            factors[i, k] = (e * u - f * v, g * v - f * u)
+        for i in range(k + 2, 8):
+            u, v = entry[i, k], entry[i, k + 1]
+            for j in range(k + 2, i + 1):
+                m, n = factors[j, k]
+                entry[i, j] = entry[i, j] - (u * m + v * n)
+        for i in range(k + 2, 8):
+            m, n = factors[i, k]
+            line[i] = line[i] - (m * line[k] + n * line[k + 1])
+    for k in range(6, -1, -2):
+        e, f, g = pivots[k]
+        x, y = e * line[k] - f * line[k + 1], g * line[k + 1] - f * line[k]
+        if k < 6:
+            x = x - tree_sum([factors[i, k][0] * line[i] for i in range(k + 2, 8)])
+            y = y - tree_sum([factors[i, k][1] * line[i] for i in range(k + 2, 8)])
+        line[k], line[k + 1] = x, y
+    return line
+
+
+def stack_left(x):
+    h, m, l = split3(x)
+    return jnp.concatenate([h, h, m, h, l, m], axis=0)
+
+
+def stack_right(x):
+    h, m, l = split3(x)
+    return jnp.concatenate([h, m, h, l, h, m], axis=0)
 
 
 def invert_half(matrix, cols, rows):
@@ -370,24 +411,29 @@
         parts = [gather(x, index, order[step]) for x, order in zip(parts, orders)]
     terms = gather(jnp.concatenate(parts, axis=0), index, 0)
 
-    def across_halves(terms):
-        mine = index & 1
+    def half_rows(terms):
         parts = terms.reshape(2, terms.shape[0] // 2, LANES)
-        part = lax.dynamic_index_in_dim(parts, mine, 0, keepdims=False)
-        return gather(part + exchange(part, 2), index, 0)
+        return lax.dynamic_index_in_dim(parts, index & 1, 0, keepdims=False)
 
     parts = invert_first(half_index, terms, coupling_two, "level_first")
     inverse = invert_second(parts, "level_second")
     x, root = call(
         panel_solve_kernel, (SQUARE, jax.ShapeDtypeStruct((384, LANES), F32)), (inverse, terms), "panel_solve"
     )
-    root = across_halves(root)
+    root = half_rows(root)
+    arriving = exchange(root, 2)
     panel_one = update(panel_kernel, [q_two, q_one], [x], 3, "panel")
+    arriving, panel_one = lax.optimization_barrier((arriving, panel_one))
+    root = gather(root + arriving, index, 0)
+    terms, panel_one = lax.optimization_barrier((terms, panel_one))
     y, side = call(
         source_solve_kernel, (SQUARE, jax.ShapeDtypeStruct((512, LANES), F32)), (inverse, x, terms), "source_solve"
     )
-    side = across_halves(side)
+    side = half_rows(side)
+    arriving = exchange(side, 2)
     parts = invert_first(no_index, root, coupling_one[None], "root_first")
+    arriving, parts = lax.optimization_barrier((arriving, parts))
+    side = gather(side + arriving, index, 0)
     inverse = invert_second(parts, "root_second")
     solution = update(
         field_kernel,

time: 82.9 us -> 79.2 us (0.955)
  Pallas kernels: 36 us -> 33.2 us
  waiting for transfers between devices: 19.1 us -> 18 us
    pallas_call x6, Pallas kernels: 21.6 us -> 18.8 us  [call(): pl.pallas_call(kernel, out_shape=out_shape, scratch_shapes=list(scratch),...]
    ppermute x18, waiting for transfers between devices: 19.1 us -> 18 us  [exchange(): return lax.ppermute(x, AXES, [(i, i ^ mask) for i in range(count)])]
where the time goes in v3:
time: 79.2 us; the launch traced here: 79 us
  Pallas kernels  33.2 us (42%)
  starting transfers between devices  25 us (32%)
  waiting for transfers between devices  18 us (23%)
  other arithmetic  1.62 us (2%)
  between operations  0.98 us (1%)
    ppermute x18, starting transfers between devices, exchange(): return lax.ppermute(x, AXES, [(i, i ^ mask) for i in range(count)])  25 us
    pallas_call x6, Pallas kernels, call(): pl.pallas_call(kernel, out_shape=out_shape, scratch_shapes=list(scratch),...  18.8 us
    ppermute x18, waiting for transfers between devices, exchange(): return lax.ppermute(x, AXES, [(i, i ^ mask) for i in range(count)])  18 us
    pallas_call x2, Pallas kernels, update(): pl.pallas_call(kernel, grid=(rows // TILE,), in_specs=[spec] * len(tall)...  7.28 us
    pallas_call x1, Pallas kernels, gram(): pl.pallas_call(gram_kernel, in_specs=[pl.BlockSpec(memory_space=pl.ANY)]...  7.17 us
  transfers between devices with their start and end apart: 18, of which 13 were waited for; matrix products, arithmetic and copies ran while one was open for 0% of the time, Pallas kernels for 15%

profile of v3, /device:TPU:0, one launch (start us, length us, event | category | flops | bytes accessed | tf_op | source)
XLA Modules:
  0.0 79.0 jit_solution(14796957345116898134)
XLA Ops:
  0.6 7.2 %gram.1 = (f32[1152,128]{1,0:T(8,128)}, f32[1152,128]{1,0:T(8,128)}) custom-call(f32[2048,256]{1,0:T(8,128)} %q_two.5, f32[2048,256]{1,0:T(8,128)} %q_one.5, f32[2048,256]{1,0:T(8,128)} %sources.3), custom_call_target="tpu_custom_call" | custom-call | flops 3489660928 | bytes 6291456 | tf_op jit(solution)/shard_map/gram/pallas_call | solution.py:134
  7.8 0.5 collective-permute-start
  8.3 1.8 %collective-permute-done = f32[1152,128]{1,0:T(8,128)S(1)} collective-permute-done((f32[1152,128]{1,0:T(8,128)}, f32[1152,128]{1,0:T(8,128)S(1)}, u32[]{:S(2)}, u32[]{:S(2)}) %collective-permute-start) | collective-permute-done | bytes 589856 | tf_op jit(solution)/shard_map/ppermute | solution.py:382
  10.2 1.1 %add.67 = f32[1152,128]{1,0:T(8,128)S(1)} add(f32[1152,128]{1,0:T(8,128)} %get-tuple-element.28, f32[1152,128]{1,0:T(8,128)S(1)} %collective-permute-done) | non-fusion elementwise | flops 147456 | bytes 1769472 | tf_op jit(solution)/shard_map/add | solution.py:406
  11.4 2.9 %collective-permute-start.1 = (f32[288,128]{1,0:T(8,128)S(1)}, f32[288,128]{1,0:T(8,128)S(1)}, u32[]{:S(2)}, u32[]{:S(2)}) collective-permute-start(f32[288,128]{1,0:T(8,128)S(1)} %dynamic-slice_bitcast_fusion.1), channel_id=1, source_target_pairs={{0,4},{1,5},{2,6},{3,7},{4,0},{5,1},{6,2},{7,3},{8,12},{9,13},{10,... | collective-permute-start | bytes 442376 | tf_op jit(solution)/shard_map/ppermute | solution.py:382
  14.3 1.6 %collective-permute-start.7 = (f32[288,128]{1,0:T(8,128)S(1)}, f32[288,128]{1,0:T(8,128)S(1)}, u32[]{:S(2)}, u32[]{:S(2)}) collective-permute-start(f32[288,128]{1,0:T(8,128)S(1)} %dynamic-slice_bitcast_fusion), channel_id=1, source_target_pairs={{0,8},{1,9},{2,10},{3,11},{4,12},{5,13},{6,14},{7,15},{8,0},{9,1},... | collective-permute-start | bytes 442376 | tf_op jit(solution)/shard_map/ppermute | solution.py:382
  16.0 2.5 %collective-permute-done.1 = f32[288,128]{1,0:T(8,128)S(1)} collective-permute-done((f32[288,128]{1,0:T(8,128)S(1)}, f32[288,128]{1,0:T(8,128)S(1)}, u32[]{:S(2)}, u32[]{:S(2)}) %collective-permute-start.1) | collective-permute-done | bytes 147488 | tf_op jit(solution)/shard_map/ppermute | solution.py:382
  18.5 1.9 %collective-permute-start.2 = (f32[144,128]{1,0:T(8,128)S(1)}, f32[144,128]{1,0:T(8,128)S(1)}, u32[]{:S(2)}, u32[]{:S(2)}) collective-permute-start(f32[144,128]{1,0:T(8,128)S(1)} %dynamic-slice_bitcast_fusion.5), channel_id=1, source_target_pairs={{0,8},{1,9},{2,10},{3,11},{4,12},{5,13},{6,14},{7,15},{8,0},{9,1},... | collective-permute-start | bytes 221192 | tf_op jit(solution)/shard_map/ppermute | solution.py:382
  20.4 0.0 collective-permute-done.7
  20.4 2.6 %collective-permute-start.8 = (f32[144,128]{1,0:T(8,128)S(1)}, f32[144,128]{1,0:T(8,128)S(1)}, u32[]{:S(2)}, u32[]{:S(2)}) collective-permute-start(f32[144,128]{1,0:T(8,128)S(1)} %dynamic-slice_bitcast_fusion.4), channel_id=1, source_target_pairs={{0,16},{1,17},{2,18},{3,19},{4,20},{5,21},{6,22},{7,23},{8,24},{9,... | collective-permute-start | bytes 221192 | tf_op jit(solution)/shard_map/ppermute | solution.py:382
  23.1 0.0 collective-permute-done.2
  23.1 2.7 %collective-permute-start.3 = (f32[72,128]{1,0:T(8,128)S(1)}, f32[72,128]{1,0:T(8,128)S(1)}, u32[]{:S(2)}, u32[]{:S(2)}) collective-permute-start(f32[72,128]{1,0:T(8,128)S(1)} %dynamic-slice_bitcast_fusion.7), channel_id=1, source_target_pairs={{0,16},{1,17},{2,18},{3,19},{4,20},{5,21},{6,22},{7,23},{8,24},{9,... | collective-permute-start | bytes 110600 | tf_op jit(solution)/shard_map/ppermute | solution.py:382
  25.8 1.5 %collective-permute-done.8 = f32[144,128]{1,0:T(8,128)S(1)} collective-permute-done((f32[144,128]{1,0:T(8,128)S(1)}, f32[144,128]{1,0:T(8,128)S(1)}, u32[]{:S(2)}, u32[]{:S(2)}) %collective-permute-start.8) | collective-permute-done | bytes 73760 | tf_op jit(solution)/shard_map/ppermute | solution.py:382
  27.4 1.6 %collective-permute-start.9 = (f32[72,128]{1,0:T(8,128)S(1)}, f32[72,128]{1,0:T(8,128)S(1)}, u32[]{:S(2)}, u32[]{:S(2)}) collective-permute-start(f32[72,128]{1,0:T(8,128)S(1)} %dynamic-slice_bitcast_fusion.6), channel_id=1, source_target_pairs={{0,4},{1,5},{2,6},{3,7},{4,0},{5,1},{6,2},{7,3},{8,12},{9,13},{10,... | collective-permute-start | bytes 110600 | tf_op jit(solution)/shard_map/ppermute | solution.py:382
  28.9 0.0 collective-permute-done.3
  28.9 1.8 %collective-permute-start.4 = (f32[72,128]{1,0:T(8,128)S(1)}, f32[72,128]{1,0:T(8,128)S(1)}, u32[]{:S(2)}, u32[]{:S(2)}) collective-permute-start(f32[72,128]{1,0:T(8,128)S(1)} %bitcast_add_fusion.5), channel_id=1, source_target_pairs={{0,16},{1,17},{2,18},{3,19},{4,20},{5,21},{6,22},{7,23},{8,24},{9,... | collective-permute-start | bytes 110600 | tf_op jit(solution)/shard_map/ppermute | solution.py:382
  30.7 0.8 %collective-permute-done.9 = f32[72,128]{1,0:T(8,128)S(1)} collective-permute-done((f32[72,128]{1,0:T(8,128)S(1)}, f32[72,128]{1,0:T(8,128)S(1)}, u32[]{:S(2)}, u32[]{:S(2)}) %collective-permute-start.9) | collective-permute-done | bytes 36896 | tf_op jit(solution)/shard_map/ppermute | solution.py:382
  31.6 1.5 %collective-permute-start.10 = (f32[72,128]{1,0:T(8,128)S(1)}, f32[72,128]{1,0:T(8,128)S(1)}, u32[]{:S(2)}, u32[]{:S(2)}) collective-permute-start(f32[72,128]{1,0:T(8,128)S(1)} %bitcast_add_fusion.4), channel_id=1, source_target_pairs={{0,4},{1,5},{2,6},{3,7},{4,0},{5,1},{6,2},{7,3},{8,12},{9,13},{10,... | collective-permute-start | bytes 110600 | tf_op jit(solution)/shard_map/ppermute | solution.py:382
  33.0 1.3 %collective-permute-done.4 = f32[72,128]{1,0:T(8,128)S(1)} collective-permute-done((f32[72,128]{1,0:T(8,128)S(1)}, f32[72,128]{1,0:T(8,128)S(1)}, u32[]{:S(2)}, u32[]{:S(2)}) %collective-permute-start.4) | collective-permute-done | bytes 36896 | tf_op jit(solution)/shard_map/ppermute | solution.py:382
  34.4 0.5 collective-permute-start.5
  34.9 0.7 collective-permute-done.10
  35.5 2.2 %collective-permute-start.11 = (f32[144,128]{1,0:T(8,128)S(1)}, f32[144,128]{1,0:T(8,128)S(1)}, u32[]{:S(2)}, u32[]{:S(2)}) collective-permute-start(f32[144,128]{1,0:T(8,128)S(1)} %pad_maximum_fusion.7), channel_id=1, source_target_pairs={{0,16},{1,17},{2,18},{3,19},{4,20},{5,21},{6,22},{7,23},{8,24},{9,... | collective-permute-start | bytes 221192 | tf_op jit(solution)/shard_map/ppermute | solution.py:382
  37.8 1.0 %collective-permute-done.5 = f32[144,128]{1,0:T(8,128)S(1)} collective-permute-done((f32[144,128]{1,0:T(8,128)S(1)}, f32[144,128]{1,0:T(8,128)S(1)}, u32[]{:S(2)}, u32[]{:S(2)}) %collective-permute-start.5) | collective-permute-done | bytes 73760 | tf_op jit(solution)/shard_map/ppermute | solution.py:382
  38.8 0.8 %collective-permute-start.6 = (f32[288,128]{1,0:T(8,128)S(1)}, f32[288,128]{1,0:T(8,128)S(1)}, u32[]{:S(2)}, u32[]{:S(2)}) collective-permute-start(f32[288,128]{1,0:T(8,128)S(1)} %pad_maximum_fusion.4), channel_id=1, source_target_pairs={{0,4},{1,5},{2,6},{3,7},{4,0},{5,1},{6,2},{7,3},{8,12},{9,13},{10,... | collective-permute-start | bytes 442376 | tf_op jit(solution)/shard_map/ppermute | solution.py:382
  39.6 1.6 %collective-permute-done.11 = f32[144,128]{1,0:T(8,128)S(1)} collective-permute-done((f32[144,128]{1,0:T(8,128)S(1)}, f32[144,128]{1,0:T(8,128)S(1)}, u32[]{:S(2)}, u32[]{:S(2)}) %collective-permute-start.11) | collective-permute-done | bytes 73760 | tf_op jit(solution)/shard_map/ppermute | solution.py:382
  41.3 1.5 %collective-permute-start.12 = (f32[288,128]{1,0:T(8,128)S(1)}, f32[288,128]{1,0:T(8,128)S(1)}, u32[]{:S(2)}, u32[]{:S(2)}) collective-permute-start(f32[288,128]{1,0:T(8,128)S(1)} %pad_maximum_fusion.5), channel_id=1, source_target_pairs={{0,8},{1,9},{2,10},{3,11},{4,12},{5,13},{6,14},{7,15},{8,0},{9,1},... | collective-permute-start | bytes 442376 | tf_op jit(solution)/shard_map/ppermute | solution.py:382
  42.7 1.3 %collective-permute-done.6 = f32[288,128]{1,0:T(8,128)S(1)} collective-permute-done((f32[288,128]{1,0:T(8,128)S(1)}, f32[288,128]{1,0:T(8,128)S(1)}, u32[]{:S(2)}, u32[]{:S(2)}) %collective-permute-start.6) | collective-permute-done | bytes 147488 | tf_op jit(solution)/shard_map/ppermute | solution.py:382
  44.1 2.4 %collective-permute-done.12 = f32[288,128]{1,0:T(8,128)S(1)} collective-permute-done((f32[288,128]{1,0:T(8,128)S(1)}, f32[288,128]{1,0:T(8,128)S(1)}, u32[]{:S(2)}, u32[]{:S(2)}) %collective-permute-start.12) | collective-permute-done | bytes 147488 | tf_op jit(solution)/shard_map/ppermute | solution.py:382
  46.6 0.1 collective-permute-start.13
  46.6 0.0 copy-start.3
  46.7 2.0 %collective-permute-done.13 = f32[1152,128]{1,0:T(8,128)S(1)} collective-permute-done((f32[1152,128]{1,0:T(8,128)S(1)}, f32[1152,128]{1,0:T(8,128)S(1)}, u32[]{:S(2)}, u32[]{:S(2)}) %collective-permute-start.13) | collective-permute-done | bytes 589856 | tf_op jit(solution)/shard_map/ppermute | solution.py:382
  48.6 0.1 broadcast_select_fusion.1
  48.7 0.1 pad_maximum_fusion.gram_ref.terms
  48.8 0.0 copy-done.3
  48.8 4.4 %level_first.1 = (f32[128,128]{1,0:T(8,128)S(1)}, f32[128,128]{1,0:T(8,128)S(1)}, f32[128,128]{1,0:T(8,128)S(1)}, f32[8,256]{1,0:T(8,128)S(1)}, f32[256,128]{1,0:T(8,128)S(1)}) custom-call(f32[2304,128]{1,0:T(8,128)S(1)} %pad_maximum_fusion.gram_ref.terms, f32[2,256,256]{2,1,0:T(8,128)S(1)} %copy-done.3), custom_call_target="tpu_custom_call" | custom-call | flops 5000000000 | bytes 262144 | tf_op jit(solution)/shard_map/level_first/pallas_call | solution.py:266
  53.2 0.0 copy-start
  53.3 0.0 copy-start.1
  53.3 4.1 %level_second.1.inverse = f32[256,256]{1,0:T(8,128)S(1)} custom-call(f32[128,128]{1,0:T(8,128)S(1)} %get-tuple-element.30.first, f32[128,128]{1,0:T(8,128)S(1)} %get-tuple-element.31.across, f32[128,128]{1,0:T(8,128)S(1)} %get-tuple-element.32.rest, f32[8,256]{1,0:T(8,128)S(1)} %get-tuple-element.33.row, f32[256,128]{1,0:T(8,128)S(1)} %get-tuple-element.34.col), custom_call_target="tpu_custom_call" | custom-call | flops 5000000000 | bytes 262144 | tf_op jit(solution)/shard_map/level_second/pallas_call | solution.py:266
  57.4 1.1 %panel_solve.1 = (f32[256,256]{1,0:T(8,128)S(1)}, f32[384,128]{1,0:T(8,128)S(1)}) custom-call(f32[256,256]{1,0:T(8,128)S(1)} %level_second.1.inverse, f32[2304,128]{1,0:T(8,128)S(1)} %pad_maximum_fusion.gram_ref.terms), custom_call_target="tpu_custom_call" | custom-call | bytes 262144 | tf_op jit(solution)/shard_map/panel_solve/pallas_call | solution.py:266
  58.5 1.3 %collective-permute-start.14 = (f32[192,128]{1,0:T(8,128)S(1)}, f32[192,128]{1,0:T(8,128)S(1)}, u32[]{:S(2)}, u32[]{:S(2)}) collective-permute-start(f32[192,128]{1,0:T(8,128)S(1)} %dynamic-slice_bitcast_fusion.3), channel_id=1, source_target_pairs={{0,2},{1,3},{2,0},{3,1},{4,6},{5,7},{6,4},{7,5},{8,10},{9,11},{10,... | collective-permute-start | bytes 294920 | tf_op jit(solution)/shard_map/ppermute | solution.py:382
  59.8 0.0 copy-done
  59.8 0.0 copy-done.1
  59.8 2.7 %panel.1 = f32[2048,256]{1,0:T(8,128)} custom-call(f32[2048,256]{1,0:T(8,128)S(1)} %copy-done, f32[2048,256]{1,0:T(8,128)S(1)} %copy-done.1, f32[256,256]{1,0:T(8,128)S(1)} %get-tuple-element.36.x), custom_call_target="tpu_custom_call" | custom-call | flops 805306368 | bytes 6291456 | tf_op jit(solution)/shard_map/panel/pallas_call | solution.py:367
  62.5 0.0 copy-start.4
  62.5 0.8 %collective-permute-done.14 = f32[192,128]{1,0:T(8,128)S(1)} collective-permute-done((f32[192,128]{1,0:T(8,128)S(1)}, f32[192,128]{1,0:T(8,128)S(1)}, u32[]{:S(2)}, u32[]{:S(2)}) %collective-permute-start.14) | collective-permute-done | bytes 98336 | tf_op jit(solution)/shard_map/ppermute | solution.py:382
  63.4 0.1 collective-permute-start.16
  63.5 0.6 source_solve.1
  64.2 1.3 %collective-permute-start.15 = (f32[256,128]{1,0:T(8,128)S(1)}, f32[256,128]{1,0:T(8,128)S(1)}, u32[]{:S(2)}, u32[]{:S(2)}) collective-permute-start(f32[256,128]{1,0:T(8,128)S(1)} %dynamic-slice_bitcast_fusion.2), channel_id=1, source_target_pairs={{0,2},{1,3},{2,0},{3,1},{4,6},{5,7},{6,4},{7,5},{8,10},{9,11},{10,... | collective-permute-start | bytes 393224 | tf_op jit(solution)/shard_map/ppermute | solution.py:382
  65.5 0.0 collective-permute-done.16
  65.5 0.0 copy-done.4
  65.5 4.4 %root_first.1 = (f32[128,128]{1,0:T(8,128)S(1)}, f32[128,128]{1,0:T(8,128)S(1)}, f32[128,128]{1,0:T(8,128)S(1)}, f32[8,256]{1,0:T(8,128)S(1)}, f32[256,128]{1,0:T(8,128)S(1)}) custom-call(f32[384,128]{1,0:T(8,128)S(1)} %pad_maximum_fusion.3.gram_ref, f32[1,256,256]{2,1,0:T(8,128)S(1)} %bitcast.45), custom_call_target="tpu_custom_call" | custom-call | flops 5000000000 | bytes 262144 | tf_op jit(solution)/shard_map/root_first/pallas_call | solution.py:266
  70.0 0.2 collective-permute-done.15
  70.1 0.1 collective-permute-start.17
  70.3 0.0 copy-start.2
  70.3 4.1 %root_second.1.inverse = f32[256,256]{1,0:T(8,128)S(1)} custom-call(f32[128,128]{1,0:T(8,128)S(1)} %get-tuple-element.47.first, f32[128,128]{1,0:T(8,128)S(1)} %get-tuple-element.48.across, f32[128,128]{1,0:T(8,128)S(1)} %get-tuple-element.49.rest, f32[8,256]{1,0:T(8,128)S(1)} %get-tuple-element.50.row, f32[256,128]{1,0:T(8,128)S(1)} %get-tuple-element.51.col), custom_call_target="tpu_custom_call" | custom-call | flops 5000000000 | bytes 262144 | tf_op jit(solution)/shard_map/root_second/pallas_call | solution.py:266
  74.4 0.0 collective-permute-done.17
  74.4 0.0 copy-done.2
  74.5 4.5 %field.1 = f32[2048,256]{1,0:T(8,128)} custom-call(f32[2048,256]{1,0:T(8,128)S(1)} %copy-done, f32[2048,256]{1,0:T(8,128)S(1)} %copy-done.1, f32[2048,256]{1,0:T(8,128)S(1)} %copy-done.2, f32[256,256]{1,0:T(8,128)S(1)} %root_second.1.inverse, f32[512,128]{1,0:T(8,128)S(1)} %pad_maximum_fusion.2.side, f32[256,256]{1,0:T(8,128)S(1)} %get-tuple-element.36.x, ...), custom_call_target="tpu_custom_call" | custom-call | flops 1610612736 | bytes 8388608 | tf_op jit(solution)/shard_map/field/pallas_call | solution.py:367
  (32 shorter events, 0.5 us)
Async XLA Ops:
  7.8 2.4 %collective-permute-start = (f32[1152,128]{1,0:T(8,128)}, f32[1152,128]{1,0:T(8,128)S(1)}, u32[]{:S(2)}, u32[]{:S(2)}) collective-permute-start(f32[1152,128]{1,0:T(8,128)} %get-tuple-element.29), channel_id=1, source_target_pairs={{0,1},{1,0},{2,3},{3,2},{4,5},{5,4},{6,7},{7,6},{8,9},{9,8},{10,11... | collective-permute-start | bytes 1769480 | tf_op jit(solution)/shard_map/ppermute | solution.py:382
  11.4 7.1 %collective-permute-start.1 = (f32[288,128]{1,0:T(8,128)S(1)}, f32[288,128]{1,0:T(8,128)S(1)}, u32[]{:S(2)}, u32[]{:S(2)}) collective-permute-start(f32[288,128]{1,0:T(8,128)S(1)} %dynamic-slice_bitcast_fusion.1), channel_id=1, source_target_pairs={{0,4},{1,5},{2,6},{3,7},{4,0},{5,1},{6,2},{7,3},{8,12},{9,13},{10,... | collective-permute-start | bytes 442376 | tf_op jit(solution)/shard_map/ppermute | solution.py:382
  14.3 6.1 %collective-permute-start.7 = (f32[288,128]{1,0:T(8,128)S(1)}, f32[288,128]{1,0:T(8,128)S(1)}, u32[]{:S(2)}, u32[]{:S(2)}) collective-permute-start(f32[288,128]{1,0:T(8,128)S(1)} %dynamic-slice_bitcast_fusion), channel_id=1, source_target_pairs={{0,8},{1,9},{2,10},{3,11},{4,12},{5,13},{6,14},{7,15},{8,0},{9,1},... | collective-permute-start | bytes 442376 | tf_op jit(solution)/shard_map/ppermute | solution.py:382
  18.5 4.6 %collective-permute-start.2 = (f32[144,128]{1,0:T(8,128)S(1)}, f32[144,128]{1,0:T(8,128)S(1)}, u32[]{:S(2)}, u32[]{:S(2)}) collective-permute-start(f32[144,128]{1,0:T(8,128)S(1)} %dynamic-slice_bitcast_fusion.5), channel_id=1, source_target_pairs={{0,8},{1,9},{2,10},{3,11},{4,12},{5,13},{6,14},{7,15},{8,0},{9,1},... | collective-permute-start | bytes 221192 | tf_op jit(solution)/shard_map/ppermute | solution.py:382
  20.4 6.9 %collective-permute-start.8 = (f32[144,128]{1,0:T(8,128)S(1)}, f32[144,128]{1,0:T(8,128)S(1)}, u32[]{:S(2)}, u32[]{:S(2)}) collective-permute-start(f32[144,128]{1,0:T(8,128)S(1)} %dynamic-slice_bitcast_fusion.4), channel_id=1, source_target_pairs={{0,16},{1,17},{2,18},{3,19},{4,20},{5,21},{6,22},{7,23},{8,24},{9,... | collective-permute-start | bytes 221192 | tf_op jit(solution)/shard_map/ppermute | solution.py:382
  23.1 5.8 %collective-permute-start.3 = (f32[72,128]{1,0:T(8,128)S(1)}, f32[72,128]{1,0:T(8,128)S(1)}, u32[]{:S(2)}, u32[]{:S(2)}) collective-permute-start(f32[72,128]{1,0:T(8,128)S(1)} %dynamic-slice_bitcast_fusion.7), channel_id=1, source_target_pairs={{0,16},{1,17},{2,18},{3,19},{4,20},{5,21},{6,22},{7,23},{8,24},{9,... | collective-permute-start | bytes 110600 | tf_op jit(solution)/shard_map/ppermute | solution.py:382
  27.4 4.2 %collective-permute-start.9 = (f32[72,128]{1,0:T(8,128)S(1)}, f32[72,128]{1,0:T(8,128)S(1)}, u32[]{:S(2)}, u32[]{:S(2)}) collective-permute-start(f32[72,128]{1,0:T(8,128)S(1)} %dynamic-slice_bitcast_fusion.6), channel_id=1, source_target_pairs={{0,4},{1,5},{2,6},{3,7},{4,0},{5,1},{6,2},{7,3},{8,12},{9,13},{10,... | collective-permute-start | bytes 110600 | tf_op jit(solution)/shard_map/ppermute | solution.py:382
  28.9 5.4 %collective-permute-start.4 = (f32[72,128]{1,0:T(8,128)S(1)}, f32[72,128]{1,0:T(8,128)S(1)}, u32[]{:S(2)}, u32[]{:S(2)}) collective-permute-start(f32[72,128]{1,0:T(8,128)S(1)} %bitcast_add_fusion.5), channel_id=1, source_target_pairs={{0,16},{1,17},{2,18},{3,19},{4,20},{5,21},{6,22},{7,23},{8,24},{9,... | collective-permute-start | bytes 110600 | tf_op jit(solution)/shard_map/ppermute | solution.py:382
  31.6 4.0 %collective-permute-start.10 = (f32[72,128]{1,0:T(8,128)S(1)}, f32[72,128]{1,0:T(8,128)S(1)}, u32[]{:S(2)}, u32[]{:S(2)}) collective-permute-start(f32[72,128]{1,0:T(8,128)S(1)} %bitcast_add_fusion.4), channel_id=1, source_target_pairs={{0,4},{1,5},{2,6},{3,7},{4,0},{5,1},{6,2},{7,3},{8,12},{9,13},{10,... | collective-permute-start | bytes 110600 | tf_op jit(solution)/shard_map/ppermute | solution.py:382
  34.4 4.4 %collective-permute-start.5 = (f32[144,128]{1,0:T(8,128)S(1)}, f32[144,128]{1,0:T(8,128)S(1)}, u32[]{:S(2)}, u32[]{:S(2)}) collective-permute-start(f32[144,128]{1,0:T(8,128)S(1)} %pad_maximum_fusion.6), channel_id=1, source_target_pairs={{0,8},{1,9},{2,10},{3,11},{4,12},{5,13},{6,14},{7,15},{8,0},{9,1},... | collective-permute-start | bytes 221192 | tf_op jit(solution)/shard_map/ppermute | solution.py:382
  35.5 5.7 %collective-permute-start.11 = (f32[144,128]{1,0:T(8,128)S(1)}, f32[144,128]{1,0:T(8,128)S(1)}, u32[]{:S(2)}, u32[]{:S(2)}) collective-permute-start(f32[144,128]{1,0:T(8,128)S(1)} %pad_maximum_fusion.7), channel_id=1, source_target_pairs={{0,16},{1,17},{2,18},{3,19},{4,20},{5,21},{6,22},{7,23},{8,24},{9,... | collective-permute-start | bytes 221192 | tf_op jit(solution)/shard_map/ppermute | solution.py:382
  38.8 5.2 %collective-permute-start.6 = (f32[288,128]{1,0:T(8,128)S(1)}, f32[288,128]{1,0:T(8,128)S(1)}, u32[]{:S(2)}, u32[]{:S(2)}) collective-permute-start(f32[288,128]{1,0:T(8,128)S(1)} %pad_maximum_fusion.4), channel_id=1, source_target_pairs={{0,4},{1,5},{2,6},{3,7},{4,0},{5,1},{6,2},{7,3},{8,12},{9,13},{10,... | collective-permute-start | bytes 442376 | tf_op jit(solution)/shard_map/ppermute | solution.py:382
  41.3 5.2 %collective-permute-start.12 = (f32[288,128]{1,0:T(8,128)S(1)}, f32[288,128]{1,0:T(8,128)S(1)}, u32[]{:S(2)}, u32[]{:S(2)}) collective-permute-start(f32[288,128]{1,0:T(8,128)S(1)} %pad_maximum_fusion.5), channel_id=1, source_target_pairs={{0,8},{1,9},{2,10},{3,11},{4,12},{5,13},{6,14},{7,15},{8,0},{9,1},... | collective-permute-start | bytes 442376 | tf_op jit(solution)/shard_map/ppermute | solution.py:382
  46.6 2.1 %collective-permute-start.13 = (f32[1152,128]{1,0:T(8,128)S(1)}, f32[1152,128]{1,0:T(8,128)S(1)}, u32[]{:S(2)}, u32[]{:S(2)}) collective-permute-start(f32[1152,128]{1,0:T(8,128)S(1)} %pad_maximum_fusion.1), channel_id=1, source_target_pairs={{0,1},{1,0},{2,3},{3,2},{4,5},{5,4},{6,7},{7,6},{8,9},{9,8},{10,11... | collective-permute-start | bytes 1769480 | tf_op jit(solution)/shard_map/ppermute | solution.py:382
  46.6 2.2 %copy-start.3 = (f32[2,256,256]{2,1,0:T(8,128)S(1)}, f32[2,256,256]{2,1,0:T(8,128)}, u32[]{:S(2)}) copy-start(f32[2,256,256]{2,1,0:T(8,128)} %coupling.1) | copy-start | bytes 1572868
  53.2 6.6 %copy-start = (f32[2048,256]{1,0:T(8,128)S(1)}, f32[2048,256]{1,0:T(8,128)}, u32[]{:S(2)}) copy-start(f32[2048,256]{1,0:T(8,128)} %q_two.5) | copy-start | bytes 6291460
  53.3 6.5 %copy-start.1 = (f32[2048,256]{1,0:T(8,128)S(1)}, f32[2048,256]{1,0:T(8,128)}, u32[]{:S(2)}) copy-start(f32[2048,256]{1,0:T(8,128)} %q_one.5) | copy-start | bytes 6291460
  58.5 4.9 %collective-permute-start.14 = (f32[192,128]{1,0:T(8,128)S(1)}, f32[192,128]{1,0:T(8,128)S(1)}, u32[]{:S(2)}, u32[]{:S(2)}) collective-permute-start(f32[192,128]{1,0:T(8,128)S(1)} %dynamic-slice_bitcast_fusion.3), channel_id=1, source_target_pairs={{0,2},{1,3},{2,0},{3,1},{4,6},{5,7},{6,4},{7,5},{8,10},{9,11},{10,... | collective-permute-start | bytes 294920 | tf_op jit(solution)/shard_map/ppermute | solution.py:382
  62.5 3.0 %copy-start.4 = (f32[256,256]{1,0:T(8,128)S(1)}, f32[256,256]{1,0:T(8,128)}, u32[]{:S(2)}) copy-start(f32[256,256]{1,0:T(8,128)} %param.9) | copy-start | bytes 786436
  63.4 2.1 %collective-permute-start.16 = (f32[192,128]{1,0:T(8,128)S(1)}, f32[192,128]{1,0:T(8,128)S(1)}, u32[]{:S(2)}, u32[]{:S(2)}) collective-permute-start(f32[192,128]{1,0:T(8,128)S(1)} %fusion.2), channel_id=1, source_target_pairs={{0,1},{1,0},{2,3},{3,2},{4,5},{5,4},{6,7},{7,6},{8,9},{9,8},{10,11... | collective-permute-start | bytes 294920 | tf_op jit(solution)/shard_map/ppermute | solution.py:382
  64.2 6.0 %collective-permute-start.15 = (f32[256,128]{1,0:T(8,128)S(1)}, f32[256,128]{1,0:T(8,128)S(1)}, u32[]{:S(2)}, u32[]{:S(2)}) collective-permute-start(f32[256,128]{1,0:T(8,128)S(1)} %dynamic-slice_bitcast_fusion.2), channel_id=1, source_target_pairs={{0,2},{1,3},{2,0},{3,1},{4,6},{5,7},{6,4},{7,5},{8,10},{9,11},{10,... | collective-permute-start | bytes 393224 | tf_op jit(solution)/shard_map/ppermute | solution.py:382
  70.1 4.2 %collective-permute-start.17 = (f32[256,128]{1,0:T(8,128)S(1)}, f32[256,128]{1,0:T(8,128)S(1)}, u32[]{:S(2)}, u32[]{:S(2)}) collective-permute-start(f32[256,128]{1,0:T(8,128)S(1)} %fusion.1), channel_id=1, source_target_pairs={{0,1},{1,0},{2,3},{3,2},{4,5},{5,4},{6,7},{7,6},{8,9},{9,8},{10,11... | collective-permute-start | bytes 393224 | tf_op jit(solution)/shard_map/ppermute | solution.py:382
  70.3 4.2 %copy-start.2 = (f32[2048,256]{1,0:T(8,128)S(1)}, f32[2048,256]{1,0:T(8,128)}, u32[]{:S(2)}) copy-start(f32[2048,256]{1,0:T(8,128)} %sources.3) | copy-start | bytes 6291460

commit v4 on v3

--- a/solution.py
+++ b/solution.py
@@ -14,9 +14,10 @@
 R = 256
 LANES = 128
 TILE = 512
-AHEAD = 2
 VMEM_LIMIT = 40 * 1024 * 1024
-OWN, CROSS, PROJECTED, ROOT, SIDE, TERMS = 0, 384, 896, 1408, 1792, 2304
+SYMMETRIC, FULL = 264, 512
+OWN, ROOT, CROSS, PANEL_TERMS = 0, 264, 528, 1040
+PROJECTED, SIDE, SOURCE_TERMS = 0, 512, 1024
 
 
 def split2(x):
@@ -49,10 +50,18 @@
     )
 
 
-def store_symmetric(ref, row, block):
-    ref[row : row + 128, :] = block[:128, :128]
-    ref[row + 128 : row + 256, :] = block[128:, :128]
-    ref[row + 256 : row + 384, :] = block[128:, 128:]
+def square_index():
+    row = lax.broadcasted_iota(jnp.int32, (LANES, LANES), 0)
+    return row, lax.broadcasted_iota(jnp.int32, (LANES, LANES), 1)
+
+
+def store_symmetric(ref, at, block):
+    row, col = square_index()
+    last = block[128:, 128:]
+    ref[at : at + 128, :] = block[128:, :128]
+    ref[at + 128 : at + 256, :] = jnp.where(row >= col, block[:128, :128], last)
+    diagonal = jnp.sum(jnp.where(row == col, last, 0.0), axis=0, keepdims=True)
+    ref[at + 256 : at + 264, :] = jnp.broadcast_to(diagonal, (8, LANES))
 
 
 def store_square(ref, row, block):
@@ -60,99 +69,128 @@
     ref[row + 256 : row + 512, :] = block[:, 128:]
 
 
-def load_symmetric(ref, row):
-    lower = ref[row + 128 : row + 256, :]
-    top = jnp.concatenate([ref[row : row + 128, :], lower.T], axis=1)
-    bottom = jnp.concatenate([lower, ref[row + 256 : row + 384, :]], axis=1)
-    return jnp.concatenate([top, bottom], axis=0)
+def load_symmetric(ref, at):
+    row, col = square_index()
+    lower = ref[at : at + 128, :]
+    mixed = ref[at + 128 : at + 256, :]
+    turned = mixed.T
+    first = jnp.where(row >= col, mixed, turned)
+    last = jnp.where(row < col, mixed, turned)
+    last = jnp.where(row == col, ref[at + 256 : at + 257, :], last)
+    top = jnp.concatenate([first, lower.T], axis=1)
+    return jnp.concatenate([top, jnp.concatenate([lower, last], axis=1)], axis=0)
 
 
 def load_square(ref, row):
     return jnp.concatenate([ref[row : row + 256, :], ref[row + 256 : row + 512, :]], axis=1)
 
 
-def gram_kernel(q_two, q_one, sources, keep, send, b2, b1, bs, acc, packed, sems):
+def half_of(rows):
+    return (rows + 15) // 16 * 8
+
+
+def store_halves(packed, keep, send):
+    half = half_of(packed.shape[0])
+    far = packed.shape[0] - half
+    mine = lax.rem(lax.axis_index("group"), 2)
+    keep[...] = packed[pl.ds(pl.multiple_of(mine * far, 8), half), :]
+    send[...] = packed[pl.ds(pl.multiple_of((1 - mine) * far, 8), half), :]
+
+
+def tile_at(tile):
+    return pl.ds(pl.multiple_of(tile * TILE, TILE), TILE)
+
+
+def panel_gram_kernel(q_two, q_one, keep, send, b2, b1, acc, packed, sems):
     tiles = b2.shape[0] // TILE
-    pairs = ((q_two, b2), (q_one, b1), (sources, bs))
+    pairs = ((q_two, b2), (q_one, b1))
 
     def copy(tile, which):
-        here = pl.ds(pl.multiple_of(tile * TILE, TILE), TILE)
         source, target = pairs[which]
+        here = tile_at(tile)
         return pltpu.make_async_copy(source.at[here], target.at[here], sems.at[which, tile])
 
-    def start(tile):
-        for which in range(3):
+    for tile in range(tiles):
+        for which in range(2):
             copy(tile, which).start()
-
-    for tile in range(AHEAD):
-        start(tile)
     acc[...] = jnp.zeros_like(acc)
 
     def step(tile, carry):
-        for which in range(3):
+        for which in range(2):
             copy(tile, which).wait()
-
-        @pl.when(tile + AHEAD < tiles)
-        def _():
-            start(tile + AHEAD)
-
-        here = pl.ds(pl.multiple_of(tile * TILE, TILE), TILE)
-        h2, l2 = split2(b2[here, :])
-        h1, l1 = split2(b1[here, :])
-        hs, ls = split2(bs[here, :])
-        h2t, l2t, h1t, l1t = h2.T, l2.T, h1.T, l1.T
-        left2 = jnp.concatenate([h2t, h2t, l2t], axis=1)
-        left1 = jnp.concatenate([h1t, h1t, l1t], axis=1)
-        right1 = jnp.concatenate([h1, l1, h1], axis=0)
-        rights = jnp.concatenate([hs, ls, hs], axis=0)
+        h2, l2 = split2(b2[tile_at(tile), :])
+        h1, l1 = split2(b1[tile_at(tile), :])
+        h2t, l2t, h1t = h2.T, l2.T, h1.T
         acc[0] += dot(h2t, h2)
         acc[1] += dot(h2t, l2)
-        acc[2] += dot(left2, right1)
-        acc[3] += dot(left2, rights)
-        acc[4] += dot(h1t, h1)
-        acc[5] += dot(h1t, l1)
-        acc[6] += dot(left1, rights)
+        left = jnp.concatenate([h2t, h2t, l2t], axis=1)
+        acc[2] += dot(left, jnp.concatenate([h1, l1, h1], axis=0))
+        acc[3] += dot(h1t, h1)
+        acc[4] += dot(h1t, l1)
         return carry
 
     lax.fori_loop(0, tiles, step, 0)
     low = acc[1]
     store_symmetric(packed, OWN, acc[0] + low + low.T)
+    low = acc[4]
+    store_symmetric(packed, ROOT, acc[3] + low + low.T)
     store_square(packed, CROSS, acc[2])
-    store_square(packed, PROJECTED, acc[3])
-    low = acc[5]
-    store_symmetric(packed, ROOT, acc[4] + low + low.T)
-    store_square(packed, SIDE, acc[6])
-    mine = lax.rem(lax.axis_index("group"), 2)
-    half = TERMS // 2
-    keep[...] = packed[pl.ds(pl.multiple_of(mine * half, 8), half), :]
-    send[...] = packed[pl.ds(pl.multiple_of((1 - mine) * half, 8), half), :]
-
-
-def gram(q_two, q_one, sources):
-    rows = q_two.shape[0]
-    part = jax.ShapeDtypeStruct((TERMS // 2, LANES), F32)
-    return pl.pallas_call(
-        gram_kernel,
-        in_specs=[pl.BlockSpec(memory_space=pl.ANY)] * 3,
-        out_shape=(part, part),
-        scratch_shapes=[
-            pltpu.VMEM((rows, R), F32),
-            pltpu.VMEM((rows, R), F32),
-            pltpu.VMEM((rows, R), F32),
-            pltpu.VMEM((7, R, R), F32),
-            pltpu.VMEM((TERMS, LANES), F32),
-            pltpu.SemaphoreType.DMA((3, rows // TILE)),
-        ],
-        compiler_params=pltpu.CompilerParams(vmem_limit_bytes=60 * 1024 * 1024),
-        cost_estimate=estimate(13, rows, 3),
-        name="gram",
-    )(q_two, q_one, sources)
-
-
-def estimate(passes, rows, arrays):
+    store_halves(packed, keep, send)
+
+
+def source_gram_kernel(b2, b1, sources, keep, send, acc, packed):
+    acc[...] = jnp.zeros_like(acc)
+
+    def step(tile, carry):
+        hs, ls = split2(sources[tile_at(tile), :])
+        right = jnp.concatenate([hs, ls, hs], axis=0)
+        for which, panel in enumerate((b2, b1)):
+            high, low = split2(panel[tile_at(tile), :])
+            turned = high.T
+            acc[which] += dot(jnp.concatenate([turned, turned, low.T], axis=1), right)
+        return carry
+
+    lax.fori_loop(0, b2.shape[0] // TILE, step, 0)
+    store_square(packed, PROJECTED, acc[0])
+    store_square(packed, SIDE, acc[1])
+    store_halves(packed, keep, send)
+
+
+def cost(passes, rows, arrays):
     return pl.CostEstimate(
         flops=2 * passes * rows * R * R, bytes_accessed=4 * arrays * rows * R, transcendentals=0
     )
+
+
+def panel_gram(q_two, q_one):
+    rows = q_two.shape[0]
+    part = jax.ShapeDtypeStruct((half_of(PANEL_TERMS), LANES), F32)
+    tall = jax.ShapeDtypeStruct((rows, R), F32)
+    return pl.pallas_call(
+        panel_gram_kernel,
+        in_specs=[pl.BlockSpec(memory_space=pl.ANY)] * 2,
+        out_shape=(part, part, tall, tall),
+        scratch_shapes=[
+            pltpu.VMEM((5, R, R), F32),
+            pltpu.VMEM((PANEL_TERMS, LANES), F32),
+            pltpu.SemaphoreType.DMA((2, rows // TILE)),
+        ],
+        compiler_params=pltpu.CompilerParams(vmem_limit_bytes=VMEM_LIMIT),
+        cost_estimate=cost(7, rows, 2),
+        name="panel_gram",
+    )(pltpu.with_memory_space_constraint(q_two, pltpu.HBM), pltpu.with_memory_space_constraint(q_one, pltpu.HBM))
+
+
+def source_gram(b2, b1, sources):
+    part = jax.ShapeDtypeStruct((half_of(SOURCE_TERMS), LANES), F32)
+    return pl.pallas_call(
+        source_gram_kernel,
+        out_shape=(part, part),
+        scratch_shapes=[pltpu.VMEM((2, R, R), F32), pltpu.VMEM((SOURCE_TERMS, LANES), F32)],
+        compiler_params=pltpu.CompilerParams(vmem_limit_bytes=VMEM_LIMIT),
+        cost_estimate=cost(6, b2.shape[0], 3),
+        name="source_gram",
+    )(b2, b1, sources)
 
 
 def spread_lane(x, lane):
@@ -341,40 +379,59 @@
     store_square(side_out, 0, load_square(terms, SIDE) - dot_t_full(x[...], projected))
 
 
-def dot_three(lh, ll, rh, rl):
-    return dot(lh, rh) + (dot(lh, rl) + dot(ll, rh))
-
-
-def panel_kernel(q_two, q_one, x, out):
-    out[...] = q_one[...] - dot_three(*split2(q_two[...]), *split2(x[...]))
-
-
-def field_kernel(q_two, q_one, sources, inverse, side, x, y, out, w_ref, z_ref):
-    @pl.when(pl.program_id(0) == 0)
-    def _():
-        w = dot_full(inverse[...], load_square(side, 0))
-        w_ref[...] = w
-        z_ref[...] = y[...] - dot_full(x[...], w)
-
-    change = dot_three(*split2(q_one[...]), *split2(w_ref[...]))
-    change += dot_three(*split2(q_two[...]), *split2(z_ref[...]))
-    out[...] = sources[...] - change
-
-
-def update(kernel, tall, small, passes, name, scratch=()):
-    rows = tall[0].shape[0]
-    spec = pl.BlockSpec((TILE, R), lambda i: (i, 0))
+def wide(x):
+    high, low = split2(x)
+    return jnp.concatenate([high, high, low], axis=1)
+
+
+def tall(x):
+    high, low = split2(x)
+    return jnp.concatenate([high, low, high], axis=0)
+
+
+def by_tiles(rows, out, stage, sems, value):
+    tiles = rows // TILE
+
+    def copy(tile):
+        return pltpu.make_async_copy(stage.at[tile_at(tile)], out.at[tile_at(tile)], sems.at[tile])
+
+    def step(tile, carry):
+        stage[tile_at(tile), :] = value(tile_at(tile))
+        copy(tile).start()
+        return carry
+
+    lax.fori_loop(0, tiles, step, 0)
+    for tile in range(tiles):
+        copy(tile).wait()
+
+
+def panel_kernel(b2, b1, x, out, stage, sems):
+    right = tall(x[...])
+    by_tiles(b2.shape[0], out, stage, sems, lambda at: b1[at, :] - dot(wide(b2[at, :]), right))
+
+
+def field_kernel(b2, panel, sources, inverse, side, y, out, stage, sems):
+    weights = dot(wide(inverse[...]), tall(load_square(side, 0)))
+    right = jnp.concatenate([tall(y[...]), tall(weights)], axis=0)
+
+    def value(at):
+        left = jnp.concatenate([wide(b2[at, :]), wide(panel[at, :])], axis=1)
+        return sources[at, :] - dot(left, right)
+
+    by_tiles(b2.shape[0], out, stage, sems, value)
+
+
+def update(kernel, args, passes, name):
+    rows = args[0].shape[0]
     return pl.pallas_call(
         kernel,
-        grid=(rows // TILE,),
-        in_specs=[spec] * len(tall) + [pl.BlockSpec(x.shape, lambda i: (0, 0)) for x in small],
-        out_specs=spec,
+        out_specs=pl.BlockSpec(memory_space=pl.ANY),
         out_shape=jax.ShapeDtypeStruct((rows, R), F32),
-        scratch_shapes=list(scratch),
+        scratch_shapes=[pltpu.VMEM((rows, R), F32), pltpu.SemaphoreType.DMA((rows // TILE,))],
         compiler_params=pltpu.CompilerParams(vmem_limit_bytes=VMEM_LIMIT),
-        cost_estimate=estimate(passes, rows, len(tall) + 1),
+        cost_estimate=cost(passes, rows, 3),
         name=name,
-    )(*tall, *small)
+    )(*args)
 
 
 def exchange(x, mask):
@@ -382,67 +439,80 @@
     return lax.ppermute(x, AXES, [(i, i ^ mask) for i in range(count)])
 
 
+def rows_of(x, bit_value):
+    half = half_of(x.shape[0])
+    return lax.dynamic_slice_in_dim(x, bit_value * (x.shape[0] - half), half, 0)
+
+
 def scatter_sum(x, index, bit):
     mine = (index >> bit) & 1
-    parts = x.reshape(2, x.shape[0] // 2, x.shape[1])
-    sent = lax.dynamic_index_in_dim(parts, 1 - mine, 0, keepdims=False)
-    kept = lax.dynamic_index_in_dim(parts, mine, 0, keepdims=False)
-    return kept + exchange(sent, 1 << bit)
-
-
-def gather(x, index, bit):
+    return rows_of(x, mine) + exchange(rows_of(x, 1 - mine), 1 << bit)
+
+
+def join(x, other, rows, index, bit):
     mine = (index >> bit) & 1
-    other = exchange(x, 1 << bit)
     low = jnp.where(mine == 0, x, other)
     high = jnp.where(mine == 0, other, x)
-    return jnp.concatenate([low, high], axis=0)
+    return jnp.concatenate([low[: rows - x.shape[0]], high], axis=0)
+
+
+def gather(x, rows, index, bit):
+    return join(x, exchange(x, 1 << bit), rows, index, bit)
 
 
 def per_device(q_two, q_one, sources, coupling_two, coupling_one):
     index = lax.axis_index(AXES)
     leaf_bits = list(range(2, lax.axis_size("leaf").bit_length() + 1))
-    orders = (leaf_bits, leaf_bits[1:] + leaf_bits[:1])
-    keep, send = gram(q_two, q_one, sources)
+    panel_order, source_order = leaf_bits, leaf_bits[1:] + leaf_bits[:1]
+
+    def scatter(x, order):
+        sizes = []
+        for bit in order:
+            sizes.append(x.shape[0])
+            x = scatter_sum(x, index, bit)
+        return x, sizes
+
+    keep, send, b2, b1 = panel_gram(q_two, q_one)
     terms = keep + exchange(send, 1)
-    parts = [terms[: TERMS // 4], terms[TERMS // 4 :]]
-    for step in range(len(leaf_bits)):
-        parts = [scatter_sum(x, index, order[step]) for x, order in zip(parts, orders)]
-    for step in reversed(range(len(leaf_bits))):
-        parts = [gather(x, index, order[step]) for x, order in zip(parts, orders)]
-    terms = gather(jnp.concatenate(parts, axis=0), index, 0)
+    keep, send = source_gram(b2, b1, sources)
+    source = keep + exchange(send, 1)
+    terms, panel_sizes = scatter(terms, panel_order)
+    source, source_sizes = scatter(source, source_order)
+    for bit, rows in zip(reversed(panel_order), reversed(panel_sizes)):
+        terms = gather(terms, rows, index, bit)
+    terms = gather(terms, PANEL_TERMS, index, 0)
+    for bit, rows in zip(reversed(source_order[1:]), reversed(source_sizes[1:])):
+        source = gather(source, rows, index, bit)
+    source_arriving = exchange(source, 1 << source_order[0])
 
     def half_rows(terms):
-        parts = terms.reshape(2, terms.shape[0] // 2, LANES)
-        return lax.dynamic_index_in_dim(parts, index & 1, 0, keepdims=False)
+        return rows_of(terms, index & 1)
 
     parts = invert_first(half_index, terms, coupling_two, "level_first")
+    source_arriving, parts = lax.optimization_barrier((source_arriving, parts))
+    source = join(source, source_arriving, source_sizes[0], index, source_order[0])
+    source_arriving = exchange(source, 1)
     inverse = invert_second(parts, "level_second")
+    source_arriving, inverse = lax.optimization_barrier((source_arriving, inverse))
     x, root = call(
-        panel_solve_kernel, (SQUARE, jax.ShapeDtypeStruct((384, LANES), F32)), (inverse, terms), "panel_solve"
+        panel_solve_kernel, (SQUARE, jax.ShapeDtypeStruct((SYMMETRIC, LANES), F32)), (inverse, terms), "panel_solve"
     )
     root = half_rows(root)
     arriving = exchange(root, 2)
-    panel_one = update(panel_kernel, [q_two, q_one], [x], 3, "panel")
-    arriving, panel_one = lax.optimization_barrier((arriving, panel_one))
-    root = gather(root + arriving, index, 0)
-    terms, panel_one = lax.optimization_barrier((terms, panel_one))
+    panel_one = update(panel_kernel, [b2, b1, x], 3, "panel")
+    arriving, panel_one, source_arriving = lax.optimization_barrier((arriving, panel_one, source_arriving))
+    root = gather(root + arriving, SYMMETRIC, index, 0)
+    source = join(source, source_arriving, SOURCE_TERMS, index, 0)
     y, side = call(
-        source_solve_kernel, (SQUARE, jax.ShapeDtypeStruct((512, LANES), F32)), (inverse, x, terms), "source_solve"
+        source_solve_kernel, (SQUARE, jax.ShapeDtypeStruct((FULL, LANES), F32)), (inverse, x, source), "source_solve"
     )
     side = half_rows(side)
     arriving = exchange(side, 2)
     parts = invert_first(no_index, root, coupling_one[None], "root_first")
     arriving, parts = lax.optimization_barrier((arriving, parts))
-    side = gather(side + arriving, index, 0)
+    side = gather(side + arriving, FULL, index, 0)
     inverse = invert_second(parts, "root_second")
-    solution = update(
-        field_kernel,
-        [q_two, q_one, sources],
-        [inverse, side, x, y],
-        6,
-        "field",
-        [pltpu.VMEM((R, R), F32), pltpu.VMEM((R, R), F32)],
-    )
+    solution = update(field_kernel, [b2, panel_one, sources, inverse, side, y], 6, "field")
     return (panel_one, solution)
 
 

time: 79.2 us -> 77.3 us (0.976)
  waiting for transfers between devices: 18 us -> 16.9 us
  Pallas kernels: 33.2 us -> 32.2 us
    pallas_call x3 -> x4, Pallas kernels: 14.4 us -> 13.3 us  [the longest x2 5.92 us: update(): pl.pallas_call(kernel, out_specs=pl.BlockSpec(memory_space=pl.ANY), out_s...]
    add x1, other arithmetic: 1.12 us -> 0.04 us  [per_device(): terms = keep + exchange(send, 1)]
    ppermute x18 -> x20, waiting for transfers between devices: 18 us -> 16.9 us  [exchange(): return lax.ppermute(x, AXES, [(i, i ^ mask) for i in range(count)])]
    add x8 -> x9, other arithmetic: 0.1 us -> 1.07 us  [the longest x1 0.98 us: per_device(): source = keep + exchange(send, 1)]
    ppermute x18 -> x20, starting transfers between devices: 25 us -> 24.4 us  [exchange(): return lax.ppermute(x, AXES, [(i, i ^ mask) for i in range(count)])]
  transfers between devices with their start and end apart: 18 -> 20, of which waited for: 13 -> 12; matrix products, arithmetic and copies ran while one was open for 0% -> 3% of each run, Pallas kernels for 15% -> 26%
where the time goes in v4:
time: 77.3 us; the launch traced here: 77.1 us
  Pallas kernels  32.2 us (42%)
  starting transfers between devices  24.4 us (32%)
  waiting for transfers between devices  16.9 us (22%)
  other arithmetic  1.53 us (2%)
  between operations  1.24 us (2%)
  local copies, waits for them, and re-layouts  0.8 us (1%)
    ppermute x20, starting transfers between devices, exchange(): return lax.ppermute(x, AXES, [(i, i ^ mask) for i in range(count)])  24.4 us
    pallas_call x6, Pallas kernels, call(): pl.pallas_call(kernel, out_shape=out_shape, scratch_shapes=list(scratch),...  18.9 us
    ppermute x20, waiting for transfers between devices, exchange(): return lax.ppermute(x, AXES, [(i, i ^ mask) for i in range(count)])  16.9 us
    pallas_call x2, Pallas kernels, update(): pl.pallas_call(kernel, out_specs=pl.BlockSpec(memory_space=pl.ANY), out_s...  5.92 us
    pallas_call x1, Pallas kernels, panel_gram(): pl.pallas_call(panel_gram_kernel, in_specs=[pl.BlockSpec(memory_space=pl....  4.59 us
    pallas_call x1, Pallas kernels, source_gram(): pl.pallas_call(source_gram_kernel, out_shape=(part, part), scratch_shapes...  2.76 us
  transfers between devices with their start and end apart: 20, of which 12 were waited for; matrix products, arithmetic and copies ran while one was open for 3% of the time, Pallas kernels for 26%

profile of v4, /device:TPU:0, one launch (start us, length us, event | category | flops | bytes accessed | tf_op | source)
XLA Modules:
  0.0 77.1 jit_solution(4673823649449534704)
XLA Ops:
  0.6 0.0 copy-start.2
  0.6 4.6 %panel_gram.1 = (f32[520,128]{1,0:T(8,128)S(1)}, f32[520,128]{1,0:T(8,128)S(1)}, f32[2048,256]{1,0:T(8,128)S(1)}, f32[2048,256]{1,0:T(8,128)S(1)}) custom-call(f32[2048,256]{1,0:T(8,128)} %q_two.1, f32[2048,256]{1,0:T(8,128)} %q_one.1), custom_call_target="tpu_custom_call" | custom-call | flops 1879048192 | bytes 4194304 | tf_op jit(solution)/shard_map/panel_gram/pallas_call | solution.py:169
  5.2 0.0 copy-start
  5.3 0.0 copy-done.2
  5.3 2.8 %source_gram.1 = (f32[512,128]{1,0:T(8,128)S(1)}, f32[512,128]{1,0:T(8,128)S(1)}) custom-call(f32[2048,256]{1,0:T(8,128)S(1)} %get-tuple-element.39.b2, f32[2048,256]{1,0:T(8,128)S(1)} %get-tuple-element.40.b1, f32[2048,256]{1,0:T(8,128)S(1)} %copy-done.2), custom_call_target="tpu_custom_call" | custom-call | flops 1610612736 | bytes 6291456 | tf_op jit(solution)/shard_map/source_gram/pallas_call | solution.py:186
  8.0 0.0 copy-done
  8.0 0.5 collective-permute-start
  8.6 0.1 collective-permute-start.7
  8.6 1.2 %collective-permute-done = f32[512,128]{1,0:T(8,128)} collective-permute-done((f32[512,128]{1,0:T(8,128)S(1)}, f32[512,128]{1,0:T(8,128)}, u32[]{:S(2)}, u32[]{:S(2)}) %collective-permute-start) | collective-permute-done | bytes 262176 | tf_op jit(solution)/shard_map/ppermute | solution.py:439
  9.9 1.0 %add.76 = f32[512,128]{1,0:T(8,128)S(1)} add(f32[512,128]{1,0:T(8,128)S(1)} %get-tuple-element.41, f32[512,128]{1,0:T(8,128)} %collective-permute-done) | non-fusion elementwise | flops 65536 | bytes 786432 | tf_op jit(solution)/shard_map/add | solution.py:478
  10.8 0.7 constant_dynamic-slice_fusion.7
  11.5 2.9 %collective-permute-start.1 = (f32[256,128]{1,0:T(8,128)}, f32[256,128]{1,0:T(8,128)S(1)}, u32[]{:S(2)}, u32[]{:S(2)}) collective-permute-start(f32[256,128]{1,0:T(8,128)} %constant_dynamic-slice_fusion.7), channel_id=1, source_target_pairs={{0,8},{1,9},{2,10},{3,11},{4,12},{5,13},{6,14},{7,15},{8,0},{9,1},... | collective-permute-start | bytes 393224 | tf_op jit(solution)/shard_map/ppermute | solution.py:439
  14.5 0.0 collective-permute-done.7
  14.5 1.6 %collective-permute-start.8 = (f32[264,128]{1,0:T(8,128)S(1)}, f32[264,128]{1,0:T(8,128)S(1)}, u32[]{:S(2)}, u32[]{:S(2)}) collective-permute-start(f32[264,128]{1,0:T(8,128)S(1)} %constant_dynamic-slice_fusion.4), channel_id=1, source_target_pairs={{0,4},{1,5},{2,6},{3,7},{4,0},{5,1},{6,2},{7,3},{8,12},{9,13},{10,... | collective-permute-start | bytes 405512 | tf_op jit(solution)/shard_map/ppermute | solution.py:439
  16.1 2.4 %collective-permute-done.1 = f32[256,128]{1,0:T(8,128)S(1)} collective-permute-done((f32[256,128]{1,0:T(8,128)}, f32[256,128]{1,0:T(8,128)S(1)}, u32[]{:S(2)}, u32[]{:S(2)}) %collective-permute-start.1) | collective-permute-done | bytes 131104 | tf_op jit(solution)/shard_map/ppermute | solution.py:439
  18.5 1.5 %collective-permute-done.8 = f32[264,128]{1,0:T(8,128)S(1)} collective-permute-done((f32[264,128]{1,0:T(8,128)S(1)}, f32[264,128]{1,0:T(8,128)S(1)}, u32[]{:S(2)}, u32[]{:S(2)}) %collective-permute-start.8) | collective-permute-done | bytes 135200 | tf_op jit(solution)/shard_map/ppermute | solution.py:439
  20.0 0.4 collective-permute-start.9
  20.4 2.7 %collective-permute-start.2 = (f32[128,128]{1,0:T(8,128)S(1)}, f32[128,128]{1,0:T(8,128)S(1)}, u32[]{:S(2)}, u32[]{:S(2)}) collective-permute-start(f32[128,128]{1,0:T(8,128)S(1)} %constant_dynamic-slice_fusion.6), channel_id=1, source_target_pairs={{0,16},{1,17},{2,18},{3,19},{4,20},{5,21},{6,22},{7,23},{8,24},{9,... | collective-permute-start | bytes 196616 | tf_op jit(solution)/shard_map/ppermute | solution.py:439
  23.1 1.3 %collective-permute-done.9 = f32[136,128]{1,0:T(8,128)S(1)} collective-permute-done((f32[136,128]{1,0:T(8,128)S(1)}, f32[136,128]{1,0:T(8,128)S(1)}, u32[]{:S(2)}, u32[]{:S(2)}) %collective-permute-start.9) | collective-permute-done | bytes 69664 | tf_op jit(solution)/shard_map/ppermute | solution.py:439
  24.4 3.0 %collective-permute-start.10 = (f32[72,128]{1,0:T(8,128)S(1)}, f32[72,128]{1,0:T(8,128)S(1)}, u32[]{:S(2)}, u32[]{:S(2)}) collective-permute-start(f32[72,128]{1,0:T(8,128)S(1)} %constant_dynamic-slice_fusion.2), channel_id=1, source_target_pairs={{0,16},{1,17},{2,18},{3,19},{4,20},{5,21},{6,22},{7,23},{8,24},{9,... | collective-permute-start | bytes 110600 | tf_op jit(solution)/shard_map/ppermute | solution.py:439
  27.4 0.0 collective-permute-done.2
  27.4 2.3 %collective-permute-done.10 = f32[72,128]{1,0:T(8,128)S(1)} collective-permute-done((f32[72,128]{1,0:T(8,128)S(1)}, f32[72,128]{1,0:T(8,128)S(1)}, u32[]{:S(2)}, u32[]{:S(2)}) %collective-permute-start.10) | collective-permute-done | bytes 36896 | tf_op jit(solution)/shard_map/ppermute | solution.py:439
  29.7 2.7 %collective-permute-start.11 = (f32[72,128]{1,0:T(8,128)S(1)}, f32[72,128]{1,0:T(8,128)S(1)}, u32[]{:S(2)}, u32[]{:S(2)}) collective-permute-start(f32[72,128]{1,0:T(8,128)S(1)} %dynamic-slice_add_fusion.4), channel_id=1, source_target_pairs={{0,16},{1,17},{2,18},{3,19},{4,20},{5,21},{6,22},{7,23},{8,24},{9,... | collective-permute-start | bytes 110600 | tf_op jit(solution)/shard_map/ppermute | solution.py:439
  32.4 1.5 %collective-permute-start.3 = (f32[64,128]{1,0:T(8,128)S(1)}, f32[64,128]{1,0:T(8,128)S(1)}, u32[]{:S(2)}, u32[]{:S(2)}) collective-permute-start(f32[64,128]{1,0:T(8,128)S(1)} %constant_dynamic-slice_fusion.5), channel_id=1, source_target_pairs={{0,4},{1,5},{2,6},{3,7},{4,0},{5,1},{6,2},{7,3},{8,12},{9,13},{10,... | collective-permute-start | bytes 98312 | tf_op jit(solution)/shard_map/ppermute | solution.py:439
  33.9 0.7 collective-permute-done.11
  34.5 0.2 collective-permute-start.12
  34.7 1.6 %collective-permute-done.3 = f32[64,128]{1,0:T(8,128)S(1)} collective-permute-done((f32[64,128]{1,0:T(8,128)S(1)}, f32[64,128]{1,0:T(8,128)S(1)}, u32[]{:S(2)}, u32[]{:S(2)}) %collective-permute-start.3) | collective-permute-done | bytes 32800 | tf_op jit(solution)/shard_map/ppermute | solution.py:439
  36.4 1.5 %collective-permute-start.4 = (f32[64,128]{1,0:T(8,128)S(1)}, f32[64,128]{1,0:T(8,128)S(1)}, u32[]{:S(2)}, u32[]{:S(2)}) collective-permute-start(f32[64,128]{1,0:T(8,128)S(1)} %dynamic-slice_add_fusion.5), channel_id=1, source_target_pairs={{0,4},{1,5},{2,6},{3,7},{4,0},{5,1},{6,2},{7,3},{8,12},{9,13},{10,... | collective-permute-start | bytes 98312 | tf_op jit(solution)/shard_map/ppermute | solution.py:439
  37.9 1.8 %collective-permute-done.12 = f32[136,128]{1,0:T(8,128)S(1)} collective-permute-done((f32[136,128]{1,0:T(8,128)S(1)}, f32[136,128]{1,0:T(8,128)S(1)}, u32[]{:S(2)}, u32[]{:S(2)}) %collective-permute-start.12) | collective-permute-done | bytes 69664 | tf_op jit(solution)/shard_map/ppermute | solution.py:439
  39.7 1.9 %collective-permute-start.13 = (f32[264,128]{1,0:T(8,128)S(1)}, f32[264,128]{1,0:T(8,128)S(1)}, u32[]{:S(2)}, u32[]{:S(2)}) collective-permute-start(f32[264,128]{1,0:T(8,128)S(1)} %pad_maximum_fusion.5), channel_id=1, source_target_pairs={{0,4},{1,5},{2,6},{3,7},{4,0},{5,1},{6,2},{7,3},{8,12},{9,13},{10,... | collective-permute-start | bytes 405512 | tf_op jit(solution)/shard_map/ppermute | solution.py:439
  41.6 0.0 collective-permute-done.4
  41.6 0.0 copy-start.5
  41.6 1.7 %collective-permute-start.5 = (f32[128,128]{1,0:T(8,128)S(1)}, f32[128,128]{1,0:T(8,128)S(1)}, u32[]{:S(2)}, u32[]{:S(2)}) collective-permute-start(f32[128,128]{1,0:T(8,128)S(1)} %pad_maximum_fusion.9), channel_id=1, source_target_pairs={{0,16},{1,17},{2,18},{3,19},{4,20},{5,21},{6,22},{7,23},{8,24},{9,... | collective-permute-start | bytes 196616 | tf_op jit(solution)/shard_map/ppermute | solution.py:439
  43.3 1.4 %collective-permute-done.13 = f32[264,128]{1,0:T(8,128)S(1)} collective-permute-done((f32[264,128]{1,0:T(8,128)S(1)}, f32[264,128]{1,0:T(8,128)S(1)}, u32[]{:S(2)}, u32[]{:S(2)}) %collective-permute-start.13) | collective-permute-done | bytes 135200 | tf_op jit(solution)/shard_map/ppermute | solution.py:439
  44.8 0.1 collective-permute-start.14
  44.9 1.9 %collective-permute-done.5 = f32[128,128]{1,0:T(8,128)S(1)} collective-permute-done((f32[128,128]{1,0:T(8,128)S(1)}, f32[128,128]{1,0:T(8,128)S(1)}, u32[]{:S(2)}, u32[]{:S(2)}) %collective-permute-start.5) | collective-permute-done | bytes 65568 | tf_op jit(solution)/shard_map/ppermute | solution.py:439
  46.9 0.1 collective-permute-start.6
  47.0 0.0 collective-permute-done.14
  47.1 0.0 copy-done.5
  47.1 4.5 %level_first.1 = (f32[128,128]{1,0:T(8,128)S(1)}, f32[128,128]{1,0:T(8,128)S(1)}, f32[128,128]{1,0:T(8,128)S(1)}, f32[8,256]{1,0:T(8,128)S(1)}, f32[256,128]{1,0:T(8,128)S(1)}) custom-call(f32[1040,128]{1,0:T(8,128)S(1)} %pad_maximum_fusion.gram_ref.terms, f32[2,256,256]{2,1,0:T(8,128)S(1)} %copy-done.5), custom_call_target="tpu_custom_call" | custom-call | flops 5000000000 | bytes 262144 | tf_op jit(solution)/shard_map/level_first/pallas_call | solution.py:304
  51.6 0.3 collective-permute-done.6
  52.0 0.1 collective-permute-start.15
  52.0 0.0 copy-start.1
  52.1 4.1 %level_second.1.inverse = f32[256,256]{1,0:T(8,128)S(1)} custom-call(f32[128,128]{1,0:T(8,128)S(1)} %get-tuple-element.51.first, f32[128,128]{1,0:T(8,128)S(1)} %get-tuple-element.52.across, f32[128,128]{1,0:T(8,128)S(1)} %get-tuple-element.53.rest, f32[8,256]{1,0:T(8,128)S(1)} %get-tuple-element.54.row, f32[256,128]{1,0:T(8,128)S(1)} %get-tuple-element.55.col), custom_call_target="tpu_custom_call" | custom-call | flops 5000000000 | bytes 262144 | tf_op jit(solution)/shard_map/level_second/pallas_call | solution.py:304
  56.2 0.0 collective-permute-done.15
  56.2 1.1 %panel_solve.1 = (f32[256,256]{1,0:T(8,128)S(1)}, f32[264,128]{1,0:T(8,128)S(1)}) custom-call(f32[256,256]{1,0:T(8,128)S(1)} %level_second.1.inverse, f32[1040,128]{1,0:T(8,128)S(1)} %pad_maximum_fusion.gram_ref.terms), custom_call_target="tpu_custom_call" | custom-call | bytes 262144 | tf_op jit(solution)/shard_map/panel_solve/pallas_call | solution.py:304
  57.3 1.6 %collective-permute-start.16 = (f32[136,128]{1,0:T(8,128)S(1)}, f32[136,128]{1,0:T(8,128)S(1)}, u32[]{:S(2)}, u32[]{:S(2)}) collective-permute-start(f32[136,128]{1,0:T(8,128)S(1)} %constant_dynamic-slice_fusion.1), channel_id=1, source_target_pairs={{0,2},{1,3},{2,0},{3,1},{4,6},{5,7},{6,4},{7,5},{8,10},{9,11},{10,... | collective-permute-start | bytes 208904 | tf_op jit(solution)/shard_map/ppermute | solution.py:439
  58.9 0.0 copy-done.1
  58.9 2.4 %panel.1 = f32[2048,256]{1,0:T(8,128)} custom-call(f32[2048,256]{1,0:T(8,128)S(1)} %get-tuple-element.39.b2, f32[2048,256]{1,0:T(8,128)S(1)} %copy-done.1, f32[256,256]{1,0:T(8,128)S(1)} %get-tuple-element.58.x), custom_call_target="tpu_custom_call" | custom-call | flops 805306368 | bytes 6291456 | tf_op jit(solution)/shard_map/panel/pallas_call | solution.py:426
  61.3 0.6 collective-permute-done.16
  61.9 0.0 copy-start.6
  61.9 0.1 collective-permute-start.18
  62.1 0.6 source_solve.1
  62.8 1.6 %collective-permute-start.17 = (f32[256,128]{1,0:T(8,128)S(1)}, f32[256,128]{1,0:T(8,128)S(1)}, u32[]{:S(2)}, u32[]{:S(2)}) collective-permute-start(f32[256,128]{1,0:T(8,128)S(1)} %constant_dynamic-slice_fusion), channel_id=1, source_target_pairs={{0,2},{1,3},{2,0},{3,1},{4,6},{5,7},{6,4},{7,5},{8,10},{9,11},{10,... | collective-permute-start | bytes 393224 | tf_op jit(solution)/shard_map/ppermute | solution.py:439
  64.4 0.0 collective-permute-done.18
  64.4 0.0 copy-done.6
  64.5 4.5 %root_first.1 = (f32[128,128]{1,0:T(8,128)S(1)}, f32[128,128]{1,0:T(8,128)S(1)}, f32[128,128]{1,0:T(8,128)S(1)}, f32[8,256]{1,0:T(8,128)S(1)}, f32[256,128]{1,0:T(8,128)S(1)}) custom-call(f32[264,128]{1,0:T(8,128)S(1)} %pad_maximum_fusion.6.gram_ref, f32[1,256,256]{2,1,0:T(8,128)S(1)} %bitcast.1), custom_call_target="tpu_custom_call" | custom-call | flops 5000000000 | bytes 262144 | tf_op jit(solution)/shard_map/root_first/pallas_call | solution.py:304
  69.0 0.0 collective-permute-done.17
  69.0 0.3 collective-permute-start.19
  69.3 4.1 %root_second.1.inverse = f32[256,256]{1,0:T(8,128)S(1)} custom-call(f32[128,128]{1,0:T(8,128)S(1)} %get-tuple-element.69.first, f32[128,128]{1,0:T(8,128)S(1)} %get-tuple-element.70.across, f32[128,128]{1,0:T(8,128)S(1)} %get-tuple-element.71.rest, f32[8,256]{1,0:T(8,128)S(1)} %get-tuple-element.72.row, f32[256,128]{1,0:T(8,128)S(1)} %get-tuple-element.73.col), custom_call_target="tpu_custom_call" | custom-call | flops 5000000000 | bytes 262144 | tf_op jit(solution)/shard_map/root_second/pallas_call | solution.py:304
  73.4 0.0 collective-permute-done.19
  73.4 0.0 copy-done.3
  73.5 0.0 copy-done.4
  73.5 3.5 %field.1 = f32[2048,256]{1,0:T(8,128)} custom-call(f32[2048,256]{1,0:T(8,128)S(1)} %get-tuple-element.39.b2, f32[2048,256]{1,0:T(8,128)S(1)} %copy-done.4, f32[2048,256]{1,0:T(8,128)S(1)} %copy-done.3, f32[256,256]{1,0:T(8,128)S(1)} %root_second.1.inverse, f32[512,128]{1,0:T(8,128)S(1)} %pad_maximum_fusion.4.side, f32[256,256]{1,0:T(8,128)S(1)} %get-tuple-element.75.y), custom_call_target="tpu_custom_call" | custom-call | flops 1610612736 | bytes 6291456 | tf_op jit(solution)/shard_map/field/pallas_call | solution.py:426
  (42 shorter events, 0.6 us)
Async XLA Ops:
  0.6 4.6 %copy-start.2 = (f32[2048,256]{1,0:T(8,128)S(1)}, f32[2048,256]{1,0:T(8,128)}, u32[]{:S(2)}) copy-start(f32[2048,256]{1,0:T(8,128)} %sources.3) | copy-start | bytes 6291460
  5.2 2.8 %copy-start = (f32[2048,256]{1,0:T(8,128)}, f32[2048,256]{1,0:T(8,128)S(1)}, u32[]{:S(2)}) copy-start(f32[2048,256]{1,0:T(8,128)S(1)} %get-tuple-element.40.b1) | copy-start | bytes 6291460
  8.0 1.8 %collective-permute-start = (f32[512,128]{1,0:T(8,128)S(1)}, f32[512,128]{1,0:T(8,128)}, u32[]{:S(2)}, u32[]{:S(2)}) collective-permute-start(f32[512,128]{1,0:T(8,128)S(1)} %get-tuple-element.42), channel_id=1, source_target_pairs={{0,1},{1,0},{2,3},{3,2},{4,5},{5,4},{6,7},{7,6},{8,9},{9,8},{10,11... | collective-permute-start | bytes 786440 | tf_op jit(solution)/shard_map/ppermute | solution.py:439
  8.6 5.9 %collective-permute-start.7 = (f32[520,128]{1,0:T(8,128)S(1)}, f32[520,128]{1,0:T(8,128)S(1)}, u32[]{:S(2)}, u32[]{:S(2)}) collective-permute-start(f32[520,128]{1,0:T(8,128)S(1)} %get-tuple-element.44), channel_id=1, source_target_pairs={{0,1},{1,0},{2,3},{3,2},{4,5},{5,4},{6,7},{7,6},{8,9},{9,8},{10,11... | collective-permute-start | bytes 798728 | tf_op jit(solution)/shard_map/ppermute | solution.py:439
  11.5 7.0 %collective-permute-start.1 = (f32[256,128]{1,0:T(8,128)}, f32[256,128]{1,0:T(8,128)S(1)}, u32[]{:S(2)}, u32[]{:S(2)}) collective-permute-start(f32[256,128]{1,0:T(8,128)} %constant_dynamic-slice_fusion.7), channel_id=1, source_target_pairs={{0,8},{1,9},{2,10},{3,11},{4,12},{5,13},{6,14},{7,15},{8,0},{9,1},... | collective-permute-start | bytes 393224 | tf_op jit(solution)/shard_map/ppermute | solution.py:439
  14.5 5.4 %collective-permute-start.8 = (f32[264,128]{1,0:T(8,128)S(1)}, f32[264,128]{1,0:T(8,128)S(1)}, u32[]{:S(2)}, u32[]{:S(2)}) collective-permute-start(f32[264,128]{1,0:T(8,128)S(1)} %constant_dynamic-slice_fusion.4), channel_id=1, source_target_pairs={{0,4},{1,5},{2,6},{3,7},{4,0},{5,1},{6,2},{7,3},{8,12},{9,13},{10,... | collective-permute-start | bytes 405512 | tf_op jit(solution)/shard_map/ppermute | solution.py:439
  20.0 4.4 %collective-permute-start.9 = (f32[136,128]{1,0:T(8,128)S(1)}, f32[136,128]{1,0:T(8,128)S(1)}, u32[]{:S(2)}, u32[]{:S(2)}) collective-permute-start(f32[136,128]{1,0:T(8,128)S(1)} %constant_dynamic-slice_fusion.3), channel_id=1, source_target_pairs={{0,8},{1,9},{2,10},{3,11},{4,12},{5,13},{6,14},{7,15},{8,0},{9,1},... | collective-permute-start | bytes 208904 | tf_op jit(solution)/shard_map/ppermute | solution.py:439
  20.4 7.0 %collective-permute-start.2 = (f32[128,128]{1,0:T(8,128)S(1)}, f32[128,128]{1,0:T(8,128)S(1)}, u32[]{:S(2)}, u32[]{:S(2)}) collective-permute-start(f32[128,128]{1,0:T(8,128)S(1)} %constant_dynamic-slice_fusion.6), channel_id=1, source_target_pairs={{0,16},{1,17},{2,18},{3,19},{4,20},{5,21},{6,22},{7,23},{8,24},{9,... | collective-permute-start | bytes 196616 | tf_op jit(solution)/shard_map/ppermute | solution.py:439
  24.4 5.3 %collective-permute-start.10 = (f32[72,128]{1,0:T(8,128)S(1)}, f32[72,128]{1,0:T(8,128)S(1)}, u32[]{:S(2)}, u32[]{:S(2)}) collective-permute-start(f32[72,128]{1,0:T(8,128)S(1)} %constant_dynamic-slice_fusion.2), channel_id=1, source_target_pairs={{0,16},{1,17},{2,18},{3,19},{4,20},{5,21},{6,22},{7,23},{8,24},{9,... | collective-permute-start | bytes 110600 | tf_op jit(solution)/shard_map/ppermute | solution.py:439
  29.7 4.9 %collective-permute-start.11 = (f32[72,128]{1,0:T(8,128)S(1)}, f32[72,128]{1,0:T(8,128)S(1)}, u32[]{:S(2)}, u32[]{:S(2)}) collective-permute-start(f32[72,128]{1,0:T(8,128)S(1)} %dynamic-slice_add_fusion.4), channel_id=1, source_target_pairs={{0,16},{1,17},{2,18},{3,19},{4,20},{5,21},{6,22},{7,23},{8,24},{9,... | collective-permute-start | bytes 110600 | tf_op jit(solution)/shard_map/ppermute | solution.py:439
  32.4 4.0 %collective-permute-start.3 = (f32[64,128]{1,0:T(8,128)S(1)}, f32[64,128]{1,0:T(8,128)S(1)}, u32[]{:S(2)}, u32[]{:S(2)}) collective-permute-start(f32[64,128]{1,0:T(8,128)S(1)} %constant_dynamic-slice_fusion.5), channel_id=1, source_target_pairs={{0,4},{1,5},{2,6},{3,7},{4,0},{5,1},{6,2},{7,3},{8,12},{9,13},{10,... | collective-permute-start | bytes 98312 | tf_op jit(solution)/shard_map/ppermute | solution.py:439
  34.5 5.1 %collective-permute-start.12 = (f32[136,128]{1,0:T(8,128)S(1)}, f32[136,128]{1,0:T(8,128)S(1)}, u32[]{:S(2)}, u32[]{:S(2)}) collective-permute-start(f32[136,128]{1,0:T(8,128)S(1)} %pad_maximum_fusion.8), channel_id=1, source_target_pairs={{0,8},{1,9},{2,10},{3,11},{4,12},{5,13},{6,14},{7,15},{8,0},{9,1},... | collective-permute-start | bytes 208904 | tf_op jit(solution)/shard_map/ppermute | solution.py:439
  36.4 5.2 %collective-permute-start.4 = (f32[64,128]{1,0:T(8,128)S(1)}, f32[64,128]{1,0:T(8,128)S(1)}, u32[]{:S(2)}, u32[]{:S(2)}) collective-permute-start(f32[64,128]{1,0:T(8,128)S(1)} %dynamic-slice_add_fusion.5), channel_id=1, source_target_pairs={{0,4},{1,5},{2,6},{3,7},{4,0},{5,1},{6,2},{7,3},{8,12},{9,13},{10,... | collective-permute-start | bytes 98312 | tf_op jit(solution)/shard_map/ppermute | solution.py:439
  39.7 5.1 %collective-permute-start.13 = (f32[264,128]{1,0:T(8,128)S(1)}, f32[264,128]{1,0:T(8,128)S(1)}, u32[]{:S(2)}, u32[]{:S(2)}) collective-permute-start(f32[264,128]{1,0:T(8,128)S(1)} %pad_maximum_fusion.5), channel_id=1, source_target_pairs={{0,4},{1,5},{2,6},{3,7},{4,0},{5,1},{6,2},{7,3},{8,12},{9,13},{10,... | collective-permute-start | bytes 405512 | tf_op jit(solution)/shard_map/ppermute | solution.py:439
  41.6 5.5 %copy-start.5 = (f32[2,256,256]{2,1,0:T(8,128)S(1)}, f32[2,256,256]{2,1,0:T(8,128)}, u32[]{:S(2)}) copy-start(f32[2,256,256]{2,1,0:T(8,128)} %coupling.1) | copy-start | bytes 1572868
  41.6 5.2 %collective-permute-start.5 = (f32[128,128]{1,0:T(8,128)S(1)}, f32[128,128]{1,0:T(8,128)S(1)}, u32[]{:S(2)}, u32[]{:S(2)}) collective-permute-start(f32[128,128]{1,0:T(8,128)S(1)} %pad_maximum_fusion.9), channel_id=1, source_target_pairs={{0,16},{1,17},{2,18},{3,19},{4,20},{5,21},{6,22},{7,23},{8,24},{9,... | collective-permute-start | bytes 196616 | tf_op jit(solution)/shard_map/ppermute | solution.py:439
  44.8 2.1 %collective-permute-start.14 = (f32[520,128]{1,0:T(8,128)S(1)}, f32[520,128]{1,0:T(8,128)S(1)}, u32[]{:S(2)}, u32[]{:S(2)}) collective-permute-start(f32[520,128]{1,0:T(8,128)S(1)} %pad_maximum_fusion.2), channel_id=1, source_target_pairs={{0,1},{1,0},{2,3},{3,2},{4,5},{5,4},{6,7},{7,6},{8,9},{9,8},{10,11... | collective-permute-start | bytes 798728 | tf_op jit(solution)/shard_map/ppermute | solution.py:439
  46.9 5.0 %collective-permute-start.6 = (f32[256,128]{1,0:T(8,128)S(1)}, f32[256,128]{1,0:T(8,128)S(1)}, u32[]{:S(2)}, u32[]{:S(2)}) collective-permute-start(f32[256,128]{1,0:T(8,128)S(1)} %pad_maximum_fusion.7), channel_id=1, source_target_pairs={{0,8},{1,9},{2,10},{3,11},{4,12},{5,13},{6,14},{7,15},{8,0},{9,1},... | collective-permute-start | bytes 393224 | tf_op jit(solution)/shard_map/ppermute | solution.py:439
  52.0 4.2 %collective-permute-start.15 = (f32[512,128]{1,0:T(8,128)S(1)}, f32[512,128]{1,0:T(8,128)S(1)}, u32[]{:S(2)}, u32[]{:S(2)}) collective-permute-start(f32[512,128]{1,0:T(8,128)S(1)} %pad_maximum_fusion.3), channel_id=1, source_target_pairs={{0,1},{1,0},{2,3},{3,2},{4,5},{5,4},{6,7},{7,6},{8,9},{9,8},{10,11... | collective-permute-start | bytes 786440 | tf_op jit(solution)/shard_map/ppermute | solution.py:439
  52.0 6.8 %copy-start.1 = (f32[2048,256]{1,0:T(8,128)S(1)}, f32[2048,256]{1,0:T(8,128)}, u32[]{:S(2)}) copy-start(f32[2048,256]{1,0:T(8,128)} %copy-done) | copy-start | bytes 6291460
  57.3 4.6 %collective-permute-start.16 = (f32[136,128]{1,0:T(8,128)S(1)}, f32[136,128]{1,0:T(8,128)S(1)}, u32[]{:S(2)}, u32[]{:S(2)}) collective-permute-start(f32[136,128]{1,0:T(8,128)S(1)} %constant_dynamic-slice_fusion.1), channel_id=1, source_target_pairs={{0,2},{1,3},{2,0},{3,1},{4,6},{5,7},{6,4},{7,5},{8,10},{9,11},{10,... | collective-permute-start | bytes 208904 | tf_op jit(solution)/shard_map/ppermute | solution.py:439
  61.9 2.5 %copy-start.6 = (f32[256,256]{1,0:T(8,128)S(1)}, f32[256,256]{1,0:T(8,128)}, u32[]{:S(2)}) copy-start(f32[256,256]{1,0:T(8,128)} %param.9) | copy-start | bytes 786436
  61.9 2.4 %collective-permute-start.18 = (f32[136,128]{1,0:T(8,128)S(1)}, f32[136,128]{1,0:T(8,128)S(1)}, u32[]{:S(2)}, u32[]{:S(2)}) collective-permute-start(f32[136,128]{1,0:T(8,128)S(1)} %fusion.5), channel_id=1, source_target_pairs={{0,1},{1,0},{2,3},{3,2},{4,5},{5,4},{6,7},{7,6},{8,9},{9,8},{10,11... | collective-permute-start | bytes 208904 | tf_op jit(solution)/shard_map/ppermute | solution.py:439
  62.8 6.2 %collective-permute-start.17 = (f32[256,128]{1,0:T(8,128)S(1)}, f32[256,128]{1,0:T(8,128)S(1)}, u32[]{:S(2)}, u32[]{:S(2)}) collective-permute-start(f32[256,128]{1,0:T(8,128)S(1)} %constant_dynamic-slice_fusion), channel_id=1, source_target_pairs={{0,2},{1,3},{2,0},{3,1},{4,6},{5,7},{6,4},{7,5},{8,10},{9,11},{10,... | collective-permute-start | bytes 393224 | tf_op jit(solution)/shard_map/ppermute | solution.py:439
  69.0 4.4 %collective-permute-start.19 = (f32[256,128]{1,0:T(8,128)S(1)}, f32[256,128]{1,0:T(8,128)S(1)}, u32[]{:S(2)}, u32[]{:S(2)}) collective-permute-start(f32[256,128]{1,0:T(8,128)S(1)} %fusion.4), channel_id=1, source_target_pairs={{0,1},{1,0},{2,3},{3,2},{4,5},{5,4},{6,7},{7,6},{8,9},{9,8},{10,11... | collective-permute-start | bytes 393224 | tf_op jit(solution)/shard_map/ppermute | solution.py:439
  69.3 4.2 %copy-start.3 = (f32[2048,256]{1,0:T(8,128)S(1)}, f32[2048,256]{1,0:T(8,128)}, u32[]{:S(2)}) copy-start(f32[2048,256]{1,0:T(8,128)} %sources.3) | copy-start | bytes 6291460
  69.3 4.2 %copy-start.4 = (f32[2048,256]{1,0:T(8,128)S(1)}, f32[2048,256]{1,0:T(8,128)}, u32[]{:S(2)}) copy-start(f32[2048,256]{1,0:T(8,128)} %panel.1) | copy-start | bytes 6291460

commit v5 on v4

--- a/solution.py
+++ b/solution.py
@@ -17,7 +17,6 @@
 VMEM_LIMIT = 40 * 1024 * 1024
 SYMMETRIC, FULL = 264, 512
 OWN, ROOT, CROSS, PANEL_TERMS = 0, 264, 528, 1040
-PROJECTED, SIDE, SOURCE_TERMS = 0, 512, 1024
 
 
 def split2(x):
@@ -138,22 +137,19 @@
     store_halves(packed, keep, send)
 
 
-def source_gram_kernel(b2, b1, sources, keep, send, acc, packed):
+def source_gram_kernel(b2, b1, sources, keep, send, acc):
     acc[...] = jnp.zeros_like(acc)
 
     def step(tile, carry):
-        hs, ls = split2(sources[tile_at(tile), :])
-        right = jnp.concatenate([hs, ls, hs], axis=0)
-        for which, panel in enumerate((b2, b1)):
-            high, low = split2(panel[tile_at(tile), :])
-            turned = high.T
-            acc[which] += dot(jnp.concatenate([turned, turned, low.T], axis=1), right)
+        high, low = split2(sources[tile_at(tile), :])
+        turned = high.T
+        left = jnp.concatenate([turned, turned, low.T], axis=1)
+        acc[:, :R] += dot(left, tall(b2[tile_at(tile), :]))
+        acc[:, R:] += dot(left, tall(b1[tile_at(tile), :]))
         return carry
 
     lax.fori_loop(0, b2.shape[0] // TILE, step, 0)
-    store_square(packed, PROJECTED, acc[0])
-    store_square(packed, SIDE, acc[1])
-    store_halves(packed, keep, send)
+    store_halves(acc, keep, send)
 
 
 def cost(passes, rows, arrays):
@@ -182,11 +178,11 @@
 
 
 def source_gram(b2, b1, sources):
-    part = jax.ShapeDtypeStruct((half_of(SOURCE_TERMS), LANES), F32)
+    part = jax.ShapeDtypeStruct((half_of(R), 2 * R), F32)
     return pl.pallas_call(
         source_gram_kernel,
         out_shape=(part, part),
-        scratch_shapes=[pltpu.VMEM((2, R, R), F32), pltpu.VMEM((SOURCE_TERMS, LANES), F32)],
+        scratch_shapes=[pltpu.VMEM((R, 2 * R), F32)],
         compiler_params=pltpu.CompilerParams(vmem_limit_bytes=VMEM_LIMIT),
         cost_estimate=cost(6, b2.shape[0], 3),
         name="source_gram",
@@ -366,17 +362,17 @@
     return 0
 
 
-def panel_solve_kernel(inverse, terms, x_out, root_out):
+def level_solve_kernel(inverse, terms, source, x_out, root_out, y_out, side_out):
     cross = load_square(terms, CROSS)
     x = dot_full(inverse[...], cross)
     x_out[...] = x
     store_symmetric(root_out, 0, load_symmetric(terms, ROOT) - dot_t_full(cross, x))
-
-
-def source_solve_kernel(inverse, x, terms, y_out, side_out):
-    projected = load_square(terms, PROJECTED)
-    y_out[...] = dot_full(inverse[...], projected)
-    store_square(side_out, 0, load_square(terms, SIDE) - dot_t_full(x[...], projected))
+    projected = source[:, :R]
+    y_out[...] = dot_full(projected, inverse[...])
+    side = source[:, R:] - dot_full(projected, x)
+    count = side.shape[0]
+    side_out[:count, :] = side[:, :LANES]
+    side_out[count:, :] = side[:, LANES:]
 
 
 def wide(x):
@@ -410,9 +406,9 @@
     by_tiles(b2.shape[0], out, stage, sems, lambda at: b1[at, :] - dot(wide(b2[at, :]), right))
 
 
-def field_kernel(b2, panel, sources, inverse, side, y, out, stage, sems):
-    weights = dot(wide(inverse[...]), tall(load_square(side, 0)))
-    right = jnp.concatenate([tall(y[...]), tall(weights)], axis=0)
+def field_kernel(b2, panel, sources, inverse, solved, out, stage, sems):
+    weights = dot(wide(solved[:, R:]), tall(inverse[...])).T
+    right = jnp.concatenate([tall(solved[:, :R].T), tall(weights)], axis=0)
 
     def value(at):
         left = jnp.concatenate([wide(b2[at, :]), wide(panel[at, :])], axis=1)
@@ -463,56 +459,83 @@
 def per_device(q_two, q_one, sources, coupling_two, coupling_one):
     index = lax.axis_index(AXES)
     leaf_bits = list(range(2, lax.axis_size("leaf").bit_length() + 1))
-    panel_order, source_order = leaf_bits, leaf_bits[1:] + leaf_bits[:1]
-
-    def scatter(x, order):
-        sizes = []
-        for bit in order:
-            sizes.append(x.shape[0])
-            x = scatter_sum(x, index, bit)
-        return x, sizes
-
-    keep, send, b2, b1 = panel_gram(q_two, q_one)
-    terms = keep + exchange(send, 1)
-    keep, send = source_gram(b2, b1, sources)
-    source = keep + exchange(send, 1)
-    terms, panel_sizes = scatter(terms, panel_order)
-    source, source_sizes = scatter(source, source_order)
-    for bit, rows in zip(reversed(panel_order), reversed(panel_sizes)):
-        terms = gather(terms, rows, index, bit)
-    terms = gather(terms, PANEL_TERMS, index, 0)
-    for bit, rows in zip(reversed(source_order[1:]), reversed(source_sizes[1:])):
-        source = gather(source, rows, index, bit)
-    source_arriving = exchange(source, 1 << source_order[0])
+    panel_order = source_order = leaf_bits
+
+    def after(x, *others):
+        return lax.optimization_barrier((x,) + others)[0]
 
     def half_rows(terms):
         return rows_of(terms, index & 1)
 
+    keep, send, b2, b1 = panel_gram(q_two, q_one)
+    arriving = exchange(send, 1)
+    source_keep, source_send = source_gram(b2, b1, sources)
+    arriving, source_send = lax.optimization_barrier((arriving, source_send))
+    terms = keep + arriving
+    source = source_keep + exchange(source_send, 1)
+    sizes, source_sizes = [], []
+    source_left = list(source_order)
+
+    def source_start(source):
+        bit = source_left.pop(0)
+        mine = (index >> bit) & 1
+        source_sizes.append(source.shape[0])
+        return rows_of(source, mine), exchange(rows_of(source, 1 - mine), 1 << bit)
+
+    for step, bit in enumerate(panel_order):
+        sizes.append(terms.shape[0])
+        terms = scatter_sum(terms, index, bit)
+        if step == 0:
+            terms, source = lax.optimization_barrier((terms, source))
+            kept, flying = source_start(source)
+    terms, flying = lax.optimization_barrier((terms, flying))
+    source = kept + flying
+    for step, bit in reversed(list(enumerate(panel_order))):
+        if step == 0:
+            terms, source = lax.optimization_barrier((terms, source))
+            kept, flying = source_start(source)
+        terms = gather(terms, sizes[step], index, bit)
+    terms, flying = lax.optimization_barrier((terms, flying))
+    source = kept + flying
+    terms = gather(terms, PANEL_TERMS, index, 0)
+    kept, flying = source_start(after(source, terms))
+    flying = (kept, flying)
+
     parts = invert_first(half_index, terms, coupling_two, "level_first")
-    source_arriving, parts = lax.optimization_barrier((source_arriving, parts))
-    source = join(source, source_arriving, source_sizes[0], index, source_order[0])
-    source_arriving = exchange(source, 1)
+    source = flying[0] + after(flying[1], *parts)
+    while source_left:
+        kept, flying = source_start(source)
+        source = kept + flying
     inverse = invert_second(parts, "level_second")
-    source_arriving, inverse = lax.optimization_barrier((source_arriving, inverse))
-    x, root = call(
-        panel_solve_kernel, (SQUARE, jax.ShapeDtypeStruct((SYMMETRIC, LANES), F32)), (inverse, terms), "panel_solve"
+    count = source.shape[0]
+    shapes = (
+        SQUARE,
+        jax.ShapeDtypeStruct((SYMMETRIC, LANES), F32),
+        jax.ShapeDtypeStruct((count, R), F32),
+        jax.ShapeDtypeStruct((2 * count, LANES), F32),
     )
-    root = half_rows(root)
-    arriving = exchange(root, 2)
+    x, root, y, side = call(level_solve_kernel, shapes, (inverse, terms, source), "level_solve")
+    both = jnp.concatenate([half_rows(root), side], axis=0)
+    arriving = exchange(both, 2)
     panel_one = update(panel_kernel, [b2, b1, x], 3, "panel")
-    arriving, panel_one, source_arriving = lax.optimization_barrier((arriving, panel_one, source_arriving))
-    root = gather(root + arriving, SYMMETRIC, index, 0)
-    source = join(source, source_arriving, SOURCE_TERMS, index, 0)
-    y, side = call(
-        source_solve_kernel, (SQUARE, jax.ShapeDtypeStruct((FULL, LANES), F32)), (inverse, x, source), "source_solve"
-    )
-    side = half_rows(side)
-    arriving = exchange(side, 2)
+    arriving, panel_one = lax.optimization_barrier((arriving, panel_one))
+    both = both + arriving
+    root, side = both[: -2 * count], both[-2 * count :]
+    solved = jnp.concatenate([y, side[:count], side[count:]], axis=1)
+
+    back = list(zip(reversed(source_order), reversed(source_sizes)))
+    *early, (middle_bit, middle_size), (last_bit, last_size) = back
+    for bit, rows in early:
+        solved = gather(solved, rows, index, bit)
+    root = gather(root, SYMMETRIC, index, 0)
+    solved_arriving = exchange(solved, 1 << middle_bit)
     parts = invert_first(no_index, root, coupling_one[None], "root_first")
-    arriving, parts = lax.optimization_barrier((arriving, parts))
-    side = gather(side + arriving, FULL, index, 0)
+    solved = join(solved, after(solved_arriving, *parts), middle_size, index, middle_bit)
+    solved_arriving = exchange(solved, 1 << last_bit)
     inverse = invert_second(parts, "root_second")
-    solution = update(field_kernel, [b2, panel_one, sources, inverse, side, y], 6, "field")
+    solved = join(solved, after(solved_arriving, inverse), last_size, index, last_bit)
+    solved = gather(solved, R, index, 0)
+    solution = update(field_kernel, [b2, panel_one, sources, inverse, solved], 6, "field")
     return (panel_one, solution)
 
 

time: 77.3 us -> 85.9 us (1.11)
  waiting for transfers between devices: 16.9 us -> 26.4 us
  local copies, waits for them, and re-layouts: 0.8 us -> 4.62 us
  starting transfers between devices: 24.4 us -> 21.5 us
  other arithmetic: 1.53 us -> 0.56 us
    ppermute x20 -> x18, waiting for transfers between devices: 16.9 us -> 26.4 us  [exchange(): return lax.ppermute(x, AXES, [(i, i ^ mask) for i in range(count)])]
    unnamed x14 -> x16, local copies, waits for them, and re-layouts: 0.04 us -> 4.52 us
    ppermute x20 -> x18, starting transfers between devices: 24.4 us -> 21.5 us  [exchange(): return lax.ppermute(x, AXES, [(i, i ^ mask) for i in range(count)])]
    add x4 -> x6, other arithmetic: 1.04 us -> 0.14 us  [the longest x1 0.04 us: per_device(): source = source_keep + exchange(source_send, 1)]
    pallas_call x6 -> x5, Pallas kernels: 18.9 us -> 18.4 us  [call(): pl.pallas_call(kernel, out_shape=out_shape, scratch_shapes=list(scratch),...]
  transfers between devices with their start and end apart: 20 -> 18, of which waited for: 12 -> 11; matrix products, arithmetic and copies ran while one was open for 3% -> 0% of each run, Pallas kernels for 26% -> 26%
where the time goes in v5:
time: 85.9 us; the launch traced here: 85.7 us
  Pallas kernels  31.4 us (37%)
  waiting for transfers between devices  26.4 us (31%)
  starting transfers between devices  21.5 us (25%)
  local copies, waits for them, and re-layouts  4.62 us (5%)
  between operations  1.24 us (1%)
    ppermute x18, waiting for transfers between devices, exchange(): return lax.ppermute(x, AXES, [(i, i ^ mask) for i in range(count)])  26.4 us
    ppermute x18, starting transfers between devices, exchange(): return lax.ppermute(x, AXES, [(i, i ^ mask) for i in range(count)])  21.5 us
    pallas_call x5, Pallas kernels, call(): pl.pallas_call(kernel, out_shape=out_shape, scratch_shapes=list(scratch),...  18.4 us
    pallas_call x2, Pallas kernels, update(): pl.pallas_call(kernel, out_specs=pl.BlockSpec(memory_space=pl.ANY), out_s...  5.96 us
    unnamed x16, local copies, waits for them, and re-layouts  4.52 us
    pallas_call x1, Pallas kernels, panel_gram(): pl.pallas_call(panel_gram_kernel, in_specs=[pl.BlockSpec(memory_space=pl....  4.44 us
    pallas_call x1, Pallas kernels, source_gram(): pl.pallas_call(source_gram_kernel, out_shape=(part, part), scratch_shapes...  2.52 us
  transfers between devices with their start and end apart: 18, of which 11 were waited for; matrix products, arithmetic and copies ran while one was open for 0% of the time, Pallas kernels for 26%

profile of v5, /device:TPU:0, one launch (start us, length us, event | category | flops | bytes accessed | tf_op | source)
XLA Modules:
  0.0 85.7 jit_solution(1878318976333058799)
XLA Ops:
  0.6 4.4 %panel_gram.1 = (f32[520,128]{1,0:T(8,128)S(1)}, f32[520,128]{1,0:T(8,128)S(1)}, f32[2048,256]{1,0:T(8,128)S(1)}, f32[2048,256]{1,0:T(8,128)S(1)}) custom-call(f32[2048,256]{1,0:T(8,128)} %q_two.1, f32[2048,256]{1,0:T(8,128)} %q_one.1), custom_call_target="tpu_custom_call" | custom-call | flops 1879048192 | bytes 4194304 | tf_op jit(solution)/shard_map/panel_gram/pallas_call | solution.py:165
  5.1 0.0 copy-start
  5.1 1.3 %copy-done = f32[2048,256]{1,0:T(8,128)} copy-done((f32[2048,256]{1,0:T(8,128)}, f32[2048,256]{1,0:T(8,128)S(1)}, u32[]{:S(2)}) %copy-start) | copy-done | bytes 2097176
  6.4 0.4 collective-permute-start
  6.8 0.0 copy-start.1
  6.9 1.6 %copy-done.1 = f32[2048,256]{1,0:T(8,128)S(1)} copy-done((f32[2048,256]{1,0:T(8,128)S(1)}, f32[2048,256]{1,0:T(8,128)}, u32[]{:S(2)}) %copy-start.1) | copy-done | bytes 2097176
  8.4 0.0 copy-start.3
  8.4 1.6 %copy-done.3 = f32[2048,256]{1,0:T(8,128)S(1)} copy-done((f32[2048,256]{1,0:T(8,128)S(1)}, f32[2048,256]{1,0:T(8,128)}, u32[]{:S(2)}) %copy-start.3) | copy-done | bytes 2097176
  10.0 2.5 %source_gram.1 = (f32[128,512]{1,0:T(8,128)S(1)}, f32[128,512]{1,0:T(8,128)S(1)}) custom-call(f32[2048,256]{1,0:T(8,128)S(1)} %get-tuple-element.40.b2, f32[2048,256]{1,0:T(8,128)S(1)} %copy-done.1, f32[2048,256]{1,0:T(8,128)S(1)} %copy-done.3), custom_call_target="tpu_custom_call" | custom-call | flops 1610612736 | bytes 6291456 | tf_op jit(solution)/shard_map/source_gram/pallas_call | solution.py:182
  12.6 0.0 collective-permute-done
  12.6 2.6 %collective-permute-start.1 = (f32[264,128]{1,0:T(8,128)S(1)}, f32[264,128]{1,0:T(8,128)S(1)}, u32[]{:S(2)}, u32[]{:S(2)}) collective-permute-start(f32[264,128]{1,0:T(8,128)S(1)} %constant_dynamic-slice_fusion.6), channel_id=1, source_target_pairs={{0,4},{1,5},{2,6},{3,7},{4,0},{5,1},{6,2},{7,3},{8,12},{9,13},{10,... | collective-permute-start | bytes 405512 | tf_op jit(solution)/shard_map/ppermute | solution.py:435
  15.2 0.2 collective-permute-start.2
  15.4 4.0 %collective-permute-done.1 = f32[264,128]{1,0:T(8,128)S(1)} collective-permute-done((f32[264,128]{1,0:T(8,128)S(1)}, f32[264,128]{1,0:T(8,128)S(1)}, u32[]{:S(2)}, u32[]{:S(2)}) %collective-permute-start.1) | collective-permute-done | bytes 135200 | tf_op jit(solution)/shard_map/ppermute | solution.py:435
  19.5 0.0 collective-permute-done.2
  19.5 1.9 %collective-permute-start.3 = (f32[136,128]{1,0:T(8,128)S(1)}, f32[136,128]{1,0:T(8,128)S(1)}, u32[]{:S(2)}, u32[]{:S(2)}) collective-permute-start(f32[136,128]{1,0:T(8,128)S(1)} %constant_dynamic-slice_fusion.5), channel_id=1, source_target_pairs={{0,8},{1,9},{2,10},{3,11},{4,12},{5,13},{6,14},{7,15},{8,0},{9,1},... | collective-permute-start | bytes 208904 | tf_op jit(solution)/shard_map/ppermute | solution.py:435
  21.4 2.5 %collective-permute-done.3 = f32[136,128]{1,0:T(8,128)S(1)} collective-permute-done((f32[136,128]{1,0:T(8,128)S(1)}, f32[136,128]{1,0:T(8,128)S(1)}, u32[]{:S(2)}, u32[]{:S(2)}) %collective-permute-start.3) | collective-permute-done | bytes 69664 | tf_op jit(solution)/shard_map/ppermute | solution.py:435
  24.0 2.9 %collective-permute-start.4 = (f32[72,128]{1,0:T(8,128)S(1)}, f32[72,128]{1,0:T(8,128)S(1)}, u32[]{:S(2)}, u32[]{:S(2)}) collective-permute-start(f32[72,128]{1,0:T(8,128)S(1)} %constant_dynamic-slice_fusion.4), channel_id=1, source_target_pairs={{0,16},{1,17},{2,18},{3,19},{4,20},{5,21},{6,22},{7,23},{8,24},{9,... | collective-permute-start | bytes 110600 | tf_op jit(solution)/shard_map/ppermute | solution.py:435
  26.9 1.6 %collective-permute-start.5 = (f32[64,512]{1,0:T(8,128)S(1)}, f32[64,512]{1,0:T(8,128)S(1)}, u32[]{:S(2)}, u32[]{:S(2)}) collective-permute-start(f32[64,512]{1,0:T(8,128)S(1)} %constant_dynamic-slice_fusion.3), channel_id=1, source_target_pairs={{0,4},{1,5},{2,6},{3,7},{4,0},{5,1},{6,2},{7,3},{8,12},{9,13},{10,... | collective-permute-start | bytes 393224 | tf_op jit(solution)/shard_map/ppermute | solution.py:435
  28.4 0.4 collective-permute-done.4
  28.9 3.0 %collective-permute-done.5 = f32[64,512]{1,0:T(8,128)S(1)} collective-permute-done((f32[64,512]{1,0:T(8,128)S(1)}, f32[64,512]{1,0:T(8,128)S(1)}, u32[]{:S(2)}, u32[]{:S(2)}) %collective-permute-start.5) | collective-permute-done | bytes 131104 | tf_op jit(solution)/shard_map/ppermute | solution.py:435
  31.9 0.1 collective-permute-start.6
  32.0 4.8 %collective-permute-done.6 = f32[72,128]{1,0:T(8,128)S(1)} collective-permute-done((f32[72,128]{1,0:T(8,128)S(1)}, f32[72,128]{1,0:T(8,128)S(1)}, u32[]{:S(2)}, u32[]{:S(2)}) %collective-permute-start.6) | collective-permute-done | bytes 36896 | tf_op jit(solution)/shard_map/ppermute | solution.py:435
  36.8 1.6 %collective-permute-start.7 = (f32[136,128]{1,0:T(8,128)S(1)}, f32[136,128]{1,0:T(8,128)S(1)}, u32[]{:S(2)}, u32[]{:S(2)}) collective-permute-start(f32[136,128]{1,0:T(8,128)S(1)} %pad_maximum_fusion.8), channel_id=1, source_target_pairs={{0,8},{1,9},{2,10},{3,11},{4,12},{5,13},{6,14},{7,15},{8,0},{9,1},... | collective-permute-start | bytes 208904 | tf_op jit(solution)/shard_map/ppermute | solution.py:435
  38.5 3.4 %collective-permute-done.7 = f32[136,128]{1,0:T(8,128)S(1)} collective-permute-done((f32[136,128]{1,0:T(8,128)S(1)}, f32[136,128]{1,0:T(8,128)S(1)}, u32[]{:S(2)}, u32[]{:S(2)}) %collective-permute-start.7) | collective-permute-done | bytes 69664 | tf_op jit(solution)/shard_map/ppermute | solution.py:435
  41.9 0.0 copy-start.6
  41.9 0.9 %collective-permute-start.8 = (f32[264,128]{1,0:T(8,128)S(1)}, f32[264,128]{1,0:T(8,128)S(1)}, u32[]{:S(2)}, u32[]{:S(2)}) collective-permute-start(f32[264,128]{1,0:T(8,128)S(1)} %pad_maximum_fusion.4), channel_id=1, source_target_pairs={{0,4},{1,5},{2,6},{3,7},{4,0},{5,1},{6,2},{7,3},{8,12},{9,13},{10,... | collective-permute-start | bytes 405512 | tf_op jit(solution)/shard_map/ppermute | solution.py:435
  42.8 1.6 %collective-permute-start.9 = (f32[32,512]{1,0:T(8,128)S(1)}, f32[32,512]{1,0:T(8,128)S(1)}, u32[]{:S(2)}, u32[]{:S(2)}) collective-permute-start(f32[32,512]{1,0:T(8,128)S(1)} %constant_dynamic-slice_fusion.2), channel_id=1, source_target_pairs={{0,8},{1,9},{2,10},{3,11},{4,12},{5,13},{6,14},{7,15},{8,0},{9,1},... | collective-permute-start | bytes 196616 | tf_op jit(solution)/shard_map/ppermute | solution.py:435
  44.4 2.6 %collective-permute-done.8 = f32[264,128]{1,0:T(8,128)S(1)} collective-permute-done((f32[264,128]{1,0:T(8,128)S(1)}, f32[264,128]{1,0:T(8,128)S(1)}, u32[]{:S(2)}, u32[]{:S(2)}) %collective-permute-start.8) | collective-permute-done | bytes 135200 | tf_op jit(solution)/shard_map/ppermute | solution.py:435
  47.1 0.0 collective-permute-done.9
  47.1 0.1 collective-permute-start.10
  47.2 1.5 %collective-permute-done.10 = f32[520,128]{1,0:T(8,128)S(1)} collective-permute-done((f32[520,128]{1,0:T(8,128)S(1)}, f32[520,128]{1,0:T(8,128)S(1)}, u32[]{:S(2)}, u32[]{:S(2)}) %collective-permute-start.10) | collective-permute-done | bytes 266272 | tf_op jit(solution)/shard_map/ppermute | solution.py:435
  48.8 0.3 collective-permute-start.11
  49.1 0.0 copy-done.6
  49.1 4.5 %level_first.1 = (f32[128,128]{1,0:T(8,128)S(1)}, f32[128,128]{1,0:T(8,128)S(1)}, f32[128,128]{1,0:T(8,128)S(1)}, f32[8,256]{1,0:T(8,128)S(1)}, f32[256,128]{1,0:T(8,128)S(1)}) custom-call(f32[1040,128]{1,0:T(8,128)S(1)} %pad_maximum_fusion.gram_ref.terms, f32[2,256,256]{2,1,0:T(8,128)S(1)} %copy-done.6), custom_call_target="tpu_custom_call" | custom-call | flops 5000000000 | bytes 262144 | tf_op jit(solution)/shard_map/level_first/pallas_call | solution.py:300
  53.6 0.0 copy-start.2
  53.7 4.1 %level_second.1.inverse = f32[256,256]{1,0:T(8,128)S(1)} custom-call(f32[128,128]{1,0:T(8,128)S(1)} %get-tuple-element.53.first, f32[128,128]{1,0:T(8,128)S(1)} %get-tuple-element.54.across, f32[128,128]{1,0:T(8,128)S(1)} %get-tuple-element.55.rest, f32[8,256]{1,0:T(8,128)S(1)} %get-tuple-element.56.row, f32[256,128]{1,0:T(8,128)S(1)} %get-tuple-element.57.col), custom_call_target="tpu_custom_call" | custom-call | flops 5000000000 | bytes 262144 | tf_op jit(solution)/shard_map/level_second/pallas_call | solution.py:300
  57.8 0.0 collective-permute-done.11
  57.8 1.3 %level_solve.1 = (f32[256,256]{1,0:T(8,128)S(1)}, f32[264,128]{1,0:T(8,128)S(1)}, f32[16,256]{1,0:T(8,128)S(1)}, f32[32,128]{1,0:T(8,128)S(1)}) custom-call(f32[256,256]{1,0:T(8,128)S(1)} %level_second.1.inverse, f32[1040,128]{1,0:T(8,128)S(1)} %pad_maximum_fusion.gram_ref.terms, f32[16,512]{1,0:T(8,128)S(1)} %dynamic-slice_add_fusion.5.source), custom_call_target="tpu_custom_call" | custom-call | bytes 262144 | tf_op jit(solution)/shard_map/level_solve/pallas_call | solution.py:300
  59.1 1.7 %collective-permute-start.12 = (f32[168,128]{1,0:T(8,128)S(1)}, f32[168,128]{1,0:T(8,128)S(1)}, u32[]{:S(2)}, u32[]{:S(2)}) collective-permute-start(f32[168,128]{1,0:T(8,128)S(1)} %pad_maximum_fusion.7), channel_id=1, source_target_pairs={{0,2},{1,3},{2,0},{3,1},{4,6},{5,7},{6,4},{7,5},{8,10},{9,11},{10,... | collective-permute-start | bytes 258056 | tf_op jit(solution)/shard_map/ppermute | solution.py:435
  60.7 0.0 copy-done.2
  60.7 0.0 copy-start.7
  60.7 2.4 %panel.1 = f32[2048,256]{1,0:T(8,128)} custom-call(f32[2048,256]{1,0:T(8,128)S(1)} %get-tuple-element.40.b2, f32[2048,256]{1,0:T(8,128)S(1)} %copy-done.2, f32[256,256]{1,0:T(8,128)S(1)} %get-tuple-element.63.x), custom_call_target="tpu_custom_call" | custom-call | flops 805306368 | bytes 6291456 | tf_op jit(solution)/shard_map/panel/pallas_call | solution.py:422
  63.2 0.5 collective-permute-done.12
  63.7 2.7 %collective-permute-start.14 = (f32[16,512]{1,0:T(8,128)S(1)}, f32[16,512]{1,0:T(8,128)S(1)}, u32[]{:S(2)}, u32[]{:S(2)}) collective-permute-start(f32[16,512]{1,0:T(8,128)S(1)} %pad_maximum_fusion.10), channel_id=1, source_target_pairs={{0,16},{1,17},{2,18},{3,19},{4,20},{5,21},{6,22},{7,23},{8,24},{9,... | collective-permute-start | bytes 98312 | tf_op jit(solution)/shard_map/ppermute | solution.py:435
  66.4 0.0 collective-permute-start.13
  66.4 2.1 %collective-permute-done.14 = f32[16,512]{1,0:T(8,128)S(1)} collective-permute-done((f32[16,512]{1,0:T(8,128)S(1)}, f32[16,512]{1,0:T(8,128)S(1)}, u32[]{:S(2)}, u32[]{:S(2)}) %collective-permute-start.14) | collective-permute-done | bytes 32800 | tf_op jit(solution)/shard_map/ppermute | solution.py:435
  68.6 1.9 %collective-permute-start.15 = (f32[32,512]{1,0:T(8,128)S(1)}, f32[32,512]{1,0:T(8,128)S(1)}, u32[]{:S(2)}, u32[]{:S(2)}) collective-permute-start(f32[32,512]{1,0:T(8,128)S(1)} %pad_maximum_fusion.9), channel_id=1, source_target_pairs={{0,8},{1,9},{2,10},{3,11},{4,12},{5,13},{6,14},{7,15},{8,0},{9,1},... | collective-permute-start | bytes 196616 | tf_op jit(solution)/shard_map/ppermute | solution.py:435
  70.5 0.0 collective-permute-done.13
  70.5 0.0 copy-done.7
  70.5 4.5 %root_first.1 = (f32[128,128]{1,0:T(8,128)S(1)}, f32[128,128]{1,0:T(8,128)S(1)}, f32[128,128]{1,0:T(8,128)S(1)}, f32[8,256]{1,0:T(8,128)S(1)}, f32[256,128]{1,0:T(8,128)S(1)}) custom-call(f32[264,128]{1,0:T(8,128)S(1)} %pad_maximum_fusion.5.gram_ref, f32[1,256,256]{2,1,0:T(8,128)S(1)} %bitcast.1), custom_call_target="tpu_custom_call" | custom-call | flops 5000000000 | bytes 262144 | tf_op jit(solution)/shard_map/root_first/pallas_call | solution.py:300
  75.0 0.0 collective-permute-done.15
  75.1 1.0 %collective-permute-start.16 = (f32[64,512]{1,0:T(8,128)S(1)}, f32[64,512]{1,0:T(8,128)S(1)}, u32[]{:S(2)}, u32[]{:S(2)}) collective-permute-start(f32[64,512]{1,0:T(8,128)S(1)} %pad_maximum_fusion.6), channel_id=1, source_target_pairs={{0,4},{1,5},{2,6},{3,7},{4,0},{5,1},{6,2},{7,3},{8,12},{9,13},{10,... | collective-permute-start | bytes 393224 | tf_op jit(solution)/shard_map/ppermute | solution.py:435
  76.1 0.0 copy-start.5
  76.1 4.1 %root_second.1.inverse = f32[256,256]{1,0:T(8,128)S(1)} custom-call(f32[128,128]{1,0:T(8,128)S(1)} %get-tuple-element.66.first, f32[128,128]{1,0:T(8,128)S(1)} %get-tuple-element.67.across, f32[128,128]{1,0:T(8,128)S(1)} %get-tuple-element.68.rest, f32[8,256]{1,0:T(8,128)S(1)} %get-tuple-element.69.row, f32[256,128]{1,0:T(8,128)S(1)} %get-tuple-element.70.col), custom_call_target="tpu_custom_call" | custom-call | flops 5000000000 | bytes 262144 | tf_op jit(solution)/shard_map/root_second/pallas_call | solution.py:300
  80.2 0.0 copy-start.4
  80.2 0.0 collective-permute-done.16
  80.2 0.1 collective-permute-start.17
  80.3 1.5 %collective-permute-done.17 = f32[128,512]{1,0:T(8,128)S(1)} collective-permute-done((f32[128,512]{1,0:T(8,128)S(1)}, f32[128,512]{1,0:T(8,128)S(1)}, u32[]{:S(2)}, u32[]{:S(2)}) %collective-permute-start.17) | collective-permute-done | bytes 262176 | tf_op jit(solution)/shard_map/ppermute | solution.py:435
  81.9 0.0 copy-done.5
  82.0 0.0 copy-done.4
  82.0 3.5 %field.1 = f32[2048,256]{1,0:T(8,128)} custom-call(f32[2048,256]{1,0:T(8,128)S(1)} %get-tuple-element.40.b2, f32[2048,256]{1,0:T(8,128)S(1)} %copy-done.5, f32[2048,256]{1,0:T(8,128)S(1)} %copy-done.4, f32[256,256]{1,0:T(8,128)S(1)} %root_second.1.inverse, f32[256,512]{1,0:T(8,128)S(1)} %pad_maximum_fusion.1.solved), custom_call_target="tpu_custom_call" | custom-call | flops 1610612736 | bytes 6291456 | tf_op jit(solution)/shard_map/field/pallas_call | solution.py:422
  (42 shorter events, 0.7 us)
Async XLA Ops:
  5.1 1.3 %copy-start = (f32[2048,256]{1,0:T(8,128)}, f32[2048,256]{1,0:T(8,128)S(1)}, u32[]{:S(2)}) copy-start(f32[2048,256]{1,0:T(8,128)S(1)} %get-tuple-element.41.b1) | copy-start | bytes 6291460
  6.4 6.2 %collective-permute-start = (f32[520,128]{1,0:T(8,128)S(1)}, f32[520,128]{1,0:T(8,128)S(1)}, u32[]{:S(2)}, u32[]{:S(2)}) collective-permute-start(f32[520,128]{1,0:T(8,128)S(1)} %get-tuple-element.39), channel_id=1, source_target_pairs={{0,1},{1,0},{2,3},{3,2},{4,5},{5,4},{6,7},{7,6},{8,9},{9,8},{10,11... | collective-permute-start | bytes 798728 | tf_op jit(solution)/shard_map/ppermute | solution.py:435
  6.8 1.6 %copy-start.1 = (f32[2048,256]{1,0:T(8,128)S(1)}, f32[2048,256]{1,0:T(8,128)}, u32[]{:S(2)}) copy-start(f32[2048,256]{1,0:T(8,128)} %copy-done) | copy-start | bytes 6291460
  8.4 1.6 %copy-start.3 = (f32[2048,256]{1,0:T(8,128)S(1)}, f32[2048,256]{1,0:T(8,128)}, u32[]{:S(2)}) copy-start(f32[2048,256]{1,0:T(8,128)} %sources.3) | copy-start | bytes 6291460
  12.6 6.8 %collective-permute-start.1 = (f32[264,128]{1,0:T(8,128)S(1)}, f32[264,128]{1,0:T(8,128)S(1)}, u32[]{:S(2)}, u32[]{:S(2)}) collective-permute-start(f32[264,128]{1,0:T(8,128)S(1)} %constant_dynamic-slice_fusion.6), channel_id=1, source_target_pairs={{0,4},{1,5},{2,6},{3,7},{4,0},{5,1},{6,2},{7,3},{8,12},{9,13},{10,... | collective-permute-start | bytes 405512 | tf_op jit(solution)/shard_map/ppermute | solution.py:435
  15.2 4.3 %collective-permute-start.2 = (f32[128,512]{1,0:T(8,128)S(1)}, f32[128,512]{1,0:T(8,128)S(1)}, u32[]{:S(2)}, u32[]{:S(2)}) collective-permute-start(f32[128,512]{1,0:T(8,128)S(1)} %get-tuple-element.45), channel_id=1, source_target_pairs={{0,1},{1,0},{2,3},{3,2},{4,5},{5,4},{6,7},{7,6},{8,9},{9,8},{10,11... | collective-permute-start | bytes 786440 | tf_op jit(solution)/shard_map/ppermute | solution.py:435
  19.5 4.4 %collective-permute-start.3 = (f32[136,128]{1,0:T(8,128)S(1)}, f32[136,128]{1,0:T(8,128)S(1)}, u32[]{:S(2)}, u32[]{:S(2)}) collective-permute-start(f32[136,128]{1,0:T(8,128)S(1)} %constant_dynamic-slice_fusion.5), channel_id=1, source_target_pairs={{0,8},{1,9},{2,10},{3,11},{4,12},{5,13},{6,14},{7,15},{8,0},{9,1},... | collective-permute-start | bytes 208904 | tf_op jit(solution)/shard_map/ppermute | solution.py:435
  24.0 4.9 %collective-permute-start.4 = (f32[72,128]{1,0:T(8,128)S(1)}, f32[72,128]{1,0:T(8,128)S(1)}, u32[]{:S(2)}, u32[]{:S(2)}) collective-permute-start(f32[72,128]{1,0:T(8,128)S(1)} %constant_dynamic-slice_fusion.4), channel_id=1, source_target_pairs={{0,16},{1,17},{2,18},{3,19},{4,20},{5,21},{6,22},{7,23},{8,24},{9,... | collective-permute-start | bytes 110600 | tf_op jit(solution)/shard_map/ppermute | solution.py:435
  26.9 5.0 %collective-permute-start.5 = (f32[64,512]{1,0:T(8,128)S(1)}, f32[64,512]{1,0:T(8,128)S(1)}, u32[]{:S(2)}, u32[]{:S(2)}) collective-permute-start(f32[64,512]{1,0:T(8,128)S(1)} %constant_dynamic-slice_fusion.3), channel_id=1, source_target_pairs={{0,4},{1,5},{2,6},{3,7},{4,0},{5,1},{6,2},{7,3},{8,12},{9,13},{10,... | collective-permute-start | bytes 393224 | tf_op jit(solution)/shard_map/ppermute | solution.py:435
  31.9 4.9 %collective-permute-start.6 = (f32[72,128]{1,0:T(8,128)S(1)}, f32[72,128]{1,0:T(8,128)S(1)}, u32[]{:S(2)}, u32[]{:S(2)}) collective-permute-start(f32[72,128]{1,0:T(8,128)S(1)} %dynamic-slice_add_fusion.4), channel_id=1, source_target_pairs={{0,16},{1,17},{2,18},{3,19},{4,20},{5,21},{6,22},{7,23},{8,24},{9,... | collective-permute-start | bytes 110600 | tf_op jit(solution)/shard_map/ppermute | solution.py:435
  36.8 5.1 %collective-permute-start.7 = (f32[136,128]{1,0:T(8,128)S(1)}, f32[136,128]{1,0:T(8,128)S(1)}, u32[]{:S(2)}, u32[]{:S(2)}) collective-permute-start(f32[136,128]{1,0:T(8,128)S(1)} %pad_maximum_fusion.8), channel_id=1, source_target_pairs={{0,8},{1,9},{2,10},{3,11},{4,12},{5,13},{6,14},{7,15},{8,0},{9,1},... | collective-permute-start | bytes 208904 | tf_op jit(solution)/shard_map/ppermute | solution.py:435
  41.9 7.2 %copy-start.6 = (f32[2,256,256]{2,1,0:T(8,128)S(1)}, f32[2,256,256]{2,1,0:T(8,128)}, u32[]{:S(2)}) copy-start(f32[2,256,256]{2,1,0:T(8,128)} %coupling.1) | copy-start | bytes 1572868
  41.9 5.1 %collective-permute-start.8 = (f32[264,128]{1,0:T(8,128)S(1)}, f32[264,128]{1,0:T(8,128)S(1)}, u32[]{:S(2)}, u32[]{:S(2)}) collective-permute-start(f32[264,128]{1,0:T(8,128)S(1)} %pad_maximum_fusion.4), channel_id=1, source_target_pairs={{0,4},{1,5},{2,6},{3,7},{4,0},{5,1},{6,2},{7,3},{8,12},{9,13},{10,... | collective-permute-start | bytes 405512 | tf_op jit(solution)/shard_map/ppermute | solution.py:435
  42.8 4.3 %collective-permute-start.9 = (f32[32,512]{1,0:T(8,128)S(1)}, f32[32,512]{1,0:T(8,128)S(1)}, u32[]{:S(2)}, u32[]{:S(2)}) collective-permute-start(f32[32,512]{1,0:T(8,128)S(1)} %constant_dynamic-slice_fusion.2), channel_id=1, source_target_pairs={{0,8},{1,9},{2,10},{3,11},{4,12},{5,13},{6,14},{7,15},{8,0},{9,1},... | collective-permute-start | bytes 196616 | tf_op jit(solution)/shard_map/ppermute | solution.py:435
  47.1 1.6 %collective-permute-start.10 = (f32[520,128]{1,0:T(8,128)S(1)}, f32[520,128]{1,0:T(8,128)S(1)}, u32[]{:S(2)}, u32[]{:S(2)}) collective-permute-start(f32[520,128]{1,0:T(8,128)S(1)} %pad_maximum_fusion.2), channel_id=1, source_target_pairs={{0,1},{1,0},{2,3},{3,2},{4,5},{5,4},{6,7},{7,6},{8,9},{9,8},{10,11... | collective-permute-start | bytes 798728 | tf_op jit(solution)/shard_map/ppermute | solution.py:435
  48.8 8.9 %collective-permute-start.11 = (f32[16,512]{1,0:T(8,128)S(1)}, f32[16,512]{1,0:T(8,128)S(1)}, u32[]{:S(2)}, u32[]{:S(2)}) collective-permute-start(f32[16,512]{1,0:T(8,128)S(1)} %constant_dynamic-slice_fusion.1), channel_id=1, source_target_pairs={{0,16},{1,17},{2,18},{3,19},{4,20},{5,21},{6,22},{7,23},{8,24},{9,... | collective-permute-start | bytes 98312 | tf_op jit(solution)/shard_map/ppermute | solution.py:435
  53.6 7.1 %copy-start.2 = (f32[2048,256]{1,0:T(8,128)S(1)}, f32[2048,256]{1,0:T(8,128)}, u32[]{:S(2)}) copy-start(f32[2048,256]{1,0:T(8,128)} %copy-done) | copy-start | bytes 6291460
  59.1 4.6 %collective-permute-start.12 = (f32[168,128]{1,0:T(8,128)S(1)}, f32[168,128]{1,0:T(8,128)S(1)}, u32[]{:S(2)}, u32[]{:S(2)}) collective-permute-start(f32[168,128]{1,0:T(8,128)S(1)} %pad_maximum_fusion.7), channel_id=1, source_target_pairs={{0,2},{1,3},{2,0},{3,1},{4,6},{5,7},{6,4},{7,5},{8,10},{9,11},{10,... | collective-permute-start | bytes 258056 | tf_op jit(solution)/shard_map/ppermute | solution.py:435
  60.7 9.8 %copy-start.7 = (f32[256,256]{1,0:T(8,128)S(1)}, f32[256,256]{1,0:T(8,128)}, u32[]{:S(2)}) copy-start(f32[256,256]{1,0:T(8,128)} %param.9) | copy-start | bytes 786436
  63.7 4.9 %collective-permute-start.14 = (f32[16,512]{1,0:T(8,128)S(1)}, f32[16,512]{1,0:T(8,128)S(1)}, u32[]{:S(2)}, u32[]{:S(2)}) collective-permute-start(f32[16,512]{1,0:T(8,128)S(1)} %pad_maximum_fusion.10), channel_id=1, source_target_pairs={{0,16},{1,17},{2,18},{3,19},{4,20},{5,21},{6,22},{7,23},{8,24},{9,... | collective-permute-start | bytes 98312 | tf_op jit(solution)/shard_map/ppermute | solution.py:435
  66.4 4.1 %collective-permute-start.13 = (f32[136,128]{1,0:T(8,128)S(1)}, f32[136,128]{1,0:T(8,128)S(1)}, u32[]{:S(2)}, u32[]{:S(2)}) collective-permute-start(f32[136,128]{1,0:T(8,128)S(1)} %slice.38), channel_id=1, source_target_pairs={{0,1},{1,0},{2,3},{3,2},{4,5},{5,4},{6,7},{7,6},{8,9},{9,8},{10,11... | collective-permute-start | bytes 208904 | tf_op jit(solution)/shard_map/ppermute | solution.py:435
  68.6 6.5 %collective-permute-start.15 = (f32[32,512]{1,0:T(8,128)S(1)}, f32[32,512]{1,0:T(8,128)S(1)}, u32[]{:S(2)}, u32[]{:S(2)}) collective-permute-start(f32[32,512]{1,0:T(8,128)S(1)} %pad_maximum_fusion.9), channel_id=1, source_target_pairs={{0,8},{1,9},{2,10},{3,11},{4,12},{5,13},{6,14},{7,15},{8,0},{9,1},... | collective-permute-start | bytes 196616 | tf_op jit(solution)/shard_map/ppermute | solution.py:435
  75.1 5.1 %collective-permute-start.16 = (f32[64,512]{1,0:T(8,128)S(1)}, f32[64,512]{1,0:T(8,128)S(1)}, u32[]{:S(2)}, u32[]{:S(2)}) collective-permute-start(f32[64,512]{1,0:T(8,128)S(1)} %pad_maximum_fusion.6), channel_id=1, source_target_pairs={{0,4},{1,5},{2,6},{3,7},{4,0},{5,1},{6,2},{7,3},{8,12},{9,13},{10,... | collective-permute-start | bytes 393224 | tf_op jit(solution)/shard_map/ppermute | solution.py:435
  76.1 5.9 %copy-start.5 = (f32[2048,256]{1,0:T(8,128)S(1)}, f32[2048,256]{1,0:T(8,128)}, u32[]{:S(2)}) copy-start(f32[2048,256]{1,0:T(8,128)} %panel.1) | copy-start | bytes 6291460
  80.2 1.8 %copy-start.4 = (f32[2048,256]{1,0:T(8,128)S(1)}, f32[2048,256]{1,0:T(8,128)}, u32[]{:S(2)}) copy-start(f32[2048,256]{1,0:T(8,128)} %sources.3) | copy-start | bytes 6291460
  80.2 1.6 %collective-permute-start.17 = (f32[128,512]{1,0:T(8,128)S(1)}, f32[128,512]{1,0:T(8,128)S(1)}, u32[]{:S(2)}, u32[]{:S(2)}) collective-permute-start(f32[128,512]{1,0:T(8,128)S(1)} %pad_maximum_fusion.3), channel_id=1, source_target_pairs={{0,1},{1,0},{2,3},{3,2},{4,5},{5,4},{6,7},{7,6},{8,9},{9,8},{10,11... | collective-permute-start | bytes 786440 | tf_op jit(solution)/shard_map/ppermute | solution.py:435

commit v6 on v5

--- a/solution.py
+++ b/solution.py
@@ -14,7 +14,7 @@
 R = 256
 LANES = 128
 TILE = 512
-VMEM_LIMIT = 40 * 1024 * 1024
+VMEM_LIMIT = 16 * 1024 * 1024
 SYMMETRIC, FULL = 264, 512
 OWN, ROOT, CROSS, PANEL_TERMS = 0, 264, 528, 1040
 
@@ -134,6 +134,7 @@
     low = acc[4]
     store_symmetric(packed, ROOT, acc[3] + low + low.T)
     store_square(packed, CROSS, acc[2])
+    packed[PANEL_TERMS:, :] = jnp.zeros((packed.shape[0] - PANEL_TERMS, LANES), F32)
     store_halves(packed, keep, send)
 
 
@@ -158,9 +159,10 @@
     )
 
 
-def panel_gram(q_two, q_one):
+def panel_gram(q_two, q_one, shares):
     rows = q_two.shape[0]
-    part = jax.ShapeDtypeStruct((half_of(PANEL_TERMS), LANES), F32)
+    half = (PANEL_TERMS + 16 * shares - 1) // (16 * shares) * 8 * shares
+    part = jax.ShapeDtypeStruct((half, LANES), F32)
     tall = jax.ShapeDtypeStruct((rows, R), F32)
     return pl.pallas_call(
         panel_gram_kernel,
@@ -168,7 +170,7 @@
         out_shape=(part, part, tall, tall),
         scratch_shapes=[
             pltpu.VMEM((5, R, R), F32),
-            pltpu.VMEM((PANEL_TERMS, LANES), F32),
+            pltpu.VMEM((2 * half, LANES), F32),
             pltpu.SemaphoreType.DMA((2, rows // TILE)),
         ],
         compiler_params=pltpu.CompilerParams(vmem_limit_bytes=VMEM_LIMIT),
@@ -459,7 +461,7 @@
 def per_device(q_two, q_one, sources, coupling_two, coupling_one):
     index = lax.axis_index(AXES)
     leaf_bits = list(range(2, lax.axis_size("leaf").bit_length() + 1))
-    panel_order = source_order = leaf_bits
+    source_order = leaf_bits
 
     def after(x, *others):
         return lax.optimization_barrier((x,) + others)[0]
@@ -467,13 +469,17 @@
     def half_rows(terms):
         return rows_of(terms, index & 1)
 
-    keep, send, b2, b1 = panel_gram(q_two, q_one)
+    leaves = lax.axis_size("leaf")
+    keep, send, b2, b1 = panel_gram(q_two, q_one, leaves)
     arriving = exchange(send, 1)
     source_keep, source_send = source_gram(b2, b1, sources)
     arriving, source_send = lax.optimization_barrier((arriving, source_send))
     terms = keep + arriving
-    source = source_keep + exchange(source_send, 1)
-    sizes, source_sizes = [], []
+    flying = exchange(source_send, 1)
+    shares = lax.all_to_all(terms.reshape(leaves, -1, LANES), "leaf", 0, 0)
+    shares, flying = lax.optimization_barrier((shares, flying))
+    source = source_keep + flying
+    source_sizes = []
     source_left = list(source_order)
 
     def source_start(source):
@@ -482,31 +488,26 @@
         source_sizes.append(source.shape[0])
         return rows_of(source, mine), exchange(rows_of(source, 1 - mine), 1 << bit)
 
-    for step, bit in enumerate(panel_order):
-        sizes.append(terms.shape[0])
-        terms = scatter_sum(terms, index, bit)
-        if step == 0:
-            terms, source = lax.optimization_barrier((terms, source))
-            kept, flying = source_start(source)
-    terms, flying = lax.optimization_barrier((terms, flying))
+    kept, flying = source_start(source)
+    share = jnp.sum(shares, axis=0)
+    shares = lax.all_to_all(jnp.broadcast_to(share[None], shares.shape), "leaf", 0, 0)
+    shares, flying = lax.optimization_barrier((shares, flying))
     source = kept + flying
-    for step, bit in reversed(list(enumerate(panel_order))):
-        if step == 0:
-            terms, source = lax.optimization_barrier((terms, source))
-            kept, flying = source_start(source)
-        terms = gather(terms, sizes[step], index, bit)
-    terms, flying = lax.optimization_barrier((terms, flying))
+    kept, flying = source_start(source)
+    terms = shares.reshape(-1, LANES)
+    terms = gather(terms, 2 * terms.shape[0], index, 0)
+    flying = (kept, flying)
+
+    parts = invert_first(half_index, terms, coupling_two, "level_first")
+    flying, parts = lax.optimization_barrier((flying, parts))
+    source = flying[0] + flying[1]
+    kept, flying = source_start(source)
+    inverse = invert_second(parts, "level_second")
+    flying, inverse = lax.optimization_barrier((flying, inverse))
     source = kept + flying
-    terms = gather(terms, PANEL_TERMS, index, 0)
-    kept, flying = source_start(after(source, terms))
-    flying = (kept, flying)
-
-    parts = invert_first(half_index, terms, coupling_two, "level_first")
-    source = flying[0] + after(flying[1], *parts)
     while source_left:
         kept, flying = source_start(source)
         source = kept + flying
-    inverse = invert_second(parts, "level_second")
     count = source.shape[0]
     shapes = (
         SQUARE,

time: 85.9 us -> 79.9 us (0.930)
  local copies, waits for them, and re-layouts: 4.62 us -> 0.84 us
  waiting for transfers between devices: 26.4 us -> 22.9 us
  other arithmetic: 0.56 us -> 2.16 us
    ppermute x18 -> x12, waiting for transfers between devices: 26.4 us -> 13.2 us  [exchange(): return lax.ppermute(x, AXES, [(i, i ^ mask) for i in range(count)])]
    ppermute x18 -> x12, starting transfers between devices: 21.5 us -> 10.7 us  [exchange(): return lax.ppermute(x, AXES, [(i, i ^ mask) for i in range(count)])]
    all_to_all x0 -> x2, starting transfers between devices: none -> 10.5 us  [the longest x1 6.82 us: per_device(): shares = lax.all_to_all(terms.reshape(leaves, -1, LANES), 'leaf', 0, 0)]
    all_to_all x0 -> x2, waiting for transfers between devices: none -> 9.64 us  [the longest x1 8.55 us: per_device(): shares = lax.all_to_all(terms.reshape(leaves, -1, LANES), 'leaf', 0, 0)]
    unnamed x16 -> x14, local copies, waits for them, and re-layouts: 4.52 us -> 0.03 us
    add x5 -> x2, other arithmetic: 0.09 us -> 1.05 us  [the longest x1 1.04 us: per_device(): source = source_keep + flying]
  transfers between devices with their start and end apart: 18 -> 14, of which waited for: 11 -> 9; matrix products, arithmetic and copies ran while one was open for 0% -> 2% of each run, Pallas kernels for 26% -> 28%
where the time goes in v6:
time: 79.9 us; the launch traced here: 79.6 us
  Pallas kernels  31.4 us (39%)
  waiting for transfers between devices  22.9 us (29%)
  starting transfers between devices  21.2 us (27%)
  other arithmetic  2.16 us (3%)
  between operations  1.15 us (1%)
  local copies, waits for them, and re-layouts  0.84 us (1%)
    pallas_call x5, Pallas kernels, call(): pl.pallas_call(kernel, out_shape=out_shape, scratch_shapes=list(scratch),...  18.4 us
    ppermute x12, waiting for transfers between devices, exchange(): return lax.ppermute(x, AXES, [(i, i ^ mask) for i in range(count)])  13.2 us
    ppermute x12, starting transfers between devices, exchange(): return lax.ppermute(x, AXES, [(i, i ^ mask) for i in range(count)])  10.7 us
    all_to_all x1, waiting for transfers between devices, per_device(): shares = lax.all_to_all(terms.reshape(leaves, -1, LANES), 'leaf', 0, 0)  8.55 us
    all_to_all x1, starting transfers between devices, per_device(): shares = lax.all_to_all(terms.reshape(leaves, -1, LANES), 'leaf', 0, 0)  6.82 us
    pallas_call x2, Pallas kernels, update(): pl.pallas_call(kernel, out_specs=pl.BlockSpec(memory_space=pl.ANY), out_s...  5.96 us
    pallas_call x1, Pallas kernels, panel_gram(): pl.pallas_call(panel_gram_kernel, in_specs=[pl.BlockSpec(memory_space=pl....  4.48 us
    all_to_all x1, starting transfers between devices, per_device(): lax.all_to_all(jnp.broadcast_to(share[None], shares.shape), 'leaf', 0, 0)  3.64 us
  transfers between devices with their start and end apart: 14, of which 9 were waited for; matrix products, arithmetic and copies ran while one was open for 2% of the time, Pallas kernels for 28%

profile of v6, /device:TPU:0, one launch (start us, length us, event | category | flops | bytes accessed | tf_op | source)
XLA Modules:
  0.0 79.6 jit_solution(13746852670525037594)
XLA Ops:
  0.6 0.0 copy-start.2
  0.6 4.5 %panel_gram.1 = (f32[576,128]{1,0:T(8,128)S(1)}, f32[576,128]{1,0:T(8,128)S(1)}, f32[2048,256]{1,0:T(8,128)S(1)}, f32[2048,256]{1,0:T(8,128)S(1)}) custom-call(f32[2048,256]{1,0:T(8,128)} %q_two.1, f32[2048,256]{1,0:T(8,128)} %q_one.1), custom_call_target="tpu_custom_call" | custom-call | flops 1879048192 | bytes 4194304 | tf_op jit(solution)/shard_map/panel_gram/pallas_call | solution.py:167
  5.1 0.0 copy-start
  5.1 0.5 collective-permute-start
  5.7 0.0 copy-done.2
  5.7 2.5 %source_gram.1 = (f32[128,512]{1,0:T(8,128)S(1)}, f32[128,512]{1,0:T(8,128)S(1)}) custom-call(f32[2048,256]{1,0:T(8,128)S(1)} %get-tuple-element.41.b2, f32[2048,256]{1,0:T(8,128)S(1)} %get-tuple-element.42.b1, f32[2048,256]{1,0:T(8,128)S(1)} %copy-done.2), custom_call_target="tpu_custom_call" | custom-call | flops 1610612736 | bytes 6291456 | tf_op jit(solution)/shard_map/source_gram/pallas_call | solution.py:184
  8.2 0.0 copy-done
  8.2 0.0 collective-permute-done
  8.2 0.7 add.42
  9.0 6.8 %all-to-all-start = ((f32[8,72,128]{2,1,0:T(8,128)}), f32[8,72,128]{2,1,0:T(8,128)S(1)}, u32[]{:S(2)}, u32[]{:S(2)}) async-start(f32[8,72,128]{2,1,0:T(8,128)} %bitcast), calls=%async_computation | async-start | bytes 589824 | tf_op jit(solution)/shard_map/all_to_all | solution.py:479
  15.8 0.2 collective-permute-start.1
  16.0 1.5 %collective-permute-done.1 = f32[128,512]{1,0:T(8,128)} collective-permute-done((f32[128,512]{1,0:T(8,128)S(1)}, f32[128,512]{1,0:T(8,128)}, u32[]{:S(2)}, u32[]{:S(2)}) %collective-permute-start.1) | collective-permute-done | bytes 262176 | tf_op jit(solution)/shard_map/ppermute | solution.py:437
  17.4 8.6 %all-to-all-done = f32[8,72,128]{2,1,0:T(8,128)S(1)} async-done(((f32[8,72,128]{2,1,0:T(8,128)}), f32[8,72,128]{2,1,0:T(8,128)S(1)}, u32[]{:S(2)}, u32[]{:S(2)}) %all-to-all-start) | async-done | bytes 294944 | tf_op jit(solution)/shard_map/all_to_all | solution.py:479
  26.0 0.7 broadcast_in_dim.4
  26.8 3.6 %all-to-all-start.1 = ((f32[8,72,128]{2,1,0:T(8,128)}), f32[8,72,128]{2,1,0:T(8,128)S(1)}, u32[]{:S(2)}, u32[]{:S(2)}) async-start(f32[8,72,128]{2,1,0:T(8,128)} %broadcast_in_dim.4), calls=%async_computation.1 | async-start | bytes 589824 | tf_op jit(solution)/shard_map/all_to_all | solution.py:493
  30.4 0.0 copy-start.5
  30.4 1.0 %add.43 = f32[128,512]{1,0:T(8,128)S(1)} add(f32[128,512]{1,0:T(8,128)S(1)} %get-tuple-element.43, f32[128,512]{1,0:T(8,128)} %collective-permute-done.1) | non-fusion elementwise | flops 65536 | bytes 786432 | tf_op jit(solution)/shard_map/add | solution.py:481
  31.5 2.1 %collective-permute-start.2 = (f32[64,512]{1,0:T(8,128)S(1)}, f32[64,512]{1,0:T(8,128)S(1)}, u32[]{:S(2)}, u32[]{:S(2)}) collective-permute-start(f32[64,512]{1,0:T(8,128)S(1)} %constant_dynamic-slice_fusion.4), channel_id=1, source_target_pairs={{0,4},{1,5},{2,6},{3,7},{4,0},{5,1},{6,2},{7,3},{8,12},{9,13},{10,... | collective-permute-start | bytes 393224 | tf_op jit(solution)/shard_map/ppermute | solution.py:437
  33.6 5.5 %collective-permute-done.2 = f32[64,512]{1,0:T(8,128)S(1)} collective-permute-done((f32[64,512]{1,0:T(8,128)S(1)}, f32[64,512]{1,0:T(8,128)S(1)}, u32[]{:S(2)}, u32[]{:S(2)}) %collective-permute-start.2) | collective-permute-done | bytes 131104 | tf_op jit(solution)/shard_map/ppermute | solution.py:437
  39.1 1.1 %all-to-all-done.1 = f32[8,72,128]{2,1,0:T(8,128)S(1)} async-done(((f32[8,72,128]{2,1,0:T(8,128)}), f32[8,72,128]{2,1,0:T(8,128)S(1)}, u32[]{:S(2)}, u32[]{:S(2)}) %all-to-all-start.1) | async-done | bytes 294944 | tf_op jit(solution)/shard_map/all_to_all | solution.py:493
  40.2 0.0 collective-permute-start.4
  40.2 1.1 %collective-permute-start.3 = (f32[32,512]{1,0:T(8,128)S(1)}, f32[32,512]{1,0:T(8,128)S(1)}, u32[]{:S(2)}, u32[]{:S(2)}) collective-permute-start(f32[32,512]{1,0:T(8,128)S(1)} %get-tuple-element.88), channel_id=1, source_target_pairs={{0,8},{1,9},{2,10},{3,11},{4,12},{5,13},{6,14},{7,15},{8,0},{9,1},... | collective-permute-start | bytes 196616 | tf_op jit(solution)/shard_map/ppermute | solution.py:437
  41.4 0.4 collective-permute-done.4
  41.9 0.0 copy-done.5
  41.9 4.5 %level_first.1 = (f32[128,128]{1,0:T(8,128)S(1)}, f32[128,128]{1,0:T(8,128)S(1)}, f32[128,128]{1,0:T(8,128)S(1)}, f32[8,256]{1,0:T(8,128)S(1)}, f32[256,128]{1,0:T(8,128)S(1)}) custom-call(f32[1152,128]{1,0:T(8,128)S(1)} %pad_maximum_fusion.gram_ref.terms, f32[2,256,256]{2,1,0:T(8,128)S(1)} %copy-done.5), custom_call_target="tpu_custom_call" | custom-call | flops 5000000000 | bytes 262144 | tf_op jit(solution)/shard_map/level_first/pallas_call | solution.py:302
  46.4 0.0 collective-permute-done.3
  46.4 1.6 %collective-permute-start.5 = (f32[16,512]{1,0:T(8,128)S(1)}, f32[16,512]{1,0:T(8,128)S(1)}, u32[]{:S(2)}, u32[]{:S(2)}) collective-permute-start(f32[16,512]{1,0:T(8,128)S(1)} %constant_dynamic-slice_fusion.1), channel_id=1, source_target_pairs={{0,16},{1,17},{2,18},{3,19},{4,20},{5,21},{6,22},{7,23},{8,24},{9,... | collective-permute-start | bytes 98312 | tf_op jit(solution)/shard_map/ppermute | solution.py:437
  48.0 0.0 copy-start.1
  48.0 4.1 %level_second.1.inverse = f32[256,256]{1,0:T(8,128)S(1)} custom-call(f32[128,128]{1,0:T(8,128)S(1)} %get-tuple-element.60.first, f32[128,128]{1,0:T(8,128)S(1)} %get-tuple-element.61.across, f32[128,128]{1,0:T(8,128)S(1)} %get-tuple-element.62.rest, f32[8,256]{1,0:T(8,128)S(1)} %get-tuple-element.63.row, f32[256,128]{1,0:T(8,128)S(1)} %get-tuple-element.64.col), custom_call_target="tpu_custom_call" | custom-call | flops 5000000000 | bytes 262144 | tf_op jit(solution)/shard_map/level_second/pallas_call | solution.py:302
  52.1 0.0 collective-permute-done.5
  52.1 1.3 %level_solve.1 = (f32[256,256]{1,0:T(8,128)S(1)}, f32[264,128]{1,0:T(8,128)S(1)}, f32[16,256]{1,0:T(8,128)S(1)}, f32[32,128]{1,0:T(8,128)S(1)}) custom-call(f32[256,256]{1,0:T(8,128)S(1)} %level_second.1.inverse, f32[1152,128]{1,0:T(8,128)S(1)} %pad_maximum_fusion.gram_ref.terms, f32[16,512]{1,0:T(8,128)S(1)} %dynamic-slice_add_fusion.1.source), custom_call_target="tpu_custom_call" | custom-call | bytes 262144 | tf_op jit(solution)/shard_map/level_solve/pallas_call | solution.py:302
  53.4 1.6 %collective-permute-start.6 = (f32[168,128]{1,0:T(8,128)S(1)}, f32[168,128]{1,0:T(8,128)S(1)}, u32[]{:S(2)}, u32[]{:S(2)}) collective-permute-start(f32[168,128]{1,0:T(8,128)S(1)} %pad_maximum_fusion.5), channel_id=1, source_target_pairs={{0,2},{1,3},{2,0},{3,1},{4,6},{5,7},{6,4},{7,5},{8,10},{9,11},{10,... | collective-permute-start | bytes 258056 | tf_op jit(solution)/shard_map/ppermute | solution.py:437
  55.0 0.0 copy-done.1
  55.0 0.0 copy-start.6
  55.0 2.4 %panel.1 = f32[2048,256]{1,0:T(8,128)} custom-call(f32[2048,256]{1,0:T(8,128)S(1)} %get-tuple-element.41.b2, f32[2048,256]{1,0:T(8,128)S(1)} %copy-done.1, f32[256,256]{1,0:T(8,128)S(1)} %get-tuple-element.69.x), custom_call_target="tpu_custom_call" | custom-call | flops 805306368 | bytes 6291456 | tf_op jit(solution)/shard_map/panel/pallas_call | solution.py:424
  57.5 0.5 collective-permute-done.6
  58.0 1.5 %collective-permute-start.8 = (f32[16,512]{1,0:T(8,128)S(1)}, f32[16,512]{1,0:T(8,128)S(1)}, u32[]{:S(2)}, u32[]{:S(2)}) collective-permute-start(f32[16,512]{1,0:T(8,128)S(1)} %pad_maximum_fusion.7), channel_id=1, source_target_pairs={{0,16},{1,17},{2,18},{3,19},{4,20},{5,21},{6,22},{7,23},{8,24},{9,... | collective-permute-start | bytes 98312 | tf_op jit(solution)/shard_map/ppermute | solution.py:437
  59.5 0.0 collective-permute-start.7
  59.5 3.4 %collective-permute-done.8 = f32[16,512]{1,0:T(8,128)S(1)} collective-permute-done((f32[16,512]{1,0:T(8,128)S(1)}, f32[16,512]{1,0:T(8,128)S(1)}, u32[]{:S(2)}, u32[]{:S(2)}) %collective-permute-start.8) | collective-permute-done | bytes 32800 | tf_op jit(solution)/shard_map/ppermute | solution.py:437
  62.9 1.5 %collective-permute-start.9 = (f32[32,512]{1,0:T(8,128)S(1)}, f32[32,512]{1,0:T(8,128)S(1)}, u32[]{:S(2)}, u32[]{:S(2)}) collective-permute-start(f32[32,512]{1,0:T(8,128)S(1)} %pad_maximum_fusion.6), channel_id=1, source_target_pairs={{0,8},{1,9},{2,10},{3,11},{4,12},{5,13},{6,14},{7,15},{8,0},{9,1},... | collective-permute-start | bytes 196616 | tf_op jit(solution)/shard_map/ppermute | solution.py:437
  64.4 0.0 collective-permute-done.7
  64.5 0.0 copy-done.6
  64.5 4.5 %root_first.1 = (f32[128,128]{1,0:T(8,128)S(1)}, f32[128,128]{1,0:T(8,128)S(1)}, f32[128,128]{1,0:T(8,128)S(1)}, f32[8,256]{1,0:T(8,128)S(1)}, f32[256,128]{1,0:T(8,128)S(1)}) custom-call(f32[264,128]{1,0:T(8,128)S(1)} %pad_maximum_fusion.3.gram_ref, f32[1,256,256]{2,1,0:T(8,128)S(1)} %bitcast.5), custom_call_target="tpu_custom_call" | custom-call | flops 5000000000 | bytes 262144 | tf_op jit(solution)/shard_map/root_first/pallas_call | solution.py:302
  69.0 0.0 collective-permute-done.9
  69.1 0.6 collective-permute-start.10
  69.6 0.0 copy-start.4
  69.7 4.1 %root_second.1.inverse = f32[256,256]{1,0:T(8,128)S(1)} custom-call(f32[128,128]{1,0:T(8,128)S(1)} %get-tuple-element.72.first, f32[128,128]{1,0:T(8,128)S(1)} %get-tuple-element.73.across, f32[128,128]{1,0:T(8,128)S(1)} %get-tuple-element.74.rest, f32[8,256]{1,0:T(8,128)S(1)} %get-tuple-element.75.row, f32[256,128]{1,0:T(8,128)S(1)} %get-tuple-element.76.col), custom_call_target="tpu_custom_call" | custom-call | flops 5000000000 | bytes 262144 | tf_op jit(solution)/shard_map/root_second/pallas_call | solution.py:302
  73.7 0.0 copy-start.3
  73.8 0.3 collective-permute-done.10
  74.2 0.1 collective-permute-start.11
  74.2 1.5 %collective-permute-done.11 = f32[128,512]{1,0:T(8,128)S(1)} collective-permute-done((f32[128,512]{1,0:T(8,128)S(1)}, f32[128,512]{1,0:T(8,128)S(1)}, u32[]{:S(2)}, u32[]{:S(2)}) %collective-permute-start.11) | collective-permute-done | bytes 262176 | tf_op jit(solution)/shard_map/ppermute | solution.py:437
  75.9 0.0 copy-done.4
  75.9 0.0 copy-done.3
  75.9 3.5 %field.1 = f32[2048,256]{1,0:T(8,128)} custom-call(f32[2048,256]{1,0:T(8,128)S(1)} %get-tuple-element.41.b2, f32[2048,256]{1,0:T(8,128)S(1)} %copy-done.4, f32[2048,256]{1,0:T(8,128)S(1)} %copy-done.3, f32[256,256]{1,0:T(8,128)S(1)} %root_second.1.inverse, f32[256,512]{1,0:T(8,128)S(1)} %pad_maximum_fusion.1.solved), custom_call_target="tpu_custom_call" | custom-call | flops 1610612736 | bytes 6291456 | tf_op jit(solution)/shard_map/field/pallas_call | solution.py:424
  (26 shorter events, 0.4 us)
Async XLA Ops:
  0.6 5.0 %copy-start.2 = (f32[2048,256]{1,0:T(8,128)S(1)}, f32[2048,256]{1,0:T(8,128)}, u32[]{:S(2)}) copy-start(f32[2048,256]{1,0:T(8,128)} %sources.3) | copy-start | bytes 6291460
  5.1 3.1 %copy-start = (f32[2048,256]{1,0:T(8,128)}, f32[2048,256]{1,0:T(8,128)S(1)}, u32[]{:S(2)}) copy-start(f32[2048,256]{1,0:T(8,128)S(1)} %get-tuple-element.42.b1) | copy-start | bytes 6291460
  5.1 3.1 %collective-permute-start = (f32[576,128]{1,0:T(8,128)S(1)}, f32[576,128]{1,0:T(8,128)S(1)}, u32[]{:S(2)}, u32[]{:S(2)}) collective-permute-start(f32[576,128]{1,0:T(8,128)S(1)} %get-tuple-element.45), channel_id=1, source_target_pairs={{0,1},{1,0},{2,3},{3,2},{4,5},{5,4},{6,7},{7,6},{8,9},{9,8},{10,11... | collective-permute-start | bytes 884744 | tf_op jit(solution)/shard_map/ppermute | solution.py:437
  9.0 17.0 %all-to-all-start = ((f32[8,72,128]{2,1,0:T(8,128)}), f32[8,72,128]{2,1,0:T(8,128)S(1)}, u32[]{:S(2)}, u32[]{:S(2)}) async-start(f32[8,72,128]{2,1,0:T(8,128)} %bitcast), calls=%async_computation | async-start | bytes 589824 | tf_op jit(solution)/shard_map/all_to_all | solution.py:479
  15.8 1.7 %collective-permute-start.1 = (f32[128,512]{1,0:T(8,128)S(1)}, f32[128,512]{1,0:T(8,128)}, u32[]{:S(2)}, u32[]{:S(2)}) collective-permute-start(f32[128,512]{1,0:T(8,128)S(1)} %get-tuple-element.48), channel_id=1, source_target_pairs={{0,1},{1,0},{2,3},{3,2},{4,5},{5,4},{6,7},{7,6},{8,9},{9,8},{10,11... | collective-permute-start | bytes 786440 | tf_op jit(solution)/shard_map/ppermute | solution.py:437
  26.8 13.4 %all-to-all-start.1 = ((f32[8,72,128]{2,1,0:T(8,128)}), f32[8,72,128]{2,1,0:T(8,128)S(1)}, u32[]{:S(2)}, u32[]{:S(2)}) async-start(f32[8,72,128]{2,1,0:T(8,128)} %broadcast_in_dim.4), calls=%async_computation.1 | async-start | bytes 589824 | tf_op jit(solution)/shard_map/all_to_all | solution.py:493
  30.4 11.5 %copy-start.5 = (f32[2,256,256]{2,1,0:T(8,128)S(1)}, f32[2,256,256]{2,1,0:T(8,128)}, u32[]{:S(2)}) copy-start(f32[2,256,256]{2,1,0:T(8,128)} %coupling.1) | copy-start | bytes 1572868
  31.5 7.6 %collective-permute-start.2 = (f32[64,512]{1,0:T(8,128)S(1)}, f32[64,512]{1,0:T(8,128)S(1)}, u32[]{:S(2)}, u32[]{:S(2)}) collective-permute-start(f32[64,512]{1,0:T(8,128)S(1)} %constant_dynamic-slice_fusion.4), channel_id=1, source_target_pairs={{0,4},{1,5},{2,6},{3,7},{4,0},{5,1},{6,2},{7,3},{8,12},{9,13},{10,... | collective-permute-start | bytes 393224 | tf_op jit(solution)/shard_map/ppermute | solution.py:437
  40.2 1.6 %collective-permute-start.4 = (f32[576,128]{1,0:T(8,128)S(1)}, f32[576,128]{1,0:T(8,128)S(1)}, u32[]{:S(2)}, u32[]{:S(2)}) collective-permute-start(f32[576,128]{1,0:T(8,128)S(1)} %bitcast.6), channel_id=1, source_target_pairs={{0,1},{1,0},{2,3},{3,2},{4,5},{5,4},{6,7},{7,6},{8,9},{9,8},{10,11... | collective-permute-start | bytes 884744 | tf_op jit(solution)/shard_map/ppermute | solution.py:437
  40.2 6.1 %collective-permute-start.3 = (f32[32,512]{1,0:T(8,128)S(1)}, f32[32,512]{1,0:T(8,128)S(1)}, u32[]{:S(2)}, u32[]{:S(2)}) collective-permute-start(f32[32,512]{1,0:T(8,128)S(1)} %get-tuple-element.88), channel_id=1, source_target_pairs={{0,8},{1,9},{2,10},{3,11},{4,12},{5,13},{6,14},{7,15},{8,0},{9,1},... | collective-permute-start | bytes 196616 | tf_op jit(solution)/shard_map/ppermute | solution.py:437
  46.4 5.7 %collective-permute-start.5 = (f32[16,512]{1,0:T(8,128)S(1)}, f32[16,512]{1,0:T(8,128)S(1)}, u32[]{:S(2)}, u32[]{:S(2)}) collective-permute-start(f32[16,512]{1,0:T(8,128)S(1)} %constant_dynamic-slice_fusion.1), channel_id=1, source_target_pairs={{0,16},{1,17},{2,18},{3,19},{4,20},{5,21},{6,22},{7,23},{8,24},{9,... | collective-permute-start | bytes 98312 | tf_op jit(solution)/shard_map/ppermute | solution.py:437
  48.0 7.0 %copy-start.1 = (f32[2048,256]{1,0:T(8,128)S(1)}, f32[2048,256]{1,0:T(8,128)}, u32[]{:S(2)}) copy-start(f32[2048,256]{1,0:T(8,128)} %copy-done) | copy-start | bytes 6291460
  53.4 4.6 %collective-permute-start.6 = (f32[168,128]{1,0:T(8,128)S(1)}, f32[168,128]{1,0:T(8,128)S(1)}, u32[]{:S(2)}, u32[]{:S(2)}) collective-permute-start(f32[168,128]{1,0:T(8,128)S(1)} %pad_maximum_fusion.5), channel_id=1, source_target_pairs={{0,2},{1,3},{2,0},{3,1},{4,6},{5,7},{6,4},{7,5},{8,10},{9,11},{10,... | collective-permute-start | bytes 258056 | tf_op jit(solution)/shard_map/ppermute | solution.py:437
  55.0 9.5 %copy-start.6 = (f32[256,256]{1,0:T(8,128)S(1)}, f32[256,256]{1,0:T(8,128)}, u32[]{:S(2)}) copy-start(f32[256,256]{1,0:T(8,128)} %param.9) | copy-start | bytes 786436
  58.0 4.9 %collective-permute-start.8 = (f32[16,512]{1,0:T(8,128)S(1)}, f32[16,512]{1,0:T(8,128)S(1)}, u32[]{:S(2)}, u32[]{:S(2)}) collective-permute-start(f32[16,512]{1,0:T(8,128)S(1)} %pad_maximum_fusion.7), channel_id=1, source_target_pairs={{0,16},{1,17},{2,18},{3,19},{4,20},{5,21},{6,22},{7,23},{8,24},{9,... | collective-permute-start | bytes 98312 | tf_op jit(solution)/shard_map/ppermute | solution.py:437
  59.5 4.9 %collective-permute-start.7 = (f32[136,128]{1,0:T(8,128)S(1)}, f32[136,128]{1,0:T(8,128)S(1)}, u32[]{:S(2)}, u32[]{:S(2)}) collective-permute-start(f32[136,128]{1,0:T(8,128)S(1)} %slice.19), channel_id=1, source_target_pairs={{0,1},{1,0},{2,3},{3,2},{4,5},{5,4},{6,7},{7,6},{8,9},{9,8},{10,11... | collective-permute-start | bytes 208904 | tf_op jit(solution)/shard_map/ppermute | solution.py:437
  62.9 6.1 %collective-permute-start.9 = (f32[32,512]{1,0:T(8,128)S(1)}, f32[32,512]{1,0:T(8,128)S(1)}, u32[]{:S(2)}, u32[]{:S(2)}) collective-permute-start(f32[32,512]{1,0:T(8,128)S(1)} %pad_maximum_fusion.6), channel_id=1, source_target_pairs={{0,8},{1,9},{2,10},{3,11},{4,12},{5,13},{6,14},{7,15},{8,0},{9,1},... | collective-permute-start | bytes 196616 | tf_op jit(solution)/shard_map/ppermute | solution.py:437
  69.1 5.0 %collective-permute-start.10 = (f32[64,512]{1,0:T(8,128)S(1)}, f32[64,512]{1,0:T(8,128)S(1)}, u32[]{:S(2)}, u32[]{:S(2)}) collective-permute-start(f32[64,512]{1,0:T(8,128)S(1)} %pad_maximum_fusion.4), channel_id=1, source_target_pairs={{0,4},{1,5},{2,6},{3,7},{4,0},{5,1},{6,2},{7,3},{8,12},{9,13},{10,... | collective-permute-start | bytes 393224 | tf_op jit(solution)/shard_map/ppermute | solution.py:437
  69.6 6.2 %copy-start.4 = (f32[2048,256]{1,0:T(8,128)S(1)}, f32[2048,256]{1,0:T(8,128)}, u32[]{:S(2)}) copy-start(f32[2048,256]{1,0:T(8,128)} %panel.1) | copy-start | bytes 6291460
  73.7 2.1 %copy-start.3 = (f32[2048,256]{1,0:T(8,128)S(1)}, f32[2048,256]{1,0:T(8,128)}, u32[]{:S(2)}) copy-start(f32[2048,256]{1,0:T(8,128)} %sources.3) | copy-start | bytes 6291460
  74.2 1.6 %collective-permute-start.11 = (f32[128,512]{1,0:T(8,128)S(1)}, f32[128,512]{1,0:T(8,128)S(1)}, u32[]{:S(2)}, u32[]{:S(2)}) collective-permute-start(f32[128,512]{1,0:T(8,128)S(1)} %pad_maximum_fusion.2), channel_id=1, source_target_pairs={{0,1},{1,0},{2,3},{3,2},{4,5},{5,4},{6,7},{7,6},{8,9},{9,8},{10,11... | collective-permute-start | bytes 786440 | tf_op jit(solution)/shard_map/ppermute | solution.py:437

commit v7 on v4

--- a/solution.py
+++ b/solution.py
@@ -14,7 +14,7 @@
 R = 256
 LANES = 128
 TILE = 512
-VMEM_LIMIT = 40 * 1024 * 1024
+VMEM_LIMIT = 16 * 1024 * 1024
 SYMMETRIC, FULL = 264, 512
 OWN, ROOT, CROSS, PANEL_TERMS = 0, 264, 528, 1040
 PROJECTED, SIDE, SOURCE_TERMS = 0, 512, 1024
@@ -373,12 +373,6 @@
     store_symmetric(root_out, 0, load_symmetric(terms, ROOT) - dot_t_full(cross, x))
 
 
-def source_solve_kernel(inverse, x, terms, y_out, side_out):
-    projected = load_square(terms, PROJECTED)
-    y_out[...] = dot_full(inverse[...], projected)
-    store_square(side_out, 0, load_square(terms, SIDE) - dot_t_full(x[...], projected))
-
-
 def wide(x):
     high, low = split2(x)
     return jnp.concatenate([high, high, low], axis=1)
@@ -389,7 +383,7 @@
     return jnp.concatenate([high, low, high], axis=0)
 
 
-def by_tiles(rows, out, stage, sems, value):
+def by_tiles(rows, out, stage, sems, value, beside=None):
     tiles = rows // TILE
 
     def copy(tile):
@@ -401,13 +395,20 @@
         return carry
 
     lax.fori_loop(0, tiles, step, 0)
+    if beside is not None:
+        beside()
     for tile in range(tiles):
         copy(tile).wait()
 
 
-def panel_kernel(b2, b1, x, out, stage, sems):
+def panel_kernel(b2, b1, x, inverse, terms, out, y_out, side_out, stage, sems):
+    def sources_part():
+        projected = load_square(terms, PROJECTED)
+        y_out[...] = dot_full(inverse[...], projected)
+        store_square(side_out, 0, load_square(terms, SIDE) - dot_t_full(x[...], projected))
+
     right = tall(x[...])
-    by_tiles(b2.shape[0], out, stage, sems, lambda at: b1[at, :] - dot(wide(b2[at, :]), right))
+    by_tiles(b2.shape[0], out, stage, sems, lambda at: b1[at, :] - dot(wide(b2[at, :]), right), sources_part)
 
 
 def field_kernel(b2, panel, sources, inverse, side, y, out, stage, sems):
@@ -421,12 +422,12 @@
     by_tiles(b2.shape[0], out, stage, sems, value)
 
 
-def update(kernel, args, passes, name):
+def update(kernel, args, passes, name, more=()):
     rows = args[0].shape[0]
     return pl.pallas_call(
         kernel,
-        out_specs=pl.BlockSpec(memory_space=pl.ANY),
-        out_shape=jax.ShapeDtypeStruct((rows, R), F32),
+        out_specs=[pl.BlockSpec(memory_space=pl.ANY)] + [pl.BlockSpec(memory_space=pltpu.VMEM)] * len(more),
+        out_shape=[jax.ShapeDtypeStruct((rows, R), F32), *more],
         scratch_shapes=[pltpu.VMEM((rows, R), F32), pltpu.SemaphoreType.DMA((rows // TILE,))],
         compiler_params=pltpu.CompilerParams(vmem_limit_bytes=VMEM_LIMIT),
         cost_estimate=cost(passes, rows, 3),
@@ -439,80 +440,96 @@
     return lax.ppermute(x, AXES, [(i, i ^ mask) for i in range(count)])
 
 
-def rows_of(x, bit_value):
+def choose(x, upper):
     half = half_of(x.shape[0])
-    return lax.dynamic_slice_in_dim(x, bit_value * (x.shape[0] - half), half, 0)
-
-
-def scatter_sum(x, index, bit):
-    mine = (index >> bit) & 1
-    return rows_of(x, mine) + exchange(rows_of(x, 1 - mine), 1 << bit)
-
-
-def join(x, other, rows, index, bit):
-    mine = (index >> bit) & 1
-    low = jnp.where(mine == 0, x, other)
-    high = jnp.where(mine == 0, other, x)
+    low, high = x[:half], x[x.shape[0] - half :]
+    return jnp.where(upper, high, low), jnp.where(upper, low, high)
+
+
+def join(x, other, rows, upper):
+    low, high = jnp.where(upper, other, x), jnp.where(upper, x, other)
     return jnp.concatenate([low[: rows - x.shape[0]], high], axis=0)
 
 
-def gather(x, rows, index, bit):
-    return join(x, exchange(x, 1 << bit), rows, index, bit)
+def summing_stages(bits):
+    down = [("scatter", bit) for bit in bits[:-1]]
+    return down + [("sum", bits[-1])] + [("gather", bit) for bit in reversed(bits[:-1])]
+
+
+class Chain:
+    def __init__(self, value, upper):
+        self.value, self.upper, self.sizes = value, upper, {}
+
+    def start(self, kind, bit):
+        self.kind, self.bit = kind, bit
+        sent = self.value
+        if kind == "scatter":
+            self.sizes[bit] = self.value.shape[0]
+            self.value, sent = choose(self.value, self.upper[bit])
+        self.flying = exchange(sent, 1 << bit)
+
+    def finish(self):
+        if self.kind == "gather":
+            self.value = join(self.value, self.flying, self.sizes[self.bit], self.upper[self.bit])
+        else:
+            self.value = self.value + self.flying
 
 
 def per_device(q_two, q_one, sources, coupling_two, coupling_one):
     index = lax.axis_index(AXES)
-    leaf_bits = list(range(2, lax.axis_size("leaf").bit_length() + 1))
-    panel_order, source_order = leaf_bits, leaf_bits[1:] + leaf_bits[:1]
-
-    def scatter(x, order):
-        sizes = []
-        for bit in order:
-            sizes.append(x.shape[0])
-            x = scatter_sum(x, index, bit)
-        return x, sizes
+    places = lax.axis_size(AXES).bit_length() - 1
+    flags = [(index >> bit) & 1 == 1 for bit in range(places)]
+    q_two, *upper = lax.optimization_barrier((q_two, *flags))
+    stages = summing_stages(list(range(2, places)))
 
     keep, send, b2, b1 = panel_gram(q_two, q_one)
-    terms = keep + exchange(send, 1)
-    keep, send = source_gram(b2, b1, sources)
-    source = keep + exchange(send, 1)
-    terms, panel_sizes = scatter(terms, panel_order)
-    source, source_sizes = scatter(source, source_order)
-    for bit, rows in zip(reversed(panel_order), reversed(panel_sizes)):
-        terms = gather(terms, rows, index, bit)
-    terms = gather(terms, PANEL_TERMS, index, 0)
-    for bit, rows in zip(reversed(source_order[1:]), reversed(source_sizes[1:])):
-        source = gather(source, rows, index, bit)
-    source_arriving = exchange(source, 1 << source_order[0])
-
-    def half_rows(terms):
-        return rows_of(terms, index & 1)
-
+    arriving = exchange(send, 1)
+    source_keep, source_send = source_gram(b2, b1, sources)
+    arriving, source_send = lax.optimization_barrier((arriving, source_send))
+
+    panels = Chain(keep + arriving, upper)
+    source = Chain(source_keep, upper)
+    panels.sizes[0], source.sizes[0] = PANEL_TERMS, SOURCE_TERMS
+    source_left = [("gather", 0)] + stages[::-1]
+    for step, stage in enumerate(stages):
+        panels.start(*stage)
+        if step == 0:
+            source.kind, source.bit, source.flying = "sum", 0, exchange(source_send, 1)
+        else:
+            source.start(*source_left.pop())
+        panels.flying, source.flying = lax.optimization_barrier((panels.flying, source.flying))
+        panels.finish()
+        source.finish()
+    panels.start("gather", 0)
+    source.start(*source_left.pop())
+    panels.finish()
+    terms = panels.value
     parts = invert_first(half_index, terms, coupling_two, "level_first")
-    source_arriving, parts = lax.optimization_barrier((source_arriving, parts))
-    source = join(source, source_arriving, source_sizes[0], index, source_order[0])
-    source_arriving = exchange(source, 1)
+    source.flying, parts = lax.optimization_barrier((source.flying, parts))
+    source.finish()
+    source.start(*source_left.pop())
     inverse = invert_second(parts, "level_second")
-    source_arriving, inverse = lax.optimization_barrier((source_arriving, inverse))
+    source.flying, inverse = lax.optimization_barrier((source.flying, inverse))
+    source.finish()
+
     x, root = call(
         panel_solve_kernel, (SQUARE, jax.ShapeDtypeStruct((SYMMETRIC, LANES), F32)), (inverse, terms), "panel_solve"
     )
-    root = half_rows(root)
     arriving = exchange(root, 2)
-    panel_one = update(panel_kernel, [b2, b1, x], 3, "panel")
-    arriving, panel_one, source_arriving = lax.optimization_barrier((arriving, panel_one, source_arriving))
-    root = gather(root + arriving, SYMMETRIC, index, 0)
-    source = join(source, source_arriving, SOURCE_TERMS, index, 0)
-    y, side = call(
-        source_solve_kernel, (SQUARE, jax.ShapeDtypeStruct((FULL, LANES), F32)), (inverse, x, source), "source_solve"
-    )
-    side = half_rows(side)
-    arriving = exchange(side, 2)
+    full = jax.ShapeDtypeStruct((FULL, LANES), F32)
+    panel_one, y, side = update(panel_kernel, [b2, b1, x, inverse, source.value], 5, "panel", [SQUARE, full])
+    side = Chain(choose(side, upper[0])[0], upper)
+    side.sizes[0] = FULL
+    side_flying = exchange(side.value, 2)
+    arriving, side.value = lax.optimization_barrier((arriving, side.value))
+    root = root + arriving
     parts = invert_first(no_index, root, coupling_one[None], "root_first")
-    arriving, parts = lax.optimization_barrier((arriving, parts))
-    side = gather(side + arriving, FULL, index, 0)
+    side_flying, parts = lax.optimization_barrier((side_flying, parts))
+    side.value = side.value + side_flying
+    side.start("gather", 0)
     inverse = invert_second(parts, "root_second")
-    solution = update(field_kernel, [b2, panel_one, sources, inverse, side, y], 6, "field")
+    side.finish()
+    (solution,) = update(field_kernel, [b2, panel_one, sources, inverse, side.value, y], 6, "field")
     return (panel_one, solution)
 
 

time: 77.3 us -> 72.2 us (0.934)
  starting transfers between devices: 24.4 us -> 18.8 us
  waiting for transfers between devices: 16.9 us -> 20.3 us
  Pallas kernels: 32.2 us -> 31.2 us
  other arithmetic: 1.53 us -> 0.64 us
  local copies, waits for them, and re-layouts: 0.8 us -> 0.02 us
    ppermute x20 -> x17, starting transfers between devices: 24.4 us -> 18.8 us  [exchange(): return lax.ppermute(x, AXES, [(i, i ^ mask) for i in range(count)])]
    ppermute x20 -> x17, waiting for transfers between devices: 16.9 us -> 20.3 us  [exchange(): return lax.ppermute(x, AXES, [(i, i ^ mask) for i in range(count)])]
    add x10, other arithmetic: 1.11 us -> 0.21 us  [the longest x7 0.14 us: finish(): self.value = self.value + self.flying]
    pallas_call x6 -> x5, Pallas kernels: 18.9 us -> 18.3 us  [call(): pl.pallas_call(kernel, out_shape=out_shape, scratch_shapes=list(scratch),...]
  transfers between devices with their start and end apart: 20 -> 17, of which waited for: 12 -> 8; matrix products, arithmetic and copies ran while one was open for 3% -> 0% of each run, Pallas kernels for 26% -> 31%
where the time goes in v7:
time: 72.2 us; the launch traced here: 72.1 us
  Pallas kernels  31.2 us (43%)
  waiting for transfers between devices  20.3 us (28%)
  starting transfers between devices  18.8 us (26%)
  between operations  1.14 us (2%)
    ppermute x17, waiting for transfers between devices, exchange(): return lax.ppermute(x, AXES, [(i, i ^ mask) for i in range(count)])  20.3 us
    ppermute x17, starting transfers between devices, exchange(): return lax.ppermute(x, AXES, [(i, i ^ mask) for i in range(count)])  18.8 us
    pallas_call x5, Pallas kernels, call(): pl.pallas_call(kernel, out_shape=out_shape, scratch_shapes=list(scratch),...  18.3 us
    pallas_call x2, Pallas kernels, update(): pl.pallas_call(kernel, out_specs=[pl.BlockSpec(memory_space=pl.ANY)] + [p...  5.85 us
    pallas_call x1, Pallas kernels, panel_gram(): pl.pallas_call(panel_gram_kernel, in_specs=[pl.BlockSpec(memory_space=pl....  4.48 us
    pallas_call x1, Pallas kernels, source_gram(): pl.pallas_call(source_gram_kernel, out_shape=(part, part), scratch_shapes...  2.58 us
  transfers between devices with their start and end apart: 17, of which 8 were waited for; matrix products, arithmetic and copies ran while one was open for 0% of the time, Pallas kernels for 31%

profile of v7, /device:TPU:0, one launch (start us, length us, event | category | flops | bytes accessed | tf_op | source)
XLA Modules:
  0.0 72.1 jit_solution(1193500753564788331)
XLA Ops:
  0.6 0.0 copy-start
  0.6 4.5 %panel_gram.1 = (f32[520,128]{1,0:T(8,128)S(1)}, f32[520,128]{1,0:T(8,128)S(1)}, f32[2048,256]{1,0:T(8,128)S(1)}, f32[2048,256]{1,0:T(8,128)S(1)}) custom-call(f32[2048,256]{1,0:T(8,128)} %q_two, f32[2048,256]{1,0:T(8,128)} %q_one.1), custom_call_target="tpu_custom_call" | custom-call | flops 1879048192 | bytes 4194304 | tf_op jit(solution)/shard_map/panel_gram/pallas_call | solution.py:169
  5.1 0.5 collective-permute-start
  5.6 0.0 copy-done
  5.7 2.6 %source_gram.1 = (f32[512,128]{1,0:T(8,128)S(1)}, f32[512,128]{1,0:T(8,128)S(1)}) custom-call(f32[2048,256]{1,0:T(8,128)S(1)} %get-tuple-element.56.b2, f32[2048,256]{1,0:T(8,128)S(1)} %get-tuple-element.57.b1, f32[2048,256]{1,0:T(8,128)S(1)} %copy-done), custom_call_target="tpu_custom_call" | custom-call | flops 1610612736 | bytes 6291456 | tf_op jit(solution)/shard_map/source_gram/pallas_call | solution.py:186
  8.2 0.0 collective-permute-done
  8.2 0.1 collective-permute-start.2
  8.4 3.0 %collective-permute-start.1 = (f32[264,128]{1,0:T(8,128)S(1)}, f32[264,128]{1,0:T(8,128)S(1)}, u32[]{:S(2)}, u32[]{:S(2)}) collective-permute-start(f32[264,128]{1,0:T(8,128)S(1)} %slice_select_fusion.1), channel_id=1, source_target_pairs={{0,4},{1,5},{2,6},{3,7},{4,0},{5,1},{6,2},{7,3},{8,12},{9,13},{10,... | collective-permute-start | bytes 405512 | tf_op jit(solution)/shard_map/ppermute | solution.py:440
  11.4 3.8 %collective-permute-done.1 = f32[264,128]{1,0:T(8,128)S(1)} collective-permute-done((f32[264,128]{1,0:T(8,128)S(1)}, f32[264,128]{1,0:T(8,128)S(1)}, u32[]{:S(2)}, u32[]{:S(2)}) %collective-permute-start.1) | collective-permute-done | bytes 135200 | tf_op jit(solution)/shard_map/ppermute | solution.py:440
  15.2 0.0 collective-permute-done.2
  15.3 1.8 %collective-permute-start.4 = (f32[256,128]{1,0:T(8,128)S(1)}, f32[256,128]{1,0:T(8,128)S(1)}, u32[]{:S(2)}, u32[]{:S(2)}) collective-permute-start(f32[256,128]{1,0:T(8,128)S(1)} %slice_select_fusion.2), channel_id=1, source_target_pairs={{0,4},{1,5},{2,6},{3,7},{4,0},{5,1},{6,2},{7,3},{8,12},{9,13},{10,... | collective-permute-start | bytes 393224 | tf_op jit(solution)/shard_map/ppermute | solution.py:440
  17.1 1.7 %collective-permute-start.3 = (f32[136,128]{1,0:T(8,128)S(1)}, f32[136,128]{1,0:T(8,128)S(1)}, u32[]{:S(2)}, u32[]{:S(2)}) collective-permute-start(f32[136,128]{1,0:T(8,128)S(1)} %slice_select_fusion.4), channel_id=1, source_target_pairs={{0,8},{1,9},{2,10},{3,11},{4,12},{5,13},{6,14},{7,15},{8,0},{9,1},... | collective-permute-start | bytes 208904 | tf_op jit(solution)/shard_map/ppermute | solution.py:440
  18.8 2.7 %collective-permute-done.3 = f32[136,128]{1,0:T(8,128)S(1)} collective-permute-done((f32[136,128]{1,0:T(8,128)S(1)}, f32[136,128]{1,0:T(8,128)S(1)}, u32[]{:S(2)}, u32[]{:S(2)}) %collective-permute-start.3) | collective-permute-done | bytes 69664 | tf_op jit(solution)/shard_map/ppermute | solution.py:440
  21.5 0.0 collective-permute-done.4
  21.5 2.7 %collective-permute-start.5 = (f32[136,128]{1,0:T(8,128)S(1)}, f32[136,128]{1,0:T(8,128)S(1)}, u32[]{:S(2)}, u32[]{:S(2)}) collective-permute-start(f32[136,128]{1,0:T(8,128)S(1)} %select_add_fusion.2), channel_id=1, source_target_pairs={{0,16},{1,17},{2,18},{3,19},{4,20},{5,21},{6,22},{7,23},{8,24},{9,... | collective-permute-start | bytes 208904 | tf_op jit(solution)/shard_map/ppermute | solution.py:440
  24.2 1.6 %collective-permute-start.6 = (f32[128,128]{1,0:T(8,128)S(1)}, f32[128,128]{1,0:T(8,128)S(1)}, u32[]{:S(2)}, u32[]{:S(2)}) collective-permute-start(f32[128,128]{1,0:T(8,128)S(1)} %slice_select_fusion.5), channel_id=1, source_target_pairs={{0,8},{1,9},{2,10},{3,11},{4,12},{5,13},{6,14},{7,15},{8,0},{9,1},... | collective-permute-start | bytes 196616 | tf_op jit(solution)/shard_map/ppermute | solution.py:440
  25.9 3.4 %collective-permute-done.6 = f32[128,128]{1,0:T(8,128)S(1)} collective-permute-done((f32[128,128]{1,0:T(8,128)S(1)}, f32[128,128]{1,0:T(8,128)S(1)}, u32[]{:S(2)}, u32[]{:S(2)}) %collective-permute-start.6) | collective-permute-done | bytes 65568 | tf_op jit(solution)/shard_map/ppermute | solution.py:440
  29.2 0.0 collective-permute-done.5
  29.3 1.7 %collective-permute-start.7 = (f32[136,128]{1,0:T(8,128)S(1)}, f32[136,128]{1,0:T(8,128)S(1)}, u32[]{:S(2)}, u32[]{:S(2)}) collective-permute-start(f32[136,128]{1,0:T(8,128)S(1)} %add.39), channel_id=1, source_target_pairs={{0,8},{1,9},{2,10},{3,11},{4,12},{5,13},{6,14},{7,15},{8,0},{9,1},... | collective-permute-start | bytes 208904 | tf_op jit(solution)/shard_map/ppermute | solution.py:440
  30.9 0.9 %collective-permute-start.8 = (f32[128,128]{1,0:T(8,128)S(1)}, f32[128,128]{1,0:T(8,128)S(1)}, u32[]{:S(2)}, u32[]{:S(2)}) collective-permute-start(f32[128,128]{1,0:T(8,128)S(1)} %select_add_fusion.3), channel_id=1, source_target_pairs={{0,16},{1,17},{2,18},{3,19},{4,20},{5,21},{6,22},{7,23},{8,24},{9,... | collective-permute-start | bytes 196616 | tf_op jit(solution)/shard_map/ppermute | solution.py:440
  31.8 4.9 %collective-permute-done.8 = f32[128,128]{1,0:T(8,128)S(1)} collective-permute-done((f32[128,128]{1,0:T(8,128)S(1)}, f32[128,128]{1,0:T(8,128)S(1)}, u32[]{:S(2)}, u32[]{:S(2)}) %collective-permute-start.8) | collective-permute-done | bytes 65568 | tf_op jit(solution)/shard_map/ppermute | solution.py:440
  36.7 0.0 collective-permute-done.7
  36.8 0.0 copy-start.2
  36.8 0.6 collective-permute-start.9
  37.5 0.2 collective-permute-start.10
  37.6 4.1 %collective-permute-done.10 = f32[128,128]{1,0:T(8,128)S(1)} collective-permute-done((f32[128,128]{1,0:T(8,128)S(1)}, f32[128,128]{1,0:T(8,128)S(1)}, u32[]{:S(2)}, u32[]{:S(2)}) %collective-permute-start.10) | collective-permute-done | bytes 65568 | tf_op jit(solution)/shard_map/ppermute | solution.py:440
  41.8 0.1 collective-permute-done.9
  42.0 0.1 collective-permute-start.12
  42.1 1.4 %collective-permute-start.11 = (f32[256,128]{1,0:T(8,128)S(1)}, f32[256,128]{1,0:T(8,128)S(1)}, u32[]{:S(2)}, u32[]{:S(2)}) collective-permute-start(f32[256,128]{1,0:T(8,128)S(1)} %pad_maximum_fusion.6), channel_id=1, source_target_pairs={{0,4},{1,5},{2,6},{3,7},{4,0},{5,1},{6,2},{7,3},{8,12},{9,13},{10,... | collective-permute-start | bytes 393224 | tf_op jit(solution)/shard_map/ppermute | solution.py:440
  43.5 0.1 collective-permute-done.12
  43.6 0.1 broadcast_select_fusion.1
  43.7 0.0 copy-done.2
  43.7 4.5 %level_first.1 = (f32[128,128]{1,0:T(8,128)S(1)}, f32[128,128]{1,0:T(8,128)S(1)}, f32[128,128]{1,0:T(8,128)S(1)}, f32[8,256]{1,0:T(8,128)S(1)}, f32[256,128]{1,0:T(8,128)S(1)}) custom-call(f32[1040,128]{1,0:T(8,128)S(1)} %pad_maximum_fusion.gram_ref.terms, f32[2,256,256]{2,1,0:T(8,128)S(1)} %copy-done.2), custom_call_target="tpu_custom_call" | custom-call | flops 5000000000 | bytes 262144 | tf_op jit(solution)/shard_map/level_first/pallas_call | solution.py:304
  48.2 0.0 collective-permute-done.11
  48.2 0.2 collective-permute-start.13
  48.5 4.1 %level_second.1.inverse = f32[256,256]{1,0:T(8,128)S(1)} custom-call(f32[128,128]{1,0:T(8,128)S(1)} %get-tuple-element.83.first, f32[128,128]{1,0:T(8,128)S(1)} %get-tuple-element.84.across, f32[128,128]{1,0:T(8,128)S(1)} %get-tuple-element.85.rest, f32[8,256]{1,0:T(8,128)S(1)} %get-tuple-element.86.row, f32[256,128]{1,0:T(8,128)S(1)} %get-tuple-element.87.col), custom_call_target="tpu_custom_call" | custom-call | flops 5000000000 | bytes 262144 | tf_op jit(solution)/shard_map/level_second/pallas_call | solution.py:304
  52.6 0.0 collective-permute-done.13
  52.6 1.1 %panel_solve.1 = (f32[256,256]{1,0:T(8,128)S(1)}, f32[264,128]{1,0:T(8,128)S(1)}) custom-call(f32[256,256]{1,0:T(8,128)S(1)} %level_second.1.inverse, f32[1040,128]{1,0:T(8,128)S(1)} %pad_maximum_fusion.gram_ref.terms), custom_call_target="tpu_custom_call" | custom-call | bytes 262144 | tf_op jit(solution)/shard_map/panel_solve/pallas_call | solution.py:304
  53.7 1.6 %collective-permute-start.15 = (f32[264,128]{1,0:T(8,128)S(1)}, f32[264,128]{1,0:T(8,128)S(1)}, u32[]{:S(2)}, u32[]{:S(2)}) collective-permute-start(f32[264,128]{1,0:T(8,128)S(1)} %get-tuple-element.93), channel_id=1, source_target_pairs={{0,2},{1,3},{2,0},{3,1},{4,6},{5,7},{6,4},{7,5},{8,10},{9,11},{10,... | collective-permute-start | bytes 405512 | tf_op jit(solution)/shard_map/ppermute | solution.py:440
  55.4 0.0 copy-start.3
  55.4 2.4 %panel.1 = (f32[2048,256]{1,0:T(8,128)}, f32[256,256]{1,0:T(8,128)S(1)}, f32[512,128]{1,0:T(8,128)S(1)}) custom-call(f32[2048,256]{1,0:T(8,128)S(1)} %get-tuple-element.56.b2, f32[2048,256]{1,0:T(8,128)S(1)} %get-tuple-element.57.b1, f32[256,256]{1,0:T(8,128)S(1)} %get-tuple-element.89.x, f32[256,256]{1,0:T(8,128)S(1)} %level_second.1.inverse, ...), custom_call_target="tpu_custom_call" | custom-call | flops 1342177280 | bytes 6291456 | tf_op jit(solution)/shard_map/panel/pallas_call | solution.py:427
  57.8 0.6 collective-permute-start.14
  58.4 1.2 %collective-permute-done.15 = f32[264,128]{1,0:T(8,128)S(1)} collective-permute-done((f32[264,128]{1,0:T(8,128)S(1)}, f32[264,128]{1,0:T(8,128)S(1)}, u32[]{:S(2)}, u32[]{:S(2)}) %collective-permute-start.15) | collective-permute-done | bytes 135200 | tf_op jit(solution)/shard_map/ppermute | solution.py:440
  59.7 0.0 copy-done.3
  59.7 4.5 %root_first.1 = (f32[128,128]{1,0:T(8,128)S(1)}, f32[128,128]{1,0:T(8,128)S(1)}, f32[128,128]{1,0:T(8,128)S(1)}, f32[8,256]{1,0:T(8,128)S(1)}, f32[256,128]{1,0:T(8,128)S(1)}) custom-call(f32[264,128]{1,0:T(8,128)S(1)} %add.42.gram_ref, f32[1,256,256]{2,1,0:T(8,128)S(1)} %bitcast.1), custom_call_target="tpu_custom_call" | custom-call | flops 5000000000 | bytes 262144 | tf_op jit(solution)/shard_map/root_first/pallas_call | solution.py:304
  64.2 0.0 collective-permute-done.14
  64.2 0.1 collective-permute-start.16
  64.3 0.0 copy-start.1
  64.3 4.1 %root_second.1.inverse = f32[256,256]{1,0:T(8,128)S(1)} custom-call(f32[128,128]{1,0:T(8,128)S(1)} %get-tuple-element.100.first, f32[128,128]{1,0:T(8,128)S(1)} %get-tuple-element.101.across, f32[128,128]{1,0:T(8,128)S(1)} %get-tuple-element.102.rest, f32[8,256]{1,0:T(8,128)S(1)} %get-tuple-element.103.row, f32[256,128]{1,0:T(8,128)S(1)} %get-tuple-element.104.col), custom_call_target="tpu_custom_call" | custom-call | flops 5000000000 | bytes 262144 | tf_op jit(solution)/shard_map/root_second/pallas_call | solution.py:304
  68.4 0.0 collective-permute-done.16
  68.5 0.0 copy-done.1
  68.5 3.4 %field.1 = f32[2048,256]{1,0:T(8,128)} custom-call(f32[2048,256]{1,0:T(8,128)S(1)} %get-tuple-element.56.b2, f32[2048,256]{1,0:T(8,128)S(1)} %copy-done.1, f32[2048,256]{1,0:T(8,128)S(1)} %copy-done, f32[256,256]{1,0:T(8,128)S(1)} %root_second.1.inverse, f32[512,128]{1,0:T(8,128)S(1)} %pad_maximum_fusion.4.side, f32[256,256]{1,0:T(8,128)S(1)} %get-tuple-element.107.y), custom_call_target="tpu_custom_call" | custom-call | flops 1610612736 | bytes 6291456 | tf_op jit(solution)/shard_map/field/pallas_call | solution.py:427
  (30 shorter events, 0.6 us)
Async XLA Ops:
  0.6 5.0 %copy-start = (f32[2048,256]{1,0:T(8,128)S(1)}, f32[2048,256]{1,0:T(8,128)}, u32[]{:S(2)}) copy-start(f32[2048,256]{1,0:T(8,128)} %sources.3) | copy-start | bytes 6291460
  5.1 3.1 %collective-permute-start = (f32[520,128]{1,0:T(8,128)S(1)}, f32[520,128]{1,0:T(8,128)S(1)}, u32[]{:S(2)}, u32[]{:S(2)}) collective-permute-start(f32[520,128]{1,0:T(8,128)S(1)} %get-tuple-element.61), channel_id=1, source_target_pairs={{0,1},{1,0},{2,3},{3,2},{4,5},{5,4},{6,7},{7,6},{8,9},{9,8},{10,11... | collective-permute-start | bytes 798728 | tf_op jit(solution)/shard_map/ppermute | solution.py:440
  8.2 6.9 %collective-permute-start.2 = (f32[512,128]{1,0:T(8,128)S(1)}, f32[512,128]{1,0:T(8,128)S(1)}, u32[]{:S(2)}, u32[]{:S(2)}) collective-permute-start(f32[512,128]{1,0:T(8,128)S(1)} %get-tuple-element.64), channel_id=1, source_target_pairs={{0,1},{1,0},{2,3},{3,2},{4,5},{5,4},{6,7},{7,6},{8,9},{9,8},{10,11... | collective-permute-start | bytes 786440 | tf_op jit(solution)/shard_map/ppermute | solution.py:440
  8.4 6.8 %collective-permute-start.1 = (f32[264,128]{1,0:T(8,128)S(1)}, f32[264,128]{1,0:T(8,128)S(1)}, u32[]{:S(2)}, u32[]{:S(2)}) collective-permute-start(f32[264,128]{1,0:T(8,128)S(1)} %slice_select_fusion.1), channel_id=1, source_target_pairs={{0,4},{1,5},{2,6},{3,7},{4,0},{5,1},{6,2},{7,3},{8,12},{9,13},{10,... | collective-permute-start | bytes 405512 | tf_op jit(solution)/shard_map/ppermute | solution.py:440
  15.3 6.2 %collective-permute-start.4 = (f32[256,128]{1,0:T(8,128)S(1)}, f32[256,128]{1,0:T(8,128)S(1)}, u32[]{:S(2)}, u32[]{:S(2)}) collective-permute-start(f32[256,128]{1,0:T(8,128)S(1)} %slice_select_fusion.2), channel_id=1, source_target_pairs={{0,4},{1,5},{2,6},{3,7},{4,0},{5,1},{6,2},{7,3},{8,12},{9,13},{10,... | collective-permute-start | bytes 393224 | tf_op jit(solution)/shard_map/ppermute | solution.py:440
  17.1 4.4 %collective-permute-start.3 = (f32[136,128]{1,0:T(8,128)S(1)}, f32[136,128]{1,0:T(8,128)S(1)}, u32[]{:S(2)}, u32[]{:S(2)}) collective-permute-start(f32[136,128]{1,0:T(8,128)S(1)} %slice_select_fusion.4), channel_id=1, source_target_pairs={{0,8},{1,9},{2,10},{3,11},{4,12},{5,13},{6,14},{7,15},{8,0},{9,1},... | collective-permute-start | bytes 208904 | tf_op jit(solution)/shard_map/ppermute | solution.py:440
  21.5 7.7 %collective-permute-start.5 = (f32[136,128]{1,0:T(8,128)S(1)}, f32[136,128]{1,0:T(8,128)S(1)}, u32[]{:S(2)}, u32[]{:S(2)}) collective-permute-start(f32[136,128]{1,0:T(8,128)S(1)} %select_add_fusion.2), channel_id=1, source_target_pairs={{0,16},{1,17},{2,18},{3,19},{4,20},{5,21},{6,22},{7,23},{8,24},{9,... | collective-permute-start | bytes 208904 | tf_op jit(solution)/shard_map/ppermute | solution.py:440
  24.2 5.0 %collective-permute-start.6 = (f32[128,128]{1,0:T(8,128)S(1)}, f32[128,128]{1,0:T(8,128)S(1)}, u32[]{:S(2)}, u32[]{:S(2)}) collective-permute-start(f32[128,128]{1,0:T(8,128)S(1)} %slice_select_fusion.5), channel_id=1, source_target_pairs={{0,8},{1,9},{2,10},{3,11},{4,12},{5,13},{6,14},{7,15},{8,0},{9,1},... | collective-permute-start | bytes 196616 | tf_op jit(solution)/shard_map/ppermute | solution.py:440
  29.3 7.5 %collective-permute-start.7 = (f32[136,128]{1,0:T(8,128)S(1)}, f32[136,128]{1,0:T(8,128)S(1)}, u32[]{:S(2)}, u32[]{:S(2)}) collective-permute-start(f32[136,128]{1,0:T(8,128)S(1)} %add.39), channel_id=1, source_target_pairs={{0,8},{1,9},{2,10},{3,11},{4,12},{5,13},{6,14},{7,15},{8,0},{9,1},... | collective-permute-start | bytes 208904 | tf_op jit(solution)/shard_map/ppermute | solution.py:440
  30.9 5.8 %collective-permute-start.8 = (f32[128,128]{1,0:T(8,128)S(1)}, f32[128,128]{1,0:T(8,128)S(1)}, u32[]{:S(2)}, u32[]{:S(2)}) collective-permute-start(f32[128,128]{1,0:T(8,128)S(1)} %select_add_fusion.3), channel_id=1, source_target_pairs={{0,16},{1,17},{2,18},{3,19},{4,20},{5,21},{6,22},{7,23},{8,24},{9,... | collective-permute-start | bytes 196616 | tf_op jit(solution)/shard_map/ppermute | solution.py:440
  36.8 6.9 %copy-start.2 = (f32[2,256,256]{2,1,0:T(8,128)S(1)}, f32[2,256,256]{2,1,0:T(8,128)}, u32[]{:S(2)}) copy-start(f32[2,256,256]{2,1,0:T(8,128)} %coupling.1) | copy-start | bytes 1572868
  36.8 5.1 %collective-permute-start.9 = (f32[264,128]{1,0:T(8,128)S(1)}, f32[264,128]{1,0:T(8,128)S(1)}, u32[]{:S(2)}, u32[]{:S(2)}) collective-permute-start(f32[264,128]{1,0:T(8,128)S(1)} %pad_maximum_fusion.5), channel_id=1, source_target_pairs={{0,4},{1,5},{2,6},{3,7},{4,0},{5,1},{6,2},{7,3},{8,12},{9,13},{10,... | collective-permute-start | bytes 405512 | tf_op jit(solution)/shard_map/ppermute | solution.py:440
  37.5 4.3 %collective-permute-start.10 = (f32[128,128]{1,0:T(8,128)S(1)}, f32[128,128]{1,0:T(8,128)S(1)}, u32[]{:S(2)}, u32[]{:S(2)}) collective-permute-start(f32[128,128]{1,0:T(8,128)S(1)} %add.41), channel_id=1, source_target_pairs={{0,8},{1,9},{2,10},{3,11},{4,12},{5,13},{6,14},{7,15},{8,0},{9,1},... | collective-permute-start | bytes 196616 | tf_op jit(solution)/shard_map/ppermute | solution.py:440
  42.0 1.6 %collective-permute-start.12 = (f32[520,128]{1,0:T(8,128)S(1)}, f32[520,128]{1,0:T(8,128)S(1)}, u32[]{:S(2)}, u32[]{:S(2)}) collective-permute-start(f32[520,128]{1,0:T(8,128)S(1)} %pad_maximum_fusion.2), channel_id=1, source_target_pairs={{0,1},{1,0},{2,3},{3,2},{4,5},{5,4},{6,7},{7,6},{8,9},{9,8},{10,11... | collective-permute-start | bytes 798728 | tf_op jit(solution)/shard_map/ppermute | solution.py:440
  42.1 6.1 %collective-permute-start.11 = (f32[256,128]{1,0:T(8,128)S(1)}, f32[256,128]{1,0:T(8,128)S(1)}, u32[]{:S(2)}, u32[]{:S(2)}) collective-permute-start(f32[256,128]{1,0:T(8,128)S(1)} %pad_maximum_fusion.6), channel_id=1, source_target_pairs={{0,4},{1,5},{2,6},{3,7},{4,0},{5,1},{6,2},{7,3},{8,12},{9,13},{10,... | collective-permute-start | bytes 393224 | tf_op jit(solution)/shard_map/ppermute | solution.py:440
  48.2 4.3 %collective-permute-start.13 = (f32[512,128]{1,0:T(8,128)S(1)}, f32[512,128]{1,0:T(8,128)S(1)}, u32[]{:S(2)}, u32[]{:S(2)}) collective-permute-start(f32[512,128]{1,0:T(8,128)S(1)} %pad_maximum_fusion.3), channel_id=1, source_target_pairs={{0,1},{1,0},{2,3},{3,2},{4,5},{5,4},{6,7},{7,6},{8,9},{9,8},{10,11... | collective-permute-start | bytes 786440 | tf_op jit(solution)/shard_map/ppermute | solution.py:440
  53.7 5.9 %collective-permute-start.15 = (f32[264,128]{1,0:T(8,128)S(1)}, f32[264,128]{1,0:T(8,128)S(1)}, u32[]{:S(2)}, u32[]{:S(2)}) collective-permute-start(f32[264,128]{1,0:T(8,128)S(1)} %get-tuple-element.93), channel_id=1, source_target_pairs={{0,2},{1,3},{2,0},{3,1},{4,6},{5,7},{6,4},{7,5},{8,10},{9,11},{10,... | collective-permute-start | bytes 405512 | tf_op jit(solution)/shard_map/ppermute | solution.py:440
  55.4 4.3 %copy-start.3 = (f32[256,256]{1,0:T(8,128)S(1)}, f32[256,256]{1,0:T(8,128)}, u32[]{:S(2)}) copy-start(f32[256,256]{1,0:T(8,128)} %param.9) | copy-start | bytes 786436
  57.8 6.3 %collective-permute-start.14 = (f32[256,128]{1,0:T(8,128)S(1)}, f32[256,128]{1,0:T(8,128)S(1)}, u32[]{:S(2)}, u32[]{:S(2)}) collective-permute-start(f32[256,128]{1,0:T(8,128)S(1)} %slice_select_fusion), channel_id=1, source_target_pairs={{0,2},{1,3},{2,0},{3,1},{4,6},{5,7},{6,4},{7,5},{8,10},{9,11},{10,... | collective-permute-start | bytes 393224 | tf_op jit(solution)/shard_map/ppermute | solution.py:440
  64.2 4.2 %collective-permute-start.16 = (f32[256,128]{1,0:T(8,128)S(1)}, f32[256,128]{1,0:T(8,128)S(1)}, u32[]{:S(2)}, u32[]{:S(2)}) collective-permute-start(f32[256,128]{1,0:T(8,128)S(1)} %add.43), channel_id=1, source_target_pairs={{0,1},{1,0},{2,3},{3,2},{4,5},{5,4},{6,7},{7,6},{8,9},{9,8},{10,11... | collective-permute-start | bytes 393224 | tf_op jit(solution)/shard_map/ppermute | solution.py:440
  64.3 4.2 %copy-start.1 = (f32[2048,256]{1,0:T(8,128)S(1)}, f32[2048,256]{1,0:T(8,128)}, u32[]{:S(2)}) copy-start(f32[2048,256]{1,0:T(8,128)} %get-tuple-element.53.panel) | copy-start | bytes 6291460

commit v8 on v7

--- a/solution.py
+++ b/solution.py
@@ -232,9 +232,15 @@
     for j in range(8):
         row = jnp.broadcast_to(rows[8 * at + j : 8 * at + j + 1, :], (8, LANES))
         line.append(jnp.where(inside, jnp.where(lane == 8 * at + j, 1.0, 0.0), row))
-    line = solve_small(entry, line)
+    after = None
+    if t < 3:
+        columns = [spread_lane(panel[t + 1], 8 * at + j) for j in range(8)]
+        after = [columns, jnp.where(inside, 0.0, panel[t + 1])]
+    line, after = solve_small(entry, line, after)
     for g in range(4):
-        if g != t:
+        if g == t + 1:
+            panel[g] = after
+        elif g != t:
             terms = [spread_lane(panel[g], 8 * at + j) * line[j] for j in range(8)]
             panel[g] = jnp.where(inside, 0.0, panel[g]) - tree_sum(terms)
     merged = line[0]
@@ -253,32 +259,36 @@
     return terms[0]
 
 
-def solve_small(entry, line):
-    factors, pivots = {}, {}
+def solve_small(entry, line, after):
+    columns, block = after or (None, None)
+    factors, scaled = {}, {}
     for k in range(0, 8, 2):
         a, b, c = entry[k, k], entry[k + 1, k], entry[k + 1, k + 1]
         inv = pl.reciprocal(a * c - b * b, approx=True)
-        e, f, g = c * inv, b * inv, a * inv
-        pivots[k] = (e, f, g)
-        for i in range(k + 2, 8):
-            u, v = entry[i, k], entry[i, k + 1]
-            factors[i, k] = (e * u - f * v, g * v - f * u)
-        for i in range(k + 2, 8):
-            u, v = entry[i, k], entry[i, k + 1]
+        below = range(k + 2, 8)
+        first = {i: c * entry[i, k] - b * entry[i, k + 1] for i in below}
+        second = {i: a * entry[i, k + 1] - b * entry[i, k] for i in below}
+        for i in below:
             for j in range(k + 2, i + 1):
-                m, n = factors[j, k]
-                entry[i, j] = entry[i, j] - (u * m + v * n)
-        for i in range(k + 2, 8):
-            m, n = factors[i, k]
+                entry[i, j] = entry[i, j] - inv * (first[i] * entry[j, k] + second[i] * entry[j, k + 1])
+        top = c * line[k] - b * line[k + 1]
+        bottom = a * line[k + 1] - b * line[k]
+        if columns is not None:
+            block = block - inv * (columns[k] * top + columns[k + 1] * bottom)
+        scaled[k], scaled[k + 1] = inv * top, inv * bottom
+        for i in below:
+            m, n = inv * first[i], inv * second[i]
+            factors[i, k] = m, n
             line[i] = line[i] - (m * line[k] + n * line[k + 1])
+            if columns is not None:
+                columns[i] = columns[i] - (m * columns[k] + n * columns[k + 1])
     for k in range(6, -1, -2):
-        e, f, g = pivots[k]
-        x, y = e * line[k] - f * line[k + 1], g * line[k + 1] - f * line[k]
+        x, y = scaled[k], scaled[k + 1]
         if k < 6:
             x = x - tree_sum([factors[i, k][0] * line[i] for i in range(k + 2, 8)])
             y = y - tree_sum([factors[i, k][1] * line[i] for i in range(k + 2, 8)])
         line[k], line[k + 1] = x, y
-    return line
+    return line, block
 
 
 def stack_left(x):

time: 72.2 us -> 70.5 us (0.976)
  Pallas kernels: 31.2 us -> 29 us
    pallas_call x5, Pallas kernels: 18.3 us -> 16.1 us  [call(): pl.pallas_call(kernel, out_shape=out_shape, scratch_shapes=list(scratch),...]
  transfers between devices with their start and end apart: 17 -> 17, of which waited for: 8 -> 9; matrix products, arithmetic and copies ran while one was open for 0% -> 0% of each run, Pallas kernels for 31% -> 28%
where the time goes in v8:
time: 70.5 us; the launch traced here: 70.3 us
  Pallas kernels  29 us (41%)
  waiting for transfers between devices  21 us (30%)
  starting transfers between devices  18.6 us (26%)
  between operations  1.14 us (2%)
    ppermute x17, waiting for transfers between devices, exchange(): return lax.ppermute(x, AXES, [(i, i ^ mask) for i in range(count)])  21 us
    ppermute x17, starting transfers between devices, exchange(): return lax.ppermute(x, AXES, [(i, i ^ mask) for i in range(count)])  18.6 us
    pallas_call x5, Pallas kernels, call(): pl.pallas_call(kernel, out_shape=out_shape, scratch_shapes=list(scratch),...  16.1 us
    pallas_call x2, Pallas kernels, update(): pl.pallas_call(kernel, out_specs=[pl.BlockSpec(memory_space=pl.ANY)] + [p...  5.84 us
    pallas_call x1, Pallas kernels, panel_gram(): pl.pallas_call(panel_gram_kernel, in_specs=[pl.BlockSpec(memory_space=pl....  4.48 us
    pallas_call x1, Pallas kernels, source_gram(): pl.pallas_call(source_gram_kernel, out_shape=(part, part), scratch_shapes...  2.58 us
  transfers between devices with their start and end apart: 17, of which 9 were waited for; matrix products, arithmetic and copies ran while one was open for 0% of the time, Pallas kernels for 28%

profile of v8, /device:TPU:0, one launch (start us, length us, event | category | flops | bytes accessed | tf_op | source)
XLA Modules:
  0.0 70.3 jit_solution(9832826024524613385)
XLA Ops:
  0.6 0.0 copy-start
  0.6 4.5 %panel_gram.1 = (f32[520,128]{1,0:T(8,128)S(1)}, f32[520,128]{1,0:T(8,128)S(1)}, f32[2048,256]{1,0:T(8,128)S(1)}, f32[2048,256]{1,0:T(8,128)S(1)}) custom-call(f32[2048,256]{1,0:T(8,128)} %q_two, f32[2048,256]{1,0:T(8,128)} %q_one.1), custom_call_target="tpu_custom_call" | custom-call | flops 1879048192 | bytes 4194304 | tf_op jit(solution)/shard_map/panel_gram/pallas_call | solution.py:169
  5.1 0.5 collective-permute-start
  5.6 0.0 copy-done
  5.7 2.6 %source_gram.1 = (f32[512,128]{1,0:T(8,128)S(1)}, f32[512,128]{1,0:T(8,128)S(1)}) custom-call(f32[2048,256]{1,0:T(8,128)S(1)} %get-tuple-element.56.b2, f32[2048,256]{1,0:T(8,128)S(1)} %get-tuple-element.57.b1, f32[2048,256]{1,0:T(8,128)S(1)} %copy-done), custom_call_target="tpu_custom_call" | custom-call | flops 1610612736 | bytes 6291456 | tf_op jit(solution)/shard_map/source_gram/pallas_call | solution.py:186
  8.2 0.0 collective-permute-done
  8.2 0.1 collective-permute-start.2
  8.4 3.0 %collective-permute-start.1 = (f32[264,128]{1,0:T(8,128)S(1)}, f32[264,128]{1,0:T(8,128)S(1)}, u32[]{:S(2)}, u32[]{:S(2)}) collective-permute-start(f32[264,128]{1,0:T(8,128)S(1)} %slice_select_fusion.1), channel_id=1, source_target_pairs={{0,4},{1,5},{2,6},{3,7},{4,0},{5,1},{6,2},{7,3},{8,12},{9,13},{10,... | collective-permute-start | bytes 405512 | tf_op jit(solution)/shard_map/ppermute | solution.py:450
  11.4 3.8 %collective-permute-done.1 = f32[264,128]{1,0:T(8,128)S(1)} collective-permute-done((f32[264,128]{1,0:T(8,128)S(1)}, f32[264,128]{1,0:T(8,128)S(1)}, u32[]{:S(2)}, u32[]{:S(2)}) %collective-permute-start.1) | collective-permute-done | bytes 135200 | tf_op jit(solution)/shard_map/ppermute | solution.py:450
  15.2 0.0 collective-permute-done.2
  15.3 1.8 %collective-permute-start.4 = (f32[256,128]{1,0:T(8,128)S(1)}, f32[256,128]{1,0:T(8,128)S(1)}, u32[]{:S(2)}, u32[]{:S(2)}) collective-permute-start(f32[256,128]{1,0:T(8,128)S(1)} %slice_select_fusion.2), channel_id=1, source_target_pairs={{0,4},{1,5},{2,6},{3,7},{4,0},{5,1},{6,2},{7,3},{8,12},{9,13},{10,... | collective-permute-start | bytes 393224 | tf_op jit(solution)/shard_map/ppermute | solution.py:450
  17.1 1.7 %collective-permute-start.3 = (f32[136,128]{1,0:T(8,128)S(1)}, f32[136,128]{1,0:T(8,128)S(1)}, u32[]{:S(2)}, u32[]{:S(2)}) collective-permute-start(f32[136,128]{1,0:T(8,128)S(1)} %slice_select_fusion.4), channel_id=1, source_target_pairs={{0,8},{1,9},{2,10},{3,11},{4,12},{5,13},{6,14},{7,15},{8,0},{9,1},... | collective-permute-start | bytes 208904 | tf_op jit(solution)/shard_map/ppermute | solution.py:450
  18.8 2.7 %collective-permute-done.3 = f32[136,128]{1,0:T(8,128)S(1)} collective-permute-done((f32[136,128]{1,0:T(8,128)S(1)}, f32[136,128]{1,0:T(8,128)S(1)}, u32[]{:S(2)}, u32[]{:S(2)}) %collective-permute-start.3) | collective-permute-done | bytes 69664 | tf_op jit(solution)/shard_map/ppermute | solution.py:450
  21.5 0.0 collective-permute-done.4
  21.5 2.7 %collective-permute-start.5 = (f32[136,128]{1,0:T(8,128)S(1)}, f32[136,128]{1,0:T(8,128)S(1)}, u32[]{:S(2)}, u32[]{:S(2)}) collective-permute-start(f32[136,128]{1,0:T(8,128)S(1)} %select_add_fusion.2), channel_id=1, source_target_pairs={{0,16},{1,17},{2,18},{3,19},{4,20},{5,21},{6,22},{7,23},{8,24},{9,... | collective-permute-start | bytes 208904 | tf_op jit(solution)/shard_map/ppermute | solution.py:450
  24.2 1.6 %collective-permute-start.6 = (f32[128,128]{1,0:T(8,128)S(1)}, f32[128,128]{1,0:T(8,128)S(1)}, u32[]{:S(2)}, u32[]{:S(2)}) collective-permute-start(f32[128,128]{1,0:T(8,128)S(1)} %slice_select_fusion.5), channel_id=1, source_target_pairs={{0,8},{1,9},{2,10},{3,11},{4,12},{5,13},{6,14},{7,15},{8,0},{9,1},... | collective-permute-start | bytes 196616 | tf_op jit(solution)/shard_map/ppermute | solution.py:450
  25.9 3.4 %collective-permute-done.6 = f32[128,128]{1,0:T(8,128)S(1)} collective-permute-done((f32[128,128]{1,0:T(8,128)S(1)}, f32[128,128]{1,0:T(8,128)S(1)}, u32[]{:S(2)}, u32[]{:S(2)}) %collective-permute-start.6) | collective-permute-done | bytes 65568 | tf_op jit(solution)/shard_map/ppermute | solution.py:450
  29.2 0.0 collective-permute-done.5
  29.3 1.7 %collective-permute-start.7 = (f32[136,128]{1,0:T(8,128)S(1)}, f32[136,128]{1,0:T(8,128)S(1)}, u32[]{:S(2)}, u32[]{:S(2)}) collective-permute-start(f32[136,128]{1,0:T(8,128)S(1)} %add.39), channel_id=1, source_target_pairs={{0,8},{1,9},{2,10},{3,11},{4,12},{5,13},{6,14},{7,15},{8,0},{9,1},... | collective-permute-start | bytes 208904 | tf_op jit(solution)/shard_map/ppermute | solution.py:450
  30.9 0.9 %collective-permute-start.8 = (f32[128,128]{1,0:T(8,128)S(1)}, f32[128,128]{1,0:T(8,128)S(1)}, u32[]{:S(2)}, u32[]{:S(2)}) collective-permute-start(f32[128,128]{1,0:T(8,128)S(1)} %select_add_fusion.3), channel_id=1, source_target_pairs={{0,16},{1,17},{2,18},{3,19},{4,20},{5,21},{6,22},{7,23},{8,24},{9,... | collective-permute-start | bytes 196616 | tf_op jit(solution)/shard_map/ppermute | solution.py:450
  31.8 4.9 %collective-permute-done.8 = f32[128,128]{1,0:T(8,128)S(1)} collective-permute-done((f32[128,128]{1,0:T(8,128)S(1)}, f32[128,128]{1,0:T(8,128)S(1)}, u32[]{:S(2)}, u32[]{:S(2)}) %collective-permute-start.8) | collective-permute-done | bytes 65568 | tf_op jit(solution)/shard_map/ppermute | solution.py:450
  36.7 0.0 collective-permute-done.7
  36.8 0.0 copy-start.2
  36.8 0.6 collective-permute-start.9
  37.5 0.2 collective-permute-start.10
  37.6 4.1 %collective-permute-done.10 = f32[128,128]{1,0:T(8,128)S(1)} collective-permute-done((f32[128,128]{1,0:T(8,128)S(1)}, f32[128,128]{1,0:T(8,128)S(1)}, u32[]{:S(2)}, u32[]{:S(2)}) %collective-permute-start.10) | collective-permute-done | bytes 65568 | tf_op jit(solution)/shard_map/ppermute | solution.py:450
  41.8 0.1 collective-permute-done.9
  42.0 0.1 collective-permute-start.12
  42.1 1.4 %collective-permute-start.11 = (f32[256,128]{1,0:T(8,128)S(1)}, f32[256,128]{1,0:T(8,128)S(1)}, u32[]{:S(2)}, u32[]{:S(2)}) collective-permute-start(f32[256,128]{1,0:T(8,128)S(1)} %pad_maximum_fusion.6), channel_id=1, source_target_pairs={{0,4},{1,5},{2,6},{3,7},{4,0},{5,1},{6,2},{7,3},{8,12},{9,13},{10,... | collective-permute-start | bytes 393224 | tf_op jit(solution)/shard_map/ppermute | solution.py:450
  43.5 0.1 collective-permute-done.12
  43.6 0.1 broadcast_select_fusion.1
  43.7 0.0 copy-done.2
  43.7 3.8 %level_first.1 = (f32[128,128]{1,0:T(8,128)S(1)}, f32[128,128]{1,0:T(8,128)S(1)}, f32[128,128]{1,0:T(8,128)S(1)}, f32[8,256]{1,0:T(8,128)S(1)}, f32[256,128]{1,0:T(8,128)S(1)}) custom-call(f32[1040,128]{1,0:T(8,128)S(1)} %pad_maximum_fusion.gram_ref.terms, f32[2,256,256]{2,1,0:T(8,128)S(1)} %copy-done.2), custom_call_target="tpu_custom_call" | custom-call | flops 5000000000 | bytes 262144 | tf_op jit(solution)/shard_map/level_first/pallas_call | solution.py:314
  47.5 0.5 collective-permute-done.11
  48.1 0.1 collective-permute-start.13
  48.2 3.7 %level_second.1.inverse = f32[256,256]{1,0:T(8,128)S(1)} custom-call(f32[128,128]{1,0:T(8,128)S(1)} %get-tuple-element.83.first, f32[128,128]{1,0:T(8,128)S(1)} %get-tuple-element.84.across, f32[128,128]{1,0:T(8,128)S(1)} %get-tuple-element.85.rest, f32[8,256]{1,0:T(8,128)S(1)} %get-tuple-element.86.row, f32[256,128]{1,0:T(8,128)S(1)} %get-tuple-element.87.col), custom_call_target="tpu_custom_call" | custom-call | flops 5000000000 | bytes 262144 | tf_op jit(solution)/shard_map/level_second/pallas_call | solution.py:314
  51.8 0.0 collective-permute-done.13
  51.8 1.1 %panel_solve.1 = (f32[256,256]{1,0:T(8,128)S(1)}, f32[264,128]{1,0:T(8,128)S(1)}) custom-call(f32[256,256]{1,0:T(8,128)S(1)} %level_second.1.inverse, f32[1040,128]{1,0:T(8,128)S(1)} %pad_maximum_fusion.gram_ref.terms), custom_call_target="tpu_custom_call" | custom-call | bytes 262144 | tf_op jit(solution)/shard_map/panel_solve/pallas_call | solution.py:314
  53.0 1.6 %collective-permute-start.15 = (f32[264,128]{1,0:T(8,128)S(1)}, f32[264,128]{1,0:T(8,128)S(1)}, u32[]{:S(2)}, u32[]{:S(2)}) collective-permute-start(f32[264,128]{1,0:T(8,128)S(1)} %get-tuple-element.93), channel_id=1, source_target_pairs={{0,2},{1,3},{2,0},{3,1},{4,6},{5,7},{6,4},{7,5},{8,10},{9,11},{10,... | collective-permute-start | bytes 405512 | tf_op jit(solution)/shard_map/ppermute | solution.py:450
  54.6 0.0 copy-start.3
  54.6 2.4 %panel.1 = (f32[2048,256]{1,0:T(8,128)}, f32[256,256]{1,0:T(8,128)S(1)}, f32[512,128]{1,0:T(8,128)S(1)}) custom-call(f32[2048,256]{1,0:T(8,128)S(1)} %get-tuple-element.56.b2, f32[2048,256]{1,0:T(8,128)S(1)} %get-tuple-element.57.b1, f32[256,256]{1,0:T(8,128)S(1)} %get-tuple-element.89.x, f32[256,256]{1,0:T(8,128)S(1)} %level_second.1.inverse, ...), custom_call_target="tpu_custom_call" | custom-call | flops 1342177280 | bytes 6291456 | tf_op jit(solution)/shard_map/panel/pallas_call | solution.py:437
  57.1 0.6 collective-permute-start.14
  57.6 1.4 %collective-permute-done.15 = f32[264,128]{1,0:T(8,128)S(1)} collective-permute-done((f32[264,128]{1,0:T(8,128)S(1)}, f32[264,128]{1,0:T(8,128)S(1)}, u32[]{:S(2)}, u32[]{:S(2)}) %collective-permute-start.15) | collective-permute-done | bytes 135200 | tf_op jit(solution)/shard_map/ppermute | solution.py:450
  59.1 0.0 copy-done.3
  59.1 3.8 %root_first.1 = (f32[128,128]{1,0:T(8,128)S(1)}, f32[128,128]{1,0:T(8,128)S(1)}, f32[128,128]{1,0:T(8,128)S(1)}, f32[8,256]{1,0:T(8,128)S(1)}, f32[256,128]{1,0:T(8,128)S(1)}) custom-call(f32[264,128]{1,0:T(8,128)S(1)} %add.42.gram_ref, f32[1,256,256]{2,1,0:T(8,128)S(1)} %bitcast.1), custom_call_target="tpu_custom_call" | custom-call | flops 5000000000 | bytes 262144 | tf_op jit(solution)/shard_map/root_first/pallas_call | solution.py:314
  62.9 0.0 collective-permute-done.14
  62.9 0.1 collective-permute-start.16
  63.0 0.0 copy-start.1
  63.0 3.7 %root_second.1.inverse = f32[256,256]{1,0:T(8,128)S(1)} custom-call(f32[128,128]{1,0:T(8,128)S(1)} %get-tuple-element.100.first, f32[128,128]{1,0:T(8,128)S(1)} %get-tuple-element.101.across, f32[128,128]{1,0:T(8,128)S(1)} %get-tuple-element.102.rest, f32[8,256]{1,0:T(8,128)S(1)} %get-tuple-element.103.row, f32[256,128]{1,0:T(8,128)S(1)} %get-tuple-element.104.col), custom_call_target="tpu_custom_call" | custom-call | flops 5000000000 | bytes 262144 | tf_op jit(solution)/shard_map/root_second/pallas_call | solution.py:314
  66.7 0.0 collective-permute-done.16
  66.8 0.0 copy-done.1
  66.8 3.4 %field.1 = f32[2048,256]{1,0:T(8,128)} custom-call(f32[2048,256]{1,0:T(8,128)S(1)} %get-tuple-element.56.b2, f32[2048,256]{1,0:T(8,128)S(1)} %copy-done.1, f32[2048,256]{1,0:T(8,128)S(1)} %copy-done, f32[256,256]{1,0:T(8,128)S(1)} %root_second.1.inverse, f32[512,128]{1,0:T(8,128)S(1)} %pad_maximum_fusion.4.side, f32[256,256]{1,0:T(8,128)S(1)} %get-tuple-element.107.y), custom_call_target="tpu_custom_call" | custom-call | flops 1610612736 | bytes 6291456 | tf_op jit(solution)/shard_map/field/pallas_call | solution.py:437
  (30 shorter events, 0.6 us)
Async XLA Ops:
  0.6 5.0 %copy-start = (f32[2048,256]{1,0:T(8,128)S(1)}, f32[2048,256]{1,0:T(8,128)}, u32[]{:S(2)}) copy-start(f32[2048,256]{1,0:T(8,128)} %sources.3) | copy-start | bytes 6291460
  5.1 3.1 %collective-permute-start = (f32[520,128]{1,0:T(8,128)S(1)}, f32[520,128]{1,0:T(8,128)S(1)}, u32[]{:S(2)}, u32[]{:S(2)}) collective-permute-start(f32[520,128]{1,0:T(8,128)S(1)} %get-tuple-element.61), channel_id=1, source_target_pairs={{0,1},{1,0},{2,3},{3,2},{4,5},{5,4},{6,7},{7,6},{8,9},{9,8},{10,11... | collective-permute-start | bytes 798728 | tf_op jit(solution)/shard_map/ppermute | solution.py:450
  8.2 6.9 %collective-permute-start.2 = (f32[512,128]{1,0:T(8,128)S(1)}, f32[512,128]{1,0:T(8,128)S(1)}, u32[]{:S(2)}, u32[]{:S(2)}) collective-permute-start(f32[512,128]{1,0:T(8,128)S(1)} %get-tuple-element.64), channel_id=1, source_target_pairs={{0,1},{1,0},{2,3},{3,2},{4,5},{5,4},{6,7},{7,6},{8,9},{9,8},{10,11... | collective-permute-start | bytes 786440 | tf_op jit(solution)/shard_map/ppermute | solution.py:450
  8.4 6.8 %collective-permute-start.1 = (f32[264,128]{1,0:T(8,128)S(1)}, f32[264,128]{1,0:T(8,128)S(1)}, u32[]{:S(2)}, u32[]{:S(2)}) collective-permute-start(f32[264,128]{1,0:T(8,128)S(1)} %slice_select_fusion.1), channel_id=1, source_target_pairs={{0,4},{1,5},{2,6},{3,7},{4,0},{5,1},{6,2},{7,3},{8,12},{9,13},{10,... | collective-permute-start | bytes 405512 | tf_op jit(solution)/shard_map/ppermute | solution.py:450
  15.3 6.2 %collective-permute-start.4 = (f32[256,128]{1,0:T(8,128)S(1)}, f32[256,128]{1,0:T(8,128)S(1)}, u32[]{:S(2)}, u32[]{:S(2)}) collective-permute-start(f32[256,128]{1,0:T(8,128)S(1)} %slice_select_fusion.2), channel_id=1, source_target_pairs={{0,4},{1,5},{2,6},{3,7},{4,0},{5,1},{6,2},{7,3},{8,12},{9,13},{10,... | collective-permute-start | bytes 393224 | tf_op jit(solution)/shard_map/ppermute | solution.py:450
  17.1 4.4 %collective-permute-start.3 = (f32[136,128]{1,0:T(8,128)S(1)}, f32[136,128]{1,0:T(8,128)S(1)}, u32[]{:S(2)}, u32[]{:S(2)}) collective-permute-start(f32[136,128]{1,0:T(8,128)S(1)} %slice_select_fusion.4), channel_id=1, source_target_pairs={{0,8},{1,9},{2,10},{3,11},{4,12},{5,13},{6,14},{7,15},{8,0},{9,1},... | collective-permute-start | bytes 208904 | tf_op jit(solution)/shard_map/ppermute | solution.py:450
  21.5 7.7 %collective-permute-start.5 = (f32[136,128]{1,0:T(8,128)S(1)}, f32[136,128]{1,0:T(8,128)S(1)}, u32[]{:S(2)}, u32[]{:S(2)}) collective-permute-start(f32[136,128]{1,0:T(8,128)S(1)} %select_add_fusion.2), channel_id=1, source_target_pairs={{0,16},{1,17},{2,18},{3,19},{4,20},{5,21},{6,22},{7,23},{8,24},{9,... | collective-permute-start | bytes 208904 | tf_op jit(solution)/shard_map/ppermute | solution.py:450
  24.2 5.0 %collective-permute-start.6 = (f32[128,128]{1,0:T(8,128)S(1)}, f32[128,128]{1,0:T(8,128)S(1)}, u32[]{:S(2)}, u32[]{:S(2)}) collective-permute-start(f32[128,128]{1,0:T(8,128)S(1)} %slice_select_fusion.5), channel_id=1, source_target_pairs={{0,8},{1,9},{2,10},{3,11},{4,12},{5,13},{6,14},{7,15},{8,0},{9,1},... | collective-permute-start | bytes 196616 | tf_op jit(solution)/shard_map/ppermute | solution.py:450
  29.3 7.5 %collective-permute-start.7 = (f32[136,128]{1,0:T(8,128)S(1)}, f32[136,128]{1,0:T(8,128)S(1)}, u32[]{:S(2)}, u32[]{:S(2)}) collective-permute-start(f32[136,128]{1,0:T(8,128)S(1)} %add.39), channel_id=1, source_target_pairs={{0,8},{1,9},{2,10},{3,11},{4,12},{5,13},{6,14},{7,15},{8,0},{9,1},... | collective-permute-start | bytes 208904 | tf_op jit(solution)/shard_map/ppermute | solution.py:450
  30.9 5.8 %collective-permute-start.8 = (f32[128,128]{1,0:T(8,128)S(1)}, f32[128,128]{1,0:T(8,128)S(1)}, u32[]{:S(2)}, u32[]{:S(2)}) collective-permute-start(f32[128,128]{1,0:T(8,128)S(1)} %select_add_fusion.3), channel_id=1, source_target_pairs={{0,16},{1,17},{2,18},{3,19},{4,20},{5,21},{6,22},{7,23},{8,24},{9,... | collective-permute-start | bytes 196616 | tf_op jit(solution)/shard_map/ppermute | solution.py:450
  36.8 6.9 %copy-start.2 = (f32[2,256,256]{2,1,0:T(8,128)S(1)}, f32[2,256,256]{2,1,0:T(8,128)}, u32[]{:S(2)}) copy-start(f32[2,256,256]{2,1,0:T(8,128)} %coupling.1) | copy-start | bytes 1572868
  36.8 5.1 %collective-permute-start.9 = (f32[264,128]{1,0:T(8,128)S(1)}, f32[264,128]{1,0:T(8,128)S(1)}, u32[]{:S(2)}, u32[]{:S(2)}) collective-permute-start(f32[264,128]{1,0:T(8,128)S(1)} %pad_maximum_fusion.5), channel_id=1, source_target_pairs={{0,4},{1,5},{2,6},{3,7},{4,0},{5,1},{6,2},{7,3},{8,12},{9,13},{10,... | collective-permute-start | bytes 405512 | tf_op jit(solution)/shard_map/ppermute | solution.py:450
  37.5 4.3 %collective-permute-start.10 = (f32[128,128]{1,0:T(8,128)S(1)}, f32[128,128]{1,0:T(8,128)S(1)}, u32[]{:S(2)}, u32[]{:S(2)}) collective-permute-start(f32[128,128]{1,0:T(8,128)S(1)} %add.41), channel_id=1, source_target_pairs={{0,8},{1,9},{2,10},{3,11},{4,12},{5,13},{6,14},{7,15},{8,0},{9,1},... | collective-permute-start | bytes 196616 | tf_op jit(solution)/shard_map/ppermute | solution.py:450
  42.0 1.6 %collective-permute-start.12 = (f32[520,128]{1,0:T(8,128)S(1)}, f32[520,128]{1,0:T(8,128)S(1)}, u32[]{:S(2)}, u32[]{:S(2)}) collective-permute-start(f32[520,128]{1,0:T(8,128)S(1)} %pad_maximum_fusion.2), channel_id=1, source_target_pairs={{0,1},{1,0},{2,3},{3,2},{4,5},{5,4},{6,7},{7,6},{8,9},{9,8},{10,11... | collective-permute-start | bytes 798728 | tf_op jit(solution)/shard_map/ppermute | solution.py:450
  42.1 6.0 %collective-permute-start.11 = (f32[256,128]{1,0:T(8,128)S(1)}, f32[256,128]{1,0:T(8,128)S(1)}, u32[]{:S(2)}, u32[]{:S(2)}) collective-permute-start(f32[256,128]{1,0:T(8,128)S(1)} %pad_maximum_fusion.6), channel_id=1, source_target_pairs={{0,4},{1,5},{2,6},{3,7},{4,0},{5,1},{6,2},{7,3},{8,12},{9,13},{10,... | collective-permute-start | bytes 393224 | tf_op jit(solution)/shard_map/ppermute | solution.py:450
  48.1 3.7 %collective-permute-start.13 = (f32[512,128]{1,0:T(8,128)S(1)}, f32[512,128]{1,0:T(8,128)S(1)}, u32[]{:S(2)}, u32[]{:S(2)}) collective-permute-start(f32[512,128]{1,0:T(8,128)S(1)} %pad_maximum_fusion.3), channel_id=1, source_target_pairs={{0,1},{1,0},{2,3},{3,2},{4,5},{5,4},{6,7},{7,6},{8,9},{9,8},{10,11... | collective-permute-start | bytes 786440 | tf_op jit(solution)/shard_map/ppermute | solution.py:450
  53.0 6.0 %collective-permute-start.15 = (f32[264,128]{1,0:T(8,128)S(1)}, f32[264,128]{1,0:T(8,128)S(1)}, u32[]{:S(2)}, u32[]{:S(2)}) collective-permute-start(f32[264,128]{1,0:T(8,128)S(1)} %get-tuple-element.93), channel_id=1, source_target_pairs={{0,2},{1,3},{2,0},{3,1},{4,6},{5,7},{6,4},{7,5},{8,10},{9,11},{10,... | collective-permute-start | bytes 405512 | tf_op jit(solution)/shard_map/ppermute | solution.py:450
  54.6 4.4 %copy-start.3 = (f32[256,256]{1,0:T(8,128)S(1)}, f32[256,256]{1,0:T(8,128)}, u32[]{:S(2)}) copy-start(f32[256,256]{1,0:T(8,128)} %param.9) | copy-start | bytes 786436
  57.1 5.8 %collective-permute-start.14 = (f32[256,128]{1,0:T(8,128)S(1)}, f32[256,128]{1,0:T(8,128)S(1)}, u32[]{:S(2)}, u32[]{:S(2)}) collective-permute-start(f32[256,128]{1,0:T(8,128)S(1)} %slice_select_fusion), channel_id=1, source_target_pairs={{0,2},{1,3},{2,0},{3,1},{4,6},{5,7},{6,4},{7,5},{8,10},{9,11},{10,... | collective-permute-start | bytes 393224 | tf_op jit(solution)/shard_map/ppermute | solution.py:450
  62.9 3.8 %collective-permute-start.16 = (f32[256,128]{1,0:T(8,128)S(1)}, f32[256,128]{1,0:T(8,128)S(1)}, u32[]{:S(2)}, u32[]{:S(2)}) collective-permute-start(f32[256,128]{1,0:T(8,128)S(1)} %add.43), channel_id=1, source_target_pairs={{0,1},{1,0},{2,3},{3,2},{4,5},{5,4},{6,7},{7,6},{8,9},{9,8},{10,11... | collective-permute-start | bytes 393224 | tf_op jit(solution)/shard_map/ppermute | solution.py:450
  63.0 3.7 %copy-start.1 = (f32[2048,256]{1,0:T(8,128)S(1)}, f32[2048,256]{1,0:T(8,128)}, u32[]{:S(2)}) copy-start(f32[2048,256]{1,0:T(8,128)} %get-tuple-element.53.panel) | copy-start | bytes 6291460

commit v9 on v8

--- a/solution.py
+++ b/solution.py
@@ -393,7 +393,7 @@
     return jnp.concatenate([high, low, high], axis=0)
 
 
-def by_tiles(rows, out, stage, sems, value, beside=None):
+def by_tiles(rows, out, stage, sems, value):
     tiles = rows // TILE
 
     def copy(tile):
@@ -405,20 +405,19 @@
         return carry
 
     lax.fori_loop(0, tiles, step, 0)
-    if beside is not None:
-        beside()
     for tile in range(tiles):
         copy(tile).wait()
 
 
-def panel_kernel(b2, b1, x, inverse, terms, out, y_out, side_out, stage, sems):
-    def sources_part():
-        projected = load_square(terms, PROJECTED)
-        y_out[...] = dot_full(inverse[...], projected)
-        store_square(side_out, 0, load_square(terms, SIDE) - dot_t_full(x[...], projected))
-
+def panel_kernel(b2, b1, x, out, stage, sems):
     right = tall(x[...])
-    by_tiles(b2.shape[0], out, stage, sems, lambda at: b1[at, :] - dot(wide(b2[at, :]), right), sources_part)
+    by_tiles(b2.shape[0], out, stage, sems, lambda at: b1[at, :] - dot(wide(b2[at, :]), right))
+
+
+def source_solve_kernel(inverse, x, terms, y_out, side_out):
+    projected = load_square(terms, PROJECTED)
+    y_out[...] = dot_full(inverse[...], projected)
+    store_square(side_out, 0, load_square(terms, SIDE) - dot_t_full(x[...], projected))
 
 
 def field_kernel(b2, panel, sources, inverse, side, y, out, stage, sems):
@@ -432,12 +431,12 @@
     by_tiles(b2.shape[0], out, stage, sems, value)
 
 
-def update(kernel, args, passes, name, more=()):
+def update(kernel, args, passes, name):
     rows = args[0].shape[0]
     return pl.pallas_call(
         kernel,
-        out_specs=[pl.BlockSpec(memory_space=pl.ANY)] + [pl.BlockSpec(memory_space=pltpu.VMEM)] * len(more),
-        out_shape=[jax.ShapeDtypeStruct((rows, R), F32), *more],
+        out_specs=pl.BlockSpec(memory_space=pl.ANY),
+        out_shape=jax.ShapeDtypeStruct((rows, R), F32),
         scratch_shapes=[pltpu.VMEM((rows, R), F32), pltpu.SemaphoreType.DMA((rows // TILE,))],
         compiler_params=pltpu.CompilerParams(vmem_limit_bytes=VMEM_LIMIT),
         cost_estimate=cost(passes, rows, 3),
@@ -490,7 +489,9 @@
     places = lax.axis_size(AXES).bit_length() - 1
     flags = [(index >> bit) & 1 == 1 for bit in range(places)]
     q_two, *upper = lax.optimization_barrier((q_two, *flags))
-    stages = summing_stages(list(range(2, places)))
+    bits = list(range(2, places))
+    stages = summing_stages(bits)
+    source_left = [("gather", 0)] + summing_stages([bits[1], bits[0], *bits[2:]])[::-1]
 
     keep, send, b2, b1 = panel_gram(q_two, q_one)
     arriving = exchange(send, 1)
@@ -500,16 +501,17 @@
     panels = Chain(keep + arriving, upper)
     source = Chain(source_keep, upper)
     panels.sizes[0], source.sizes[0] = PANEL_TERMS, SOURCE_TERMS
-    source_left = [("gather", 0)] + stages[::-1]
+    source.kind, source.bit, source.flying = "sum", 0, exchange(source_send, 1)
+    down = len(bits) - 1
     for step, stage in enumerate(stages):
         panels.start(*stage)
         if step == 0:
-            source.kind, source.bit, source.flying = "sum", 0, exchange(source_send, 1)
-        else:
+            source.finish()
+        if step < down or step >= down + 2:
             source.start(*source_left.pop())
-        panels.flying, source.flying = lax.optimization_barrier((panels.flying, source.flying))
+            panels.flying, source.flying = lax.optimization_barrier((panels.flying, source.flying))
+            source.finish()
         panels.finish()
-        source.finish()
     panels.start("gather", 0)
     source.start(*source_left.pop())
     panels.finish()
@@ -519,19 +521,21 @@
     source.finish()
     source.start(*source_left.pop())
     inverse = invert_second(parts, "level_second")
-    source.flying, inverse = lax.optimization_barrier((source.flying, inverse))
-    source.finish()
-
     x, root = call(
         panel_solve_kernel, (SQUARE, jax.ShapeDtypeStruct((SYMMETRIC, LANES), F32)), (inverse, terms), "panel_solve"
     )
+    source.flying, x = lax.optimization_barrier((source.flying, x))
+    source.finish()
+    source.start(*source_left.pop())
     arriving = exchange(root, 2)
+    panel_one = update(panel_kernel, [b2, b1, x], 3, "panel")
+    arriving, source.flying, panel_one = lax.optimization_barrier((arriving, source.flying, panel_one))
+    source.finish()
     full = jax.ShapeDtypeStruct((FULL, LANES), F32)
-    panel_one, y, side = update(panel_kernel, [b2, b1, x, inverse, source.value], 5, "panel", [SQUARE, full])
+    y, side = call(source_solve_kernel, (SQUARE, full), (inverse, x, source.value), "source_solve")
     side = Chain(choose(side, upper[0])[0], upper)
     side.sizes[0] = FULL
     side_flying = exchange(side.value, 2)
-    arriving, side.value = lax.optimization_barrier((arriving, side.value))
     root = root + arriving
     parts = invert_first(no_index, root, coupling_one[None], "root_first")
     side_flying, parts = lax.optimization_barrier((side_flying, parts))
@@ -539,7 +543,7 @@
     side.start("gather", 0)
     inverse = invert_second(parts, "root_second")
     side.finish()
-    (solution,) = update(field_kernel, [b2, panel_one, sources, inverse, side.value, y], 6, "field")
+    solution = update(field_kernel, [b2, panel_one, sources, inverse, side.value, y], 6, "field")
     return (panel_one, solution)
 
 

time: 70.5 us -> 71.6 us (1.016)
  starting transfers between devices: 18.6 us -> 19.4 us
    ppermute x17, starting transfers between devices: 18.6 us -> 19.4 us  [exchange(): return lax.ppermute(x, AXES, [(i, i ^ mask) for i in range(count)])]
    pallas_call x5 -> x6, Pallas kernels: 16.1 us -> 16.7 us  [call(): pl.pallas_call(kernel, out_shape=out_shape, scratch_shapes=list(scratch),...]
  transfers between devices with their start and end apart: 17 -> 17, of which waited for: 9 -> 9; matrix products, arithmetic and copies ran while one was open for 0% -> 0% of each run, Pallas kernels for 28% -> 29%
where the time goes in v9:
time: 71.6 us; the launch traced here: 71.4 us
  Pallas kernels  29.6 us (41%)
  waiting for transfers between devices  20.6 us (29%)
  starting transfers between devices  19.4 us (27%)
  between operations  1.17 us (2%)
    ppermute x17, waiting for transfers between devices, exchange(): return lax.ppermute(x, AXES, [(i, i ^ mask) for i in range(count)])  20.6 us
    ppermute x17, starting transfers between devices, exchange(): return lax.ppermute(x, AXES, [(i, i ^ mask) for i in range(count)])  19.4 us
    pallas_call x6, Pallas kernels, call(): pl.pallas_call(kernel, out_shape=out_shape, scratch_shapes=list(scratch),...  16.7 us
    pallas_call x2, Pallas kernels, update(): pl.pallas_call(kernel, out_specs=pl.BlockSpec(memory_space=pl.ANY), out_s...  5.81 us
    pallas_call x1, Pallas kernels, panel_gram(): pl.pallas_call(panel_gram_kernel, in_specs=[pl.BlockSpec(memory_space=pl....  4.48 us
    pallas_call x1, Pallas kernels, source_gram(): pl.pallas_call(source_gram_kernel, out_shape=(part, part), scratch_shapes...  2.58 us
  transfers between devices with their start and end apart: 17, of which 9 were waited for; matrix products, arithmetic and copies ran while one was open for 0% of the time, Pallas kernels for 29%

profile of v9, /device:TPU:0, one launch (start us, length us, event | category | flops | bytes accessed | tf_op | source)
XLA Modules:
  0.0 71.4 jit_solution(17559850379203091580)
XLA Ops:
  0.6 0.0 copy-start
  0.6 4.5 %panel_gram.1 = (f32[520,128]{1,0:T(8,128)S(1)}, f32[520,128]{1,0:T(8,128)S(1)}, f32[2048,256]{1,0:T(8,128)S(1)}, f32[2048,256]{1,0:T(8,128)S(1)}) custom-call(f32[2048,256]{1,0:T(8,128)} %q_two, f32[2048,256]{1,0:T(8,128)} %q_one.1), custom_call_target="tpu_custom_call" | custom-call | flops 1879048192 | bytes 4194304 | tf_op jit(solution)/shard_map/panel_gram/pallas_call | solution.py:169
  5.1 0.5 collective-permute-start
  5.6 0.0 copy-done
  5.7 2.6 %source_gram.1 = (f32[512,128]{1,0:T(8,128)S(1)}, f32[512,128]{1,0:T(8,128)S(1)}) custom-call(f32[2048,256]{1,0:T(8,128)S(1)} %get-tuple-element.54.b2, f32[2048,256]{1,0:T(8,128)S(1)} %get-tuple-element.55.b1, f32[2048,256]{1,0:T(8,128)S(1)} %copy-done), custom_call_target="tpu_custom_call" | custom-call | flops 1610612736 | bytes 6291456 | tf_op jit(solution)/shard_map/source_gram/pallas_call | solution.py:186
  8.2 0.0 collective-permute-done
  8.2 0.1 collective-permute-start.1
  8.4 3.0 %collective-permute-start.2 = (f32[264,128]{1,0:T(8,128)S(1)}, f32[264,128]{1,0:T(8,128)S(1)}, u32[]{:S(2)}, u32[]{:S(2)}) collective-permute-start(f32[264,128]{1,0:T(8,128)S(1)} %slice_select_fusion.1), channel_id=1, source_target_pairs={{0,4},{1,5},{2,6},{3,7},{4,0},{5,1},{6,2},{7,3},{8,12},{9,13},{10,... | collective-permute-start | bytes 405512 | tf_op jit(solution)/shard_map/ppermute | solution.py:449
  11.4 0.0 collective-permute-done.1
  11.5 1.7 %collective-permute-start.3 = (f32[256,128]{1,0:T(8,128)S(1)}, f32[256,128]{1,0:T(8,128)S(1)}, u32[]{:S(2)}, u32[]{:S(2)}) collective-permute-start(f32[256,128]{1,0:T(8,128)S(1)} %slice_select_fusion.2), channel_id=1, source_target_pairs={{0,8},{1,9},{2,10},{3,11},{4,12},{5,13},{6,14},{7,15},{8,0},{9,1},... | collective-permute-start | bytes 393224 | tf_op jit(solution)/shard_map/ppermute | solution.py:449
  13.1 2.0 %collective-permute-done.2 = f32[264,128]{1,0:T(8,128)S(1)} collective-permute-done((f32[264,128]{1,0:T(8,128)S(1)}, f32[264,128]{1,0:T(8,128)S(1)}, u32[]{:S(2)}, u32[]{:S(2)}) %collective-permute-start.2) | collective-permute-done | bytes 135200 | tf_op jit(solution)/shard_map/ppermute | solution.py:449
  15.2 1.5 %collective-permute-done.3 = f32[256,128]{1,0:T(8,128)S(1)} collective-permute-done((f32[256,128]{1,0:T(8,128)S(1)}, f32[256,128]{1,0:T(8,128)S(1)}, u32[]{:S(2)}, u32[]{:S(2)}) %collective-permute-start.3) | collective-permute-done | bytes 131104 | tf_op jit(solution)/shard_map/ppermute | solution.py:449
  16.8 1.8 %collective-permute-start.4 = (f32[136,128]{1,0:T(8,128)S(1)}, f32[136,128]{1,0:T(8,128)S(1)}, u32[]{:S(2)}, u32[]{:S(2)}) collective-permute-start(f32[136,128]{1,0:T(8,128)S(1)} %slice_select_fusion.4), channel_id=1, source_target_pairs={{0,8},{1,9},{2,10},{3,11},{4,12},{5,13},{6,14},{7,15},{8,0},{9,1},... | collective-permute-start | bytes 208904 | tf_op jit(solution)/shard_map/ppermute | solution.py:449
  18.6 1.5 %collective-permute-start.5 = (f32[128,128]{1,0:T(8,128)S(1)}, f32[128,128]{1,0:T(8,128)S(1)}, u32[]{:S(2)}, u32[]{:S(2)}) collective-permute-start(f32[128,128]{1,0:T(8,128)S(1)} %slice_select_fusion.5), channel_id=1, source_target_pairs={{0,4},{1,5},{2,6},{3,7},{4,0},{5,1},{6,2},{7,3},{8,12},{9,13},{10,... | collective-permute-start | bytes 196616 | tf_op jit(solution)/shard_map/ppermute | solution.py:449
  20.2 2.8 %collective-permute-done.5 = f32[128,128]{1,0:T(8,128)S(1)} collective-permute-done((f32[128,128]{1,0:T(8,128)S(1)}, f32[128,128]{1,0:T(8,128)S(1)}, u32[]{:S(2)}, u32[]{:S(2)}) %collective-permute-start.5) | collective-permute-done | bytes 65568 | tf_op jit(solution)/shard_map/ppermute | solution.py:449
  22.9 0.0 collective-permute-done.4
  23.0 2.7 %collective-permute-start.6 = (f32[136,128]{1,0:T(8,128)S(1)}, f32[136,128]{1,0:T(8,128)S(1)}, u32[]{:S(2)}, u32[]{:S(2)}) collective-permute-start(f32[136,128]{1,0:T(8,128)S(1)} %select_add_fusion.2), channel_id=1, source_target_pairs={{0,16},{1,17},{2,18},{3,19},{4,20},{5,21},{6,22},{7,23},{8,24},{9,... | collective-permute-start | bytes 208904 | tf_op jit(solution)/shard_map/ppermute | solution.py:449
  25.6 3.1 %collective-permute-done.6 = f32[136,128]{1,0:T(8,128)S(1)} collective-permute-done((f32[136,128]{1,0:T(8,128)S(1)}, f32[136,128]{1,0:T(8,128)S(1)}, u32[]{:S(2)}, u32[]{:S(2)}) %collective-permute-start.6) | collective-permute-done | bytes 69664 | tf_op jit(solution)/shard_map/ppermute | solution.py:449
  28.8 0.1 collective-permute-start.7
  28.9 4.3 %collective-permute-done.7 = f32[136,128]{1,0:T(8,128)S(1)} collective-permute-done((f32[136,128]{1,0:T(8,128)S(1)}, f32[136,128]{1,0:T(8,128)S(1)}, u32[]{:S(2)}, u32[]{:S(2)}) %collective-permute-start.7) | collective-permute-done | bytes 69664 | tf_op jit(solution)/shard_map/ppermute | solution.py:449
  33.2 0.0 copy-start.2
  33.2 1.7 %collective-permute-start.8 = (f32[264,128]{1,0:T(8,128)S(1)}, f32[264,128]{1,0:T(8,128)S(1)}, u32[]{:S(2)}, u32[]{:S(2)}) collective-permute-start(f32[264,128]{1,0:T(8,128)S(1)} %pad_maximum_fusion.5), channel_id=1, source_target_pairs={{0,4},{1,5},{2,6},{3,7},{4,0},{5,1},{6,2},{7,3},{8,12},{9,13},{10,... | collective-permute-start | bytes 405512 | tf_op jit(solution)/shard_map/ppermute | solution.py:449
  34.9 2.4 %collective-permute-start.9 = (f32[128,128]{1,0:T(8,128)S(1)}, f32[128,128]{1,0:T(8,128)S(1)}, u32[]{:S(2)}, u32[]{:S(2)}) collective-permute-start(f32[128,128]{1,0:T(8,128)S(1)} %select_add_fusion.3), channel_id=1, source_target_pairs={{0,16},{1,17},{2,18},{3,19},{4,20},{5,21},{6,22},{7,23},{8,24},{9,... | collective-permute-start | bytes 196616 | tf_op jit(solution)/shard_map/ppermute | solution.py:449
  37.3 3.0 %collective-permute-done.9 = f32[128,128]{1,0:T(8,128)S(1)} collective-permute-done((f32[128,128]{1,0:T(8,128)S(1)}, f32[128,128]{1,0:T(8,128)S(1)}, u32[]{:S(2)}, u32[]{:S(2)}) %collective-permute-start.9) | collective-permute-done | bytes 65568 | tf_op jit(solution)/shard_map/ppermute | solution.py:449
  40.3 0.0 collective-permute-done.8
  40.4 0.1 collective-permute-start.11
  40.5 0.5 collective-permute-start.10
  40.9 1.0 %collective-permute-done.11 = f32[520,128]{1,0:T(8,128)S(1)} collective-permute-done((f32[520,128]{1,0:T(8,128)S(1)}, f32[520,128]{1,0:T(8,128)S(1)}, u32[]{:S(2)}, u32[]{:S(2)}) %collective-permute-start.11) | collective-permute-done | bytes 266272 | tf_op jit(solution)/shard_map/ppermute | solution.py:449
  42.0 0.1 broadcast_select_fusion.1
  42.1 0.0 copy-done.2
  42.1 3.8 %level_first.1 = (f32[128,128]{1,0:T(8,128)S(1)}, f32[128,128]{1,0:T(8,128)S(1)}, f32[128,128]{1,0:T(8,128)S(1)}, f32[8,256]{1,0:T(8,128)S(1)}, f32[256,128]{1,0:T(8,128)S(1)}) custom-call(f32[1040,128]{1,0:T(8,128)S(1)} %pad_maximum_fusion.gram_ref.terms, f32[2,256,256]{2,1,0:T(8,128)S(1)} %copy-done.2), custom_call_target="tpu_custom_call" | custom-call | flops 5000000000 | bytes 262144 | tf_op jit(solution)/shard_map/level_first/pallas_call | solution.py:314
  45.9 0.0 collective-permute-done.10
  46.0 0.1 collective-permute-start.13
  46.0 3.7 %level_second.1.inverse = f32[256,256]{1,0:T(8,128)S(1)} custom-call(f32[128,128]{1,0:T(8,128)S(1)} %get-tuple-element.74.first, f32[128,128]{1,0:T(8,128)S(1)} %get-tuple-element.75.across, f32[128,128]{1,0:T(8,128)S(1)} %get-tuple-element.76.rest, f32[8,256]{1,0:T(8,128)S(1)} %get-tuple-element.77.row, f32[256,128]{1,0:T(8,128)S(1)} %get-tuple-element.78.col), custom_call_target="tpu_custom_call" | custom-call | flops 5000000000 | bytes 262144 | tf_op jit(solution)/shard_map/level_second/pallas_call | solution.py:314
  49.7 1.1 %panel_solve.1 = (f32[256,256]{1,0:T(8,128)S(1)}, f32[264,128]{1,0:T(8,128)S(1)}) custom-call(f32[256,256]{1,0:T(8,128)S(1)} %level_second.1.inverse, f32[1040,128]{1,0:T(8,128)S(1)} %pad_maximum_fusion.gram_ref.terms), custom_call_target="tpu_custom_call" | custom-call | bytes 262144 | tf_op jit(solution)/shard_map/panel_solve/pallas_call | solution.py:314
  50.8 0.8 %collective-permute-done.13 = f32[256,128]{1,0:T(8,128)S(1)} collective-permute-done((f32[256,128]{1,0:T(8,128)S(1)}, f32[256,128]{1,0:T(8,128)S(1)}, u32[]{:S(2)}, u32[]{:S(2)}) %collective-permute-start.13) | collective-permute-done | bytes 131104 | tf_op jit(solution)/shard_map/ppermute | solution.py:449
  51.6 0.1 collective-permute-start.14
  51.7 1.6 %collective-permute-start.12 = (f32[264,128]{1,0:T(8,128)S(1)}, f32[264,128]{1,0:T(8,128)S(1)}, u32[]{:S(2)}, u32[]{:S(2)}) collective-permute-start(f32[264,128]{1,0:T(8,128)S(1)} %get-tuple-element.79), channel_id=1, source_target_pairs={{0,2},{1,3},{2,0},{3,1},{4,6},{5,7},{6,4},{7,5},{8,10},{9,11},{10,... | collective-permute-start | bytes 405512 | tf_op jit(solution)/shard_map/ppermute | solution.py:449
  53.3 2.4 %panel.1 = f32[2048,256]{1,0:T(8,128)} custom-call(f32[2048,256]{1,0:T(8,128)S(1)} %get-tuple-element.54.b2, f32[2048,256]{1,0:T(8,128)S(1)} %get-tuple-element.55.b1, f32[256,256]{1,0:T(8,128)S(1)} %get-tuple-element.83.x), custom_call_target="tpu_custom_call" | custom-call | flops 805306368 | bytes 6291456 | tf_op jit(solution)/shard_map/panel/pallas_call | solution.py:436
  55.7 0.0 copy-start.3
  55.7 2.0 %collective-permute-done.12 = f32[264,128]{1,0:T(8,128)S(1)} collective-permute-done((f32[264,128]{1,0:T(8,128)S(1)}, f32[264,128]{1,0:T(8,128)S(1)}, u32[]{:S(2)}, u32[]{:S(2)}) %collective-permute-start.12) | collective-permute-done | bytes 135200 | tf_op jit(solution)/shard_map/ppermute | solution.py:449
  57.7 0.0 collective-permute-done.14
  57.8 0.6 source_solve.1
  58.5 1.6 %collective-permute-start.15 = (f32[256,128]{1,0:T(8,128)S(1)}, f32[256,128]{1,0:T(8,128)S(1)}, u32[]{:S(2)}, u32[]{:S(2)}) collective-permute-start(f32[256,128]{1,0:T(8,128)S(1)} %slice_select_fusion), channel_id=1, source_target_pairs={{0,2},{1,3},{2,0},{3,1},{4,6},{5,7},{6,4},{7,5},{8,10},{9,11},{10,... | collective-permute-start | bytes 393224 | tf_op jit(solution)/shard_map/ppermute | solution.py:449
  60.1 0.0 copy-done.3
  60.1 3.8 %root_first.1 = (f32[128,128]{1,0:T(8,128)S(1)}, f32[128,128]{1,0:T(8,128)S(1)}, f32[128,128]{1,0:T(8,128)S(1)}, f32[8,256]{1,0:T(8,128)S(1)}, f32[256,128]{1,0:T(8,128)S(1)}) custom-call(f32[264,128]{1,0:T(8,128)S(1)} %add.42.gram_ref, f32[1,256,256]{2,1,0:T(8,128)S(1)} %bitcast.1), custom_call_target="tpu_custom_call" | custom-call | flops 5000000000 | bytes 262144 | tf_op jit(solution)/shard_map/root_first/pallas_call | solution.py:314
  63.9 0.0 collective-permute-done.15
  64.0 0.1 collective-permute-start.16
  64.0 0.0 copy-start.1
  64.1 3.7 %root_second.1.inverse = f32[256,256]{1,0:T(8,128)S(1)} custom-call(f32[128,128]{1,0:T(8,128)S(1)} %get-tuple-element.93.first, f32[128,128]{1,0:T(8,128)S(1)} %get-tuple-element.94.across, f32[128,128]{1,0:T(8,128)S(1)} %get-tuple-element.95.rest, f32[8,256]{1,0:T(8,128)S(1)} %get-tuple-element.96.row, f32[256,128]{1,0:T(8,128)S(1)} %get-tuple-element.97.col), custom_call_target="tpu_custom_call" | custom-call | flops 5000000000 | bytes 262144 | tf_op jit(solution)/shard_map/root_second/pallas_call | solution.py:314
  67.7 0.0 collective-permute-done.16
  67.8 0.0 copy-done.1
  67.8 3.4 %field.1 = f32[2048,256]{1,0:T(8,128)} custom-call(f32[2048,256]{1,0:T(8,128)S(1)} %get-tuple-element.54.b2, f32[2048,256]{1,0:T(8,128)S(1)} %copy-done.1, f32[2048,256]{1,0:T(8,128)S(1)} %copy-done, f32[256,256]{1,0:T(8,128)S(1)} %root_second.1.inverse, f32[512,128]{1,0:T(8,128)S(1)} %pad_maximum_fusion.4.side, f32[256,256]{1,0:T(8,128)S(1)} %get-tuple-element.99.y), custom_call_target="tpu_custom_call" | custom-call | flops 1610612736 | bytes 6291456 | tf_op jit(solution)/shard_map/field/pallas_call | solution.py:436
  (30 shorter events, 0.6 us)
Async XLA Ops:
  0.6 5.0 %copy-start = (f32[2048,256]{1,0:T(8,128)S(1)}, f32[2048,256]{1,0:T(8,128)}, u32[]{:S(2)}) copy-start(f32[2048,256]{1,0:T(8,128)} %sources.3) | copy-start | bytes 6291460
  5.1 3.1 %collective-permute-start = (f32[520,128]{1,0:T(8,128)S(1)}, f32[520,128]{1,0:T(8,128)S(1)}, u32[]{:S(2)}, u32[]{:S(2)}) collective-permute-start(f32[520,128]{1,0:T(8,128)S(1)} %get-tuple-element.57), channel_id=1, source_target_pairs={{0,1},{1,0},{2,3},{3,2},{4,5},{5,4},{6,7},{7,6},{8,9},{9,8},{10,11... | collective-permute-start | bytes 798728 | tf_op jit(solution)/shard_map/ppermute | solution.py:449
  8.2 3.2 %collective-permute-start.1 = (f32[512,128]{1,0:T(8,128)S(1)}, f32[512,128]{1,0:T(8,128)S(1)}, u32[]{:S(2)}, u32[]{:S(2)}) collective-permute-start(f32[512,128]{1,0:T(8,128)S(1)} %get-tuple-element.59), channel_id=1, source_target_pairs={{0,1},{1,0},{2,3},{3,2},{4,5},{5,4},{6,7},{7,6},{8,9},{9,8},{10,11... | collective-permute-start | bytes 786440 | tf_op jit(solution)/shard_map/ppermute | solution.py:449
  8.4 6.8 %collective-permute-start.2 = (f32[264,128]{1,0:T(8,128)S(1)}, f32[264,128]{1,0:T(8,128)S(1)}, u32[]{:S(2)}, u32[]{:S(2)}) collective-permute-start(f32[264,128]{1,0:T(8,128)S(1)} %slice_select_fusion.1), channel_id=1, source_target_pairs={{0,4},{1,5},{2,6},{3,7},{4,0},{5,1},{6,2},{7,3},{8,12},{9,13},{10,... | collective-permute-start | bytes 405512 | tf_op jit(solution)/shard_map/ppermute | solution.py:449
  11.5 5.2 %collective-permute-start.3 = (f32[256,128]{1,0:T(8,128)S(1)}, f32[256,128]{1,0:T(8,128)S(1)}, u32[]{:S(2)}, u32[]{:S(2)}) collective-permute-start(f32[256,128]{1,0:T(8,128)S(1)} %slice_select_fusion.2), channel_id=1, source_target_pairs={{0,8},{1,9},{2,10},{3,11},{4,12},{5,13},{6,14},{7,15},{8,0},{9,1},... | collective-permute-start | bytes 393224 | tf_op jit(solution)/shard_map/ppermute | solution.py:449
  16.8 6.2 %collective-permute-start.4 = (f32[136,128]{1,0:T(8,128)S(1)}, f32[136,128]{1,0:T(8,128)S(1)}, u32[]{:S(2)}, u32[]{:S(2)}) collective-permute-start(f32[136,128]{1,0:T(8,128)S(1)} %slice_select_fusion.4), channel_id=1, source_target_pairs={{0,8},{1,9},{2,10},{3,11},{4,12},{5,13},{6,14},{7,15},{8,0},{9,1},... | collective-permute-start | bytes 208904 | tf_op jit(solution)/shard_map/ppermute | solution.py:449
  18.6 4.3 %collective-permute-start.5 = (f32[128,128]{1,0:T(8,128)S(1)}, f32[128,128]{1,0:T(8,128)S(1)}, u32[]{:S(2)}, u32[]{:S(2)}) collective-permute-start(f32[128,128]{1,0:T(8,128)S(1)} %slice_select_fusion.5), channel_id=1, source_target_pairs={{0,4},{1,5},{2,6},{3,7},{4,0},{5,1},{6,2},{7,3},{8,12},{9,13},{10,... | collective-permute-start | bytes 196616 | tf_op jit(solution)/shard_map/ppermute | solution.py:449
  23.0 5.8 %collective-permute-start.6 = (f32[136,128]{1,0:T(8,128)S(1)}, f32[136,128]{1,0:T(8,128)S(1)}, u32[]{:S(2)}, u32[]{:S(2)}) collective-permute-start(f32[136,128]{1,0:T(8,128)S(1)} %select_add_fusion.2), channel_id=1, source_target_pairs={{0,16},{1,17},{2,18},{3,19},{4,20},{5,21},{6,22},{7,23},{8,24},{9,... | collective-permute-start | bytes 208904 | tf_op jit(solution)/shard_map/ppermute | solution.py:449
  28.8 4.4 %collective-permute-start.7 = (f32[136,128]{1,0:T(8,128)S(1)}, f32[136,128]{1,0:T(8,128)S(1)}, u32[]{:S(2)}, u32[]{:S(2)}) collective-permute-start(f32[136,128]{1,0:T(8,128)S(1)} %add.40), channel_id=1, source_target_pairs={{0,8},{1,9},{2,10},{3,11},{4,12},{5,13},{6,14},{7,15},{8,0},{9,1},... | collective-permute-start | bytes 208904 | tf_op jit(solution)/shard_map/ppermute | solution.py:449
  33.2 8.9 %copy-start.2 = (f32[2,256,256]{2,1,0:T(8,128)S(1)}, f32[2,256,256]{2,1,0:T(8,128)}, u32[]{:S(2)}) copy-start(f32[2,256,256]{2,1,0:T(8,128)} %coupling.1) | copy-start | bytes 1572868
  33.2 7.1 %collective-permute-start.8 = (f32[264,128]{1,0:T(8,128)S(1)}, f32[264,128]{1,0:T(8,128)S(1)}, u32[]{:S(2)}, u32[]{:S(2)}) collective-permute-start(f32[264,128]{1,0:T(8,128)S(1)} %pad_maximum_fusion.5), channel_id=1, source_target_pairs={{0,4},{1,5},{2,6},{3,7},{4,0},{5,1},{6,2},{7,3},{8,12},{9,13},{10,... | collective-permute-start | bytes 405512 | tf_op jit(solution)/shard_map/ppermute | solution.py:449
  34.9 5.4 %collective-permute-start.9 = (f32[128,128]{1,0:T(8,128)S(1)}, f32[128,128]{1,0:T(8,128)S(1)}, u32[]{:S(2)}, u32[]{:S(2)}) collective-permute-start(f32[128,128]{1,0:T(8,128)S(1)} %select_add_fusion.3), channel_id=1, source_target_pairs={{0,16},{1,17},{2,18},{3,19},{4,20},{5,21},{6,22},{7,23},{8,24},{9,... | collective-permute-start | bytes 196616 | tf_op jit(solution)/shard_map/ppermute | solution.py:449
  40.4 1.6 %collective-permute-start.11 = (f32[520,128]{1,0:T(8,128)S(1)}, f32[520,128]{1,0:T(8,128)S(1)}, u32[]{:S(2)}, u32[]{:S(2)}) collective-permute-start(f32[520,128]{1,0:T(8,128)S(1)} %pad_maximum_fusion.2), channel_id=1, source_target_pairs={{0,1},{1,0},{2,3},{3,2},{4,5},{5,4},{6,7},{7,6},{8,9},{9,8},{10,11... | collective-permute-start | bytes 798728 | tf_op jit(solution)/shard_map/ppermute | solution.py:449
  40.5 5.5 %collective-permute-start.10 = (f32[128,128]{1,0:T(8,128)S(1)}, f32[128,128]{1,0:T(8,128)S(1)}, u32[]{:S(2)}, u32[]{:S(2)}) collective-permute-start(f32[128,128]{1,0:T(8,128)S(1)} %add.41), channel_id=1, source_target_pairs={{0,4},{1,5},{2,6},{3,7},{4,0},{5,1},{6,2},{7,3},{8,12},{9,13},{10,... | collective-permute-start | bytes 196616 | tf_op jit(solution)/shard_map/ppermute | solution.py:449
  46.0 5.6 %collective-permute-start.13 = (f32[256,128]{1,0:T(8,128)S(1)}, f32[256,128]{1,0:T(8,128)S(1)}, u32[]{:S(2)}, u32[]{:S(2)}) collective-permute-start(f32[256,128]{1,0:T(8,128)S(1)} %pad_maximum_fusion.6), channel_id=1, source_target_pairs={{0,8},{1,9},{2,10},{3,11},{4,12},{5,13},{6,14},{7,15},{8,0},{9,1},... | collective-permute-start | bytes 393224 | tf_op jit(solution)/shard_map/ppermute | solution.py:449
  51.6 6.1 %collective-permute-start.14 = (f32[512,128]{1,0:T(8,128)S(1)}, f32[512,128]{1,0:T(8,128)S(1)}, u32[]{:S(2)}, u32[]{:S(2)}) collective-permute-start(f32[512,128]{1,0:T(8,128)S(1)} %pad_maximum_fusion.3), channel_id=1, source_target_pairs={{0,1},{1,0},{2,3},{3,2},{4,5},{5,4},{6,7},{7,6},{8,9},{9,8},{10,11... | collective-permute-start | bytes 786440 | tf_op jit(solution)/shard_map/ppermute | solution.py:449
  51.7 6.0 %collective-permute-start.12 = (f32[264,128]{1,0:T(8,128)S(1)}, f32[264,128]{1,0:T(8,128)S(1)}, u32[]{:S(2)}, u32[]{:S(2)}) collective-permute-start(f32[264,128]{1,0:T(8,128)S(1)} %get-tuple-element.79), channel_id=1, source_target_pairs={{0,2},{1,3},{2,0},{3,1},{4,6},{5,7},{6,4},{7,5},{8,10},{9,11},{10,... | collective-permute-start | bytes 405512 | tf_op jit(solution)/shard_map/ppermute | solution.py:449
  55.7 4.4 %copy-start.3 = (f32[256,256]{1,0:T(8,128)S(1)}, f32[256,256]{1,0:T(8,128)}, u32[]{:S(2)}) copy-start(f32[256,256]{1,0:T(8,128)} %param.9) | copy-start | bytes 786436
  58.5 5.4 %collective-permute-start.15 = (f32[256,128]{1,0:T(8,128)S(1)}, f32[256,128]{1,0:T(8,128)S(1)}, u32[]{:S(2)}, u32[]{:S(2)}) collective-permute-start(f32[256,128]{1,0:T(8,128)S(1)} %slice_select_fusion), channel_id=1, source_target_pairs={{0,2},{1,3},{2,0},{3,1},{4,6},{5,7},{6,4},{7,5},{8,10},{9,11},{10,... | collective-permute-start | bytes 393224 | tf_op jit(solution)/shard_map/ppermute | solution.py:449
  64.0 3.8 %collective-permute-start.16 = (f32[256,128]{1,0:T(8,128)S(1)}, f32[256,128]{1,0:T(8,128)S(1)}, u32[]{:S(2)}, u32[]{:S(2)}) collective-permute-start(f32[256,128]{1,0:T(8,128)S(1)} %fusion.2), channel_id=1, source_target_pairs={{0,1},{1,0},{2,3},{3,2},{4,5},{5,4},{6,7},{7,6},{8,9},{9,8},{10,11... | collective-permute-start | bytes 393224 | tf_op jit(solution)/shard_map/ppermute | solution.py:449
  64.0 3.7 %copy-start.1 = (f32[2048,256]{1,0:T(8,128)S(1)}, f32[2048,256]{1,0:T(8,128)}, u32[]{:S(2)}) copy-start(f32[2048,256]{1,0:T(8,128)} %panel.1) | copy-start | bytes 6291460

commit v10 on v8

--- a/solution.py
+++ b/solution.py
@@ -14,6 +14,7 @@
 R = 256
 LANES = 128
 TILE = 512
+GROUPS = 8
 VMEM_LIMIT = 16 * 1024 * 1024
 SYMMETRIC, FULL = 264, 512
 OWN, ROOT, CROSS, PANEL_TERMS = 0, 264, 528, 1040
@@ -105,21 +106,27 @@
     tiles = b2.shape[0] // TILE
     pairs = ((q_two, b2), (q_one, b1))
 
-    def copy(tile, which):
-        source, target = pairs[which]
-        here = tile_at(tile)
-        return pltpu.make_async_copy(source.at[here], target.at[here], sems.at[which, tile])
-
-    for tile in range(tiles):
-        for which in range(2):
-            copy(tile, which).start()
+    def copies(at, sem):
+        return [
+            pltpu.make_async_copy(source.at[at], target.at[at], sems.at[which, sem])
+            for which, (source, target) in enumerate(pairs)
+        ]
+
+    small = TILE // 2
+    parts = (pl.ds(0, small), pl.ds(small, small))
+    for sem, at in enumerate(parts):
+        for copy in copies(at, sem):
+            copy.start()
+    for tile in range(1, tiles):
+        for copy in copies(tile_at(tile), tile + 1):
+            copy.start()
     acc[...] = jnp.zeros_like(acc)
 
-    def step(tile, carry):
-        for which in range(2):
-            copy(tile, which).wait()
-        h2, l2 = split2(b2[tile_at(tile), :])
-        h1, l1 = split2(b1[tile_at(tile), :])
+    def add_rows(at, sem):
+        for copy in copies(at, sem):
+            copy.wait()
+        h2, l2 = split2(b2[at, :])
+        h1, l1 = split2(b1[at, :])
         h2t, l2t, h1t = h2.T, l2.T, h1.T
         acc[0] += dot(h2t, h2)
         acc[1] += dot(h2t, l2)
@@ -127,9 +134,14 @@
         acc[2] += dot(left, jnp.concatenate([h1, l1, h1], axis=0))
         acc[3] += dot(h1t, h1)
         acc[4] += dot(h1t, l1)
+
+    def step(tile, carry):
+        add_rows(tile_at(tile), tile + 1)
         return carry
 
-    lax.fori_loop(0, tiles, step, 0)
+    for sem, at in enumerate(parts):
+        add_rows(at, sem)
+    lax.fori_loop(1, tiles, step, 0)
     low = acc[1]
     store_symmetric(packed, OWN, acc[0] + low + low.T)
     low = acc[4]
@@ -173,7 +185,7 @@
         scratch_shapes=[
             pltpu.VMEM((5, R, R), F32),
             pltpu.VMEM((PANEL_TERMS, LANES), F32),
-            pltpu.SemaphoreType.DMA((2, rows // TILE)),
+            pltpu.SemaphoreType.DMA((2, rows // TILE + 1)),
         ],
         compiler_params=pltpu.CompilerParams(vmem_limit_bytes=VMEM_LIMIT),
         cost_estimate=cost(7, rows, 2),
@@ -200,16 +212,16 @@
 def eliminate(block, cols, rows):
     count = len(block)
     lane = lax.broadcasted_iota(jnp.int32, (8, LANES), 1)
-    for start in range(0, count, 4):
-        panel = block[start : start + 4]
+    for start in range(0, count, GROUPS):
+        panel = block[start : start + GROUPS]
         left = stack_left(jnp.concatenate(panel, axis=0))
-        for t in range(4):
+        for t in range(GROUPS):
             panel = eliminate_group(panel, t, start + t, cols, rows)
-        inside = (lane >= 8 * start) & (lane < 8 * start + 32)
+        inside = (lane >= 8 * start) & (lane < 8 * (start + GROUPS))
         panel = [jnp.where(inside, -x, x) for x in panel]
         change = dot_t(left, stack_right(jnp.concatenate(panel, axis=0)))
         for g in range(count):
-            if start <= g < start + 4:
+            if start <= g < start + GROUPS:
                 block[g] = panel[g - start]
             else:
                 block[g] = jnp.where(inside, 0.0, block[g]) - change[8 * g : 8 * g + 8, :]
@@ -233,11 +245,11 @@
         row = jnp.broadcast_to(rows[8 * at + j : 8 * at + j + 1, :], (8, LANES))
         line.append(jnp.where(inside, jnp.where(lane == 8 * at + j, 1.0, 0.0), row))
     after = None
-    if t < 3:
+    if t < GROUPS - 1:
         columns = [spread_lane(panel[t + 1], 8 * at + j) for j in range(8)]
         after = [columns, jnp.where(inside, 0.0, panel[t + 1])]
     line, after = solve_small(entry, line, after)
-    for g in range(4):
+    for g in range(GROUPS):
         if g == t + 1:
             panel[g] = after
         elif g != t:
@@ -411,25 +423,30 @@
         copy(tile).wait()
 
 
-def panel_kernel(b2, b1, x, inverse, terms, out, y_out, side_out, stage, sems):
-    def sources_part():
-        projected = load_square(terms, PROJECTED)
-        y_out[...] = dot_full(inverse[...], projected)
-        store_square(side_out, 0, load_square(terms, SIDE) - dot_t_full(x[...], projected))
-
-    right = tall(x[...])
-    by_tiles(b2.shape[0], out, stage, sems, lambda at: b1[at, :] - dot(wide(b2[at, :]), right), sources_part)
-
-
-def field_kernel(b2, panel, sources, inverse, side, y, out, stage, sems):
-    weights = dot(wide(inverse[...]), tall(load_square(side, 0)))
-    right = jnp.concatenate([tall(y[...]), tall(weights)], axis=0)
+def panel_kernel(b2, b1, sources, x, inverse, terms, out, level, high, low, side_out, stage, sems):
+    projected = load_square(terms, PROJECTED)
+    y = dot_full(inverse[...], projected)
+    store_square(side_out, 0, load_square(terms, SIDE) - dot_t_full(x[...], projected))
+    right = jnp.concatenate([tall(x[...]), tall(y)], axis=1)
 
     def value(at):
-        left = jnp.concatenate([wide(b2[at, :]), wide(panel[at, :])], axis=1)
-        return sources[at, :] - dot(left, right)
+        change = dot(wide(b2[at, :]), right)
+        panel = b1[at, :] - change[:, :R]
+        level[at, :] = sources[at, :] - change[:, R:]
+        high[at, :], low[at, :] = split2(panel)
+        return panel
 
     by_tiles(b2.shape[0], out, stage, sems, value)
+
+
+def field_kernel(level, high, low, inverse, side, out, stage, sems):
+    weights = tall(dot(wide(inverse[...]), tall(load_square(side, 0))))
+
+    def value(at):
+        left = jnp.concatenate([high[at, :], high[at, :], low[at, :]], axis=1)
+        return level[at, :] - dot(left, weights)
+
+    by_tiles(level.shape[0], out, stage, sems, value)
 
 
 def update(kernel, args, passes, name, more=()):
@@ -526,8 +543,11 @@
         panel_solve_kernel, (SQUARE, jax.ShapeDtypeStruct((SYMMETRIC, LANES), F32)), (inverse, terms), "panel_solve"
     )
     arriving = exchange(root, 2)
-    full = jax.ShapeDtypeStruct((FULL, LANES), F32)
-    panel_one, y, side = update(panel_kernel, [b2, b1, x, inverse, source.value], 5, "panel", [SQUARE, full])
+    rows = b2.shape[0]
+    shapes = [jax.ShapeDtypeStruct((rows, R), kind) for kind in (F32, BF16, BF16)]
+    shapes.append(jax.ShapeDtypeStruct((FULL, LANES), F32))
+    args = [b2, b1, sources, x, inverse, source.value]
+    panel_one, level, high, low, side = update(panel_kernel, args, 8, "panel", shapes)
     side = Chain(choose(side, upper[0])[0], upper)
     side.sizes[0] = FULL
     side_flying = exchange(side.value, 2)
@@ -539,7 +559,7 @@
     side.start("gather", 0)
     inverse = invert_second(parts, "root_second")
     side.finish()
-    (solution,) = update(field_kernel, [b2, panel_one, sources, inverse, side.value, y], 6, "field")
+    (solution,) = update(field_kernel, [level, high, low, inverse, side.value], 3, "field")
     return (panel_one, solution)
 
 

time: 70.5 us -> 70.1 us (level)
  Pallas kernels: 29 us -> 27.7 us
  waiting for transfers between devices: 21 us -> 21.9 us
    pallas_call x5, Pallas kernels: 16.1 us -> 14.2 us  [call(): pl.pallas_call(kernel, out_shape=out_shape, scratch_shapes=list(scratch),...]
    ppermute x17, waiting for transfers between devices: 21 us -> 21.9 us  [exchange(): return lax.ppermute(x, AXES, [(i, i ^ mask) for i in range(count)])]
where the time goes in v10:
time: 70.1 us; the launch traced here: 69.9 us
  Pallas kernels  27.7 us (40%)
  waiting for transfers between devices  21.9 us (31%)
  starting transfers between devices  18.6 us (27%)
  between operations  1.11 us (2%)
    ppermute x17, waiting for transfers between devices, exchange(): return lax.ppermute(x, AXES, [(i, i ^ mask) for i in range(count)])  21.9 us
    ppermute x17, starting transfers between devices, exchange(): return lax.ppermute(x, AXES, [(i, i ^ mask) for i in range(count)])  18.6 us
    pallas_call x5, Pallas kernels, call(): pl.pallas_call(kernel, out_shape=out_shape, scratch_shapes=list(scratch),...  14.2 us
    pallas_call x2, Pallas kernels, update(): pl.pallas_call(kernel, out_specs=[pl.BlockSpec(memory_space=pl.ANY)] + [p...  6.43 us
    pallas_call x1, Pallas kernels, panel_gram(): pl.pallas_call(panel_gram_kernel, in_specs=[pl.BlockSpec(memory_space=pl....  4.47 us
    pallas_call x1, Pallas kernels, source_gram(): pl.pallas_call(source_gram_kernel, out_shape=(part, part), scratch_shapes...  2.55 us
  transfers between devices with their start and end apart: 17, of which 9 were waited for; matrix products, arithmetic and copies ran while one was open for 0% of the time, Pallas kernels for 28%

profile of v10, /device:TPU:0, one launch (start us, length us, event | category | flops | bytes accessed | tf_op | source)
XLA Modules:
  0.0 69.9 jit_solution(13505098148229040630)
XLA Ops:
  0.6 0.0 copy-start
  0.6 4.5 %panel_gram.1 = (f32[520,128]{1,0:T(8,128)S(1)}, f32[520,128]{1,0:T(8,128)S(1)}, f32[2048,256]{1,0:T(8,128)S(1)}, f32[2048,256]{1,0:T(8,128)S(1)}) custom-call(f32[2048,256]{1,0:T(8,128)} %q_two, f32[2048,256]{1,0:T(8,128)} %q_one.1), custom_call_target="tpu_custom_call" | custom-call | flops 1879048192 | bytes 4194304 | tf_op jit(solution)/shard_map/panel_gram/pallas_call | solution.py:181
  5.1 0.5 collective-permute-start
  5.6 0.0 copy-done
  5.6 2.6 %source_gram.1 = (f32[512,128]{1,0:T(8,128)S(1)}, f32[512,128]{1,0:T(8,128)S(1)}) custom-call(f32[2048,256]{1,0:T(8,128)S(1)} %get-tuple-element.58.b2, f32[2048,256]{1,0:T(8,128)S(1)} %get-tuple-element.59.b1, f32[2048,256]{1,0:T(8,128)S(1)} %copy-done), custom_call_target="tpu_custom_call" | custom-call | flops 1610612736 | bytes 6291456 | tf_op jit(solution)/shard_map/source_gram/pallas_call | solution.py:198
  8.2 0.0 collective-permute-done
  8.2 0.1 collective-permute-start.2
  8.4 3.0 %collective-permute-start.1 = (f32[264,128]{1,0:T(8,128)S(1)}, f32[264,128]{1,0:T(8,128)S(1)}, u32[]{:S(2)}, u32[]{:S(2)}) collective-permute-start(f32[264,128]{1,0:T(8,128)S(1)} %slice_select_fusion.1), channel_id=1, source_target_pairs={{0,4},{1,5},{2,6},{3,7},{4,0},{5,1},{6,2},{7,3},{8,12},{9,13},{10,... | collective-permute-start | bytes 405512 | tf_op jit(solution)/shard_map/ppermute | solution.py:467
  11.4 3.8 %collective-permute-done.1 = f32[264,128]{1,0:T(8,128)S(1)} collective-permute-done((f32[264,128]{1,0:T(8,128)S(1)}, f32[264,128]{1,0:T(8,128)S(1)}, u32[]{:S(2)}, u32[]{:S(2)}) %collective-permute-start.1) | collective-permute-done | bytes 135200 | tf_op jit(solution)/shard_map/ppermute | solution.py:467
  15.2 0.0 collective-permute-done.2
  15.2 1.8 %collective-permute-start.4 = (f32[256,128]{1,0:T(8,128)S(1)}, f32[256,128]{1,0:T(8,128)S(1)}, u32[]{:S(2)}, u32[]{:S(2)}) collective-permute-start(f32[256,128]{1,0:T(8,128)S(1)} %slice_select_fusion.2), channel_id=1, source_target_pairs={{0,4},{1,5},{2,6},{3,7},{4,0},{5,1},{6,2},{7,3},{8,12},{9,13},{10,... | collective-permute-start | bytes 393224 | tf_op jit(solution)/shard_map/ppermute | solution.py:467
  17.1 1.7 %collective-permute-start.3 = (f32[136,128]{1,0:T(8,128)S(1)}, f32[136,128]{1,0:T(8,128)S(1)}, u32[]{:S(2)}, u32[]{:S(2)}) collective-permute-start(f32[136,128]{1,0:T(8,128)S(1)} %slice_select_fusion.4), channel_id=1, source_target_pairs={{0,8},{1,9},{2,10},{3,11},{4,12},{5,13},{6,14},{7,15},{8,0},{9,1},... | collective-permute-start | bytes 208904 | tf_op jit(solution)/shard_map/ppermute | solution.py:467
  18.8 2.7 %collective-permute-done.3 = f32[136,128]{1,0:T(8,128)S(1)} collective-permute-done((f32[136,128]{1,0:T(8,128)S(1)}, f32[136,128]{1,0:T(8,128)S(1)}, u32[]{:S(2)}, u32[]{:S(2)}) %collective-permute-start.3) | collective-permute-done | bytes 69664 | tf_op jit(solution)/shard_map/ppermute | solution.py:467
  21.5 0.0 collective-permute-done.4
  21.5 2.7 %collective-permute-start.5 = (f32[136,128]{1,0:T(8,128)S(1)}, f32[136,128]{1,0:T(8,128)S(1)}, u32[]{:S(2)}, u32[]{:S(2)}) collective-permute-start(f32[136,128]{1,0:T(8,128)S(1)} %select_add_fusion.2), channel_id=1, source_target_pairs={{0,16},{1,17},{2,18},{3,19},{4,20},{5,21},{6,22},{7,23},{8,24},{9,... | collective-permute-start | bytes 208904 | tf_op jit(solution)/shard_map/ppermute | solution.py:467
  24.2 1.6 %collective-permute-start.6 = (f32[128,128]{1,0:T(8,128)S(1)}, f32[128,128]{1,0:T(8,128)S(1)}, u32[]{:S(2)}, u32[]{:S(2)}) collective-permute-start(f32[128,128]{1,0:T(8,128)S(1)} %slice_select_fusion.5), channel_id=1, source_target_pairs={{0,8},{1,9},{2,10},{3,11},{4,12},{5,13},{6,14},{7,15},{8,0},{9,1},... | collective-permute-start | bytes 196616 | tf_op jit(solution)/shard_map/ppermute | solution.py:467
  25.8 3.4 %collective-permute-done.6 = f32[128,128]{1,0:T(8,128)S(1)} collective-permute-done((f32[128,128]{1,0:T(8,128)S(1)}, f32[128,128]{1,0:T(8,128)S(1)}, u32[]{:S(2)}, u32[]{:S(2)}) %collective-permute-start.6) | collective-permute-done | bytes 65568 | tf_op jit(solution)/shard_map/ppermute | solution.py:467
  29.2 0.0 collective-permute-done.5
  29.3 1.6 %collective-permute-start.7 = (f32[136,128]{1,0:T(8,128)S(1)}, f32[136,128]{1,0:T(8,128)S(1)}, u32[]{:S(2)}, u32[]{:S(2)}) collective-permute-start(f32[136,128]{1,0:T(8,128)S(1)} %add.39), channel_id=1, source_target_pairs={{0,8},{1,9},{2,10},{3,11},{4,12},{5,13},{6,14},{7,15},{8,0},{9,1},... | collective-permute-start | bytes 208904 | tf_op jit(solution)/shard_map/ppermute | solution.py:467
  30.9 0.9 %collective-permute-start.8 = (f32[128,128]{1,0:T(8,128)S(1)}, f32[128,128]{1,0:T(8,128)S(1)}, u32[]{:S(2)}, u32[]{:S(2)}) collective-permute-start(f32[128,128]{1,0:T(8,128)S(1)} %select_add_fusion.3), channel_id=1, source_target_pairs={{0,16},{1,17},{2,18},{3,19},{4,20},{5,21},{6,22},{7,23},{8,24},{9,... | collective-permute-start | bytes 196616 | tf_op jit(solution)/shard_map/ppermute | solution.py:467
  31.8 4.9 %collective-permute-done.8 = f32[128,128]{1,0:T(8,128)S(1)} collective-permute-done((f32[128,128]{1,0:T(8,128)S(1)}, f32[128,128]{1,0:T(8,128)S(1)}, u32[]{:S(2)}, u32[]{:S(2)}) %collective-permute-start.8) | collective-permute-done | bytes 65568 | tf_op jit(solution)/shard_map/ppermute | solution.py:467
  36.7 0.0 collective-permute-done.7
  36.8 0.0 copy-start.1
  36.8 0.6 collective-permute-start.9
  37.4 0.2 collective-permute-start.10
  37.6 4.1 %collective-permute-done.10 = f32[128,128]{1,0:T(8,128)S(1)} collective-permute-done((f32[128,128]{1,0:T(8,128)S(1)}, f32[128,128]{1,0:T(8,128)S(1)}, u32[]{:S(2)}, u32[]{:S(2)}) %collective-permute-start.10) | collective-permute-done | bytes 65568 | tf_op jit(solution)/shard_map/ppermute | solution.py:467
  41.8 0.1 collective-permute-done.9
  42.0 0.1 collective-permute-start.12
  42.1 1.4 %collective-permute-start.11 = (f32[256,128]{1,0:T(8,128)S(1)}, f32[256,128]{1,0:T(8,128)S(1)}, u32[]{:S(2)}, u32[]{:S(2)}) collective-permute-start(f32[256,128]{1,0:T(8,128)S(1)} %pad_maximum_fusion.6), channel_id=1, source_target_pairs={{0,4},{1,5},{2,6},{3,7},{4,0},{5,1},{6,2},{7,3},{8,12},{9,13},{10,... | collective-permute-start | bytes 393224 | tf_op jit(solution)/shard_map/ppermute | solution.py:467
  43.5 0.1 collective-permute-done.12
  43.6 0.1 broadcast_select_fusion.1
  43.7 0.0 copy-done.1
  43.7 3.3 %level_first.1 = (f32[128,128]{1,0:T(8,128)S(1)}, f32[128,128]{1,0:T(8,128)S(1)}, f32[128,128]{1,0:T(8,128)S(1)}, f32[8,256]{1,0:T(8,128)S(1)}, f32[256,128]{1,0:T(8,128)S(1)}) custom-call(f32[1040,128]{1,0:T(8,128)S(1)} %pad_maximum_fusion.gram_ref.terms, f32[2,256,256]{2,1,0:T(8,128)S(1)} %copy-done.1), custom_call_target="tpu_custom_call" | custom-call | flops 5000000000 | bytes 262144 | tf_op jit(solution)/shard_map/level_first/pallas_call | solution.py:326
  47.0 1.0 %collective-permute-done.11 = f32[256,128]{1,0:T(8,128)S(1)} collective-permute-done((f32[256,128]{1,0:T(8,128)S(1)}, f32[256,128]{1,0:T(8,128)S(1)}, u32[]{:S(2)}, u32[]{:S(2)}) %collective-permute-start.11) | collective-permute-done | bytes 131104 | tf_op jit(solution)/shard_map/ppermute | solution.py:467
  48.1 0.1 collective-permute-start.13
  48.2 3.2 %level_second.1.inverse = f32[256,256]{1,0:T(8,128)S(1)} custom-call(f32[128,128]{1,0:T(8,128)S(1)} %get-tuple-element.85.first, f32[128,128]{1,0:T(8,128)S(1)} %get-tuple-element.86.across, f32[128,128]{1,0:T(8,128)S(1)} %get-tuple-element.87.rest, f32[8,256]{1,0:T(8,128)S(1)} %get-tuple-element.88.row, f32[256,128]{1,0:T(8,128)S(1)} %get-tuple-element.89.col), custom_call_target="tpu_custom_call" | custom-call | flops 5000000000 | bytes 262144 | tf_op jit(solution)/shard_map/level_second/pallas_call | solution.py:326
  51.4 0.0 collective-permute-done.13
  51.5 1.1 %panel_solve.1 = (f32[256,256]{1,0:T(8,128)S(1)}, f32[264,128]{1,0:T(8,128)S(1)}) custom-call(f32[256,256]{1,0:T(8,128)S(1)} %level_second.1.inverse, f32[1040,128]{1,0:T(8,128)S(1)} %pad_maximum_fusion.gram_ref.terms), custom_call_target="tpu_custom_call" | custom-call | bytes 262144 | tf_op jit(solution)/shard_map/panel_solve/pallas_call | solution.py:326
  52.5 1.6 %collective-permute-start.15 = (f32[264,128]{1,0:T(8,128)S(1)}, f32[264,128]{1,0:T(8,128)S(1)}, u32[]{:S(2)}, u32[]{:S(2)}) collective-permute-start(f32[264,128]{1,0:T(8,128)S(1)} %get-tuple-element.98), channel_id=1, source_target_pairs={{0,2},{1,3},{2,0},{3,1},{4,6},{5,7},{6,4},{7,5},{8,10},{9,11},{10,... | collective-permute-start | bytes 405512 | tf_op jit(solution)/shard_map/ppermute | solution.py:467
  54.2 0.0 copy-start.2
  54.2 3.8 %panel.1 = (f32[2048,256]{1,0:T(8,128)}, f32[2048,256]{1,0:T(8,128)S(1)}, bf16[2048,256]{1,0:T(8,128)(2,1)S(1)}, bf16[2048,256]{1,0:T(8,128)(2,1)S(1)}, f32[512,128]{1,0:T(8,128)S(1)}) custom-call(f32[2048,256]{1,0:T(8,128)S(1)} %get-tuple-element.58.b2, f32[2048,256]{1,0:T(8,128)S(1)} %get-tuple-element.59.b1, f32[2048,256]{1,0:T(8,128)S(1)} %copy-done, ...), custom_call_target="tpu_custom_call" | custom-call | flops 2147483648 | bytes 6291456 | tf_op jit(solution)/shard_map/panel/pallas_call | solution.py:454
  58.0 0.6 collective-permute-start.14
  58.6 0.0 collective-permute-done.15
  58.6 0.0 copy-done.2
  58.6 3.3 %root_first.1 = (f32[128,128]{1,0:T(8,128)S(1)}, f32[128,128]{1,0:T(8,128)S(1)}, f32[128,128]{1,0:T(8,128)S(1)}, f32[8,256]{1,0:T(8,128)S(1)}, f32[256,128]{1,0:T(8,128)S(1)}) custom-call(f32[264,128]{1,0:T(8,128)S(1)} %add.42.gram_ref, f32[1,256,256]{2,1,0:T(8,128)S(1)} %bitcast.1), custom_call_target="tpu_custom_call" | custom-call | flops 5000000000 | bytes 262144 | tf_op jit(solution)/shard_map/root_first/pallas_call | solution.py:326
  62.0 1.7 %collective-permute-done.14 = f32[256,128]{1,0:T(8,128)S(1)} collective-permute-done((f32[256,128]{1,0:T(8,128)S(1)}, f32[256,128]{1,0:T(8,128)S(1)}, u32[]{:S(2)}, u32[]{:S(2)}) %collective-permute-start.14) | collective-permute-done | bytes 131104 | tf_op jit(solution)/shard_map/ppermute | solution.py:467
  63.7 0.1 collective-permute-start.16
  63.8 3.2 %root_second.1.inverse = f32[256,256]{1,0:T(8,128)S(1)} custom-call(f32[128,128]{1,0:T(8,128)S(1)} %get-tuple-element.105.first, f32[128,128]{1,0:T(8,128)S(1)} %get-tuple-element.106.across, f32[128,128]{1,0:T(8,128)S(1)} %get-tuple-element.107.rest, f32[8,256]{1,0:T(8,128)S(1)} %get-tuple-element.108.row, f32[256,128]{1,0:T(8,128)S(1)} %get-tuple-element.109.col), custom_call_target="tpu_custom_call" | custom-call | flops 5000000000 | bytes 262144 | tf_op jit(solution)/shard_map/root_second/pallas_call | solution.py:326
  67.0 0.0 collective-permute-done.16
  67.1 2.6 %field.1 = f32[2048,256]{1,0:T(8,128)} custom-call(f32[2048,256]{1,0:T(8,128)S(1)} %get-tuple-element.94.level, bf16[2048,256]{1,0:T(8,128)(2,1)S(1)} %get-tuple-element.95.high, bf16[2048,256]{1,0:T(8,128)(2,1)S(1)} %get-tuple-element.96.low, f32[256,256]{1,0:T(8,128)S(1)} %root_second.1.inverse, f32[512,128]{1,0:T(8,128)S(1)} %pad_maximum_fusion.4.side), custom_call_target="tpu_custom_call" | custom-call | flops 805306368 | bytes 6291456 | tf_op jit(solution)/shard_map/field/pallas_call | solution.py:454
  (30 shorter events, 0.6 us)
Async XLA Ops:
  0.6 5.0 %copy-start = (f32[2048,256]{1,0:T(8,128)S(1)}, f32[2048,256]{1,0:T(8,128)}, u32[]{:S(2)}) copy-start(f32[2048,256]{1,0:T(8,128)} %sources.3) | copy-start | bytes 6291460
  5.1 3.1 %collective-permute-start = (f32[520,128]{1,0:T(8,128)S(1)}, f32[520,128]{1,0:T(8,128)S(1)}, u32[]{:S(2)}, u32[]{:S(2)}) collective-permute-start(f32[520,128]{1,0:T(8,128)S(1)} %get-tuple-element.63), channel_id=1, source_target_pairs={{0,1},{1,0},{2,3},{3,2},{4,5},{5,4},{6,7},{7,6},{8,9},{9,8},{10,11... | collective-permute-start | bytes 798728 | tf_op jit(solution)/shard_map/ppermute | solution.py:467
  8.2 7.0 %collective-permute-start.2 = (f32[512,128]{1,0:T(8,128)S(1)}, f32[512,128]{1,0:T(8,128)S(1)}, u32[]{:S(2)}, u32[]{:S(2)}) collective-permute-start(f32[512,128]{1,0:T(8,128)S(1)} %get-tuple-element.66), channel_id=1, source_target_pairs={{0,1},{1,0},{2,3},{3,2},{4,5},{5,4},{6,7},{7,6},{8,9},{9,8},{10,11... | collective-permute-start | bytes 786440 | tf_op jit(solution)/shard_map/ppermute | solution.py:467
  8.4 6.7 %collective-permute-start.1 = (f32[264,128]{1,0:T(8,128)S(1)}, f32[264,128]{1,0:T(8,128)S(1)}, u32[]{:S(2)}, u32[]{:S(2)}) collective-permute-start(f32[264,128]{1,0:T(8,128)S(1)} %slice_select_fusion.1), channel_id=1, source_target_pairs={{0,4},{1,5},{2,6},{3,7},{4,0},{5,1},{6,2},{7,3},{8,12},{9,13},{10,... | collective-permute-start | bytes 405512 | tf_op jit(solution)/shard_map/ppermute | solution.py:467
  15.2 6.2 %collective-permute-start.4 = (f32[256,128]{1,0:T(8,128)S(1)}, f32[256,128]{1,0:T(8,128)S(1)}, u32[]{:S(2)}, u32[]{:S(2)}) collective-permute-start(f32[256,128]{1,0:T(8,128)S(1)} %slice_select_fusion.2), channel_id=1, source_target_pairs={{0,4},{1,5},{2,6},{3,7},{4,0},{5,1},{6,2},{7,3},{8,12},{9,13},{10,... | collective-permute-start | bytes 393224 | tf_op jit(solution)/shard_map/ppermute | solution.py:467
  17.1 4.4 %collective-permute-start.3 = (f32[136,128]{1,0:T(8,128)S(1)}, f32[136,128]{1,0:T(8,128)S(1)}, u32[]{:S(2)}, u32[]{:S(2)}) collective-permute-start(f32[136,128]{1,0:T(8,128)S(1)} %slice_select_fusion.4), channel_id=1, source_target_pairs={{0,8},{1,9},{2,10},{3,11},{4,12},{5,13},{6,14},{7,15},{8,0},{9,1},... | collective-permute-start | bytes 208904 | tf_op jit(solution)/shard_map/ppermute | solution.py:467
  21.5 7.7 %collective-permute-start.5 = (f32[136,128]{1,0:T(8,128)S(1)}, f32[136,128]{1,0:T(8,128)S(1)}, u32[]{:S(2)}, u32[]{:S(2)}) collective-permute-start(f32[136,128]{1,0:T(8,128)S(1)} %select_add_fusion.2), channel_id=1, source_target_pairs={{0,16},{1,17},{2,18},{3,19},{4,20},{5,21},{6,22},{7,23},{8,24},{9,... | collective-permute-start | bytes 208904 | tf_op jit(solution)/shard_map/ppermute | solution.py:467
  24.2 5.0 %collective-permute-start.6 = (f32[128,128]{1,0:T(8,128)S(1)}, f32[128,128]{1,0:T(8,128)S(1)}, u32[]{:S(2)}, u32[]{:S(2)}) collective-permute-start(f32[128,128]{1,0:T(8,128)S(1)} %slice_select_fusion.5), channel_id=1, source_target_pairs={{0,8},{1,9},{2,10},{3,11},{4,12},{5,13},{6,14},{7,15},{8,0},{9,1},... | collective-permute-start | bytes 196616 | tf_op jit(solution)/shard_map/ppermute | solution.py:467
  29.3 7.5 %collective-permute-start.7 = (f32[136,128]{1,0:T(8,128)S(1)}, f32[136,128]{1,0:T(8,128)S(1)}, u32[]{:S(2)}, u32[]{:S(2)}) collective-permute-start(f32[136,128]{1,0:T(8,128)S(1)} %add.39), channel_id=1, source_target_pairs={{0,8},{1,9},{2,10},{3,11},{4,12},{5,13},{6,14},{7,15},{8,0},{9,1},... | collective-permute-start | bytes 208904 | tf_op jit(solution)/shard_map/ppermute | solution.py:467
  30.9 5.8 %collective-permute-start.8 = (f32[128,128]{1,0:T(8,128)S(1)}, f32[128,128]{1,0:T(8,128)S(1)}, u32[]{:S(2)}, u32[]{:S(2)}) collective-permute-start(f32[128,128]{1,0:T(8,128)S(1)} %select_add_fusion.3), channel_id=1, source_target_pairs={{0,16},{1,17},{2,18},{3,19},{4,20},{5,21},{6,22},{7,23},{8,24},{9,... | collective-permute-start | bytes 196616 | tf_op jit(solution)/shard_map/ppermute | solution.py:467
  36.8 6.9 %copy-start.1 = (f32[2,256,256]{2,1,0:T(8,128)S(1)}, f32[2,256,256]{2,1,0:T(8,128)}, u32[]{:S(2)}) copy-start(f32[2,256,256]{2,1,0:T(8,128)} %coupling.1) | copy-start | bytes 1572868
  36.8 5.1 %collective-permute-start.9 = (f32[264,128]{1,0:T(8,128)S(1)}, f32[264,128]{1,0:T(8,128)S(1)}, u32[]{:S(2)}, u32[]{:S(2)}) collective-permute-start(f32[264,128]{1,0:T(8,128)S(1)} %pad_maximum_fusion.5), channel_id=1, source_target_pairs={{0,4},{1,5},{2,6},{3,7},{4,0},{5,1},{6,2},{7,3},{8,12},{9,13},{10,... | collective-permute-start | bytes 405512 | tf_op jit(solution)/shard_map/ppermute | solution.py:467
  37.4 4.3 %collective-permute-start.10 = (f32[128,128]{1,0:T(8,128)S(1)}, f32[128,128]{1,0:T(8,128)S(1)}, u32[]{:S(2)}, u32[]{:S(2)}) collective-permute-start(f32[128,128]{1,0:T(8,128)S(1)} %add.41), channel_id=1, source_target_pairs={{0,8},{1,9},{2,10},{3,11},{4,12},{5,13},{6,14},{7,15},{8,0},{9,1},... | collective-permute-start | bytes 196616 | tf_op jit(solution)/shard_map/ppermute | solution.py:467
  42.0 1.6 %collective-permute-start.12 = (f32[520,128]{1,0:T(8,128)S(1)}, f32[520,128]{1,0:T(8,128)S(1)}, u32[]{:S(2)}, u32[]{:S(2)}) collective-permute-start(f32[520,128]{1,0:T(8,128)S(1)} %pad_maximum_fusion.2), channel_id=1, source_target_pairs={{0,1},{1,0},{2,3},{3,2},{4,5},{5,4},{6,7},{7,6},{8,9},{9,8},{10,11... | collective-permute-start | bytes 798728 | tf_op jit(solution)/shard_map/ppermute | solution.py:467
  42.1 6.0 %collective-permute-start.11 = (f32[256,128]{1,0:T(8,128)S(1)}, f32[256,128]{1,0:T(8,128)S(1)}, u32[]{:S(2)}, u32[]{:S(2)}) collective-permute-start(f32[256,128]{1,0:T(8,128)S(1)} %pad_maximum_fusion.6), channel_id=1, source_target_pairs={{0,4},{1,5},{2,6},{3,7},{4,0},{5,1},{6,2},{7,3},{8,12},{9,13},{10,... | collective-permute-start | bytes 393224 | tf_op jit(solution)/shard_map/ppermute | solution.py:467
  48.1 3.3 %collective-permute-start.13 = (f32[512,128]{1,0:T(8,128)S(1)}, f32[512,128]{1,0:T(8,128)S(1)}, u32[]{:S(2)}, u32[]{:S(2)}) collective-permute-start(f32[512,128]{1,0:T(8,128)S(1)} %pad_maximum_fusion.3), channel_id=1, source_target_pairs={{0,1},{1,0},{2,3},{3,2},{4,5},{5,4},{6,7},{7,6},{8,9},{9,8},{10,11... | collective-permute-start | bytes 786440 | tf_op jit(solution)/shard_map/ppermute | solution.py:467
  52.5 6.1 %collective-permute-start.15 = (f32[264,128]{1,0:T(8,128)S(1)}, f32[264,128]{1,0:T(8,128)S(1)}, u32[]{:S(2)}, u32[]{:S(2)}) collective-permute-start(f32[264,128]{1,0:T(8,128)S(1)} %get-tuple-element.98), channel_id=1, source_target_pairs={{0,2},{1,3},{2,0},{3,1},{4,6},{5,7},{6,4},{7,5},{8,10},{9,11},{10,... | collective-permute-start | bytes 405512 | tf_op jit(solution)/shard_map/ppermute | solution.py:467
  54.2 4.4 %copy-start.2 = (f32[256,256]{1,0:T(8,128)S(1)}, f32[256,256]{1,0:T(8,128)}, u32[]{:S(2)}) copy-start(f32[256,256]{1,0:T(8,128)} %param.9) | copy-start | bytes 786436
  58.0 5.7 %collective-permute-start.14 = (f32[256,128]{1,0:T(8,128)S(1)}, f32[256,128]{1,0:T(8,128)S(1)}, u32[]{:S(2)}, u32[]{:S(2)}) collective-permute-start(f32[256,128]{1,0:T(8,128)S(1)} %slice_select_fusion), channel_id=1, source_target_pairs={{0,2},{1,3},{2,0},{3,1},{4,6},{5,7},{6,4},{7,5},{8,10},{9,11},{10,... | collective-permute-start | bytes 393224 | tf_op jit(solution)/shard_map/ppermute | solution.py:467
  63.7 3.3 %collective-permute-start.16 = (f32[256,128]{1,0:T(8,128)S(1)}, f32[256,128]{1,0:T(8,128)S(1)}, u32[]{:S(2)}, u32[]{:S(2)}) collective-permute-start(f32[256,128]{1,0:T(8,128)S(1)} %add.43), channel_id=1, source_target_pairs={{0,1},{1,0},{2,3},{3,2},{4,5},{5,4},{6,7},{7,6},{8,9},{9,8},{10,11... | collective-permute-start | bytes 393224 | tf_op jit(solution)/shard_map/ppermute | solution.py:467

commit v11 on v10

--- a/solution.py
+++ b/solution.py
@@ -209,23 +209,22 @@
     return jnp.broadcast_to(x[:, lane : lane + 1], (8, LANES))
 
 
-def eliminate(block, cols, rows):
-    count = len(block)
+def sweep_panel(block, start, cols, rows):
     lane = lax.broadcasted_iota(jnp.int32, (8, LANES), 1)
-    for start in range(0, count, GROUPS):
-        panel = block[start : start + GROUPS]
-        left = stack_left(jnp.concatenate(panel, axis=0))
-        for t in range(GROUPS):
-            panel = eliminate_group(panel, t, start + t, cols, rows)
-        inside = (lane >= 8 * start) & (lane < 8 * (start + GROUPS))
-        panel = [jnp.where(inside, -x, x) for x in panel]
-        change = dot_t(left, stack_right(jnp.concatenate(panel, axis=0)))
-        for g in range(count):
-            if start <= g < start + GROUPS:
-                block[g] = panel[g - start]
-            else:
-                block[g] = jnp.where(inside, 0.0, block[g]) - change[8 * g : 8 * g + 8, :]
-    return [-x for x in block]
+    panel = block[start : start + GROUPS]
+    left = stack_left(jnp.concatenate(panel, axis=0))
+    for t in range(GROUPS):
+        panel = eliminate_group(panel, t, start + t, cols, rows)
+    inside = (lane >= 8 * start) & (lane < 8 * (start + GROUPS))
+    panel = [jnp.where(inside, -x, x) for x in panel]
+    change = dot_t(left, stack_right(jnp.concatenate(panel, axis=0)))
+    swept = []
+    for g in range(len(block)):
+        if start <= g < start + GROUPS:
+            swept.append(panel[g - start])
+        else:
+            swept.append(jnp.where(inside, 0.0, block[g]) - change[8 * g : 8 * g + 8, :])
+    return swept
 
 
 def eliminate_group(panel, t, at, cols, rows):
@@ -313,9 +312,14 @@
     return jnp.concatenate([h, m, h, l, h, m], axis=0)
 
 
-def invert_half(matrix, cols, rows):
-    block = eliminate([matrix[8 * i : 8 * i + 8, :] for i in range(LANES // 8)], cols, rows)
+def sweep(matrix, panels, cols, rows):
+    block = [matrix[8 * i : 8 * i + 8, :] for i in range(LANES // 8)]
+    for panel in panels:
+        block = sweep_panel(block, panel * GROUPS, cols, rows)
     return jnp.concatenate(block, axis=0)
+
+
+PANELS = LANES // (8 * GROUPS)
 
 
 SQUARE = jax.ShapeDtypeStruct((R, R), F32)
@@ -341,7 +345,7 @@
     scale_col = lax.rsqrt(jnp.sum(diagonal, axis=1, keepdims=True))
     matrix = matrix * scale_col * scale_row
     side = matrix[:LANES, LANES:]
-    first = invert_half(matrix[:LANES, :LANES], cols, rows)
+    first = -sweep(matrix[:LANES, :LANES], range(PANELS), cols, rows)
     across = dot_full(first, side)
     first_out[...] = first
     across_out[...] = across
@@ -350,8 +354,12 @@
     col_out[...] = jnp.broadcast_to(scale_col, (R, LANES))
 
 
-def second_kernel(first, across, rest, row, col, out, cols, rows):
-    second = invert_half(rest[...], cols, rows)
+def middle_kernel(rest, out, cols, rows):
+    out[...] = sweep(rest[...], range(PANELS - 1), cols, rows)
+
+
+def second_kernel(first, across, swept, row, col, out, cols, rows):
+    second = -sweep(swept[...], range(PANELS - 1, PANELS), cols, rows)
     corner = -dot_full(across[...], second)
     top = first[...] - dot_full(corner, across[...].T)
     out[:LANES, :LANES] = top * col[:LANES, :] * row[:1, :LANES]
@@ -376,8 +384,14 @@
     return call(kernel, shapes, (packed, coupling), name, SCRATCH, HALF_FLOPS)
 
 
+def invert_middle(parts, name):
+    first, across, rest, row, col = parts
+    rest = call(middle_kernel, CORNER, (rest,), name, SCRATCH, HALF_FLOPS // 2)
+    return first, across, rest, row, col
+
+
 def invert_second(parts, name):
-    return call(second_kernel, SQUARE, parts, name, SCRATCH, HALF_FLOPS)
+    return call(second_kernel, SQUARE, parts, name, SCRATCH, HALF_FLOPS // 2)
 
 
 def half_index():
@@ -532,16 +546,16 @@
     panels.finish()
     terms = panels.value
     parts = invert_first(half_index, terms, coupling_two, "level_first")
+    parts = invert_middle(parts, "level_middle")
     source.flying, parts = lax.optimization_barrier((source.flying, parts))
     source.finish()
     source.start(*source_left.pop())
     inverse = invert_second(parts, "level_second")
-    source.flying, inverse = lax.optimization_barrier((source.flying, inverse))
-    source.finish()
-
     x, root = call(
         panel_solve_kernel, (SQUARE, jax.ShapeDtypeStruct((SYMMETRIC, LANES), F32)), (inverse, terms), "panel_solve"
     )
+    source.flying, x = lax.optimization_barrier((source.flying, x))
+    source.finish()
     arriving = exchange(root, 2)
     rows = b2.shape[0]
     shapes = [jax.ShapeDtypeStruct((rows, R), kind) for kind in (F32, BF16, BF16)]
@@ -554,6 +568,7 @@
     arriving, side.value = lax.optimization_barrier((arriving, side.value))
     root = root + arriving
     parts = invert_first(no_index, root, coupling_one[None], "root_first")
+    parts = invert_middle(parts, "root_middle")
     side_flying, parts = lax.optimization_barrier((side_flying, parts))
     side.value = side.value + side_flying
     side.start("gather", 0)

time: 70.1 us -> 68.1 us (0.971)
  waiting for transfers between devices: 21.9 us -> 19.3 us
    ppermute x17, waiting for transfers between devices: 21.9 us -> 19.3 us  [exchange(): return lax.ppermute(x, AXES, [(i, i ^ mask) for i in range(count)])]
    pallas_call x5 -> x7, Pallas kernels: 14.2 us -> 14.7 us  [call(): pl.pallas_call(kernel, out_shape=out_shape, scratch_shapes=list(scratch),...]
  transfers between devices with their start and end apart: 17 -> 17, of which waited for: 9 -> 8; matrix products, arithmetic and copies ran while one was open for 0% -> 1% of each run, Pallas kernels for 28% -> 31%
where the time goes in v11:
time: 68.1 us; the launch traced here: 67.9 us
  Pallas kernels  28.1 us (41%)
  waiting for transfers between devices  19.3 us (28%)
  starting transfers between devices  18.7 us (27%)
  between operations  1.13 us (2%)
    ppermute x17, waiting for transfers between devices, exchange(): return lax.ppermute(x, AXES, [(i, i ^ mask) for i in range(count)])  19.3 us
    ppermute x17, starting transfers between devices, exchange(): return lax.ppermute(x, AXES, [(i, i ^ mask) for i in range(count)])  18.7 us
    pallas_call x7, Pallas kernels, call(): pl.pallas_call(kernel, out_shape=out_shape, scratch_shapes=list(scratch),...  14.7 us
    pallas_call x2, Pallas kernels, update(): pl.pallas_call(kernel, out_specs=[pl.BlockSpec(memory_space=pl.ANY)] + [p...  6.43 us
    pallas_call x1, Pallas kernels, panel_gram(): pl.pallas_call(panel_gram_kernel, in_specs=[pl.BlockSpec(memory_space=pl....  4.47 us
    pallas_call x1, Pallas kernels, source_gram(): pl.pallas_call(source_gram_kernel, out_shape=(part, part), scratch_shapes...  2.55 us
  transfers between devices with their start and end apart: 17, of which 8 were waited for; matrix products, arithmetic and copies ran while one was open for 1% of the time, Pallas kernels for 31%

profile of v11, /device:TPU:0, one launch (start us, length us, event | category | flops | bytes accessed | tf_op | source)
XLA Modules:
  0.0 67.9 jit_solution(12023849321024119065)
XLA Ops:
  0.6 0.0 copy-start
  0.6 4.5 %panel_gram.1 = (f32[520,128]{1,0:T(8,128)S(1)}, f32[520,128]{1,0:T(8,128)S(1)}, f32[2048,256]{1,0:T(8,128)S(1)}, f32[2048,256]{1,0:T(8,128)S(1)}) custom-call(f32[2048,256]{1,0:T(8,128)} %q_two, f32[2048,256]{1,0:T(8,128)} %q_one.1), custom_call_target="tpu_custom_call" | custom-call | flops 1879048192 | bytes 4194304 | tf_op jit(solution)/shard_map/panel_gram/pallas_call | solution.py:181
  5.1 0.5 collective-permute-start
  5.6 0.0 copy-done
  5.6 2.6 %source_gram.1 = (f32[512,128]{1,0:T(8,128)S(1)}, f32[512,128]{1,0:T(8,128)S(1)}) custom-call(f32[2048,256]{1,0:T(8,128)S(1)} %get-tuple-element.58.b2, f32[2048,256]{1,0:T(8,128)S(1)} %get-tuple-element.59.b1, f32[2048,256]{1,0:T(8,128)S(1)} %copy-done), custom_call_target="tpu_custom_call" | custom-call | flops 1610612736 | bytes 6291456 | tf_op jit(solution)/shard_map/source_gram/pallas_call | solution.py:198
  8.2 0.0 collective-permute-done
  8.2 0.1 collective-permute-start.2
  8.4 3.0 %collective-permute-start.1 = (f32[264,128]{1,0:T(8,128)S(1)}, f32[264,128]{1,0:T(8,128)S(1)}, u32[]{:S(2)}, u32[]{:S(2)}) collective-permute-start(f32[264,128]{1,0:T(8,128)S(1)} %slice_select_fusion.1), channel_id=1, source_target_pairs={{0,4},{1,5},{2,6},{3,7},{4,0},{5,1},{6,2},{7,3},{8,12},{9,13},{10,... | collective-permute-start | bytes 405512 | tf_op jit(solution)/shard_map/ppermute | solution.py:481
  11.4 3.8 %collective-permute-done.1 = f32[264,128]{1,0:T(8,128)S(1)} collective-permute-done((f32[264,128]{1,0:T(8,128)S(1)}, f32[264,128]{1,0:T(8,128)S(1)}, u32[]{:S(2)}, u32[]{:S(2)}) %collective-permute-start.1) | collective-permute-done | bytes 135200 | tf_op jit(solution)/shard_map/ppermute | solution.py:481
  15.2 0.0 collective-permute-done.2
  15.2 1.8 %collective-permute-start.4 = (f32[256,128]{1,0:T(8,128)S(1)}, f32[256,128]{1,0:T(8,128)S(1)}, u32[]{:S(2)}, u32[]{:S(2)}) collective-permute-start(f32[256,128]{1,0:T(8,128)S(1)} %slice_select_fusion.2), channel_id=1, source_target_pairs={{0,4},{1,5},{2,6},{3,7},{4,0},{5,1},{6,2},{7,3},{8,12},{9,13},{10,... | collective-permute-start | bytes 393224 | tf_op jit(solution)/shard_map/ppermute | solution.py:481
  17.1 1.7 %collective-permute-start.3 = (f32[136,128]{1,0:T(8,128)S(1)}, f32[136,128]{1,0:T(8,128)S(1)}, u32[]{:S(2)}, u32[]{:S(2)}) collective-permute-start(f32[136,128]{1,0:T(8,128)S(1)} %slice_select_fusion.4), channel_id=1, source_target_pairs={{0,8},{1,9},{2,10},{3,11},{4,12},{5,13},{6,14},{7,15},{8,0},{9,1},... | collective-permute-start | bytes 208904 | tf_op jit(solution)/shard_map/ppermute | solution.py:481
  18.8 2.7 %collective-permute-done.3 = f32[136,128]{1,0:T(8,128)S(1)} collective-permute-done((f32[136,128]{1,0:T(8,128)S(1)}, f32[136,128]{1,0:T(8,128)S(1)}, u32[]{:S(2)}, u32[]{:S(2)}) %collective-permute-start.3) | collective-permute-done | bytes 69664 | tf_op jit(solution)/shard_map/ppermute | solution.py:481
  21.5 0.0 collective-permute-done.4
  21.5 2.7 %collective-permute-start.5 = (f32[136,128]{1,0:T(8,128)S(1)}, f32[136,128]{1,0:T(8,128)S(1)}, u32[]{:S(2)}, u32[]{:S(2)}) collective-permute-start(f32[136,128]{1,0:T(8,128)S(1)} %select_add_fusion.2), channel_id=1, source_target_pairs={{0,16},{1,17},{2,18},{3,19},{4,20},{5,21},{6,22},{7,23},{8,24},{9,... | collective-permute-start | bytes 208904 | tf_op jit(solution)/shard_map/ppermute | solution.py:481
  24.2 1.6 %collective-permute-start.6 = (f32[128,128]{1,0:T(8,128)S(1)}, f32[128,128]{1,0:T(8,128)S(1)}, u32[]{:S(2)}, u32[]{:S(2)}) collective-permute-start(f32[128,128]{1,0:T(8,128)S(1)} %slice_select_fusion.5), channel_id=1, source_target_pairs={{0,8},{1,9},{2,10},{3,11},{4,12},{5,13},{6,14},{7,15},{8,0},{9,1},... | collective-permute-start | bytes 196616 | tf_op jit(solution)/shard_map/ppermute | solution.py:481
  25.8 3.4 %collective-permute-done.6 = f32[128,128]{1,0:T(8,128)S(1)} collective-permute-done((f32[128,128]{1,0:T(8,128)S(1)}, f32[128,128]{1,0:T(8,128)S(1)}, u32[]{:S(2)}, u32[]{:S(2)}) %collective-permute-start.6) | collective-permute-done | bytes 65568 | tf_op jit(solution)/shard_map/ppermute | solution.py:481
  29.2 0.0 collective-permute-done.5
  29.3 1.6 %collective-permute-start.7 = (f32[136,128]{1,0:T(8,128)S(1)}, f32[136,128]{1,0:T(8,128)S(1)}, u32[]{:S(2)}, u32[]{:S(2)}) collective-permute-start(f32[136,128]{1,0:T(8,128)S(1)} %add.39), channel_id=1, source_target_pairs={{0,8},{1,9},{2,10},{3,11},{4,12},{5,13},{6,14},{7,15},{8,0},{9,1},... | collective-permute-start | bytes 208904 | tf_op jit(solution)/shard_map/ppermute | solution.py:481
  30.9 0.9 %collective-permute-start.8 = (f32[128,128]{1,0:T(8,128)S(1)}, f32[128,128]{1,0:T(8,128)S(1)}, u32[]{:S(2)}, u32[]{:S(2)}) collective-permute-start(f32[128,128]{1,0:T(8,128)S(1)} %select_add_fusion.3), channel_id=1, source_target_pairs={{0,16},{1,17},{2,18},{3,19},{4,20},{5,21},{6,22},{7,23},{8,24},{9,... | collective-permute-start | bytes 196616 | tf_op jit(solution)/shard_map/ppermute | solution.py:481
  31.8 4.9 %collective-permute-done.8 = f32[128,128]{1,0:T(8,128)S(1)} collective-permute-done((f32[128,128]{1,0:T(8,128)S(1)}, f32[128,128]{1,0:T(8,128)S(1)}, u32[]{:S(2)}, u32[]{:S(2)}) %collective-permute-start.8) | collective-permute-done | bytes 65568 | tf_op jit(solution)/shard_map/ppermute | solution.py:481
  36.7 0.0 collective-permute-done.7
  36.8 0.0 copy-start.1
  36.8 0.6 collective-permute-start.9
  37.4 0.2 collective-permute-start.10
  37.6 4.1 %collective-permute-done.10 = f32[128,128]{1,0:T(8,128)S(1)} collective-permute-done((f32[128,128]{1,0:T(8,128)S(1)}, f32[128,128]{1,0:T(8,128)S(1)}, u32[]{:S(2)}, u32[]{:S(2)}) %collective-permute-start.10) | collective-permute-done | bytes 65568 | tf_op jit(solution)/shard_map/ppermute | solution.py:481
  41.8 0.1 collective-permute-done.9
  42.0 0.1 collective-permute-start.12
  42.1 1.4 %collective-permute-start.11 = (f32[256,128]{1,0:T(8,128)S(1)}, f32[256,128]{1,0:T(8,128)S(1)}, u32[]{:S(2)}, u32[]{:S(2)}) collective-permute-start(f32[256,128]{1,0:T(8,128)S(1)} %pad_maximum_fusion.6), channel_id=1, source_target_pairs={{0,4},{1,5},{2,6},{3,7},{4,0},{5,1},{6,2},{7,3},{8,12},{9,13},{10,... | collective-permute-start | bytes 393224 | tf_op jit(solution)/shard_map/ppermute | solution.py:481
  43.5 0.1 collective-permute-done.12
  43.6 0.1 broadcast_select_fusion.1
  43.7 0.0 copy-done.1
  43.7 3.3 %level_first.1 = (f32[128,128]{1,0:T(8,128)S(1)}, f32[128,128]{1,0:T(8,128)S(1)}, f32[128,128]{1,0:T(8,128)S(1)}, f32[8,256]{1,0:T(8,128)S(1)}, f32[256,128]{1,0:T(8,128)S(1)}) custom-call(f32[1040,128]{1,0:T(8,128)S(1)} %pad_maximum_fusion.gram_ref.terms, f32[2,256,256]{2,1,0:T(8,128)S(1)} %copy-done.1), custom_call_target="tpu_custom_call" | custom-call | flops 5000000000 | bytes 262144 | tf_op jit(solution)/shard_map/level_first/pallas_call | solution.py:330
  47.0 1.4 %level_middle.1.swept = f32[128,128]{1,0:T(8,128)S(1)} custom-call(f32[128,128]{1,0:T(8,128)S(1)} %get-tuple-element.81.rest), custom_call_target="tpu_custom_call" | custom-call | flops 2500000000 | bytes 262144 | tf_op jit(solution)/shard_map/level_middle/pallas_call | solution.py:330
  48.4 0.0 collective-permute-done.11
  48.5 0.2 collective-permute-start.13
  48.7 2.1 %level_second.1.inverse = f32[256,256]{1,0:T(8,128)S(1)} custom-call(f32[128,128]{1,0:T(8,128)S(1)} %get-tuple-element.85.first, f32[128,128]{1,0:T(8,128)S(1)} %get-tuple-element.86.across, f32[128,128]{1,0:T(8,128)S(1)} %level_middle.1.swept, f32[8,256]{1,0:T(8,128)S(1)} %get-tuple-element.88.row, f32[256,128]{1,0:T(8,128)S(1)} %get-tuple-element.89.col), custom_call_target="tpu_custom_call" | custom-call | flops 2500000000 | bytes 262144 | tf_op jit(solution)/shard_map/level_second/pallas_call | solution.py:330
  50.7 1.1 %panel_solve.1 = (f32[256,256]{1,0:T(8,128)S(1)}, f32[264,128]{1,0:T(8,128)S(1)}) custom-call(f32[256,256]{1,0:T(8,128)S(1)} %level_second.1.inverse, f32[1040,128]{1,0:T(8,128)S(1)} %pad_maximum_fusion.gram_ref.terms), custom_call_target="tpu_custom_call" | custom-call | bytes 262144 | tf_op jit(solution)/shard_map/panel_solve/pallas_call | solution.py:330
  51.8 1.6 %collective-permute-start.15 = (f32[264,128]{1,0:T(8,128)S(1)}, f32[264,128]{1,0:T(8,128)S(1)}, u32[]{:S(2)}, u32[]{:S(2)}) collective-permute-start(f32[264,128]{1,0:T(8,128)S(1)} %get-tuple-element.98), channel_id=1, source_target_pairs={{0,2},{1,3},{2,0},{3,1},{4,6},{5,7},{6,4},{7,5},{8,10},{9,11},{10,... | collective-permute-start | bytes 405512 | tf_op jit(solution)/shard_map/ppermute | solution.py:481
  53.5 0.0 collective-permute-done.13
  53.5 0.0 copy-start.2
  53.6 3.8 %panel.1 = (f32[2048,256]{1,0:T(8,128)}, f32[2048,256]{1,0:T(8,128)S(1)}, bf16[2048,256]{1,0:T(8,128)(2,1)S(1)}, bf16[2048,256]{1,0:T(8,128)(2,1)S(1)}, f32[512,128]{1,0:T(8,128)S(1)}) custom-call(f32[2048,256]{1,0:T(8,128)S(1)} %get-tuple-element.58.b2, f32[2048,256]{1,0:T(8,128)S(1)} %get-tuple-element.59.b1, f32[2048,256]{1,0:T(8,128)S(1)} %copy-done, ...), custom_call_target="tpu_custom_call" | custom-call | flops 2147483648 | bytes 6291456 | tf_op jit(solution)/shard_map/panel/pallas_call | solution.py:468
  57.4 0.6 collective-permute-start.14
  57.9 0.0 collective-permute-done.15
  58.0 0.0 copy-done.2
  58.0 3.3 %root_first.1 = (f32[128,128]{1,0:T(8,128)S(1)}, f32[128,128]{1,0:T(8,128)S(1)}, f32[128,128]{1,0:T(8,128)S(1)}, f32[8,256]{1,0:T(8,128)S(1)}, f32[256,128]{1,0:T(8,128)S(1)}) custom-call(f32[264,128]{1,0:T(8,128)S(1)} %add.42.gram_ref, f32[1,256,256]{2,1,0:T(8,128)S(1)} %bitcast.1), custom_call_target="tpu_custom_call" | custom-call | flops 5000000000 | bytes 262144 | tf_op jit(solution)/shard_map/root_first/pallas_call | solution.py:330
  61.3 1.4 %root_middle.1.swept = f32[128,128]{1,0:T(8,128)S(1)} custom-call(f32[128,128]{1,0:T(8,128)S(1)} %get-tuple-element.102.rest), custom_call_target="tpu_custom_call" | custom-call | flops 2500000000 | bytes 262144 | tf_op jit(solution)/shard_map/root_middle/pallas_call | solution.py:330
  62.7 0.2 collective-permute-done.14
  62.9 0.1 collective-permute-start.16
  63.0 2.1 %root_second.1.inverse = f32[256,256]{1,0:T(8,128)S(1)} custom-call(f32[128,128]{1,0:T(8,128)S(1)} %get-tuple-element.105.first, f32[128,128]{1,0:T(8,128)S(1)} %get-tuple-element.106.across, f32[128,128]{1,0:T(8,128)S(1)} %root_middle.1.swept, f32[8,256]{1,0:T(8,128)S(1)} %get-tuple-element.108.row, f32[256,128]{1,0:T(8,128)S(1)} %get-tuple-element.109.col), custom_call_target="tpu_custom_call" | custom-call | flops 2500000000 | bytes 262144 | tf_op jit(solution)/shard_map/root_second/pallas_call | solution.py:330
  65.1 0.0 collective-permute-done.16
  65.2 2.6 %field.1 = f32[2048,256]{1,0:T(8,128)} custom-call(f32[2048,256]{1,0:T(8,128)S(1)} %get-tuple-element.94.level, bf16[2048,256]{1,0:T(8,128)(2,1)S(1)} %get-tuple-element.95.high, bf16[2048,256]{1,0:T(8,128)(2,1)S(1)} %get-tuple-element.96.low, f32[256,256]{1,0:T(8,128)S(1)} %root_second.1.inverse, f32[512,128]{1,0:T(8,128)S(1)} %pad_maximum_fusion.4.side), custom_call_target="tpu_custom_call" | custom-call | flops 805306368 | bytes 6291456 | tf_op jit(solution)/shard_map/field/pallas_call | solution.py:468
  (30 shorter events, 0.6 us)
Async XLA Ops:
  0.6 5.0 %copy-start = (f32[2048,256]{1,0:T(8,128)S(1)}, f32[2048,256]{1,0:T(8,128)}, u32[]{:S(2)}) copy-start(f32[2048,256]{1,0:T(8,128)} %sources.3) | copy-start | bytes 6291460
  5.1 3.1 %collective-permute-start = (f32[520,128]{1,0:T(8,128)S(1)}, f32[520,128]{1,0:T(8,128)S(1)}, u32[]{:S(2)}, u32[]{:S(2)}) collective-permute-start(f32[520,128]{1,0:T(8,128)S(1)} %get-tuple-element.63), channel_id=1, source_target_pairs={{0,1},{1,0},{2,3},{3,2},{4,5},{5,4},{6,7},{7,6},{8,9},{9,8},{10,11... | collective-permute-start | bytes 798728 | tf_op jit(solution)/shard_map/ppermute | solution.py:481
  8.2 7.0 %collective-permute-start.2 = (f32[512,128]{1,0:T(8,128)S(1)}, f32[512,128]{1,0:T(8,128)S(1)}, u32[]{:S(2)}, u32[]{:S(2)}) collective-permute-start(f32[512,128]{1,0:T(8,128)S(1)} %get-tuple-element.66), channel_id=1, source_target_pairs={{0,1},{1,0},{2,3},{3,2},{4,5},{5,4},{6,7},{7,6},{8,9},{9,8},{10,11... | collective-permute-start | bytes 786440 | tf_op jit(solution)/shard_map/ppermute | solution.py:481
  8.4 6.7 %collective-permute-start.1 = (f32[264,128]{1,0:T(8,128)S(1)}, f32[264,128]{1,0:T(8,128)S(1)}, u32[]{:S(2)}, u32[]{:S(2)}) collective-permute-start(f32[264,128]{1,0:T(8,128)S(1)} %slice_select_fusion.1), channel_id=1, source_target_pairs={{0,4},{1,5},{2,6},{3,7},{4,0},{5,1},{6,2},{7,3},{8,12},{9,13},{10,... | collective-permute-start | bytes 405512 | tf_op jit(solution)/shard_map/ppermute | solution.py:481
  15.2 6.2 %collective-permute-start.4 = (f32[256,128]{1,0:T(8,128)S(1)}, f32[256,128]{1,0:T(8,128)S(1)}, u32[]{:S(2)}, u32[]{:S(2)}) collective-permute-start(f32[256,128]{1,0:T(8,128)S(1)} %slice_select_fusion.2), channel_id=1, source_target_pairs={{0,4},{1,5},{2,6},{3,7},{4,0},{5,1},{6,2},{7,3},{8,12},{9,13},{10,... | collective-permute-start | bytes 393224 | tf_op jit(solution)/shard_map/ppermute | solution.py:481
  17.1 4.4 %collective-permute-start.3 = (f32[136,128]{1,0:T(8,128)S(1)}, f32[136,128]{1,0:T(8,128)S(1)}, u32[]{:S(2)}, u32[]{:S(2)}) collective-permute-start(f32[136,128]{1,0:T(8,128)S(1)} %slice_select_fusion.4), channel_id=1, source_target_pairs={{0,8},{1,9},{2,10},{3,11},{4,12},{5,13},{6,14},{7,15},{8,0},{9,1},... | collective-permute-start | bytes 208904 | tf_op jit(solution)/shard_map/ppermute | solution.py:481
  21.5 7.7 %collective-permute-start.5 = (f32[136,128]{1,0:T(8,128)S(1)}, f32[136,128]{1,0:T(8,128)S(1)}, u32[]{:S(2)}, u32[]{:S(2)}) collective-permute-start(f32[136,128]{1,0:T(8,128)S(1)} %select_add_fusion.2), channel_id=1, source_target_pairs={{0,16},{1,17},{2,18},{3,19},{4,20},{5,21},{6,22},{7,23},{8,24},{9,... | collective-permute-start | bytes 208904 | tf_op jit(solution)/shard_map/ppermute | solution.py:481
  24.2 5.0 %collective-permute-start.6 = (f32[128,128]{1,0:T(8,128)S(1)}, f32[128,128]{1,0:T(8,128)S(1)}, u32[]{:S(2)}, u32[]{:S(2)}) collective-permute-start(f32[128,128]{1,0:T(8,128)S(1)} %slice_select_fusion.5), channel_id=1, source_target_pairs={{0,8},{1,9},{2,10},{3,11},{4,12},{5,13},{6,14},{7,15},{8,0},{9,1},... | collective-permute-start | bytes 196616 | tf_op jit(solution)/shard_map/ppermute | solution.py:481
  29.3 7.5 %collective-permute-start.7 = (f32[136,128]{1,0:T(8,128)S(1)}, f32[136,128]{1,0:T(8,128)S(1)}, u32[]{:S(2)}, u32[]{:S(2)}) collective-permute-start(f32[136,128]{1,0:T(8,128)S(1)} %add.39), channel_id=1, source_target_pairs={{0,8},{1,9},{2,10},{3,11},{4,12},{5,13},{6,14},{7,15},{8,0},{9,1},... | collective-permute-start | bytes 208904 | tf_op jit(solution)/shard_map/ppermute | solution.py:481
  30.9 5.8 %collective-permute-start.8 = (f32[128,128]{1,0:T(8,128)S(1)}, f32[128,128]{1,0:T(8,128)S(1)}, u32[]{:S(2)}, u32[]{:S(2)}) collective-permute-start(f32[128,128]{1,0:T(8,128)S(1)} %select_add_fusion.3), channel_id=1, source_target_pairs={{0,16},{1,17},{2,18},{3,19},{4,20},{5,21},{6,22},{7,23},{8,24},{9,... | collective-permute-start | bytes 196616 | tf_op jit(solution)/shard_map/ppermute | solution.py:481
  36.8 6.9 %copy-start.1 = (f32[2,256,256]{2,1,0:T(8,128)S(1)}, f32[2,256,256]{2,1,0:T(8,128)}, u32[]{:S(2)}) copy-start(f32[2,256,256]{2,1,0:T(8,128)} %coupling.1) | copy-start | bytes 1572868
  36.8 5.1 %collective-permute-start.9 = (f32[264,128]{1,0:T(8,128)S(1)}, f32[264,128]{1,0:T(8,128)S(1)}, u32[]{:S(2)}, u32[]{:S(2)}) collective-permute-start(f32[264,128]{1,0:T(8,128)S(1)} %pad_maximum_fusion.5), channel_id=1, source_target_pairs={{0,4},{1,5},{2,6},{3,7},{4,0},{5,1},{6,2},{7,3},{8,12},{9,13},{10,... | collective-permute-start | bytes 405512 | tf_op jit(solution)/shard_map/ppermute | solution.py:481
  37.4 4.3 %collective-permute-start.10 = (f32[128,128]{1,0:T(8,128)S(1)}, f32[128,128]{1,0:T(8,128)S(1)}, u32[]{:S(2)}, u32[]{:S(2)}) collective-permute-start(f32[128,128]{1,0:T(8,128)S(1)} %add.41), channel_id=1, source_target_pairs={{0,8},{1,9},{2,10},{3,11},{4,12},{5,13},{6,14},{7,15},{8,0},{9,1},... | collective-permute-start | bytes 196616 | tf_op jit(solution)/shard_map/ppermute | solution.py:481
  42.0 1.6 %collective-permute-start.12 = (f32[520,128]{1,0:T(8,128)S(1)}, f32[520,128]{1,0:T(8,128)S(1)}, u32[]{:S(2)}, u32[]{:S(2)}) collective-permute-start(f32[520,128]{1,0:T(8,128)S(1)} %pad_maximum_fusion.2), channel_id=1, source_target_pairs={{0,1},{1,0},{2,3},{3,2},{4,5},{5,4},{6,7},{7,6},{8,9},{9,8},{10,11... | collective-permute-start | bytes 798728 | tf_op jit(solution)/shard_map/ppermute | solution.py:481
  42.1 6.3 %collective-permute-start.11 = (f32[256,128]{1,0:T(8,128)S(1)}, f32[256,128]{1,0:T(8,128)S(1)}, u32[]{:S(2)}, u32[]{:S(2)}) collective-permute-start(f32[256,128]{1,0:T(8,128)S(1)} %pad_maximum_fusion.6), channel_id=1, source_target_pairs={{0,4},{1,5},{2,6},{3,7},{4,0},{5,1},{6,2},{7,3},{8,12},{9,13},{10,... | collective-permute-start | bytes 393224 | tf_op jit(solution)/shard_map/ppermute | solution.py:481
  48.5 5.0 %collective-permute-start.13 = (f32[512,128]{1,0:T(8,128)S(1)}, f32[512,128]{1,0:T(8,128)S(1)}, u32[]{:S(2)}, u32[]{:S(2)}) collective-permute-start(f32[512,128]{1,0:T(8,128)S(1)} %pad_maximum_fusion.3), channel_id=1, source_target_pairs={{0,1},{1,0},{2,3},{3,2},{4,5},{5,4},{6,7},{7,6},{8,9},{9,8},{10,11... | collective-permute-start | bytes 786440 | tf_op jit(solution)/shard_map/ppermute | solution.py:481
  51.8 6.1 %collective-permute-start.15 = (f32[264,128]{1,0:T(8,128)S(1)}, f32[264,128]{1,0:T(8,128)S(1)}, u32[]{:S(2)}, u32[]{:S(2)}) collective-permute-start(f32[264,128]{1,0:T(8,128)S(1)} %get-tuple-element.98), channel_id=1, source_target_pairs={{0,2},{1,3},{2,0},{3,1},{4,6},{5,7},{6,4},{7,5},{8,10},{9,11},{10,... | collective-permute-start | bytes 405512 | tf_op jit(solution)/shard_map/ppermute | solution.py:481
  53.5 4.4 %copy-start.2 = (f32[256,256]{1,0:T(8,128)S(1)}, f32[256,256]{1,0:T(8,128)}, u32[]{:S(2)}) copy-start(f32[256,256]{1,0:T(8,128)} %param.9) | copy-start | bytes 786436
  57.4 5.5 %collective-permute-start.14 = (f32[256,128]{1,0:T(8,128)S(1)}, f32[256,128]{1,0:T(8,128)S(1)}, u32[]{:S(2)}, u32[]{:S(2)}) collective-permute-start(f32[256,128]{1,0:T(8,128)S(1)} %slice_select_fusion), channel_id=1, source_target_pairs={{0,2},{1,3},{2,0},{3,1},{4,6},{5,7},{6,4},{7,5},{8,10},{9,11},{10,... | collective-permute-start | bytes 393224 | tf_op jit(solution)/shard_map/ppermute | solution.py:481
  62.9 2.1 %collective-permute-start.16 = (f32[256,128]{1,0:T(8,128)S(1)}, f32[256,128]{1,0:T(8,128)S(1)}, u32[]{:S(2)}, u32[]{:S(2)}) collective-permute-start(f32[256,128]{1,0:T(8,128)S(1)} %add.43), channel_id=1, source_target_pairs={{0,1},{1,0},{2,3},{3,2},{4,5},{5,4},{6,7},{7,6},{8,9},{9,8},{10,11... | collective-permute-start | bytes 393224 | tf_op jit(solution)/shard_map/ppermute | solution.py:481

commit v12 on v11

--- a/solution.py
+++ b/solution.py
@@ -150,7 +150,7 @@
     store_halves(packed, keep, send)
 
 
-def source_gram_kernel(b2, b1, sources, keep, send, acc, packed):
+def source_gram_kernel(b2, b1, sources, packed, acc):
     acc[...] = jnp.zeros_like(acc)
 
     def step(tile, carry):
@@ -165,7 +165,6 @@
     lax.fori_loop(0, b2.shape[0] // TILE, step, 0)
     store_square(packed, PROJECTED, acc[0])
     store_square(packed, SIDE, acc[1])
-    store_halves(packed, keep, send)
 
 
 def cost(passes, rows, arrays):
@@ -194,11 +193,10 @@
 
 
 def source_gram(b2, b1, sources):
-    part = jax.ShapeDtypeStruct((half_of(SOURCE_TERMS), LANES), F32)
     return pl.pallas_call(
         source_gram_kernel,
-        out_shape=(part, part),
-        scratch_shapes=[pltpu.VMEM((2, R, R), F32), pltpu.VMEM((SOURCE_TERMS, LANES), F32)],
+        out_shape=jax.ShapeDtypeStruct((SOURCE_TERMS, LANES), F32),
+        scratch_shapes=[pltpu.VMEM((2, R, R), F32)],
         compiler_params=pltpu.CompilerParams(vmem_limit_bytes=VMEM_LIMIT),
         cost_estimate=cost(6, b2.shape[0], 3),
         name="source_gram",
@@ -476,9 +474,9 @@
     )(*args)
 
 
-def exchange(x, mask):
+def exchange(x, mask, senders=(0, 1)):
     count = lax.axis_size(AXES)
-    return lax.ppermute(x, AXES, [(i, i ^ mask) for i in range(count)])
+    return lax.ppermute(x, AXES, [(i, i ^ mask) for i in range(count) if i & 1 in senders])
 
 
 def choose(x, upper):
@@ -498,8 +496,8 @@
 
 
 class Chain:
-    def __init__(self, value, upper):
-        self.value, self.upper, self.sizes = value, upper, {}
+    def __init__(self, value, upper, senders=(0, 1)):
+        self.value, self.upper, self.senders, self.sizes = value, upper, senders, {}
 
     def start(self, kind, bit):
         self.kind, self.bit = kind, bit
@@ -507,7 +505,7 @@
         if kind == "scatter":
             self.sizes[bit] = self.value.shape[0]
             self.value, sent = choose(self.value, self.upper[bit])
-        self.flying = exchange(sent, 1 << bit)
+        self.flying = exchange(sent, 1 << bit, self.senders)
 
     def finish(self):
         if self.kind == "gather":
@@ -525,17 +523,17 @@
 
     keep, send, b2, b1 = panel_gram(q_two, q_one)
     arriving = exchange(send, 1)
-    source_keep, source_send = source_gram(b2, b1, sources)
-    arriving, source_send = lax.optimization_barrier((arriving, source_send))
+    source_terms = source_gram(b2, b1, sources)
+    arriving, source_terms = lax.optimization_barrier((arriving, source_terms))
 
     panels = Chain(keep + arriving, upper)
-    source = Chain(source_keep, upper)
-    panels.sizes[0], source.sizes[0] = PANEL_TERMS, SOURCE_TERMS
-    source_left = [("gather", 0)] + stages[::-1]
+    source = Chain(source_terms, upper, (1,))
+    panels.sizes[0] = PANEL_TERMS
+    source_left = stages[::-1]
     for step, stage in enumerate(stages):
         panels.start(*stage)
         if step == 0:
-            source.kind, source.bit, source.flying = "sum", 0, exchange(source_send, 1)
+            source.kind, source.bit, source.flying = "sum", 0, exchange(source_terms, 1, (0,))
         else:
             source.start(*source_left.pop())
         panels.flying, source.flying = lax.optimization_barrier((panels.flying, source.flying))
@@ -549,18 +547,18 @@
     parts = invert_middle(parts, "level_middle")
     source.flying, parts = lax.optimization_barrier((source.flying, parts))
     source.finish()
-    source.start(*source_left.pop())
+    source_arriving = exchange(source.value, 1, (1,))
     inverse = invert_second(parts, "level_second")
     x, root = call(
         panel_solve_kernel, (SQUARE, jax.ShapeDtypeStruct((SYMMETRIC, LANES), F32)), (inverse, terms), "panel_solve"
     )
-    source.flying, x = lax.optimization_barrier((source.flying, x))
-    source.finish()
+    source_arriving, x = lax.optimization_barrier((source_arriving, x))
+    source_sums = jnp.where(upper[0], source.value, source_arriving)
     arriving = exchange(root, 2)
     rows = b2.shape[0]
     shapes = [jax.ShapeDtypeStruct((rows, R), kind) for kind in (F32, BF16, BF16)]
     shapes.append(jax.ShapeDtypeStruct((FULL, LANES), F32))
-    args = [b2, b1, sources, x, inverse, source.value]
+    args = [b2, b1, sources, x, inverse, source_sums]
     panel_one, level, high, low, side = update(panel_kernel, args, 8, "panel", shapes)
     side = Chain(choose(side, upper[0])[0], upper)
     side.sizes[0] = FULL

time: 68.1 us -> 72.9 us (1.070)
  starting transfers between devices: 18.7 us -> 27.3 us
  waiting for transfers between devices: 19.3 us -> 15.4 us
    ppermute x17, starting transfers between devices: 18.7 us -> 27.3 us  [exchange(): lax.ppermute(x, AXES, [(i, i ^ mask) for i in range(count) if i & 1 in se...]
    ppermute x17, waiting for transfers between devices: 19.3 us -> 15.4 us  [exchange(): lax.ppermute(x, AXES, [(i, i ^ mask) for i in range(count) if i & 1 in se...]
  transfers between devices with their start and end apart: 17 -> 17, of which waited for: 8 -> 7; matrix products, arithmetic and copies ran while one was open for 1% -> 0% of each run, Pallas kernels for 31% -> 29%
where the time goes in v12:
time: 72.9 us; the launch traced here: 72.7 us
  Pallas kernels  28.1 us (39%)
  starting transfers between devices  27.3 us (37%)
  waiting for transfers between devices  15.4 us (21%)
  between operations  1.18 us (2%)
  other arithmetic  0.76 us (1%)
    ppermute x17, starting transfers between devices, exchange(): lax.ppermute(x, AXES, [(i, i ^ mask) for i in range(count) if i & 1 in se...  27.3 us
    ppermute x17, waiting for transfers between devices, exchange(): lax.ppermute(x, AXES, [(i, i ^ mask) for i in range(count) if i & 1 in se...  15.4 us
    pallas_call x7, Pallas kernels, call(): pl.pallas_call(kernel, out_shape=out_shape, scratch_shapes=list(scratch),...  14.7 us
    pallas_call x2, Pallas kernels, update(): pl.pallas_call(kernel, out_specs=[pl.BlockSpec(memory_space=pl.ANY)] + [p...  6.43 us
    pallas_call x1, Pallas kernels, panel_gram(): pl.pallas_call(panel_gram_kernel, in_specs=[pl.BlockSpec(memory_space=pl....  4.47 us
    pallas_call x1, Pallas kernels, source_gram(): pl.pallas_call(source_gram_kernel, out_shape=jax.ShapeDtypeStruct((SOURCE...  2.52 us
  transfers between devices with their start and end apart: 17, of which 7 were waited for; matrix products, arithmetic and copies ran while one was open for 0% of the time, Pallas kernels for 29%

profile of v12, /device:TPU:0, one launch (start us, length us, event | category | flops | bytes accessed | tf_op | source)
XLA Modules:
  0.0 72.7 jit_solution(6143610000404183832)
XLA Ops:
  0.6 0.0 copy-start
  0.6 4.5 %panel_gram.1 = (f32[520,128]{1,0:T(8,128)S(1)}, f32[520,128]{1,0:T(8,128)S(1)}, f32[2048,256]{1,0:T(8,128)S(1)}, f32[2048,256]{1,0:T(8,128)S(1)}) custom-call(f32[2048,256]{1,0:T(8,128)} %q_two, f32[2048,256]{1,0:T(8,128)} %q_one.1), custom_call_target="tpu_custom_call" | custom-call | flops 1879048192 | bytes 4194304 | tf_op jit(solution)/shard_map/panel_gram/pallas_call | solution.py:180
  5.1 0.5 collective-permute-start
  5.6 0.0 copy-done
  5.6 2.5 %source_gram.1 = f32[1024,128]{1,0:T(8,128)S(1)} custom-call(f32[2048,256]{1,0:T(8,128)S(1)} %get-tuple-element.56.b2, f32[2048,256]{1,0:T(8,128)S(1)} %get-tuple-element.57.b1, f32[2048,256]{1,0:T(8,128)S(1)} %copy-done), custom_call_target="tpu_custom_call" | custom-call | flops 1610612736 | bytes 6291456 | tf_op jit(solution)/shard_map/source_gram/pallas_call | solution.py:196
  8.2 0.0 collective-permute-done
  8.2 2.0 %collective-permute-start.2 = (f32[1024,128]{1,0:T(8,128)S(1)}, f32[1024,128]{1,0:T(8,128)S(1)}, u32[]{:S(2)}, u32[]{:S(2)}) collective-permute-start(f32[1024,128]{1,0:T(8,128)S(1)} %source_gram.1), channel_id=1, source_target_pairs={{0,1},{2,3},{4,5},{6,7},{8,9},{10,11},{12,13},{14,15},{16,17},{18,... | collective-permute-start | bytes 1572872 | tf_op jit(solution)/shard_map/ppermute | solution.py:479
  10.3 3.0 %collective-permute-start.1 = (f32[264,128]{1,0:T(8,128)S(1)}, f32[264,128]{1,0:T(8,128)S(1)}, u32[]{:S(2)}, u32[]{:S(2)}) collective-permute-start(f32[264,128]{1,0:T(8,128)S(1)} %slice_select_fusion.2), channel_id=1, source_target_pairs={{0,4},{1,5},{2,6},{3,7},{4,0},{5,1},{6,2},{7,3},{8,12},{9,13},{10,... | collective-permute-start | bytes 405512 | tf_op jit(solution)/shard_map/ppermute | solution.py:479
  13.3 3.1 %collective-permute-done.1 = f32[264,128]{1,0:T(8,128)S(1)} collective-permute-done((f32[264,128]{1,0:T(8,128)S(1)}, f32[264,128]{1,0:T(8,128)S(1)}, u32[]{:S(2)}, u32[]{:S(2)}) %collective-permute-start.1) | collective-permute-done | bytes 135200 | tf_op jit(solution)/shard_map/ppermute | solution.py:479
  16.4 0.0 collective-permute-done.2
  16.4 0.1 add.36
  16.5 0.7 collective-permute-start.4
  17.2 2.1 %collective-permute-start.3 = (f32[136,128]{1,0:T(8,128)S(1)}, f32[136,128]{1,0:T(8,128)S(1)}, u32[]{:S(2)}, u32[]{:S(2)}) collective-permute-start(f32[136,128]{1,0:T(8,128)S(1)} %slice_select_fusion.5), channel_id=1, source_target_pairs={{0,8},{1,9},{2,10},{3,11},{4,12},{5,13},{6,14},{7,15},{8,0},{9,1},... | collective-permute-start | bytes 208904 | tf_op jit(solution)/shard_map/ppermute | solution.py:479
  19.3 3.0 %collective-permute-done.3 = f32[136,128]{1,0:T(8,128)S(1)} collective-permute-done((f32[136,128]{1,0:T(8,128)S(1)}, f32[136,128]{1,0:T(8,128)S(1)}, u32[]{:S(2)}, u32[]{:S(2)}) %collective-permute-start.3) | collective-permute-done | bytes 69664 | tf_op jit(solution)/shard_map/ppermute | solution.py:479
  22.2 0.0 collective-permute-done.4
  22.3 0.7 collective-permute-start.6
  23.0 2.9 %collective-permute-start.5 = (f32[136,128]{1,0:T(8,128)S(1)}, f32[136,128]{1,0:T(8,128)S(1)}, u32[]{:S(2)}, u32[]{:S(2)}) collective-permute-start(f32[136,128]{1,0:T(8,128)S(1)} %select_add_fusion.3), channel_id=1, source_target_pairs={{0,16},{1,17},{2,18},{3,19},{4,20},{5,21},{6,22},{7,23},{8,24},{9,... | collective-permute-start | bytes 208904 | tf_op jit(solution)/shard_map/ppermute | solution.py:479
  25.9 2.5 %collective-permute-done.5 = f32[136,128]{1,0:T(8,128)S(1)} collective-permute-done((f32[136,128]{1,0:T(8,128)S(1)}, f32[136,128]{1,0:T(8,128)S(1)}, u32[]{:S(2)}, u32[]{:S(2)}) %collective-permute-start.5) | collective-permute-done | bytes 69664 | tf_op jit(solution)/shard_map/ppermute | solution.py:479
  28.4 0.0 collective-permute-done.6
  28.4 0.7 collective-permute-start.8
  29.1 2.2 %collective-permute-start.7 = (f32[136,128]{1,0:T(8,128)S(1)}, f32[136,128]{1,0:T(8,128)S(1)}, u32[]{:S(2)}, u32[]{:S(2)}) collective-permute-start(f32[136,128]{1,0:T(8,128)S(1)} %add.39), channel_id=1, source_target_pairs={{0,8},{1,9},{2,10},{3,11},{4,12},{5,13},{6,14},{7,15},{8,0},{9,1},... | collective-permute-start | bytes 208904 | tf_op jit(solution)/shard_map/ppermute | solution.py:479
  31.3 2.3 %collective-permute-done.7 = f32[136,128]{1,0:T(8,128)S(1)} collective-permute-done((f32[136,128]{1,0:T(8,128)S(1)}, f32[136,128]{1,0:T(8,128)S(1)}, u32[]{:S(2)}, u32[]{:S(2)}) %collective-permute-start.7) | collective-permute-done | bytes 69664 | tf_op jit(solution)/shard_map/ppermute | solution.py:479
  33.6 0.0 collective-permute-done.8
  33.7 1.2 %collective-permute-start.9 = (f32[264,128]{1,0:T(8,128)S(1)}, f32[264,128]{1,0:T(8,128)S(1)}, u32[]{:S(2)}, u32[]{:S(2)}) collective-permute-start(f32[264,128]{1,0:T(8,128)S(1)} %pad_maximum_fusion.5), channel_id=1, source_target_pairs={{0,4},{1,5},{2,6},{3,7},{4,0},{5,1},{6,2},{7,3},{8,12},{9,13},{10,... | collective-permute-start | bytes 405512 | tf_op jit(solution)/shard_map/ppermute | solution.py:479
  34.9 0.7 collective-permute-start.10
  35.6 0.0 collective-permute-done.10
  35.6 3.2 %collective-permute-done.9 = f32[264,128]{1,0:T(8,128)S(1)} collective-permute-done((f32[264,128]{1,0:T(8,128)S(1)}, f32[264,128]{1,0:T(8,128)S(1)}, u32[]{:S(2)}, u32[]{:S(2)}) %collective-permute-start.9) | collective-permute-done | bytes 135200 | tf_op jit(solution)/shard_map/ppermute | solution.py:479
  38.8 0.0 copy-start.1
  38.8 6.3 %collective-permute-start.12 = (f32[520,128]{1,0:T(8,128)S(1)}, f32[520,128]{1,0:T(8,128)S(1)}, u32[]{:S(2)}, u32[]{:S(2)}) collective-permute-start(f32[520,128]{1,0:T(8,128)S(1)} %pad_maximum_fusion.2), channel_id=1, source_target_pairs={{0,1},{1,0},{2,3},{3,2},{4,5},{5,4},{6,7},{7,6},{8,9},{9,8},{10,11... | collective-permute-start | bytes 798728 | tf_op jit(solution)/shard_map/ppermute | solution.py:479
  45.2 0.7 collective-permute-start.11
  45.8 0.4 collective-permute-done.12
  46.4 0.0 copy-done.1
  46.4 3.3 %level_first.1 = (f32[128,128]{1,0:T(8,128)S(1)}, f32[128,128]{1,0:T(8,128)S(1)}, f32[128,128]{1,0:T(8,128)S(1)}, f32[8,256]{1,0:T(8,128)S(1)}, f32[256,128]{1,0:T(8,128)S(1)}) custom-call(f32[1040,128]{1,0:T(8,128)S(1)} %pad_maximum_fusion.gram_ref.terms, f32[2,256,256]{2,1,0:T(8,128)S(1)} %copy-done.1), custom_call_target="tpu_custom_call" | custom-call | flops 5000000000 | bytes 262144 | tf_op jit(solution)/shard_map/level_first/pallas_call | solution.py:328
  49.7 1.4 %level_middle.1.swept = f32[128,128]{1,0:T(8,128)S(1)} custom-call(f32[128,128]{1,0:T(8,128)S(1)} %get-tuple-element.77.rest), custom_call_target="tpu_custom_call" | custom-call | flops 2500000000 | bytes 262144 | tf_op jit(solution)/shard_map/level_middle/pallas_call | solution.py:328
  51.1 0.0 collective-permute-done.11
  51.2 1.5 %collective-permute-start.13 = (f32[1024,128]{1,0:T(8,128)S(1)}, f32[1024,128]{1,0:T(8,128)S(1)}, u32[]{:S(2)}, u32[]{:S(2)}) collective-permute-start(f32[1024,128]{1,0:T(8,128)S(1)} %pad_maximum_fusion.1), channel_id=1, source_target_pairs={{1,0},{3,2},{5,4},{7,6},{9,8},{11,10},{13,12},{15,14},{17,16},{19,... | collective-permute-start | bytes 1572872 | tf_op jit(solution)/shard_map/ppermute | solution.py:479
  52.7 2.1 %level_second.1.inverse = f32[256,256]{1,0:T(8,128)S(1)} custom-call(f32[128,128]{1,0:T(8,128)S(1)} %get-tuple-element.81.first, f32[128,128]{1,0:T(8,128)S(1)} %get-tuple-element.82.across, f32[128,128]{1,0:T(8,128)S(1)} %level_middle.1.swept, f32[8,256]{1,0:T(8,128)S(1)} %get-tuple-element.84.row, f32[256,128]{1,0:T(8,128)S(1)} %get-tuple-element.85.col), custom_call_target="tpu_custom_call" | custom-call | flops 2500000000 | bytes 262144 | tf_op jit(solution)/shard_map/level_second/pallas_call | solution.py:328
  54.7 1.1 %panel_solve.1 = (f32[256,256]{1,0:T(8,128)S(1)}, f32[264,128]{1,0:T(8,128)S(1)}) custom-call(f32[256,256]{1,0:T(8,128)S(1)} %level_second.1.inverse, f32[1040,128]{1,0:T(8,128)S(1)} %pad_maximum_fusion.gram_ref.terms), custom_call_target="tpu_custom_call" | custom-call | bytes 262144 | tf_op jit(solution)/shard_map/panel_solve/pallas_call | solution.py:328
  55.8 1.5 %collective-permute-start.15 = (f32[264,128]{1,0:T(8,128)S(1)}, f32[264,128]{1,0:T(8,128)S(1)}, u32[]{:S(2)}, u32[]{:S(2)}) collective-permute-start(f32[264,128]{1,0:T(8,128)S(1)} %get-tuple-element.94), channel_id=1, source_target_pairs={{0,2},{1,3},{2,0},{3,1},{4,6},{5,7},{6,4},{7,5},{8,10},{9,11},{10,... | collective-permute-start | bytes 405512 | tf_op jit(solution)/shard_map/ppermute | solution.py:479
  57.4 0.0 collective-permute-done.13
  57.4 0.1 broadcast_select_fusion.terms
  57.4 0.0 copy-start.2
  57.4 3.8 %panel.1 = (f32[2048,256]{1,0:T(8,128)}, f32[2048,256]{1,0:T(8,128)S(1)}, bf16[2048,256]{1,0:T(8,128)(2,1)S(1)}, bf16[2048,256]{1,0:T(8,128)(2,1)S(1)}, f32[512,128]{1,0:T(8,128)S(1)}) custom-call(f32[2048,256]{1,0:T(8,128)S(1)} %get-tuple-element.56.b2, f32[2048,256]{1,0:T(8,128)S(1)} %get-tuple-element.57.b1, f32[2048,256]{1,0:T(8,128)S(1)} %copy-done, ...), custom_call_target="tpu_custom_call" | custom-call | flops 2147483648 | bytes 6291456 | tf_op jit(solution)/shard_map/panel/pallas_call | solution.py:466
  61.3 0.6 collective-permute-start.14
  61.9 0.0 collective-permute-done.15
  61.9 0.0 copy-done.2
  61.9 3.3 %root_first.1 = (f32[128,128]{1,0:T(8,128)S(1)}, f32[128,128]{1,0:T(8,128)S(1)}, f32[128,128]{1,0:T(8,128)S(1)}, f32[8,256]{1,0:T(8,128)S(1)}, f32[256,128]{1,0:T(8,128)S(1)}) custom-call(f32[264,128]{1,0:T(8,128)S(1)} %add.42.gram_ref, f32[1,256,256]{2,1,0:T(8,128)S(1)} %bitcast.1), custom_call_target="tpu_custom_call" | custom-call | flops 5000000000 | bytes 262144 | tf_op jit(solution)/shard_map/root_first/pallas_call | solution.py:328
  65.3 1.4 %root_middle.1.swept = f32[128,128]{1,0:T(8,128)S(1)} custom-call(f32[128,128]{1,0:T(8,128)S(1)} %get-tuple-element.98.rest), custom_call_target="tpu_custom_call" | custom-call | flops 2500000000 | bytes 262144 | tf_op jit(solution)/shard_map/root_middle/pallas_call | solution.py:328
  66.7 0.8 %collective-permute-done.14 = f32[256,128]{1,0:T(8,128)S(1)} collective-permute-done((f32[256,128]{1,0:T(8,128)S(1)}, f32[256,128]{1,0:T(8,128)S(1)}, u32[]{:S(2)}, u32[]{:S(2)}) %collective-permute-start.14) | collective-permute-done | bytes 131104 | tf_op jit(solution)/shard_map/ppermute | solution.py:479
  67.5 0.2 collective-permute-start.16
  67.8 2.1 %root_second.1.inverse = f32[256,256]{1,0:T(8,128)S(1)} custom-call(f32[128,128]{1,0:T(8,128)S(1)} %get-tuple-element.101.first, f32[128,128]{1,0:T(8,128)S(1)} %get-tuple-element.102.across, f32[128,128]{1,0:T(8,128)S(1)} %root_middle.1.swept, f32[8,256]{1,0:T(8,128)S(1)} %get-tuple-element.104.row, f32[256,128]{1,0:T(8,128)S(1)} %get-tuple-element.105.col), custom_call_target="tpu_custom_call" | custom-call | flops 2500000000 | bytes 262144 | tf_op jit(solution)/shard_map/root_second/pallas_call | solution.py:328
  69.8 0.0 collective-permute-done.16
  69.9 2.6 %field.1 = f32[2048,256]{1,0:T(8,128)} custom-call(f32[2048,256]{1,0:T(8,128)S(1)} %get-tuple-element.90.level, bf16[2048,256]{1,0:T(8,128)(2,1)S(1)} %get-tuple-element.91.high, bf16[2048,256]{1,0:T(8,128)(2,1)S(1)} %get-tuple-element.92.low, f32[256,256]{1,0:T(8,128)S(1)} %root_second.1.inverse, f32[512,128]{1,0:T(8,128)S(1)} %pad_maximum_fusion.4.side), custom_call_target="tpu_custom_call" | custom-call | flops 805306368 | bytes 6291456 | tf_op jit(solution)/shard_map/field/pallas_call | solution.py:466
  (28 shorter events, 0.6 us)
Async XLA Ops:
  0.6 5.0 %copy-start = (f32[2048,256]{1,0:T(8,128)S(1)}, f32[2048,256]{1,0:T(8,128)}, u32[]{:S(2)}) copy-start(f32[2048,256]{1,0:T(8,128)} %sources.3) | copy-start | bytes 6291460
  5.1 3.1 %collective-permute-start = (f32[520,128]{1,0:T(8,128)S(1)}, f32[520,128]{1,0:T(8,128)S(1)}, u32[]{:S(2)}, u32[]{:S(2)}) collective-permute-start(f32[520,128]{1,0:T(8,128)S(1)} %get-tuple-element.61), channel_id=1, source_target_pairs={{0,1},{1,0},{2,3},{3,2},{4,5},{5,4},{6,7},{7,6},{8,9},{9,8},{10,11... | collective-permute-start | bytes 798728 | tf_op jit(solution)/shard_map/ppermute | solution.py:479
  8.2 8.2 %collective-permute-start.2 = (f32[1024,128]{1,0:T(8,128)S(1)}, f32[1024,128]{1,0:T(8,128)S(1)}, u32[]{:S(2)}, u32[]{:S(2)}) collective-permute-start(f32[1024,128]{1,0:T(8,128)S(1)} %source_gram.1), channel_id=1, source_target_pairs={{0,1},{2,3},{4,5},{6,7},{8,9},{10,11},{12,13},{14,15},{16,17},{18,... | collective-permute-start | bytes 1572872 | tf_op jit(solution)/shard_map/ppermute | solution.py:479
  10.3 6.1 %collective-permute-start.1 = (f32[264,128]{1,0:T(8,128)S(1)}, f32[264,128]{1,0:T(8,128)S(1)}, u32[]{:S(2)}, u32[]{:S(2)}) collective-permute-start(f32[264,128]{1,0:T(8,128)S(1)} %slice_select_fusion.2), channel_id=1, source_target_pairs={{0,4},{1,5},{2,6},{3,7},{4,0},{5,1},{6,2},{7,3},{8,12},{9,13},{10,... | collective-permute-start | bytes 405512 | tf_op jit(solution)/shard_map/ppermute | solution.py:479
  16.5 5.8 %collective-permute-start.4 = (f32[512,128]{1,0:T(8,128)S(1)}, f32[512,128]{1,0:T(8,128)S(1)}, u32[]{:S(2)}, u32[]{:S(2)}) collective-permute-start(f32[512,128]{1,0:T(8,128)S(1)} %slice_select_fusion), channel_id=1, source_target_pairs={{1,5},{3,7},{5,1},{7,3},{9,13},{11,15},{13,9},{15,11},{17,21},{19,... | collective-permute-start | bytes 786440 | tf_op jit(solution)/shard_map/ppermute | solution.py:479
  17.2 5.0 %collective-permute-start.3 = (f32[136,128]{1,0:T(8,128)S(1)}, f32[136,128]{1,0:T(8,128)S(1)}, u32[]{:S(2)}, u32[]{:S(2)}) collective-permute-start(f32[136,128]{1,0:T(8,128)S(1)} %slice_select_fusion.5), channel_id=1, source_target_pairs={{0,8},{1,9},{2,10},{3,11},{4,12},{5,13},{6,14},{7,15},{8,0},{9,1},... | collective-permute-start | bytes 208904 | tf_op jit(solution)/shard_map/ppermute | solution.py:479
  22.3 6.1 %collective-permute-start.6 = (f32[256,128]{1,0:T(8,128)S(1)}, f32[256,128]{1,0:T(8,128)S(1)}, u32[]{:S(2)}, u32[]{:S(2)}) collective-permute-start(f32[256,128]{1,0:T(8,128)S(1)} %slice_select_fusion.3), channel_id=1, source_target_pairs={{1,9},{3,11},{5,13},{7,15},{9,1},{11,3},{13,5},{15,7},{17,25},{19,... | collective-permute-start | bytes 393224 | tf_op jit(solution)/shard_map/ppermute | solution.py:479
  23.0 5.4 %collective-permute-start.5 = (f32[136,128]{1,0:T(8,128)S(1)}, f32[136,128]{1,0:T(8,128)S(1)}, u32[]{:S(2)}, u32[]{:S(2)}) collective-permute-start(f32[136,128]{1,0:T(8,128)S(1)} %select_add_fusion.3), channel_id=1, source_target_pairs={{0,16},{1,17},{2,18},{3,19},{4,20},{5,21},{6,22},{7,23},{8,24},{9,... | collective-permute-start | bytes 208904 | tf_op jit(solution)/shard_map/ppermute | solution.py:479
  28.4 5.2 %collective-permute-start.8 = (f32[256,128]{1,0:T(8,128)S(1)}, f32[256,128]{1,0:T(8,128)S(1)}, u32[]{:S(2)}, u32[]{:S(2)}) collective-permute-start(f32[256,128]{1,0:T(8,128)S(1)} %select_add_fusion.2), channel_id=1, source_target_pairs={{1,17},{3,19},{5,21},{7,23},{9,25},{11,27},{13,29},{15,31},{17,1},... | collective-permute-start | bytes 393224 | tf_op jit(solution)/shard_map/ppermute | solution.py:479
  29.1 4.5 %collective-permute-start.7 = (f32[136,128]{1,0:T(8,128)S(1)}, f32[136,128]{1,0:T(8,128)S(1)}, u32[]{:S(2)}, u32[]{:S(2)}) collective-permute-start(f32[136,128]{1,0:T(8,128)S(1)} %add.39), channel_id=1, source_target_pairs={{0,8},{1,9},{2,10},{3,11},{4,12},{5,13},{6,14},{7,15},{8,0},{9,1},... | collective-permute-start | bytes 208904 | tf_op jit(solution)/shard_map/ppermute | solution.py:479
  33.7 5.1 %collective-permute-start.9 = (f32[264,128]{1,0:T(8,128)S(1)}, f32[264,128]{1,0:T(8,128)S(1)}, u32[]{:S(2)}, u32[]{:S(2)}) collective-permute-start(f32[264,128]{1,0:T(8,128)S(1)} %pad_maximum_fusion.5), channel_id=1, source_target_pairs={{0,4},{1,5},{2,6},{3,7},{4,0},{5,1},{6,2},{7,3},{8,12},{9,13},{10,... | collective-permute-start | bytes 405512 | tf_op jit(solution)/shard_map/ppermute | solution.py:479
  34.9 0.7 collective-permute-start.10
  38.8 7.6 %copy-start.1 = (f32[2,256,256]{2,1,0:T(8,128)S(1)}, f32[2,256,256]{2,1,0:T(8,128)}, u32[]{:S(2)}) copy-start(f32[2,256,256]{2,1,0:T(8,128)} %coupling.1) | copy-start | bytes 1572868
  38.8 7.4 %collective-permute-start.12 = (f32[520,128]{1,0:T(8,128)S(1)}, f32[520,128]{1,0:T(8,128)S(1)}, u32[]{:S(2)}, u32[]{:S(2)}) collective-permute-start(f32[520,128]{1,0:T(8,128)S(1)} %pad_maximum_fusion.2), channel_id=1, source_target_pairs={{0,1},{1,0},{2,3},{3,2},{4,5},{5,4},{6,7},{7,6},{8,9},{9,8},{10,11... | collective-permute-start | bytes 798728 | tf_op jit(solution)/shard_map/ppermute | solution.py:479
  45.2 5.9 %collective-permute-start.11 = (f32[512,128]{1,0:T(8,128)S(1)}, f32[512,128]{1,0:T(8,128)S(1)}, u32[]{:S(2)}, u32[]{:S(2)}) collective-permute-start(f32[512,128]{1,0:T(8,128)S(1)} %pad_maximum_fusion.3), channel_id=1, source_target_pairs={{1,5},{3,7},{5,1},{7,3},{9,13},{11,15},{13,9},{15,11},{17,21},{19,... | collective-permute-start | bytes 786440 | tf_op jit(solution)/shard_map/ppermute | solution.py:479
  51.2 6.2 %collective-permute-start.13 = (f32[1024,128]{1,0:T(8,128)S(1)}, f32[1024,128]{1,0:T(8,128)S(1)}, u32[]{:S(2)}, u32[]{:S(2)}) collective-permute-start(f32[1024,128]{1,0:T(8,128)S(1)} %pad_maximum_fusion.1), channel_id=1, source_target_pairs={{1,0},{3,2},{5,4},{7,6},{9,8},{11,10},{13,12},{15,14},{17,16},{19,... | collective-permute-start | bytes 1572872 | tf_op jit(solution)/shard_map/ppermute | solution.py:479
  55.8 6.1 %collective-permute-start.15 = (f32[264,128]{1,0:T(8,128)S(1)}, f32[264,128]{1,0:T(8,128)S(1)}, u32[]{:S(2)}, u32[]{:S(2)}) collective-permute-start(f32[264,128]{1,0:T(8,128)S(1)} %get-tuple-element.94), channel_id=1, source_target_pairs={{0,2},{1,3},{2,0},{3,1},{4,6},{5,7},{6,4},{7,5},{8,10},{9,11},{10,... | collective-permute-start | bytes 405512 | tf_op jit(solution)/shard_map/ppermute | solution.py:479
  57.4 4.5 %copy-start.2 = (f32[256,256]{1,0:T(8,128)S(1)}, f32[256,256]{1,0:T(8,128)}, u32[]{:S(2)}) copy-start(f32[256,256]{1,0:T(8,128)} %param.9) | copy-start | bytes 786436
  61.3 6.2 %collective-permute-start.14 = (f32[256,128]{1,0:T(8,128)S(1)}, f32[256,128]{1,0:T(8,128)S(1)}, u32[]{:S(2)}, u32[]{:S(2)}) collective-permute-start(f32[256,128]{1,0:T(8,128)S(1)} %slice_select_fusion.1), channel_id=1, source_target_pairs={{0,2},{1,3},{2,0},{3,1},{4,6},{5,7},{6,4},{7,5},{8,10},{9,11},{10,... | collective-permute-start | bytes 393224 | tf_op jit(solution)/shard_map/ppermute | solution.py:479
  67.5 2.3 %collective-permute-start.16 = (f32[256,128]{1,0:T(8,128)S(1)}, f32[256,128]{1,0:T(8,128)S(1)}, u32[]{:S(2)}, u32[]{:S(2)}) collective-permute-start(f32[256,128]{1,0:T(8,128)S(1)} %add.43), channel_id=1, source_target_pairs={{0,1},{1,0},{2,3},{3,2},{4,5},{5,4},{6,7},{7,6},{8,9},{9,8},{10,11... | collective-permute-start | bytes 393224 | tf_op jit(solution)/shard_map/ppermute | solution.py:479

commit v13 on v11

--- a/solution.py
+++ b/solution.py
@@ -14,7 +14,7 @@
 R = 256
 LANES = 128
 TILE = 512
-GROUPS = 8
+OUT_TILE = 256
 VMEM_LIMIT = 16 * 1024 * 1024
 SYMMETRIC, FULL = 264, 512
 OWN, ROOT, CROSS, PANEL_TERMS = 0, 264, 528, 1040
@@ -127,11 +127,11 @@
             copy.wait()
         h2, l2 = split2(b2[at, :])
         h1, l1 = split2(b1[at, :])
-        h2t, l2t, h1t = h2.T, l2.T, h1.T
+        h2t, h1t = h2.T, h1.T
         acc[0] += dot(h2t, h2)
         acc[1] += dot(h2t, l2)
-        left = jnp.concatenate([h2t, h2t, l2t], axis=1)
-        acc[2] += dot(left, jnp.concatenate([h1, l1, h1], axis=0))
+        acc[2] += dot(jnp.concatenate([h2t, h2t], axis=1), jnp.concatenate([h1, l1], axis=0))
+        acc[5] += dot(h1t, l2)
         acc[3] += dot(h1t, h1)
         acc[4] += dot(h1t, l1)
 
@@ -146,7 +146,7 @@
     store_symmetric(packed, OWN, acc[0] + low + low.T)
     low = acc[4]
     store_symmetric(packed, ROOT, acc[3] + low + low.T)
-    store_square(packed, CROSS, acc[2])
+    store_square(packed, CROSS, acc[2] + acc[5].T)
     store_halves(packed, keep, send)
 
 
@@ -183,7 +183,7 @@
         in_specs=[pl.BlockSpec(memory_space=pl.ANY)] * 2,
         out_shape=(part, part, tall, tall),
         scratch_shapes=[
-            pltpu.VMEM((5, R, R), F32),
+            pltpu.VMEM((6, R, R), F32),
             pltpu.VMEM((PANEL_TERMS, LANES), F32),
             pltpu.SemaphoreType.DMA((2, rows // TILE + 1)),
         ],
@@ -209,25 +209,8 @@
     return jnp.broadcast_to(x[:, lane : lane + 1], (8, LANES))
 
 
-def sweep_panel(block, start, cols, rows):
-    lane = lax.broadcasted_iota(jnp.int32, (8, LANES), 1)
-    panel = block[start : start + GROUPS]
-    left = stack_left(jnp.concatenate(panel, axis=0))
-    for t in range(GROUPS):
-        panel = eliminate_group(panel, t, start + t, cols, rows)
-    inside = (lane >= 8 * start) & (lane < 8 * (start + GROUPS))
-    panel = [jnp.where(inside, -x, x) for x in panel]
-    change = dot_t(left, stack_right(jnp.concatenate(panel, axis=0)))
-    swept = []
-    for g in range(len(block)):
-        if start <= g < start + GROUPS:
-            swept.append(panel[g - start])
-        else:
-            swept.append(jnp.where(inside, 0.0, block[g]) - change[8 * g : 8 * g + 8, :])
-    return swept
-
-
-def eliminate_group(panel, t, at, cols, rows):
+def eliminate_group(panel, t, cols, rows):
+    at, count = t, len(panel)
     lane = lax.broadcasted_iota(jnp.int32, (8, LANES), 1)
     sub = lax.broadcasted_iota(jnp.int32, (8, LANES), 0)
     for j in range(8):
@@ -244,11 +227,11 @@
         row = jnp.broadcast_to(rows[8 * at + j : 8 * at + j + 1, :], (8, LANES))
         line.append(jnp.where(inside, jnp.where(lane == 8 * at + j, 1.0, 0.0), row))
     after = None
-    if t < GROUPS - 1:
+    if t < count - 1:
         columns = [spread_lane(panel[t + 1], 8 * at + j) for j in range(8)]
         after = [columns, jnp.where(inside, 0.0, panel[t + 1])]
     line, after = solve_small(entry, line, after)
-    for g in range(GROUPS):
+    for g in range(count):
         if g == t + 1:
             panel[g] = after
         elif g != t:
@@ -302,24 +285,14 @@
     return line, block
 
 
-def stack_left(x):
-    h, m, l = split3(x)
-    return jnp.concatenate([h, h, m, h, l, m], axis=0)
-
-
-def stack_right(x):
-    h, m, l = split3(x)
-    return jnp.concatenate([h, m, h, l, h, m], axis=0)
-
-
-def sweep(matrix, panels, cols, rows):
+def eliminate(matrix, groups, cols, rows):
     block = [matrix[8 * i : 8 * i + 8, :] for i in range(LANES // 8)]
-    for panel in panels:
-        block = sweep_panel(block, panel * GROUPS, cols, rows)
+    for t in groups:
+        block = eliminate_group(block, t, cols, rows)
     return jnp.concatenate(block, axis=0)
 
 
-PANELS = LANES // (8 * GROUPS)
+GROUPS = LANES // 8
 
 
 SQUARE = jax.ShapeDtypeStruct((R, R), F32)
@@ -345,7 +318,7 @@
     scale_col = lax.rsqrt(jnp.sum(diagonal, axis=1, keepdims=True))
     matrix = matrix * scale_col * scale_row
     side = matrix[:LANES, LANES:]
-    first = -sweep(matrix[:LANES, :LANES], range(PANELS), cols, rows)
+    first = eliminate(matrix[:LANES, :LANES], range(GROUPS), cols, rows)
     across = dot_full(first, side)
     first_out[...] = first
     across_out[...] = across
@@ -355,17 +328,30 @@
 
 
 def middle_kernel(rest, out, cols, rows):
-    out[...] = sweep(rest[...], range(PANELS - 1), cols, rows)
-
-
-def second_kernel(first, across, swept, row, col, out, cols, rows):
-    second = -sweep(swept[...], range(PANELS - 1, PANELS), cols, rows)
+    out[...] = eliminate(rest[...], range(GROUPS // 2), cols, rows)
+
+
+def finish_inverse(first, across, begun, row, col, cols, rows):
+    second = eliminate(begun[...], range(GROUPS // 2, GROUPS), cols, rows)
     corner = -dot_full(across[...], second)
     top = first[...] - dot_full(corner, across[...].T)
-    out[:LANES, :LANES] = top * col[:LANES, :] * row[:1, :LANES]
-    out[:LANES, LANES:] = corner * col[:LANES, :] * row[:1, LANES:]
-    out[LANES:, :LANES] = corner.T * col[LANES:, :] * row[:1, :LANES]
-    out[LANES:, LANES:] = second * col[LANES:, :] * row[:1, LANES:]
+    upper = jnp.concatenate([top, corner], axis=1)
+    lower = jnp.concatenate([corner.T, second], axis=1)
+    scale_col = jnp.concatenate([col[...], col[...]], axis=1)
+    return jnp.concatenate([upper, lower], axis=0) * scale_col * row[:1, :]
+
+
+def root_second_kernel(first, across, begun, row, col, out, cols, rows):
+    out[...] = finish_inverse(first, across, begun, row, col, cols, rows)
+
+
+def level_second_kernel(first, across, begun, row, col, terms, out, x_out, root_out, cols, rows):
+    inverse = finish_inverse(first, across, begun, row, col, cols, rows)
+    out[...] = inverse
+    cross = load_square(terms, CROSS)
+    x = dot_full(inverse, cross)
+    x_out[...] = x
+    store_symmetric(root_out, 0, load_symmetric(terms, ROOT) - dot_t_full(cross, x))
 
 
 SCRATCH = [pltpu.VMEM((1024, LANES), F32), pltpu.VMEM((LANES, LANES), F32)]
@@ -390,23 +376,12 @@
     return first, across, rest, row, col
 
 
-def invert_second(parts, name):
-    return call(second_kernel, SQUARE, parts, name, SCRATCH, HALF_FLOPS // 2)
-
-
 def half_index():
     return lax.axis_index("group") // 2
 
 
 def no_index():
     return 0
-
-
-def panel_solve_kernel(inverse, terms, x_out, root_out):
-    cross = load_square(terms, CROSS)
-    x = dot_full(inverse[...], cross)
-    x_out[...] = x
-    store_symmetric(root_out, 0, load_symmetric(terms, ROOT) - dot_t_full(cross, x))
 
 
 def wide(x):
@@ -420,13 +395,16 @@
 
 
 def by_tiles(rows, out, stage, sems, value, beside=None):
-    tiles = rows // TILE
+    tiles = rows // OUT_TILE
+
+    def at(tile):
+        return pl.ds(pl.multiple_of(tile * OUT_TILE, OUT_TILE), OUT_TILE)
 
     def copy(tile):
-        return pltpu.make_async_copy(stage.at[tile_at(tile)], out.at[tile_at(tile)], sems.at[tile])
+        return pltpu.make_async_copy(stage.at[at(tile)], out.at[at(tile)], sems.at[tile])
 
     def step(tile, carry):
-        stage[tile_at(tile), :] = value(tile_at(tile))
+        stage[at(tile), :] = value(at(tile))
         copy(tile).start()
         return carry
 
@@ -469,7 +447,7 @@
         kernel,
         out_specs=[pl.BlockSpec(memory_space=pl.ANY)] + [pl.BlockSpec(memory_space=pltpu.VMEM)] * len(more),
         out_shape=[jax.ShapeDtypeStruct((rows, R), F32), *more],
-        scratch_shapes=[pltpu.VMEM((rows, R), F32), pltpu.SemaphoreType.DMA((rows // TILE,))],
+        scratch_shapes=[pltpu.VMEM((rows, R), F32), pltpu.SemaphoreType.DMA((rows // OUT_TILE,))],
         compiler_params=pltpu.CompilerParams(vmem_limit_bytes=VMEM_LIMIT),
         cost_estimate=cost(passes, rows, 3),
         name=name,
@@ -550,9 +528,9 @@
     source.flying, parts = lax.optimization_barrier((source.flying, parts))
     source.finish()
     source.start(*source_left.pop())
-    inverse = invert_second(parts, "level_second")
-    x, root = call(
-        panel_solve_kernel, (SQUARE, jax.ShapeDtypeStruct((SYMMETRIC, LANES), F32)), (inverse, terms), "panel_solve"
+    shapes = (SQUARE, SQUARE, jax.ShapeDtypeStruct((SYMMETRIC, LANES), F32))
+    inverse, x, root = call(
+        level_second_kernel, shapes, (*parts, terms), "level_second", SCRATCH, HALF_FLOPS // 2
     )
     source.flying, x = lax.optimization_barrier((source.flying, x))
     source.finish()
@@ -572,7 +550,7 @@
     side_flying, parts = lax.optimization_barrier((side_flying, parts))
     side.value = side.value + side_flying
     side.start("gather", 0)
-    inverse = invert_second(parts, "root_second")
+    inverse = call(root_second_kernel, SQUARE, parts, "root_second", SCRATCH, HALF_FLOPS // 2)
     side.finish()
     (solution,) = update(field_kernel, [level, high, low, inverse, side.value], 3, "field")
     return (panel_one, solution)

time: 68.1 us -> 74.3 us (1.091)
  Pallas kernels: 28.1 us -> 34.4 us
    pallas_call x7 -> x6, Pallas kernels: 14.7 us -> 19.5 us  [call(): pl.pallas_call(kernel, out_shape=out_shape, scratch_shapes=list(scratch),...]
    pallas_call x2, Pallas kernels: 6.43 us -> 7.67 us  [update(): pl.pallas_call(kernel, out_specs=[pl.BlockSpec(memory_space=pl.ANY)] + [p...]
  transfers between devices with their start and end apart: 17 -> 17, of which waited for: 8 -> 7; matrix products, arithmetic and copies ran while one was open for 1% -> 0% of each run, Pallas kernels for 31% -> 36%
where the time goes in v13:
time: 74.3 us; the launch traced here: 74.1 us
  Pallas kernels  34.4 us (46%)
  waiting for transfers between devices  19.1 us (26%)
  starting transfers between devices  18.7 us (25%)
  between operations  1.14 us (2%)
    pallas_call x6, Pallas kernels, call(): pl.pallas_call(kernel, out_shape=out_shape, scratch_shapes=list(scratch),...  19.5 us
    ppermute x17, waiting for transfers between devices, exchange(): return lax.ppermute(x, AXES, [(i, i ^ mask) for i in range(count)])  19.1 us
    ppermute x17, starting transfers between devices, exchange(): return lax.ppermute(x, AXES, [(i, i ^ mask) for i in range(count)])  18.7 us
    pallas_call x2, Pallas kernels, update(): pl.pallas_call(kernel, out_specs=[pl.BlockSpec(memory_space=pl.ANY)] + [p...  7.67 us
    pallas_call x1, Pallas kernels, panel_gram(): pl.pallas_call(panel_gram_kernel, in_specs=[pl.BlockSpec(memory_space=pl....  4.44 us
    pallas_call x1, Pallas kernels, source_gram(): pl.pallas_call(source_gram_kernel, out_shape=(part, part), scratch_shapes...  2.76 us
  transfers between devices with their start and end apart: 17, of which 7 were waited for; matrix products, arithmetic and copies ran while one was open for 0% of the time, Pallas kernels for 36%

profile of v13, /device:TPU:0, one launch (start us, length us, event | category | flops | bytes accessed | tf_op | source)
XLA Modules:
  0.0 74.1 jit_solution(7888602896066271134)
XLA Ops:
  0.6 0.0 copy-start
  0.6 4.4 %panel_gram.1 = (f32[520,128]{1,0:T(8,128)S(1)}, f32[520,128]{1,0:T(8,128)S(1)}, f32[2048,256]{1,0:T(8,128)S(1)}, f32[2048,256]{1,0:T(8,128)S(1)}) custom-call(f32[2048,256]{1,0:T(8,128)} %q_two, f32[2048,256]{1,0:T(8,128)} %q_one.1), custom_call_target="tpu_custom_call" | custom-call | flops 1879048192 | bytes 4194304 | tf_op jit(solution)/shard_map/panel_gram/pallas_call | solution.py:181
  5.1 0.5 collective-permute-start
  5.6 0.0 copy-done
  5.6 2.8 %source_gram.1 = (f32[512,128]{1,0:T(8,128)S(1)}, f32[512,128]{1,0:T(8,128)S(1)}) custom-call(f32[2048,256]{1,0:T(8,128)S(1)} %get-tuple-element.59.b2, f32[2048,256]{1,0:T(8,128)S(1)} %get-tuple-element.60.b1, f32[2048,256]{1,0:T(8,128)S(1)} %copy-done), custom_call_target="tpu_custom_call" | custom-call | flops 1610612736 | bytes 6291456 | tf_op jit(solution)/shard_map/source_gram/pallas_call | solution.py:198
  8.4 0.0 collective-permute-done
  8.4 0.1 collective-permute-start.2
  8.6 3.0 %collective-permute-start.1 = (f32[264,128]{1,0:T(8,128)S(1)}, f32[264,128]{1,0:T(8,128)S(1)}, u32[]{:S(2)}, u32[]{:S(2)}) collective-permute-start(f32[264,128]{1,0:T(8,128)S(1)} %slice_select_fusion.1), channel_id=1, source_target_pairs={{0,4},{1,5},{2,6},{3,7},{4,0},{5,1},{6,2},{7,3},{8,12},{9,13},{10,... | collective-permute-start | bytes 405512 | tf_op jit(solution)/shard_map/ppermute | solution.py:459
  11.6 3.8 %collective-permute-done.1 = f32[264,128]{1,0:T(8,128)S(1)} collective-permute-done((f32[264,128]{1,0:T(8,128)S(1)}, f32[264,128]{1,0:T(8,128)S(1)}, u32[]{:S(2)}, u32[]{:S(2)}) %collective-permute-start.1) | collective-permute-done | bytes 135200 | tf_op jit(solution)/shard_map/ppermute | solution.py:459
  15.3 0.0 collective-permute-done.2
  15.4 1.8 %collective-permute-start.4 = (f32[256,128]{1,0:T(8,128)S(1)}, f32[256,128]{1,0:T(8,128)S(1)}, u32[]{:S(2)}, u32[]{:S(2)}) collective-permute-start(f32[256,128]{1,0:T(8,128)S(1)} %slice_select_fusion.2), channel_id=1, source_target_pairs={{0,4},{1,5},{2,6},{3,7},{4,0},{5,1},{6,2},{7,3},{8,12},{9,13},{10,... | collective-permute-start | bytes 393224 | tf_op jit(solution)/shard_map/ppermute | solution.py:459
  17.3 1.7 %collective-permute-start.3 = (f32[136,128]{1,0:T(8,128)S(1)}, f32[136,128]{1,0:T(8,128)S(1)}, u32[]{:S(2)}, u32[]{:S(2)}) collective-permute-start(f32[136,128]{1,0:T(8,128)S(1)} %slice_select_fusion.4), channel_id=1, source_target_pairs={{0,8},{1,9},{2,10},{3,11},{4,12},{5,13},{6,14},{7,15},{8,0},{9,1},... | collective-permute-start | bytes 208904 | tf_op jit(solution)/shard_map/ppermute | solution.py:459
  18.9 2.7 %collective-permute-done.3 = f32[136,128]{1,0:T(8,128)S(1)} collective-permute-done((f32[136,128]{1,0:T(8,128)S(1)}, f32[136,128]{1,0:T(8,128)S(1)}, u32[]{:S(2)}, u32[]{:S(2)}) %collective-permute-start.3) | collective-permute-done | bytes 69664 | tf_op jit(solution)/shard_map/ppermute | solution.py:459
  21.6 0.0 collective-permute-done.4
  21.7 2.7 %collective-permute-start.5 = (f32[136,128]{1,0:T(8,128)S(1)}, f32[136,128]{1,0:T(8,128)S(1)}, u32[]{:S(2)}, u32[]{:S(2)}) collective-permute-start(f32[136,128]{1,0:T(8,128)S(1)} %select_add_fusion.2), channel_id=1, source_target_pairs={{0,16},{1,17},{2,18},{3,19},{4,20},{5,21},{6,22},{7,23},{8,24},{9,... | collective-permute-start | bytes 208904 | tf_op jit(solution)/shard_map/ppermute | solution.py:459
  24.4 1.6 %collective-permute-start.6 = (f32[128,128]{1,0:T(8,128)S(1)}, f32[128,128]{1,0:T(8,128)S(1)}, u32[]{:S(2)}, u32[]{:S(2)}) collective-permute-start(f32[128,128]{1,0:T(8,128)S(1)} %slice_select_fusion.5), channel_id=1, source_target_pairs={{0,8},{1,9},{2,10},{3,11},{4,12},{5,13},{6,14},{7,15},{8,0},{9,1},... | collective-permute-start | bytes 196616 | tf_op jit(solution)/shard_map/ppermute | solution.py:459
  26.0 3.4 %collective-permute-done.6 = f32[128,128]{1,0:T(8,128)S(1)} collective-permute-done((f32[128,128]{1,0:T(8,128)S(1)}, f32[128,128]{1,0:T(8,128)S(1)}, u32[]{:S(2)}, u32[]{:S(2)}) %collective-permute-start.6) | collective-permute-done | bytes 65568 | tf_op jit(solution)/shard_map/ppermute | solution.py:459
  29.4 0.0 collective-permute-done.5
  29.4 1.6 %collective-permute-start.7 = (f32[136,128]{1,0:T(8,128)S(1)}, f32[136,128]{1,0:T(8,128)S(1)}, u32[]{:S(2)}, u32[]{:S(2)}) collective-permute-start(f32[136,128]{1,0:T(8,128)S(1)} %add.39), channel_id=1, source_target_pairs={{0,8},{1,9},{2,10},{3,11},{4,12},{5,13},{6,14},{7,15},{8,0},{9,1},... | collective-permute-start | bytes 208904 | tf_op jit(solution)/shard_map/ppermute | solution.py:459
  31.1 0.9 %collective-permute-start.8 = (f32[128,128]{1,0:T(8,128)S(1)}, f32[128,128]{1,0:T(8,128)S(1)}, u32[]{:S(2)}, u32[]{:S(2)}) collective-permute-start(f32[128,128]{1,0:T(8,128)S(1)} %select_add_fusion.3), channel_id=1, source_target_pairs={{0,16},{1,17},{2,18},{3,19},{4,20},{5,21},{6,22},{7,23},{8,24},{9,... | collective-permute-start | bytes 196616 | tf_op jit(solution)/shard_map/ppermute | solution.py:459
  32.0 4.9 %collective-permute-done.8 = f32[128,128]{1,0:T(8,128)S(1)} collective-permute-done((f32[128,128]{1,0:T(8,128)S(1)}, f32[128,128]{1,0:T(8,128)S(1)}, u32[]{:S(2)}, u32[]{:S(2)}) %collective-permute-start.8) | collective-permute-done | bytes 65568 | tf_op jit(solution)/shard_map/ppermute | solution.py:459
  36.9 0.0 collective-permute-done.7
  37.0 0.0 copy-start.1
  37.0 0.6 collective-permute-start.9
  37.6 0.1 collective-permute-start.10
  37.7 4.2 %collective-permute-done.10 = f32[128,128]{1,0:T(8,128)S(1)} collective-permute-done((f32[128,128]{1,0:T(8,128)S(1)}, f32[128,128]{1,0:T(8,128)S(1)}, u32[]{:S(2)}, u32[]{:S(2)}) %collective-permute-start.10) | collective-permute-done | bytes 65568 | tf_op jit(solution)/shard_map/ppermute | solution.py:459
  41.9 0.1 collective-permute-done.9
  42.1 0.1 collective-permute-start.12
  42.2 1.4 %collective-permute-start.11 = (f32[256,128]{1,0:T(8,128)S(1)}, f32[256,128]{1,0:T(8,128)S(1)}, u32[]{:S(2)}, u32[]{:S(2)}) collective-permute-start(f32[256,128]{1,0:T(8,128)S(1)} %pad_maximum_fusion.6), channel_id=1, source_target_pairs={{0,4},{1,5},{2,6},{3,7},{4,0},{5,1},{6,2},{7,3},{8,12},{9,13},{10,... | collective-permute-start | bytes 393224 | tf_op jit(solution)/shard_map/ppermute | solution.py:459
  43.7 0.1 collective-permute-done.12
  43.7 0.1 broadcast_select_fusion.1
  43.8 0.0 copy-done.1
  43.8 4.6 %level_first.1 = (f32[128,128]{1,0:T(8,128)S(1)}, f32[128,128]{1,0:T(8,128)S(1)}, f32[128,128]{1,0:T(8,128)S(1)}, f32[8,256]{1,0:T(8,128)S(1)}, f32[256,128]{1,0:T(8,128)S(1)}) custom-call(f32[1040,128]{1,0:T(8,128)S(1)} %pad_maximum_fusion.gram_ref.terms, f32[2,256,256]{2,1,0:T(8,128)S(1)} %copy-done.1), custom_call_target="tpu_custom_call" | custom-call | flops 5000000000 | bytes 262144 | tf_op jit(solution)/shard_map/level_first/pallas_call | solution.py:303
  48.4 1.9 %level_middle.1.begun = f32[128,128]{1,0:T(8,128)S(1)} custom-call(f32[128,128]{1,0:T(8,128)S(1)} %get-tuple-element.82.rest), custom_call_target="tpu_custom_call" | custom-call | flops 2500000000 | bytes 262144 | tf_op jit(solution)/shard_map/level_middle/pallas_call | solution.py:303
  50.3 0.0 collective-permute-done.11
  50.4 0.2 collective-permute-start.13
  50.6 4.0 %level_second.1 = (f32[256,256]{1,0:T(8,128)S(1)}, f32[256,256]{1,0:T(8,128)S(1)}, f32[264,128]{1,0:T(8,128)S(1)}) custom-call(f32[128,128]{1,0:T(8,128)S(1)} %get-tuple-element.86.first, f32[128,128]{1,0:T(8,128)S(1)} %get-tuple-element.87.across, f32[128,128]{1,0:T(8,128)S(1)} %level_middle.1.begun, f32[8,256]{1,0:T(8,128)S(1)} %get-tuple-element.89.row, ...), custom_call_target="tpu_custom_call" | custom-call | flops 2500000000 | bytes 262144 | tf_op jit(solution)/shard_map/level_second/pallas_call | solution.py:303
  54.6 1.6 %collective-permute-start.15 = (f32[264,128]{1,0:T(8,128)S(1)}, f32[264,128]{1,0:T(8,128)S(1)}, u32[]{:S(2)}, u32[]{:S(2)}) collective-permute-start(f32[264,128]{1,0:T(8,128)S(1)} %get-tuple-element.100), channel_id=1, source_target_pairs={{0,2},{1,3},{2,0},{3,1},{4,6},{5,7},{6,4},{7,5},{8,10},{9,11},{10,... | collective-permute-start | bytes 405512 | tf_op jit(solution)/shard_map/ppermute | solution.py:459
  56.2 0.0 collective-permute-done.13
  56.3 0.0 copy-start.2
  56.3 4.4 %panel.1 = (f32[2048,256]{1,0:T(8,128)}, f32[2048,256]{1,0:T(8,128)S(1)}, bf16[2048,256]{1,0:T(8,128)(2,1)S(1)}, bf16[2048,256]{1,0:T(8,128)(2,1)S(1)}, f32[512,128]{1,0:T(8,128)S(1)}) custom-call(f32[2048,256]{1,0:T(8,128)S(1)} %get-tuple-element.59.b2, f32[2048,256]{1,0:T(8,128)S(1)} %get-tuple-element.60.b1, f32[2048,256]{1,0:T(8,128)S(1)} %copy-done, ...), custom_call_target="tpu_custom_call" | custom-call | flops 2147483648 | bytes 6291456 | tf_op jit(solution)/shard_map/panel/pallas_call | solution.py:446
  60.8 0.6 collective-permute-start.14
  61.3 0.0 collective-permute-done.15
  61.4 0.0 copy-done.2
  61.4 4.6 %root_first.1 = (f32[128,128]{1,0:T(8,128)S(1)}, f32[128,128]{1,0:T(8,128)S(1)}, f32[128,128]{1,0:T(8,128)S(1)}, f32[8,256]{1,0:T(8,128)S(1)}, f32[256,128]{1,0:T(8,128)S(1)}) custom-call(f32[264,128]{1,0:T(8,128)S(1)} %add.42.gram_ref, f32[1,256,256]{2,1,0:T(8,128)S(1)} %bitcast.1), custom_call_target="tpu_custom_call" | custom-call | flops 5000000000 | bytes 262144 | tf_op jit(solution)/shard_map/root_first/pallas_call | solution.py:303
  66.0 1.9 %root_middle.1.begun = f32[128,128]{1,0:T(8,128)S(1)} custom-call(f32[128,128]{1,0:T(8,128)S(1)} %get-tuple-element.104.rest), custom_call_target="tpu_custom_call" | custom-call | flops 2500000000 | bytes 262144 | tf_op jit(solution)/shard_map/root_middle/pallas_call | solution.py:303
  67.9 0.0 collective-permute-done.14
  67.9 0.1 collective-permute-start.16
  68.0 2.6 %root_second.1.inverse = f32[256,256]{1,0:T(8,128)S(1)} custom-call(f32[128,128]{1,0:T(8,128)S(1)} %get-tuple-element.107.first, f32[128,128]{1,0:T(8,128)S(1)} %get-tuple-element.108.across, f32[128,128]{1,0:T(8,128)S(1)} %root_middle.1.begun, f32[8,256]{1,0:T(8,128)S(1)} %get-tuple-element.110.row, f32[256,128]{1,0:T(8,128)S(1)} %get-tuple-element.111.col), custom_call_target="tpu_custom_call" | custom-call | flops 2500000000 | bytes 262144 | tf_op jit(solution)/shard_map/root_second/pallas_call | solution.py:303
  70.6 0.0 collective-permute-done.16
  70.6 3.2 %field.1 = f32[2048,256]{1,0:T(8,128)} custom-call(f32[2048,256]{1,0:T(8,128)S(1)} %get-tuple-element.96.level, bf16[2048,256]{1,0:T(8,128)(2,1)S(1)} %get-tuple-element.97.high, bf16[2048,256]{1,0:T(8,128)(2,1)S(1)} %get-tuple-element.98.low, f32[256,256]{1,0:T(8,128)S(1)} %root_second.1.inverse, f32[512,128]{1,0:T(8,128)S(1)} %pad_maximum_fusion.4.side), custom_call_target="tpu_custom_call" | custom-call | flops 805306368 | bytes 6291456 | tf_op jit(solution)/shard_map/field/pallas_call | solution.py:446
  (30 shorter events, 0.6 us)
Async XLA Ops:
  0.6 5.0 %copy-start = (f32[2048,256]{1,0:T(8,128)S(1)}, f32[2048,256]{1,0:T(8,128)}, u32[]{:S(2)}) copy-start(f32[2048,256]{1,0:T(8,128)} %sources.3) | copy-start | bytes 6291460
  5.1 3.3 %collective-permute-start = (f32[520,128]{1,0:T(8,128)S(1)}, f32[520,128]{1,0:T(8,128)S(1)}, u32[]{:S(2)}, u32[]{:S(2)}) collective-permute-start(f32[520,128]{1,0:T(8,128)S(1)} %get-tuple-element.64), channel_id=1, source_target_pairs={{0,1},{1,0},{2,3},{3,2},{4,5},{5,4},{6,7},{7,6},{8,9},{9,8},{10,11... | collective-permute-start | bytes 798728 | tf_op jit(solution)/shard_map/ppermute | solution.py:459
  8.4 6.9 %collective-permute-start.2 = (f32[512,128]{1,0:T(8,128)S(1)}, f32[512,128]{1,0:T(8,128)S(1)}, u32[]{:S(2)}, u32[]{:S(2)}) collective-permute-start(f32[512,128]{1,0:T(8,128)S(1)} %get-tuple-element.67), channel_id=1, source_target_pairs={{0,1},{1,0},{2,3},{3,2},{4,5},{5,4},{6,7},{7,6},{8,9},{9,8},{10,11... | collective-permute-start | bytes 786440 | tf_op jit(solution)/shard_map/ppermute | solution.py:459
  8.6 6.8 %collective-permute-start.1 = (f32[264,128]{1,0:T(8,128)S(1)}, f32[264,128]{1,0:T(8,128)S(1)}, u32[]{:S(2)}, u32[]{:S(2)}) collective-permute-start(f32[264,128]{1,0:T(8,128)S(1)} %slice_select_fusion.1), channel_id=1, source_target_pairs={{0,4},{1,5},{2,6},{3,7},{4,0},{5,1},{6,2},{7,3},{8,12},{9,13},{10,... | collective-permute-start | bytes 405512 | tf_op jit(solution)/shard_map/ppermute | solution.py:459
  15.4 6.2 %collective-permute-start.4 = (f32[256,128]{1,0:T(8,128)S(1)}, f32[256,128]{1,0:T(8,128)S(1)}, u32[]{:S(2)}, u32[]{:S(2)}) collective-permute-start(f32[256,128]{1,0:T(8,128)S(1)} %slice_select_fusion.2), channel_id=1, source_target_pairs={{0,4},{1,5},{2,6},{3,7},{4,0},{5,1},{6,2},{7,3},{8,12},{9,13},{10,... | collective-permute-start | bytes 393224 | tf_op jit(solution)/shard_map/ppermute | solution.py:459
  17.3 4.4 %collective-permute-start.3 = (f32[136,128]{1,0:T(8,128)S(1)}, f32[136,128]{1,0:T(8,128)S(1)}, u32[]{:S(2)}, u32[]{:S(2)}) collective-permute-start(f32[136,128]{1,0:T(8,128)S(1)} %slice_select_fusion.4), channel_id=1, source_target_pairs={{0,8},{1,9},{2,10},{3,11},{4,12},{5,13},{6,14},{7,15},{8,0},{9,1},... | collective-permute-start | bytes 208904 | tf_op jit(solution)/shard_map/ppermute | solution.py:459
  21.7 7.7 %collective-permute-start.5 = (f32[136,128]{1,0:T(8,128)S(1)}, f32[136,128]{1,0:T(8,128)S(1)}, u32[]{:S(2)}, u32[]{:S(2)}) collective-permute-start(f32[136,128]{1,0:T(8,128)S(1)} %select_add_fusion.2), channel_id=1, source_target_pairs={{0,16},{1,17},{2,18},{3,19},{4,20},{5,21},{6,22},{7,23},{8,24},{9,... | collective-permute-start | bytes 208904 | tf_op jit(solution)/shard_map/ppermute | solution.py:459
  24.4 5.0 %collective-permute-start.6 = (f32[128,128]{1,0:T(8,128)S(1)}, f32[128,128]{1,0:T(8,128)S(1)}, u32[]{:S(2)}, u32[]{:S(2)}) collective-permute-start(f32[128,128]{1,0:T(8,128)S(1)} %slice_select_fusion.5), channel_id=1, source_target_pairs={{0,8},{1,9},{2,10},{3,11},{4,12},{5,13},{6,14},{7,15},{8,0},{9,1},... | collective-permute-start | bytes 196616 | tf_op jit(solution)/shard_map/ppermute | solution.py:459
  29.4 7.5 %collective-permute-start.7 = (f32[136,128]{1,0:T(8,128)S(1)}, f32[136,128]{1,0:T(8,128)S(1)}, u32[]{:S(2)}, u32[]{:S(2)}) collective-permute-start(f32[136,128]{1,0:T(8,128)S(1)} %add.39), channel_id=1, source_target_pairs={{0,8},{1,9},{2,10},{3,11},{4,12},{5,13},{6,14},{7,15},{8,0},{9,1},... | collective-permute-start | bytes 208904 | tf_op jit(solution)/shard_map/ppermute | solution.py:459
  31.1 5.8 %collective-permute-start.8 = (f32[128,128]{1,0:T(8,128)S(1)}, f32[128,128]{1,0:T(8,128)S(1)}, u32[]{:S(2)}, u32[]{:S(2)}) collective-permute-start(f32[128,128]{1,0:T(8,128)S(1)} %select_add_fusion.3), channel_id=1, source_target_pairs={{0,16},{1,17},{2,18},{3,19},{4,20},{5,21},{6,22},{7,23},{8,24},{9,... | collective-permute-start | bytes 196616 | tf_op jit(solution)/shard_map/ppermute | solution.py:459
  37.0 6.9 %copy-start.1 = (f32[2,256,256]{2,1,0:T(8,128)S(1)}, f32[2,256,256]{2,1,0:T(8,128)}, u32[]{:S(2)}) copy-start(f32[2,256,256]{2,1,0:T(8,128)} %coupling.1) | copy-start | bytes 1572868
  37.0 5.1 %collective-permute-start.9 = (f32[264,128]{1,0:T(8,128)S(1)}, f32[264,128]{1,0:T(8,128)S(1)}, u32[]{:S(2)}, u32[]{:S(2)}) collective-permute-start(f32[264,128]{1,0:T(8,128)S(1)} %pad_maximum_fusion.5), channel_id=1, source_target_pairs={{0,4},{1,5},{2,6},{3,7},{4,0},{5,1},{6,2},{7,3},{8,12},{9,13},{10,... | collective-permute-start | bytes 405512 | tf_op jit(solution)/shard_map/ppermute | solution.py:459
  37.6 4.3 %collective-permute-start.10 = (f32[128,128]{1,0:T(8,128)S(1)}, f32[128,128]{1,0:T(8,128)S(1)}, u32[]{:S(2)}, u32[]{:S(2)}) collective-permute-start(f32[128,128]{1,0:T(8,128)S(1)} %add.41), channel_id=1, source_target_pairs={{0,8},{1,9},{2,10},{3,11},{4,12},{5,13},{6,14},{7,15},{8,0},{9,1},... | collective-permute-start | bytes 196616 | tf_op jit(solution)/shard_map/ppermute | solution.py:459
  42.1 1.6 %collective-permute-start.12 = (f32[520,128]{1,0:T(8,128)S(1)}, f32[520,128]{1,0:T(8,128)S(1)}, u32[]{:S(2)}, u32[]{:S(2)}) collective-permute-start(f32[520,128]{1,0:T(8,128)S(1)} %pad_maximum_fusion.2), channel_id=1, source_target_pairs={{0,1},{1,0},{2,3},{3,2},{4,5},{5,4},{6,7},{7,6},{8,9},{9,8},{10,11... | collective-permute-start | bytes 798728 | tf_op jit(solution)/shard_map/ppermute | solution.py:459
  42.2 8.1 %collective-permute-start.11 = (f32[256,128]{1,0:T(8,128)S(1)}, f32[256,128]{1,0:T(8,128)S(1)}, u32[]{:S(2)}, u32[]{:S(2)}) collective-permute-start(f32[256,128]{1,0:T(8,128)S(1)} %pad_maximum_fusion.6), channel_id=1, source_target_pairs={{0,4},{1,5},{2,6},{3,7},{4,0},{5,1},{6,2},{7,3},{8,12},{9,13},{10,... | collective-permute-start | bytes 393224 | tf_op jit(solution)/shard_map/ppermute | solution.py:459
  50.4 5.8 %collective-permute-start.13 = (f32[512,128]{1,0:T(8,128)S(1)}, f32[512,128]{1,0:T(8,128)S(1)}, u32[]{:S(2)}, u32[]{:S(2)}) collective-permute-start(f32[512,128]{1,0:T(8,128)S(1)} %pad_maximum_fusion.3), channel_id=1, source_target_pairs={{0,1},{1,0},{2,3},{3,2},{4,5},{5,4},{6,7},{7,6},{8,9},{9,8},{10,11... | collective-permute-start | bytes 786440 | tf_op jit(solution)/shard_map/ppermute | solution.py:459
  54.6 6.7 %collective-permute-start.15 = (f32[264,128]{1,0:T(8,128)S(1)}, f32[264,128]{1,0:T(8,128)S(1)}, u32[]{:S(2)}, u32[]{:S(2)}) collective-permute-start(f32[264,128]{1,0:T(8,128)S(1)} %get-tuple-element.100), channel_id=1, source_target_pairs={{0,2},{1,3},{2,0},{3,1},{4,6},{5,7},{6,4},{7,5},{8,10},{9,11},{10,... | collective-permute-start | bytes 405512 | tf_op jit(solution)/shard_map/ppermute | solution.py:459
  56.3 5.1 %copy-start.2 = (f32[256,256]{1,0:T(8,128)S(1)}, f32[256,256]{1,0:T(8,128)}, u32[]{:S(2)}) copy-start(f32[256,256]{1,0:T(8,128)} %param.9) | copy-start | bytes 786436
  60.8 7.1 %collective-permute-start.14 = (f32[256,128]{1,0:T(8,128)S(1)}, f32[256,128]{1,0:T(8,128)S(1)}, u32[]{:S(2)}, u32[]{:S(2)}) collective-permute-start(f32[256,128]{1,0:T(8,128)S(1)} %slice_select_fusion), channel_id=1, source_target_pairs={{0,2},{1,3},{2,0},{3,1},{4,6},{5,7},{6,4},{7,5},{8,10},{9,11},{10,... | collective-permute-start | bytes 393224 | tf_op jit(solution)/shard_map/ppermute | solution.py:459
  67.9 2.6 %collective-permute-start.16 = (f32[256,128]{1,0:T(8,128)S(1)}, f32[256,128]{1,0:T(8,128)S(1)}, u32[]{:S(2)}, u32[]{:S(2)}) collective-permute-start(f32[256,128]{1,0:T(8,128)S(1)} %add.43), channel_id=1, source_target_pairs={{0,1},{1,0},{2,3},{3,2},{4,5},{5,4},{6,7},{7,6},{8,9},{9,8},{10,11... | collective-permute-start | bytes 393224 | tf_op jit(solution)/shard_map/ppermute | solution.py:459

commit v14 on v11

--- a/solution.py
+++ b/solution.py
@@ -14,6 +14,7 @@
 R = 256
 LANES = 128
 TILE = 512
+OUT_TILE = 1024
 GROUPS = 8
 VMEM_LIMIT = 16 * 1024 * 1024
 SYMMETRIC, FULL = 264, 512
@@ -127,13 +128,12 @@
             copy.wait()
         h2, l2 = split2(b2[at, :])
         h1, l1 = split2(b1[at, :])
-        h2t, l2t, h1t = h2.T, l2.T, h1.T
-        acc[0] += dot(h2t, h2)
-        acc[1] += dot(h2t, l2)
-        left = jnp.concatenate([h2t, h2t, l2t], axis=1)
-        acc[2] += dot(left, jnp.concatenate([h1, l1, h1], axis=0))
-        acc[3] += dot(h1t, h1)
-        acc[4] += dot(h1t, l1)
+        h2t = h2.T
+        left = jnp.concatenate([h2t, h1.T], axis=0)
+        acc[:R, :] += dot(h2t, h2)
+        acc[R : 3 * R, :] += dot(left, l2)
+        acc[3 * R : 5 * R, :] += dot(left, h1)
+        acc[5 * R :, :] += dot(left, l1)
 
     def step(tile, carry):
         add_rows(tile_at(tile), tile + 1)
@@ -142,11 +142,10 @@
     for sem, at in enumerate(parts):
         add_rows(at, sem)
     lax.fori_loop(1, tiles, step, 0)
-    low = acc[1]
-    store_symmetric(packed, OWN, acc[0] + low + low.T)
-    low = acc[4]
-    store_symmetric(packed, ROOT, acc[3] + low + low.T)
-    store_square(packed, CROSS, acc[2])
+    parts = [acc[i * R : i * R + R, :] for i in range(7)]
+    store_symmetric(packed, OWN, parts[0] + parts[1] + parts[1].T)
+    store_symmetric(packed, ROOT, parts[4] + parts[6] + parts[6].T)
+    store_square(packed, CROSS, parts[3] + parts[5] + parts[2].T)
     store_halves(packed, keep, send)
 
 
@@ -155,16 +154,18 @@
 
     def step(tile, carry):
         hs, ls = split2(sources[tile_at(tile), :])
-        right = jnp.concatenate([hs, ls, hs], axis=0)
+        hst = hs.T
+        left = jnp.concatenate([hst, ls.T], axis=0)
         for which, panel in enumerate((b2, b1)):
             high, low = split2(panel[tile_at(tile), :])
-            turned = high.T
-            acc[which] += dot(jnp.concatenate([turned, turned, low.T], axis=1), right)
+            acc[which, : 2 * R, :] += dot(left, high)
+            acc[which, 2 * R :, :] += dot(hst, low)
         return carry
 
     lax.fori_loop(0, b2.shape[0] // TILE, step, 0)
-    store_square(packed, PROJECTED, acc[0])
-    store_square(packed, SIDE, acc[1])
+    for which, at in enumerate((PROJECTED, SIDE)):
+        total = acc[which, :R, :] + acc[which, R : 2 * R, :] + acc[which, 2 * R :, :]
+        store_square(packed, at, total.T)
     store_halves(packed, keep, send)
 
 
@@ -183,7 +184,7 @@
         in_specs=[pl.BlockSpec(memory_space=pl.ANY)] * 2,
         out_shape=(part, part, tall, tall),
         scratch_shapes=[
-            pltpu.VMEM((5, R, R), F32),
+            pltpu.VMEM((7 * R, R), F32),
             pltpu.VMEM((PANEL_TERMS, LANES), F32),
             pltpu.SemaphoreType.DMA((2, rows // TILE + 1)),
         ],
@@ -198,7 +199,7 @@
     return pl.pallas_call(
         source_gram_kernel,
         out_shape=(part, part),
-        scratch_shapes=[pltpu.VMEM((2, R, R), F32), pltpu.VMEM((SOURCE_TERMS, LANES), F32)],
+        scratch_shapes=[pltpu.VMEM((2, 3 * R, R), F32), pltpu.VMEM((SOURCE_TERMS, LANES), F32)],
         compiler_params=pltpu.CompilerParams(vmem_limit_bytes=VMEM_LIMIT),
         cost_estimate=cost(6, b2.shape[0], 3),
         name="source_gram",
@@ -420,13 +421,16 @@
 
 
 def by_tiles(rows, out, stage, sems, value, beside=None):
-    tiles = rows // TILE
+    tiles = rows // OUT_TILE
+
+    def at(tile):
+        return pl.ds(pl.multiple_of(tile * OUT_TILE, OUT_TILE), OUT_TILE)
 
     def copy(tile):
-        return pltpu.make_async_copy(stage.at[tile_at(tile)], out.at[tile_at(tile)], sems.at[tile])
+        return pltpu.make_async_copy(stage.at[at(tile)], out.at[at(tile)], sems.at[tile])
 
     def step(tile, carry):
-        stage[tile_at(tile), :] = value(tile_at(tile))
+        stage[at(tile), :] = value(at(tile))
         copy(tile).start()
         return carry
 
@@ -469,7 +473,7 @@
         kernel,
         out_specs=[pl.BlockSpec(memory_space=pl.ANY)] + [pl.BlockSpec(memory_space=pltpu.VMEM)] * len(more),
         out_shape=[jax.ShapeDtypeStruct((rows, R), F32), *more],
-        scratch_shapes=[pltpu.VMEM((rows, R), F32), pltpu.SemaphoreType.DMA((rows // TILE,))],
+        scratch_shapes=[pltpu.VMEM((rows, R), F32), pltpu.SemaphoreType.DMA((rows // OUT_TILE,))],
         compiler_params=pltpu.CompilerParams(vmem_limit_bytes=VMEM_LIMIT),
         cost_estimate=cost(passes, rows, 3),
         name=name,

time: 68.1 us -> 68 us (level)
  no operation moved by 1% of the time
where the time goes in v14:
time: 68 us; the launch traced here: 67.8 us
  Pallas kernels  27.9 us (41%)
  waiting for transfers between devices  19.4 us (29%)
  starting transfers between devices  18.7 us (28%)
  between operations  1.13 us (2%)
    ppermute x17, waiting for transfers between devices, exchange(): return lax.ppermute(x, AXES, [(i, i ^ mask) for i in range(count)])  19.4 us
    ppermute x17, starting transfers between devices, exchange(): return lax.ppermute(x, AXES, [(i, i ^ mask) for i in range(count)])  18.7 us
    pallas_call x7, Pallas kernels, call(): pl.pallas_call(kernel, out_shape=out_shape, scratch_shapes=list(scratch),...  14.7 us
    pallas_call x2, Pallas kernels, update(): pl.pallas_call(kernel, out_specs=[pl.BlockSpec(memory_space=pl.ANY)] + [p...  6.07 us
    pallas_call x1, Pallas kernels, panel_gram(): pl.pallas_call(panel_gram_kernel, in_specs=[pl.BlockSpec(memory_space=pl....  4.45 us
    pallas_call x1, Pallas kernels, source_gram(): pl.pallas_call(source_gram_kernel, out_shape=(part, part), scratch_shapes...  2.78 us
  transfers between devices with their start and end apart: 17, of which 8 were waited for; matrix products, arithmetic and copies ran while one was open for 1% of the time, Pallas kernels for 31%

profile of v14, /device:TPU:0, one launch (start us, length us, event | category | flops | bytes accessed | tf_op | source)
XLA Modules:
  0.0 67.8 jit_solution(14181299039572599214)
XLA Ops:
  0.6 0.0 copy-start
  0.6 4.4 %panel_gram.1 = (f32[520,128]{1,0:T(8,128)S(1)}, f32[520,128]{1,0:T(8,128)S(1)}, f32[2048,256]{1,0:T(8,128)S(1)}, f32[2048,256]{1,0:T(8,128)S(1)}) custom-call(f32[2048,256]{1,0:T(8,128)} %q_two, f32[2048,256]{1,0:T(8,128)} %q_one.1), custom_call_target="tpu_custom_call" | custom-call | flops 1879048192 | bytes 4194304 | tf_op jit(solution)/shard_map/panel_gram/pallas_call | solution.py:182
  5.1 0.5 collective-permute-start
  5.6 0.0 copy-done
  5.6 2.8 %source_gram.1 = (f32[512,128]{1,0:T(8,128)S(1)}, f32[512,128]{1,0:T(8,128)S(1)}) custom-call(f32[2048,256]{1,0:T(8,128)S(1)} %get-tuple-element.58.b2, f32[2048,256]{1,0:T(8,128)S(1)} %get-tuple-element.59.b1, f32[2048,256]{1,0:T(8,128)S(1)} %copy-done), custom_call_target="tpu_custom_call" | custom-call | flops 1610612736 | bytes 6291456 | tf_op jit(solution)/shard_map/source_gram/pallas_call | solution.py:199
  8.4 0.0 collective-permute-done
  8.4 0.1 collective-permute-start.2
  8.6 3.0 %collective-permute-start.1 = (f32[264,128]{1,0:T(8,128)S(1)}, f32[264,128]{1,0:T(8,128)S(1)}, u32[]{:S(2)}, u32[]{:S(2)}) collective-permute-start(f32[264,128]{1,0:T(8,128)S(1)} %slice_select_fusion.1), channel_id=1, source_target_pairs={{0,4},{1,5},{2,6},{3,7},{4,0},{5,1},{6,2},{7,3},{8,12},{9,13},{10,... | collective-permute-start | bytes 405512 | tf_op jit(solution)/shard_map/ppermute | solution.py:485
  11.6 3.8 %collective-permute-done.1 = f32[264,128]{1,0:T(8,128)S(1)} collective-permute-done((f32[264,128]{1,0:T(8,128)S(1)}, f32[264,128]{1,0:T(8,128)S(1)}, u32[]{:S(2)}, u32[]{:S(2)}) %collective-permute-start.1) | collective-permute-done | bytes 135200 | tf_op jit(solution)/shard_map/ppermute | solution.py:485
  15.4 0.0 collective-permute-done.2
  15.5 1.8 %collective-permute-start.4 = (f32[256,128]{1,0:T(8,128)S(1)}, f32[256,128]{1,0:T(8,128)S(1)}, u32[]{:S(2)}, u32[]{:S(2)}) collective-permute-start(f32[256,128]{1,0:T(8,128)S(1)} %slice_select_fusion.2), channel_id=1, source_target_pairs={{0,4},{1,5},{2,6},{3,7},{4,0},{5,1},{6,2},{7,3},{8,12},{9,13},{10,... | collective-permute-start | bytes 393224 | tf_op jit(solution)/shard_map/ppermute | solution.py:485
  17.3 1.6 %collective-permute-start.3 = (f32[136,128]{1,0:T(8,128)S(1)}, f32[136,128]{1,0:T(8,128)S(1)}, u32[]{:S(2)}, u32[]{:S(2)}) collective-permute-start(f32[136,128]{1,0:T(8,128)S(1)} %slice_select_fusion.4), channel_id=1, source_target_pairs={{0,8},{1,9},{2,10},{3,11},{4,12},{5,13},{6,14},{7,15},{8,0},{9,1},... | collective-permute-start | bytes 208904 | tf_op jit(solution)/shard_map/ppermute | solution.py:485
  19.0 2.7 %collective-permute-done.3 = f32[136,128]{1,0:T(8,128)S(1)} collective-permute-done((f32[136,128]{1,0:T(8,128)S(1)}, f32[136,128]{1,0:T(8,128)S(1)}, u32[]{:S(2)}, u32[]{:S(2)}) %collective-permute-start.3) | collective-permute-done | bytes 69664 | tf_op jit(solution)/shard_map/ppermute | solution.py:485
  21.7 0.0 collective-permute-done.4
  21.8 2.6 %collective-permute-start.5 = (f32[136,128]{1,0:T(8,128)S(1)}, f32[136,128]{1,0:T(8,128)S(1)}, u32[]{:S(2)}, u32[]{:S(2)}) collective-permute-start(f32[136,128]{1,0:T(8,128)S(1)} %select_add_fusion.2), channel_id=1, source_target_pairs={{0,16},{1,17},{2,18},{3,19},{4,20},{5,21},{6,22},{7,23},{8,24},{9,... | collective-permute-start | bytes 208904 | tf_op jit(solution)/shard_map/ppermute | solution.py:485
  24.4 1.6 %collective-permute-start.6 = (f32[128,128]{1,0:T(8,128)S(1)}, f32[128,128]{1,0:T(8,128)S(1)}, u32[]{:S(2)}, u32[]{:S(2)}) collective-permute-start(f32[128,128]{1,0:T(8,128)S(1)} %slice_select_fusion.5), channel_id=1, source_target_pairs={{0,8},{1,9},{2,10},{3,11},{4,12},{5,13},{6,14},{7,15},{8,0},{9,1},... | collective-permute-start | bytes 196616 | tf_op jit(solution)/shard_map/ppermute | solution.py:485
  26.0 3.4 %collective-permute-done.6 = f32[128,128]{1,0:T(8,128)S(1)} collective-permute-done((f32[128,128]{1,0:T(8,128)S(1)}, f32[128,128]{1,0:T(8,128)S(1)}, u32[]{:S(2)}, u32[]{:S(2)}) %collective-permute-start.6) | collective-permute-done | bytes 65568 | tf_op jit(solution)/shard_map/ppermute | solution.py:485
  29.4 0.0 collective-permute-done.5
  29.5 1.6 %collective-permute-start.7 = (f32[136,128]{1,0:T(8,128)S(1)}, f32[136,128]{1,0:T(8,128)S(1)}, u32[]{:S(2)}, u32[]{:S(2)}) collective-permute-start(f32[136,128]{1,0:T(8,128)S(1)} %add.39), channel_id=1, source_target_pairs={{0,8},{1,9},{2,10},{3,11},{4,12},{5,13},{6,14},{7,15},{8,0},{9,1},... | collective-permute-start | bytes 208904 | tf_op jit(solution)/shard_map/ppermute | solution.py:485
  31.1 0.9 %collective-permute-start.8 = (f32[128,128]{1,0:T(8,128)S(1)}, f32[128,128]{1,0:T(8,128)S(1)}, u32[]{:S(2)}, u32[]{:S(2)}) collective-permute-start(f32[128,128]{1,0:T(8,128)S(1)} %select_add_fusion.3), channel_id=1, source_target_pairs={{0,16},{1,17},{2,18},{3,19},{4,20},{5,21},{6,22},{7,23},{8,24},{9,... | collective-permute-start | bytes 196616 | tf_op jit(solution)/shard_map/ppermute | solution.py:485
  32.0 4.9 %collective-permute-done.8 = f32[128,128]{1,0:T(8,128)S(1)} collective-permute-done((f32[128,128]{1,0:T(8,128)S(1)}, f32[128,128]{1,0:T(8,128)S(1)}, u32[]{:S(2)}, u32[]{:S(2)}) %collective-permute-start.8) | collective-permute-done | bytes 65568 | tf_op jit(solution)/shard_map/ppermute | solution.py:485
  36.9 0.0 collective-permute-done.7
  37.0 0.0 copy-start.1
  37.0 0.6 collective-permute-start.9
  37.6 0.2 collective-permute-start.10
  37.8 4.1 %collective-permute-done.10 = f32[128,128]{1,0:T(8,128)S(1)} collective-permute-done((f32[128,128]{1,0:T(8,128)S(1)}, f32[128,128]{1,0:T(8,128)S(1)}, u32[]{:S(2)}, u32[]{:S(2)}) %collective-permute-start.10) | collective-permute-done | bytes 65568 | tf_op jit(solution)/shard_map/ppermute | solution.py:485
  42.0 0.1 collective-permute-done.9
  42.2 0.1 collective-permute-start.12
  42.3 1.4 %collective-permute-start.11 = (f32[256,128]{1,0:T(8,128)S(1)}, f32[256,128]{1,0:T(8,128)S(1)}, u32[]{:S(2)}, u32[]{:S(2)}) collective-permute-start(f32[256,128]{1,0:T(8,128)S(1)} %pad_maximum_fusion.6), channel_id=1, source_target_pairs={{0,4},{1,5},{2,6},{3,7},{4,0},{5,1},{6,2},{7,3},{8,12},{9,13},{10,... | collective-permute-start | bytes 393224 | tf_op jit(solution)/shard_map/ppermute | solution.py:485
  43.7 0.1 collective-permute-done.12
  43.8 0.1 broadcast_select_fusion.1
  43.9 0.0 copy-done.1
  43.9 3.3 %level_first.1 = (f32[128,128]{1,0:T(8,128)S(1)}, f32[128,128]{1,0:T(8,128)S(1)}, f32[128,128]{1,0:T(8,128)S(1)}, f32[8,256]{1,0:T(8,128)S(1)}, f32[256,128]{1,0:T(8,128)S(1)}) custom-call(f32[1040,128]{1,0:T(8,128)S(1)} %pad_maximum_fusion.gram_ref.terms, f32[2,256,256]{2,1,0:T(8,128)S(1)} %copy-done.1), custom_call_target="tpu_custom_call" | custom-call | flops 5000000000 | bytes 262144 | tf_op jit(solution)/shard_map/level_first/pallas_call | solution.py:331
  47.2 1.4 %level_middle.1.swept = f32[128,128]{1,0:T(8,128)S(1)} custom-call(f32[128,128]{1,0:T(8,128)S(1)} %get-tuple-element.81.rest), custom_call_target="tpu_custom_call" | custom-call | flops 2500000000 | bytes 262144 | tf_op jit(solution)/shard_map/level_middle/pallas_call | solution.py:331
  48.6 0.0 collective-permute-done.11
  48.7 0.2 collective-permute-start.13
  48.9 2.1 %level_second.1.inverse = f32[256,256]{1,0:T(8,128)S(1)} custom-call(f32[128,128]{1,0:T(8,128)S(1)} %get-tuple-element.85.first, f32[128,128]{1,0:T(8,128)S(1)} %get-tuple-element.86.across, f32[128,128]{1,0:T(8,128)S(1)} %level_middle.1.swept, f32[8,256]{1,0:T(8,128)S(1)} %get-tuple-element.88.row, f32[256,128]{1,0:T(8,128)S(1)} %get-tuple-element.89.col), custom_call_target="tpu_custom_call" | custom-call | flops 2500000000 | bytes 262144 | tf_op jit(solution)/shard_map/level_second/pallas_call | solution.py:331
  51.0 1.1 %panel_solve.1 = (f32[256,256]{1,0:T(8,128)S(1)}, f32[264,128]{1,0:T(8,128)S(1)}) custom-call(f32[256,256]{1,0:T(8,128)S(1)} %level_second.1.inverse, f32[1040,128]{1,0:T(8,128)S(1)} %pad_maximum_fusion.gram_ref.terms), custom_call_target="tpu_custom_call" | custom-call | bytes 262144 | tf_op jit(solution)/shard_map/panel_solve/pallas_call | solution.py:331
  52.0 1.6 %collective-permute-start.15 = (f32[264,128]{1,0:T(8,128)S(1)}, f32[264,128]{1,0:T(8,128)S(1)}, u32[]{:S(2)}, u32[]{:S(2)}) collective-permute-start(f32[264,128]{1,0:T(8,128)S(1)} %get-tuple-element.98), channel_id=1, source_target_pairs={{0,2},{1,3},{2,0},{3,1},{4,6},{5,7},{6,4},{7,5},{8,10},{9,11},{10,... | collective-permute-start | bytes 405512 | tf_op jit(solution)/shard_map/ppermute | solution.py:485
  53.6 0.0 collective-permute-done.13
  53.7 0.0 copy-start.2
  53.7 3.6 %panel.1 = (f32[2048,256]{1,0:T(8,128)}, f32[2048,256]{1,0:T(8,128)S(1)}, bf16[2048,256]{1,0:T(8,128)(2,1)S(1)}, bf16[2048,256]{1,0:T(8,128)(2,1)S(1)}, f32[512,128]{1,0:T(8,128)S(1)}) custom-call(f32[2048,256]{1,0:T(8,128)S(1)} %get-tuple-element.58.b2, f32[2048,256]{1,0:T(8,128)S(1)} %get-tuple-element.59.b1, f32[2048,256]{1,0:T(8,128)S(1)} %copy-done, ...), custom_call_target="tpu_custom_call" | custom-call | flops 2147483648 | bytes 6291456 | tf_op jit(solution)/shard_map/panel/pallas_call | solution.py:472
  57.4 0.6 collective-permute-start.14
  58.0 0.0 collective-permute-done.15
  58.0 0.0 copy-done.2
  58.0 3.3 %root_first.1 = (f32[128,128]{1,0:T(8,128)S(1)}, f32[128,128]{1,0:T(8,128)S(1)}, f32[128,128]{1,0:T(8,128)S(1)}, f32[8,256]{1,0:T(8,128)S(1)}, f32[256,128]{1,0:T(8,128)S(1)}) custom-call(f32[264,128]{1,0:T(8,128)S(1)} %add.42.gram_ref, f32[1,256,256]{2,1,0:T(8,128)S(1)} %bitcast.1), custom_call_target="tpu_custom_call" | custom-call | flops 5000000000 | bytes 262144 | tf_op jit(solution)/shard_map/root_first/pallas_call | solution.py:331
  61.4 1.4 %root_middle.1.swept = f32[128,128]{1,0:T(8,128)S(1)} custom-call(f32[128,128]{1,0:T(8,128)S(1)} %get-tuple-element.102.rest), custom_call_target="tpu_custom_call" | custom-call | flops 2500000000 | bytes 262144 | tf_op jit(solution)/shard_map/root_middle/pallas_call | solution.py:331
  62.8 0.2 collective-permute-done.14
  62.9 0.1 collective-permute-start.16
  63.0 2.1 %root_second.1.inverse = f32[256,256]{1,0:T(8,128)S(1)} custom-call(f32[128,128]{1,0:T(8,128)S(1)} %get-tuple-element.105.first, f32[128,128]{1,0:T(8,128)S(1)} %get-tuple-element.106.across, f32[128,128]{1,0:T(8,128)S(1)} %root_middle.1.swept, f32[8,256]{1,0:T(8,128)S(1)} %get-tuple-element.108.row, f32[256,128]{1,0:T(8,128)S(1)} %get-tuple-element.109.col), custom_call_target="tpu_custom_call" | custom-call | flops 2500000000 | bytes 262144 | tf_op jit(solution)/shard_map/root_second/pallas_call | solution.py:331
  65.1 0.0 collective-permute-done.16
  65.2 2.4 %field.1 = f32[2048,256]{1,0:T(8,128)} custom-call(f32[2048,256]{1,0:T(8,128)S(1)} %get-tuple-element.94.level, bf16[2048,256]{1,0:T(8,128)(2,1)S(1)} %get-tuple-element.95.high, bf16[2048,256]{1,0:T(8,128)(2,1)S(1)} %get-tuple-element.96.low, f32[256,256]{1,0:T(8,128)S(1)} %root_second.1.inverse, f32[512,128]{1,0:T(8,128)S(1)} %pad_maximum_fusion.4.side), custom_call_target="tpu_custom_call" | custom-call | flops 805306368 | bytes 6291456 | tf_op jit(solution)/shard_map/field/pallas_call | solution.py:472
  (30 shorter events, 0.6 us)
Async XLA Ops:
  0.6 5.0 %copy-start = (f32[2048,256]{1,0:T(8,128)S(1)}, f32[2048,256]{1,0:T(8,128)}, u32[]{:S(2)}) copy-start(f32[2048,256]{1,0:T(8,128)} %sources.3) | copy-start | bytes 6291460
  5.1 3.3 %collective-permute-start = (f32[520,128]{1,0:T(8,128)S(1)}, f32[520,128]{1,0:T(8,128)S(1)}, u32[]{:S(2)}, u32[]{:S(2)}) collective-permute-start(f32[520,128]{1,0:T(8,128)S(1)} %get-tuple-element.63), channel_id=1, source_target_pairs={{0,1},{1,0},{2,3},{3,2},{4,5},{5,4},{6,7},{7,6},{8,9},{9,8},{10,11... | collective-permute-start | bytes 798728 | tf_op jit(solution)/shard_map/ppermute | solution.py:485
  8.4 7.0 %collective-permute-start.2 = (f32[512,128]{1,0:T(8,128)S(1)}, f32[512,128]{1,0:T(8,128)S(1)}, u32[]{:S(2)}, u32[]{:S(2)}) collective-permute-start(f32[512,128]{1,0:T(8,128)S(1)} %get-tuple-element.66), channel_id=1, source_target_pairs={{0,1},{1,0},{2,3},{3,2},{4,5},{5,4},{6,7},{7,6},{8,9},{9,8},{10,11... | collective-permute-start | bytes 786440 | tf_op jit(solution)/shard_map/ppermute | solution.py:485
  8.6 6.8 %collective-permute-start.1 = (f32[264,128]{1,0:T(8,128)S(1)}, f32[264,128]{1,0:T(8,128)S(1)}, u32[]{:S(2)}, u32[]{:S(2)}) collective-permute-start(f32[264,128]{1,0:T(8,128)S(1)} %slice_select_fusion.1), channel_id=1, source_target_pairs={{0,4},{1,5},{2,6},{3,7},{4,0},{5,1},{6,2},{7,3},{8,12},{9,13},{10,... | collective-permute-start | bytes 405512 | tf_op jit(solution)/shard_map/ppermute | solution.py:485
  15.5 6.2 %collective-permute-start.4 = (f32[256,128]{1,0:T(8,128)S(1)}, f32[256,128]{1,0:T(8,128)S(1)}, u32[]{:S(2)}, u32[]{:S(2)}) collective-permute-start(f32[256,128]{1,0:T(8,128)S(1)} %slice_select_fusion.2), channel_id=1, source_target_pairs={{0,4},{1,5},{2,6},{3,7},{4,0},{5,1},{6,2},{7,3},{8,12},{9,13},{10,... | collective-permute-start | bytes 393224 | tf_op jit(solution)/shard_map/ppermute | solution.py:485
  17.3 4.4 %collective-permute-start.3 = (f32[136,128]{1,0:T(8,128)S(1)}, f32[136,128]{1,0:T(8,128)S(1)}, u32[]{:S(2)}, u32[]{:S(2)}) collective-permute-start(f32[136,128]{1,0:T(8,128)S(1)} %slice_select_fusion.4), channel_id=1, source_target_pairs={{0,8},{1,9},{2,10},{3,11},{4,12},{5,13},{6,14},{7,15},{8,0},{9,1},... | collective-permute-start | bytes 208904 | tf_op jit(solution)/shard_map/ppermute | solution.py:485
  21.8 7.7 %collective-permute-start.5 = (f32[136,128]{1,0:T(8,128)S(1)}, f32[136,128]{1,0:T(8,128)S(1)}, u32[]{:S(2)}, u32[]{:S(2)}) collective-permute-start(f32[136,128]{1,0:T(8,128)S(1)} %select_add_fusion.2), channel_id=1, source_target_pairs={{0,16},{1,17},{2,18},{3,19},{4,20},{5,21},{6,22},{7,23},{8,24},{9,... | collective-permute-start | bytes 208904 | tf_op jit(solution)/shard_map/ppermute | solution.py:485
  24.4 5.0 %collective-permute-start.6 = (f32[128,128]{1,0:T(8,128)S(1)}, f32[128,128]{1,0:T(8,128)S(1)}, u32[]{:S(2)}, u32[]{:S(2)}) collective-permute-start(f32[128,128]{1,0:T(8,128)S(1)} %slice_select_fusion.5), channel_id=1, source_target_pairs={{0,8},{1,9},{2,10},{3,11},{4,12},{5,13},{6,14},{7,15},{8,0},{9,1},... | collective-permute-start | bytes 196616 | tf_op jit(solution)/shard_map/ppermute | solution.py:485
  29.5 7.5 %collective-permute-start.7 = (f32[136,128]{1,0:T(8,128)S(1)}, f32[136,128]{1,0:T(8,128)S(1)}, u32[]{:S(2)}, u32[]{:S(2)}) collective-permute-start(f32[136,128]{1,0:T(8,128)S(1)} %add.39), channel_id=1, source_target_pairs={{0,8},{1,9},{2,10},{3,11},{4,12},{5,13},{6,14},{7,15},{8,0},{9,1},... | collective-permute-start | bytes 208904 | tf_op jit(solution)/shard_map/ppermute | solution.py:485
  31.1 5.8 %collective-permute-start.8 = (f32[128,128]{1,0:T(8,128)S(1)}, f32[128,128]{1,0:T(8,128)S(1)}, u32[]{:S(2)}, u32[]{:S(2)}) collective-permute-start(f32[128,128]{1,0:T(8,128)S(1)} %select_add_fusion.3), channel_id=1, source_target_pairs={{0,16},{1,17},{2,18},{3,19},{4,20},{5,21},{6,22},{7,23},{8,24},{9,... | collective-permute-start | bytes 196616 | tf_op jit(solution)/shard_map/ppermute | solution.py:485
  37.0 6.9 %copy-start.1 = (f32[2,256,256]{2,1,0:T(8,128)S(1)}, f32[2,256,256]{2,1,0:T(8,128)}, u32[]{:S(2)}) copy-start(f32[2,256,256]{2,1,0:T(8,128)} %coupling.1) | copy-start | bytes 1572868
  37.0 5.1 %collective-permute-start.9 = (f32[264,128]{1,0:T(8,128)S(1)}, f32[264,128]{1,0:T(8,128)S(1)}, u32[]{:S(2)}, u32[]{:S(2)}) collective-permute-start(f32[264,128]{1,0:T(8,128)S(1)} %pad_maximum_fusion.5), channel_id=1, source_target_pairs={{0,4},{1,5},{2,6},{3,7},{4,0},{5,1},{6,2},{7,3},{8,12},{9,13},{10,... | collective-permute-start | bytes 405512 | tf_op jit(solution)/shard_map/ppermute | solution.py:485
  37.6 4.3 %collective-permute-start.10 = (f32[128,128]{1,0:T(8,128)S(1)}, f32[128,128]{1,0:T(8,128)S(1)}, u32[]{:S(2)}, u32[]{:S(2)}) collective-permute-start(f32[128,128]{1,0:T(8,128)S(1)} %add.41), channel_id=1, source_target_pairs={{0,8},{1,9},{2,10},{3,11},{4,12},{5,13},{6,14},{7,15},{8,0},{9,1},... | collective-permute-start | bytes 196616 | tf_op jit(solution)/shard_map/ppermute | solution.py:485
  42.2 1.6 %collective-permute-start.12 = (f32[520,128]{1,0:T(8,128)S(1)}, f32[520,128]{1,0:T(8,128)S(1)}, u32[]{:S(2)}, u32[]{:S(2)}) collective-permute-start(f32[520,128]{1,0:T(8,128)S(1)} %pad_maximum_fusion.2), channel_id=1, source_target_pairs={{0,1},{1,0},{2,3},{3,2},{4,5},{5,4},{6,7},{7,6},{8,9},{9,8},{10,11... | collective-permute-start | bytes 798728 | tf_op jit(solution)/shard_map/ppermute | solution.py:485
  42.3 6.3 %collective-permute-start.11 = (f32[256,128]{1,0:T(8,128)S(1)}, f32[256,128]{1,0:T(8,128)S(1)}, u32[]{:S(2)}, u32[]{:S(2)}) collective-permute-start(f32[256,128]{1,0:T(8,128)S(1)} %pad_maximum_fusion.6), channel_id=1, source_target_pairs={{0,4},{1,5},{2,6},{3,7},{4,0},{5,1},{6,2},{7,3},{8,12},{9,13},{10,... | collective-permute-start | bytes 393224 | tf_op jit(solution)/shard_map/ppermute | solution.py:485
  48.7 5.0 %collective-permute-start.13 = (f32[512,128]{1,0:T(8,128)S(1)}, f32[512,128]{1,0:T(8,128)S(1)}, u32[]{:S(2)}, u32[]{:S(2)}) collective-permute-start(f32[512,128]{1,0:T(8,128)S(1)} %pad_maximum_fusion.3), channel_id=1, source_target_pairs={{0,1},{1,0},{2,3},{3,2},{4,5},{5,4},{6,7},{7,6},{8,9},{9,8},{10,11... | collective-permute-start | bytes 786440 | tf_op jit(solution)/shard_map/ppermute | solution.py:485
  52.0 5.9 %collective-permute-start.15 = (f32[264,128]{1,0:T(8,128)S(1)}, f32[264,128]{1,0:T(8,128)S(1)}, u32[]{:S(2)}, u32[]{:S(2)}) collective-permute-start(f32[264,128]{1,0:T(8,128)S(1)} %get-tuple-element.98), channel_id=1, source_target_pairs={{0,2},{1,3},{2,0},{3,1},{4,6},{5,7},{6,4},{7,5},{8,10},{9,11},{10,... | collective-permute-start | bytes 405512 | tf_op jit(solution)/shard_map/ppermute | solution.py:485
  53.7 4.3 %copy-start.2 = (f32[256,256]{1,0:T(8,128)S(1)}, f32[256,256]{1,0:T(8,128)}, u32[]{:S(2)}) copy-start(f32[256,256]{1,0:T(8,128)} %param.9) | copy-start | bytes 786436
  57.4 5.5 %collective-permute-start.14 = (f32[256,128]{1,0:T(8,128)S(1)}, f32[256,128]{1,0:T(8,128)S(1)}, u32[]{:S(2)}, u32[]{:S(2)}) collective-permute-start(f32[256,128]{1,0:T(8,128)S(1)} %slice_select_fusion), channel_id=1, source_target_pairs={{0,2},{1,3},{2,0},{3,1},{4,6},{5,7},{6,4},{7,5},{8,10},{9,11},{10,... | collective-permute-start | bytes 393224 | tf_op jit(solution)/shard_map/ppermute | solution.py:485
  62.9 2.2 %collective-permute-start.16 = (f32[256,128]{1,0:T(8,128)S(1)}, f32[256,128]{1,0:T(8,128)S(1)}, u32[]{:S(2)}, u32[]{:S(2)}) collective-permute-start(f32[256,128]{1,0:T(8,128)S(1)} %add.43), channel_id=1, source_target_pairs={{0,1},{1,0},{2,3},{3,2},{4,5},{5,4},{6,7},{7,6},{8,9},{9,8},{10,11... | collective-permute-start | bytes 393224 | tf_op jit(solution)/shard_map/ppermute | solution.py:485

commit v15 on v11

--- a/solution.py
+++ b/solution.py
@@ -14,6 +14,7 @@
 R = 256
 LANES = 128
 TILE = 512
+OUT_TILE = 1024
 GROUPS = 8
 VMEM_LIMIT = 16 * 1024 * 1024
 SYMMETRIC, FULL = 264, 512
@@ -112,21 +113,16 @@
             for which, (source, target) in enumerate(pairs)
         ]
 
-    small = TILE // 2
-    parts = (pl.ds(0, small), pl.ds(small, small))
-    for sem, at in enumerate(parts):
-        for copy in copies(at, sem):
-            copy.start()
-    for tile in range(1, tiles):
-        for copy in copies(tile_at(tile), tile + 1):
+    for tile in range(tiles):
+        for copy in copies(tile_at(tile), tile):
             copy.start()
     acc[...] = jnp.zeros_like(acc)
 
-    def add_rows(at, sem):
-        for copy in copies(at, sem):
+    def step(tile, carry):
+        for copy in copies(tile_at(tile), tile):
             copy.wait()
-        h2, l2 = split2(b2[at, :])
-        h1, l1 = split2(b1[at, :])
+        h2, l2 = split2(b2[tile_at(tile), :])
+        h1, l1 = split2(b1[tile_at(tile), :])
         h2t, l2t, h1t = h2.T, l2.T, h1.T
         acc[0] += dot(h2t, h2)
         acc[1] += dot(h2t, l2)
@@ -134,14 +130,9 @@
         acc[2] += dot(left, jnp.concatenate([h1, l1, h1], axis=0))
         acc[3] += dot(h1t, h1)
         acc[4] += dot(h1t, l1)
-
-    def step(tile, carry):
-        add_rows(tile_at(tile), tile + 1)
         return carry
 
-    for sem, at in enumerate(parts):
-        add_rows(at, sem)
-    lax.fori_loop(1, tiles, step, 0)
+    lax.fori_loop(0, tiles, step, 0)
     low = acc[1]
     store_symmetric(packed, OWN, acc[0] + low + low.T)
     low = acc[4]
@@ -185,7 +176,7 @@
         scratch_shapes=[
             pltpu.VMEM((5, R, R), F32),
             pltpu.VMEM((PANEL_TERMS, LANES), F32),
-            pltpu.SemaphoreType.DMA((2, rows // TILE + 1)),
+            pltpu.SemaphoreType.DMA((2, rows // TILE)),
         ],
         compiler_params=pltpu.CompilerParams(vmem_limit_bytes=VMEM_LIMIT),
         cost_estimate=cost(7, rows, 2),
@@ -420,13 +411,16 @@
 
 
 def by_tiles(rows, out, stage, sems, value, beside=None):
-    tiles = rows // TILE
+    tiles = rows // OUT_TILE
+
+    def at(tile):
+        return pl.ds(pl.multiple_of(tile * OUT_TILE, OUT_TILE), OUT_TILE)
 
     def copy(tile):
-        return pltpu.make_async_copy(stage.at[tile_at(tile)], out.at[tile_at(tile)], sems.at[tile])
+        return pltpu.make_async_copy(stage.at[at(tile)], out.at[at(tile)], sems.at[tile])
 
     def step(tile, carry):
-        stage[tile_at(tile), :] = value(tile_at(tile))
+        stage[at(tile), :] = value(at(tile))
         copy(tile).start()
         return carry
 
@@ -469,7 +463,7 @@
         kernel,
         out_specs=[pl.BlockSpec(memory_space=pl.ANY)] + [pl.BlockSpec(memory_space=pltpu.VMEM)] * len(more),
         out_shape=[jax.ShapeDtypeStruct((rows, R), F32), *more],
-        scratch_shapes=[pltpu.VMEM((rows, R), F32), pltpu.SemaphoreType.DMA((rows // TILE,))],
+        scratch_shapes=[pltpu.VMEM((rows, R), F32), pltpu.SemaphoreType.DMA((rows // OUT_TILE,))],
         compiler_params=pltpu.CompilerParams(vmem_limit_bytes=VMEM_LIMIT),
         cost_estimate=cost(passes, rows, 3),
         name=name,

time: 68.1 us -> 67.8 us (level)
  no operation moved by 1% of the time
where the time goes in v15:
time: 67.8 us; the launch traced here: 67.6 us
  Pallas kernels  27.8 us (41%)
  waiting for transfers between devices  19.4 us (29%)
  starting transfers between devices  18.7 us (28%)
  between operations  1.13 us (2%)
    ppermute x17, waiting for transfers between devices, exchange(): return lax.ppermute(x, AXES, [(i, i ^ mask) for i in range(count)])  19.4 us
    ppermute x17, starting transfers between devices, exchange(): return lax.ppermute(x, AXES, [(i, i ^ mask) for i in range(count)])  18.7 us
    pallas_call x7, Pallas kernels, call(): pl.pallas_call(kernel, out_shape=out_shape, scratch_shapes=list(scratch),...  14.7 us
    pallas_call x2, Pallas kernels, update(): pl.pallas_call(kernel, out_specs=[pl.BlockSpec(memory_space=pl.ANY)] + [p...  6.07 us
    pallas_call x1, Pallas kernels, panel_gram(): pl.pallas_call(panel_gram_kernel, in_specs=[pl.BlockSpec(memory_space=pl....  4.48 us
    pallas_call x1, Pallas kernels, source_gram(): pl.pallas_call(source_gram_kernel, out_shape=(part, part), scratch_shapes...  2.58 us
  transfers between devices with their start and end apart: 17, of which 8 were waited for; matrix products, arithmetic and copies ran while one was open for 1% of the time, Pallas kernels for 31%

profile of v15, /device:TPU:0, one launch (start us, length us, event | category | flops | bytes accessed | tf_op | source)
XLA Modules:
  0.0 67.6 jit_solution(1257031386537532079)
XLA Ops:
  0.6 0.0 copy-start
  0.6 4.5 %panel_gram.1 = (f32[520,128]{1,0:T(8,128)S(1)}, f32[520,128]{1,0:T(8,128)S(1)}, f32[2048,256]{1,0:T(8,128)S(1)}, f32[2048,256]{1,0:T(8,128)S(1)}) custom-call(f32[2048,256]{1,0:T(8,128)} %q_two, f32[2048,256]{1,0:T(8,128)} %q_one.1), custom_call_target="tpu_custom_call" | custom-call | flops 1879048192 | bytes 4194304 | tf_op jit(solution)/shard_map/panel_gram/pallas_call | solution.py:172
  5.1 0.5 collective-permute-start
  5.6 0.0 copy-done
  5.7 2.6 %source_gram.1 = (f32[512,128]{1,0:T(8,128)S(1)}, f32[512,128]{1,0:T(8,128)S(1)}) custom-call(f32[2048,256]{1,0:T(8,128)S(1)} %get-tuple-element.58.b2, f32[2048,256]{1,0:T(8,128)S(1)} %get-tuple-element.59.b1, f32[2048,256]{1,0:T(8,128)S(1)} %copy-done), custom_call_target="tpu_custom_call" | custom-call | flops 1610612736 | bytes 6291456 | tf_op jit(solution)/shard_map/source_gram/pallas_call | solution.py:189
  8.2 0.0 collective-permute-done
  8.2 0.1 collective-permute-start.2
  8.4 3.0 %collective-permute-start.1 = (f32[264,128]{1,0:T(8,128)S(1)}, f32[264,128]{1,0:T(8,128)S(1)}, u32[]{:S(2)}, u32[]{:S(2)}) collective-permute-start(f32[264,128]{1,0:T(8,128)S(1)} %slice_select_fusion.1), channel_id=1, source_target_pairs={{0,4},{1,5},{2,6},{3,7},{4,0},{5,1},{6,2},{7,3},{8,12},{9,13},{10,... | collective-permute-start | bytes 405512 | tf_op jit(solution)/shard_map/ppermute | solution.py:475
  11.4 3.8 %collective-permute-done.1 = f32[264,128]{1,0:T(8,128)S(1)} collective-permute-done((f32[264,128]{1,0:T(8,128)S(1)}, f32[264,128]{1,0:T(8,128)S(1)}, u32[]{:S(2)}, u32[]{:S(2)}) %collective-permute-start.1) | collective-permute-done | bytes 135200 | tf_op jit(solution)/shard_map/ppermute | solution.py:475
  15.2 0.0 collective-permute-done.2
  15.3 1.8 %collective-permute-start.4 = (f32[256,128]{1,0:T(8,128)S(1)}, f32[256,128]{1,0:T(8,128)S(1)}, u32[]{:S(2)}, u32[]{:S(2)}) collective-permute-start(f32[256,128]{1,0:T(8,128)S(1)} %slice_select_fusion.2), channel_id=1, source_target_pairs={{0,4},{1,5},{2,6},{3,7},{4,0},{5,1},{6,2},{7,3},{8,12},{9,13},{10,... | collective-permute-start | bytes 393224 | tf_op jit(solution)/shard_map/ppermute | solution.py:475
  17.1 1.7 %collective-permute-start.3 = (f32[136,128]{1,0:T(8,128)S(1)}, f32[136,128]{1,0:T(8,128)S(1)}, u32[]{:S(2)}, u32[]{:S(2)}) collective-permute-start(f32[136,128]{1,0:T(8,128)S(1)} %slice_select_fusion.4), channel_id=1, source_target_pairs={{0,8},{1,9},{2,10},{3,11},{4,12},{5,13},{6,14},{7,15},{8,0},{9,1},... | collective-permute-start | bytes 208904 | tf_op jit(solution)/shard_map/ppermute | solution.py:475
  18.8 2.7 %collective-permute-done.3 = f32[136,128]{1,0:T(8,128)S(1)} collective-permute-done((f32[136,128]{1,0:T(8,128)S(1)}, f32[136,128]{1,0:T(8,128)S(1)}, u32[]{:S(2)}, u32[]{:S(2)}) %collective-permute-start.3) | collective-permute-done | bytes 69664 | tf_op jit(solution)/shard_map/ppermute | solution.py:475
  21.5 0.0 collective-permute-done.4
  21.5 2.7 %collective-permute-start.5 = (f32[136,128]{1,0:T(8,128)S(1)}, f32[136,128]{1,0:T(8,128)S(1)}, u32[]{:S(2)}, u32[]{:S(2)}) collective-permute-start(f32[136,128]{1,0:T(8,128)S(1)} %select_add_fusion.2), channel_id=1, source_target_pairs={{0,16},{1,17},{2,18},{3,19},{4,20},{5,21},{6,22},{7,23},{8,24},{9,... | collective-permute-start | bytes 208904 | tf_op jit(solution)/shard_map/ppermute | solution.py:475
  24.2 1.6 %collective-permute-start.6 = (f32[128,128]{1,0:T(8,128)S(1)}, f32[128,128]{1,0:T(8,128)S(1)}, u32[]{:S(2)}, u32[]{:S(2)}) collective-permute-start(f32[128,128]{1,0:T(8,128)S(1)} %slice_select_fusion.5), channel_id=1, source_target_pairs={{0,8},{1,9},{2,10},{3,11},{4,12},{5,13},{6,14},{7,15},{8,0},{9,1},... | collective-permute-start | bytes 196616 | tf_op jit(solution)/shard_map/ppermute | solution.py:475
  25.9 3.4 %collective-permute-done.6 = f32[128,128]{1,0:T(8,128)S(1)} collective-permute-done((f32[128,128]{1,0:T(8,128)S(1)}, f32[128,128]{1,0:T(8,128)S(1)}, u32[]{:S(2)}, u32[]{:S(2)}) %collective-permute-start.6) | collective-permute-done | bytes 65568 | tf_op jit(solution)/shard_map/ppermute | solution.py:475
  29.2 0.0 collective-permute-done.5
  29.3 1.7 %collective-permute-start.7 = (f32[136,128]{1,0:T(8,128)S(1)}, f32[136,128]{1,0:T(8,128)S(1)}, u32[]{:S(2)}, u32[]{:S(2)}) collective-permute-start(f32[136,128]{1,0:T(8,128)S(1)} %add.39), channel_id=1, source_target_pairs={{0,8},{1,9},{2,10},{3,11},{4,12},{5,13},{6,14},{7,15},{8,0},{9,1},... | collective-permute-start | bytes 208904 | tf_op jit(solution)/shard_map/ppermute | solution.py:475
  30.9 0.9 %collective-permute-start.8 = (f32[128,128]{1,0:T(8,128)S(1)}, f32[128,128]{1,0:T(8,128)S(1)}, u32[]{:S(2)}, u32[]{:S(2)}) collective-permute-start(f32[128,128]{1,0:T(8,128)S(1)} %select_add_fusion.3), channel_id=1, source_target_pairs={{0,16},{1,17},{2,18},{3,19},{4,20},{5,21},{6,22},{7,23},{8,24},{9,... | collective-permute-start | bytes 196616 | tf_op jit(solution)/shard_map/ppermute | solution.py:475
  31.8 4.9 %collective-permute-done.8 = f32[128,128]{1,0:T(8,128)S(1)} collective-permute-done((f32[128,128]{1,0:T(8,128)S(1)}, f32[128,128]{1,0:T(8,128)S(1)}, u32[]{:S(2)}, u32[]{:S(2)}) %collective-permute-start.8) | collective-permute-done | bytes 65568 | tf_op jit(solution)/shard_map/ppermute | solution.py:475
  36.8 0.0 collective-permute-done.7
  36.8 0.0 copy-start.1
  36.8 0.6 collective-permute-start.9
  37.4 0.1 collective-permute-start.10
  37.6 4.2 %collective-permute-done.10 = f32[128,128]{1,0:T(8,128)S(1)} collective-permute-done((f32[128,128]{1,0:T(8,128)S(1)}, f32[128,128]{1,0:T(8,128)S(1)}, u32[]{:S(2)}, u32[]{:S(2)}) %collective-permute-start.10) | collective-permute-done | bytes 65568 | tf_op jit(solution)/shard_map/ppermute | solution.py:475
  41.8 0.1 collective-permute-done.9
  42.0 0.1 collective-permute-start.12
  42.1 1.4 %collective-permute-start.11 = (f32[256,128]{1,0:T(8,128)S(1)}, f32[256,128]{1,0:T(8,128)S(1)}, u32[]{:S(2)}, u32[]{:S(2)}) collective-permute-start(f32[256,128]{1,0:T(8,128)S(1)} %pad_maximum_fusion.6), channel_id=1, source_target_pairs={{0,4},{1,5},{2,6},{3,7},{4,0},{5,1},{6,2},{7,3},{8,12},{9,13},{10,... | collective-permute-start | bytes 393224 | tf_op jit(solution)/shard_map/ppermute | solution.py:475
  43.5 0.1 collective-permute-done.12
  43.6 0.1 broadcast_select_fusion.1
  43.7 0.0 copy-done.1
  43.7 3.3 %level_first.1 = (f32[128,128]{1,0:T(8,128)S(1)}, f32[128,128]{1,0:T(8,128)S(1)}, f32[128,128]{1,0:T(8,128)S(1)}, f32[8,256]{1,0:T(8,128)S(1)}, f32[256,128]{1,0:T(8,128)S(1)}) custom-call(f32[1040,128]{1,0:T(8,128)S(1)} %pad_maximum_fusion.gram_ref.terms, f32[2,256,256]{2,1,0:T(8,128)S(1)} %copy-done.1), custom_call_target="tpu_custom_call" | custom-call | flops 5000000000 | bytes 262144 | tf_op jit(solution)/shard_map/level_first/pallas_call | solution.py:321
  47.0 1.4 %level_middle.1.swept = f32[128,128]{1,0:T(8,128)S(1)} custom-call(f32[128,128]{1,0:T(8,128)S(1)} %get-tuple-element.81.rest), custom_call_target="tpu_custom_call" | custom-call | flops 2500000000 | bytes 262144 | tf_op jit(solution)/shard_map/level_middle/pallas_call | solution.py:321
  48.4 0.0 collective-permute-done.11
  48.5 0.2 collective-permute-start.13
  48.7 2.1 %level_second.1.inverse = f32[256,256]{1,0:T(8,128)S(1)} custom-call(f32[128,128]{1,0:T(8,128)S(1)} %get-tuple-element.85.first, f32[128,128]{1,0:T(8,128)S(1)} %get-tuple-element.86.across, f32[128,128]{1,0:T(8,128)S(1)} %level_middle.1.swept, f32[8,256]{1,0:T(8,128)S(1)} %get-tuple-element.88.row, f32[256,128]{1,0:T(8,128)S(1)} %get-tuple-element.89.col), custom_call_target="tpu_custom_call" | custom-call | flops 2500000000 | bytes 262144 | tf_op jit(solution)/shard_map/level_second/pallas_call | solution.py:321
  50.8 1.1 %panel_solve.1 = (f32[256,256]{1,0:T(8,128)S(1)}, f32[264,128]{1,0:T(8,128)S(1)}) custom-call(f32[256,256]{1,0:T(8,128)S(1)} %level_second.1.inverse, f32[1040,128]{1,0:T(8,128)S(1)} %pad_maximum_fusion.gram_ref.terms), custom_call_target="tpu_custom_call" | custom-call | bytes 262144 | tf_op jit(solution)/shard_map/panel_solve/pallas_call | solution.py:321
  51.9 1.6 %collective-permute-start.15 = (f32[264,128]{1,0:T(8,128)S(1)}, f32[264,128]{1,0:T(8,128)S(1)}, u32[]{:S(2)}, u32[]{:S(2)}) collective-permute-start(f32[264,128]{1,0:T(8,128)S(1)} %get-tuple-element.98), channel_id=1, source_target_pairs={{0,2},{1,3},{2,0},{3,1},{4,6},{5,7},{6,4},{7,5},{8,10},{9,11},{10,... | collective-permute-start | bytes 405512 | tf_op jit(solution)/shard_map/ppermute | solution.py:475
  53.5 0.0 collective-permute-done.13
  53.5 0.0 copy-start.2
  53.6 3.6 %panel.1 = (f32[2048,256]{1,0:T(8,128)}, f32[2048,256]{1,0:T(8,128)S(1)}, bf16[2048,256]{1,0:T(8,128)(2,1)S(1)}, bf16[2048,256]{1,0:T(8,128)(2,1)S(1)}, f32[512,128]{1,0:T(8,128)S(1)}) custom-call(f32[2048,256]{1,0:T(8,128)S(1)} %get-tuple-element.58.b2, f32[2048,256]{1,0:T(8,128)S(1)} %get-tuple-element.59.b1, f32[2048,256]{1,0:T(8,128)S(1)} %copy-done, ...), custom_call_target="tpu_custom_call" | custom-call | flops 2147483648 | bytes 6291456 | tf_op jit(solution)/shard_map/panel/pallas_call | solution.py:462
  57.2 0.6 collective-permute-start.14
  57.8 0.0 collective-permute-done.15
  57.8 0.0 copy-done.2
  57.8 3.3 %root_first.1 = (f32[128,128]{1,0:T(8,128)S(1)}, f32[128,128]{1,0:T(8,128)S(1)}, f32[128,128]{1,0:T(8,128)S(1)}, f32[8,256]{1,0:T(8,128)S(1)}, f32[256,128]{1,0:T(8,128)S(1)}) custom-call(f32[264,128]{1,0:T(8,128)S(1)} %add.42.gram_ref, f32[1,256,256]{2,1,0:T(8,128)S(1)} %bitcast.1), custom_call_target="tpu_custom_call" | custom-call | flops 5000000000 | bytes 262144 | tf_op jit(solution)/shard_map/root_first/pallas_call | solution.py:321
  61.2 1.4 %root_middle.1.swept = f32[128,128]{1,0:T(8,128)S(1)} custom-call(f32[128,128]{1,0:T(8,128)S(1)} %get-tuple-element.102.rest), custom_call_target="tpu_custom_call" | custom-call | flops 2500000000 | bytes 262144 | tf_op jit(solution)/shard_map/root_middle/pallas_call | solution.py:321
  62.6 0.2 collective-permute-done.14
  62.8 0.1 collective-permute-start.16
  62.8 2.1 %root_second.1.inverse = f32[256,256]{1,0:T(8,128)S(1)} custom-call(f32[128,128]{1,0:T(8,128)S(1)} %get-tuple-element.105.first, f32[128,128]{1,0:T(8,128)S(1)} %get-tuple-element.106.across, f32[128,128]{1,0:T(8,128)S(1)} %root_middle.1.swept, f32[8,256]{1,0:T(8,128)S(1)} %get-tuple-element.108.row, f32[256,128]{1,0:T(8,128)S(1)} %get-tuple-element.109.col), custom_call_target="tpu_custom_call" | custom-call | flops 2500000000 | bytes 262144 | tf_op jit(solution)/shard_map/root_second/pallas_call | solution.py:321
  64.9 0.0 collective-permute-done.16
  65.0 2.4 %field.1 = f32[2048,256]{1,0:T(8,128)} custom-call(f32[2048,256]{1,0:T(8,128)S(1)} %get-tuple-element.94.level, bf16[2048,256]{1,0:T(8,128)(2,1)S(1)} %get-tuple-element.95.high, bf16[2048,256]{1,0:T(8,128)(2,1)S(1)} %get-tuple-element.96.low, f32[256,256]{1,0:T(8,128)S(1)} %root_second.1.inverse, f32[512,128]{1,0:T(8,128)S(1)} %pad_maximum_fusion.4.side), custom_call_target="tpu_custom_call" | custom-call | flops 805306368 | bytes 6291456 | tf_op jit(solution)/shard_map/field/pallas_call | solution.py:462
  (30 shorter events, 0.6 us)
Async XLA Ops:
  0.6 5.0 %copy-start = (f32[2048,256]{1,0:T(8,128)S(1)}, f32[2048,256]{1,0:T(8,128)}, u32[]{:S(2)}) copy-start(f32[2048,256]{1,0:T(8,128)} %sources.3) | copy-start | bytes 6291460
  5.1 3.1 %collective-permute-start = (f32[520,128]{1,0:T(8,128)S(1)}, f32[520,128]{1,0:T(8,128)S(1)}, u32[]{:S(2)}, u32[]{:S(2)}) collective-permute-start(f32[520,128]{1,0:T(8,128)S(1)} %get-tuple-element.63), channel_id=1, source_target_pairs={{0,1},{1,0},{2,3},{3,2},{4,5},{5,4},{6,7},{7,6},{8,9},{9,8},{10,11... | collective-permute-start | bytes 798728 | tf_op jit(solution)/shard_map/ppermute | solution.py:475
  8.2 6.9 %collective-permute-start.2 = (f32[512,128]{1,0:T(8,128)S(1)}, f32[512,128]{1,0:T(8,128)S(1)}, u32[]{:S(2)}, u32[]{:S(2)}) collective-permute-start(f32[512,128]{1,0:T(8,128)S(1)} %get-tuple-element.66), channel_id=1, source_target_pairs={{0,1},{1,0},{2,3},{3,2},{4,5},{5,4},{6,7},{7,6},{8,9},{9,8},{10,11... | collective-permute-start | bytes 786440 | tf_op jit(solution)/shard_map/ppermute | solution.py:475
  8.4 6.8 %collective-permute-start.1 = (f32[264,128]{1,0:T(8,128)S(1)}, f32[264,128]{1,0:T(8,128)S(1)}, u32[]{:S(2)}, u32[]{:S(2)}) collective-permute-start(f32[264,128]{1,0:T(8,128)S(1)} %slice_select_fusion.1), channel_id=1, source_target_pairs={{0,4},{1,5},{2,6},{3,7},{4,0},{5,1},{6,2},{7,3},{8,12},{9,13},{10,... | collective-permute-start | bytes 405512 | tf_op jit(solution)/shard_map/ppermute | solution.py:475
  15.3 6.2 %collective-permute-start.4 = (f32[256,128]{1,0:T(8,128)S(1)}, f32[256,128]{1,0:T(8,128)S(1)}, u32[]{:S(2)}, u32[]{:S(2)}) collective-permute-start(f32[256,128]{1,0:T(8,128)S(1)} %slice_select_fusion.2), channel_id=1, source_target_pairs={{0,4},{1,5},{2,6},{3,7},{4,0},{5,1},{6,2},{7,3},{8,12},{9,13},{10,... | collective-permute-start | bytes 393224 | tf_op jit(solution)/shard_map/ppermute | solution.py:475
  17.1 4.4 %collective-permute-start.3 = (f32[136,128]{1,0:T(8,128)S(1)}, f32[136,128]{1,0:T(8,128)S(1)}, u32[]{:S(2)}, u32[]{:S(2)}) collective-permute-start(f32[136,128]{1,0:T(8,128)S(1)} %slice_select_fusion.4), channel_id=1, source_target_pairs={{0,8},{1,9},{2,10},{3,11},{4,12},{5,13},{6,14},{7,15},{8,0},{9,1},... | collective-permute-start | bytes 208904 | tf_op jit(solution)/shard_map/ppermute | solution.py:475
  21.5 7.7 %collective-permute-start.5 = (f32[136,128]{1,0:T(8,128)S(1)}, f32[136,128]{1,0:T(8,128)S(1)}, u32[]{:S(2)}, u32[]{:S(2)}) collective-permute-start(f32[136,128]{1,0:T(8,128)S(1)} %select_add_fusion.2), channel_id=1, source_target_pairs={{0,16},{1,17},{2,18},{3,19},{4,20},{5,21},{6,22},{7,23},{8,24},{9,... | collective-permute-start | bytes 208904 | tf_op jit(solution)/shard_map/ppermute | solution.py:475
  24.2 5.0 %collective-permute-start.6 = (f32[128,128]{1,0:T(8,128)S(1)}, f32[128,128]{1,0:T(8,128)S(1)}, u32[]{:S(2)}, u32[]{:S(2)}) collective-permute-start(f32[128,128]{1,0:T(8,128)S(1)} %slice_select_fusion.5), channel_id=1, source_target_pairs={{0,8},{1,9},{2,10},{3,11},{4,12},{5,13},{6,14},{7,15},{8,0},{9,1},... | collective-permute-start | bytes 196616 | tf_op jit(solution)/shard_map/ppermute | solution.py:475
  29.3 7.5 %collective-permute-start.7 = (f32[136,128]{1,0:T(8,128)S(1)}, f32[136,128]{1,0:T(8,128)S(1)}, u32[]{:S(2)}, u32[]{:S(2)}) collective-permute-start(f32[136,128]{1,0:T(8,128)S(1)} %add.39), channel_id=1, source_target_pairs={{0,8},{1,9},{2,10},{3,11},{4,12},{5,13},{6,14},{7,15},{8,0},{9,1},... | collective-permute-start | bytes 208904 | tf_op jit(solution)/shard_map/ppermute | solution.py:475
  30.9 5.8 %collective-permute-start.8 = (f32[128,128]{1,0:T(8,128)S(1)}, f32[128,128]{1,0:T(8,128)S(1)}, u32[]{:S(2)}, u32[]{:S(2)}) collective-permute-start(f32[128,128]{1,0:T(8,128)S(1)} %select_add_fusion.3), channel_id=1, source_target_pairs={{0,16},{1,17},{2,18},{3,19},{4,20},{5,21},{6,22},{7,23},{8,24},{9,... | collective-permute-start | bytes 196616 | tf_op jit(solution)/shard_map/ppermute | solution.py:475
  36.8 6.9 %copy-start.1 = (f32[2,256,256]{2,1,0:T(8,128)S(1)}, f32[2,256,256]{2,1,0:T(8,128)}, u32[]{:S(2)}) copy-start(f32[2,256,256]{2,1,0:T(8,128)} %coupling.1) | copy-start | bytes 1572868
  36.8 5.1 %collective-permute-start.9 = (f32[264,128]{1,0:T(8,128)S(1)}, f32[264,128]{1,0:T(8,128)S(1)}, u32[]{:S(2)}, u32[]{:S(2)}) collective-permute-start(f32[264,128]{1,0:T(8,128)S(1)} %pad_maximum_fusion.5), channel_id=1, source_target_pairs={{0,4},{1,5},{2,6},{3,7},{4,0},{5,1},{6,2},{7,3},{8,12},{9,13},{10,... | collective-permute-start | bytes 405512 | tf_op jit(solution)/shard_map/ppermute | solution.py:475
  37.4 4.3 %collective-permute-start.10 = (f32[128,128]{1,0:T(8,128)S(1)}, f32[128,128]{1,0:T(8,128)S(1)}, u32[]{:S(2)}, u32[]{:S(2)}) collective-permute-start(f32[128,128]{1,0:T(8,128)S(1)} %add.41), channel_id=1, source_target_pairs={{0,8},{1,9},{2,10},{3,11},{4,12},{5,13},{6,14},{7,15},{8,0},{9,1},... | collective-permute-start | bytes 196616 | tf_op jit(solution)/shard_map/ppermute | solution.py:475
  42.0 1.6 %collective-permute-start.12 = (f32[520,128]{1,0:T(8,128)S(1)}, f32[520,128]{1,0:T(8,128)S(1)}, u32[]{:S(2)}, u32[]{:S(2)}) collective-permute-start(f32[520,128]{1,0:T(8,128)S(1)} %pad_maximum_fusion.2), channel_id=1, source_target_pairs={{0,1},{1,0},{2,3},{3,2},{4,5},{5,4},{6,7},{7,6},{8,9},{9,8},{10,11... | collective-permute-start | bytes 798728 | tf_op jit(solution)/shard_map/ppermute | solution.py:475
  42.1 6.3 %collective-permute-start.11 = (f32[256,128]{1,0:T(8,128)S(1)}, f32[256,128]{1,0:T(8,128)S(1)}, u32[]{:S(2)}, u32[]{:S(2)}) collective-permute-start(f32[256,128]{1,0:T(8,128)S(1)} %pad_maximum_fusion.6), channel_id=1, source_target_pairs={{0,4},{1,5},{2,6},{3,7},{4,0},{5,1},{6,2},{7,3},{8,12},{9,13},{10,... | collective-permute-start | bytes 393224 | tf_op jit(solution)/shard_map/ppermute | solution.py:475
  48.5 5.0 %collective-permute-start.13 = (f32[512,128]{1,0:T(8,128)S(1)}, f32[512,128]{1,0:T(8,128)S(1)}, u32[]{:S(2)}, u32[]{:S(2)}) collective-permute-start(f32[512,128]{1,0:T(8,128)S(1)} %pad_maximum_fusion.3), channel_id=1, source_target_pairs={{0,1},{1,0},{2,3},{3,2},{4,5},{5,4},{6,7},{7,6},{8,9},{9,8},{10,11... | collective-permute-start | bytes 786440 | tf_op jit(solution)/shard_map/ppermute | solution.py:475
  51.9 5.9 %collective-permute-start.15 = (f32[264,128]{1,0:T(8,128)S(1)}, f32[264,128]{1,0:T(8,128)S(1)}, u32[]{:S(2)}, u32[]{:S(2)}) collective-permute-start(f32[264,128]{1,0:T(8,128)S(1)} %get-tuple-element.98), channel_id=1, source_target_pairs={{0,2},{1,3},{2,0},{3,1},{4,6},{5,7},{6,4},{7,5},{8,10},{9,11},{10,... | collective-permute-start | bytes 405512 | tf_op jit(solution)/shard_map/ppermute | solution.py:475
  53.5 4.3 %copy-start.2 = (f32[256,256]{1,0:T(8,128)S(1)}, f32[256,256]{1,0:T(8,128)}, u32[]{:S(2)}) copy-start(f32[256,256]{1,0:T(8,128)} %param.9) | copy-start | bytes 786436
  57.2 5.5 %collective-permute-start.14 = (f32[256,128]{1,0:T(8,128)S(1)}, f32[256,128]{1,0:T(8,128)S(1)}, u32[]{:S(2)}, u32[]{:S(2)}) collective-permute-start(f32[256,128]{1,0:T(8,128)S(1)} %slice_select_fusion), channel_id=1, source_target_pairs={{0,2},{1,3},{2,0},{3,1},{4,6},{5,7},{6,4},{7,5},{8,10},{9,11},{10,... | collective-permute-start | bytes 393224 | tf_op jit(solution)/shard_map/ppermute | solution.py:475
  62.8 2.2 %collective-permute-start.16 = (f32[256,128]{1,0:T(8,128)S(1)}, f32[256,128]{1,0:T(8,128)S(1)}, u32[]{:S(2)}, u32[]{:S(2)}) collective-permute-start(f32[256,128]{1,0:T(8,128)S(1)} %add.43), channel_id=1, source_target_pairs={{0,1},{1,0},{2,3},{3,2},{4,5},{5,4},{6,7},{7,6},{8,9},{9,8},{10,11... | collective-permute-start | bytes 393224 | tf_op jit(solution)/shard_map/ppermute | solution.py:475

commit v16 on v15

--- a/solution.py
+++ b/solution.py
@@ -99,8 +99,8 @@
     send[...] = packed[pl.ds(pl.multiple_of((1 - mine) * far, 8), half), :]
 
 
-def tile_at(tile):
-    return pl.ds(pl.multiple_of(tile * TILE, TILE), TILE)
+def tile_at(tile, size=TILE):
+    return pl.ds(pl.multiple_of(tile * size, size), size)
 
 
 def panel_gram_kernel(q_two, q_one, keep, send, b2, b1, acc, packed, sems):
@@ -145,15 +145,15 @@
     acc[...] = jnp.zeros_like(acc)
 
     def step(tile, carry):
-        hs, ls = split2(sources[tile_at(tile), :])
+        hs, ls = split2(sources[tile_at(tile, OUT_TILE), :])
         right = jnp.concatenate([hs, ls, hs], axis=0)
         for which, panel in enumerate((b2, b1)):
-            high, low = split2(panel[tile_at(tile), :])
+            high, low = split2(panel[tile_at(tile, OUT_TILE), :])
             turned = high.T
             acc[which] += dot(jnp.concatenate([turned, turned, low.T], axis=1), right)
         return carry
 
-    lax.fori_loop(0, b2.shape[0] // TILE, step, 0)
+    lax.fori_loop(0, b2.shape[0] // OUT_TILE, step, 0)
     store_square(packed, PROJECTED, acc[0])
     store_square(packed, SIDE, acc[1])
     store_halves(packed, keep, send)
@@ -433,8 +433,9 @@
 
 def panel_kernel(b2, b1, sources, x, inverse, terms, out, level, high, low, side_out, stage, sems):
     projected = load_square(terms, PROJECTED)
-    y = dot_full(inverse[...], projected)
-    store_square(side_out, 0, load_square(terms, SIDE) - dot_t_full(x[...], projected))
+    pieces = tall(projected)
+    y = dot(wide(inverse[...]), pieces)
+    store_square(side_out, 0, load_square(terms, SIDE) - dot(wide(x[...].T), pieces))
     right = jnp.concatenate([tall(x[...]), tall(y)], axis=1)
 
     def value(at):

time: 67.8 us -> 67.2 us (level)
  Pallas kernels: 27.8 us -> 27.1 us
  transfers between devices with their start and end apart: 17 -> 17, of which waited for: 8 -> 8; matrix products, arithmetic and copies ran while one was open for 1% -> 1% of each run, Pallas kernels for 31% -> 30%
where the time goes in v16:
time: 67.2 us; the launch traced here: 67 us
  Pallas kernels  27.1 us (40%)
  waiting for transfers between devices  19.4 us (29%)
  starting transfers between devices  18.7 us (28%)
  between operations  1.14 us (2%)
    ppermute x17, waiting for transfers between devices, exchange(): return lax.ppermute(x, AXES, [(i, i ^ mask) for i in range(count)])  19.4 us
    ppermute x17, starting transfers between devices, exchange(): return lax.ppermute(x, AXES, [(i, i ^ mask) for i in range(count)])  18.7 us
    pallas_call x7, Pallas kernels, call(): pl.pallas_call(kernel, out_shape=out_shape, scratch_shapes=list(scratch),...  14.6 us
    pallas_call x2, Pallas kernels, update(): pl.pallas_call(kernel, out_specs=[pl.BlockSpec(memory_space=pl.ANY)] + [p...  5.83 us
    pallas_call x1, Pallas kernels, panel_gram(): pl.pallas_call(panel_gram_kernel, in_specs=[pl.BlockSpec(memory_space=pl....  4.48 us
    pallas_call x1, Pallas kernels, source_gram(): pl.pallas_call(source_gram_kernel, out_shape=(part, part), scratch_shapes...  2.15 us
  transfers between devices with their start and end apart: 17, of which 8 were waited for; matrix products, arithmetic and copies ran while one was open for 1% of the time, Pallas kernels for 30%

profile of v16, /device:TPU:0, one launch (start us, length us, event | category | flops | bytes accessed | tf_op | source)
XLA Modules:
  0.0 67.0 jit_solution(4936131768541906709)
XLA Ops:
  0.6 0.0 copy-start
  0.6 4.5 %panel_gram.1 = (f32[520,128]{1,0:T(8,128)S(1)}, f32[520,128]{1,0:T(8,128)S(1)}, f32[2048,256]{1,0:T(8,128)S(1)}, f32[2048,256]{1,0:T(8,128)S(1)}) custom-call(f32[2048,256]{1,0:T(8,128)} %q_two, f32[2048,256]{1,0:T(8,128)} %q_one.1), custom_call_target="tpu_custom_call" | custom-call | flops 1879048192 | bytes 4194304 | tf_op jit(solution)/shard_map/panel_gram/pallas_call | solution.py:172
  5.1 0.5 collective-permute-start
  5.6 0.0 copy-done
  5.7 2.1 %source_gram.1 = (f32[512,128]{1,0:T(8,128)S(1)}, f32[512,128]{1,0:T(8,128)S(1)}) custom-call(f32[2048,256]{1,0:T(8,128)S(1)} %get-tuple-element.58.b2, f32[2048,256]{1,0:T(8,128)S(1)} %get-tuple-element.59.b1, f32[2048,256]{1,0:T(8,128)S(1)} %copy-done), custom_call_target="tpu_custom_call" | custom-call | flops 1610612736 | bytes 6291456 | tf_op jit(solution)/shard_map/source_gram/pallas_call | solution.py:189
  7.8 0.0 collective-permute-done
  7.8 0.1 collective-permute-start.2
  8.0 3.0 %collective-permute-start.1 = (f32[264,128]{1,0:T(8,128)S(1)}, f32[264,128]{1,0:T(8,128)S(1)}, u32[]{:S(2)}, u32[]{:S(2)}) collective-permute-start(f32[264,128]{1,0:T(8,128)S(1)} %slice_select_fusion.1), channel_id=1, source_target_pairs={{0,4},{1,5},{2,6},{3,7},{4,0},{5,1},{6,2},{7,3},{8,12},{9,13},{10,... | collective-permute-start | bytes 405512 | tf_op jit(solution)/shard_map/ppermute | solution.py:476
  11.0 3.8 %collective-permute-done.1 = f32[264,128]{1,0:T(8,128)S(1)} collective-permute-done((f32[264,128]{1,0:T(8,128)S(1)}, f32[264,128]{1,0:T(8,128)S(1)}, u32[]{:S(2)}, u32[]{:S(2)}) %collective-permute-start.1) | collective-permute-done | bytes 135200 | tf_op jit(solution)/shard_map/ppermute | solution.py:476
  14.8 0.0 collective-permute-done.2
  14.8 1.8 %collective-permute-start.4 = (f32[256,128]{1,0:T(8,128)S(1)}, f32[256,128]{1,0:T(8,128)S(1)}, u32[]{:S(2)}, u32[]{:S(2)}) collective-permute-start(f32[256,128]{1,0:T(8,128)S(1)} %slice_select_fusion.2), channel_id=1, source_target_pairs={{0,4},{1,5},{2,6},{3,7},{4,0},{5,1},{6,2},{7,3},{8,12},{9,13},{10,... | collective-permute-start | bytes 393224 | tf_op jit(solution)/shard_map/ppermute | solution.py:476
  16.7 1.6 %collective-permute-start.3 = (f32[136,128]{1,0:T(8,128)S(1)}, f32[136,128]{1,0:T(8,128)S(1)}, u32[]{:S(2)}, u32[]{:S(2)}) collective-permute-start(f32[136,128]{1,0:T(8,128)S(1)} %slice_select_fusion.4), channel_id=1, source_target_pairs={{0,8},{1,9},{2,10},{3,11},{4,12},{5,13},{6,14},{7,15},{8,0},{9,1},... | collective-permute-start | bytes 208904 | tf_op jit(solution)/shard_map/ppermute | solution.py:476
  18.3 2.7 %collective-permute-done.3 = f32[136,128]{1,0:T(8,128)S(1)} collective-permute-done((f32[136,128]{1,0:T(8,128)S(1)}, f32[136,128]{1,0:T(8,128)S(1)}, u32[]{:S(2)}, u32[]{:S(2)}) %collective-permute-start.3) | collective-permute-done | bytes 69664 | tf_op jit(solution)/shard_map/ppermute | solution.py:476
  21.1 0.0 collective-permute-done.4
  21.1 2.7 %collective-permute-start.5 = (f32[136,128]{1,0:T(8,128)S(1)}, f32[136,128]{1,0:T(8,128)S(1)}, u32[]{:S(2)}, u32[]{:S(2)}) collective-permute-start(f32[136,128]{1,0:T(8,128)S(1)} %select_add_fusion.2), channel_id=1, source_target_pairs={{0,16},{1,17},{2,18},{3,19},{4,20},{5,21},{6,22},{7,23},{8,24},{9,... | collective-permute-start | bytes 208904 | tf_op jit(solution)/shard_map/ppermute | solution.py:476
  23.8 1.6 %collective-permute-start.6 = (f32[128,128]{1,0:T(8,128)S(1)}, f32[128,128]{1,0:T(8,128)S(1)}, u32[]{:S(2)}, u32[]{:S(2)}) collective-permute-start(f32[128,128]{1,0:T(8,128)S(1)} %slice_select_fusion.5), channel_id=1, source_target_pairs={{0,8},{1,9},{2,10},{3,11},{4,12},{5,13},{6,14},{7,15},{8,0},{9,1},... | collective-permute-start | bytes 196616 | tf_op jit(solution)/shard_map/ppermute | solution.py:476
  25.4 3.4 %collective-permute-done.6 = f32[128,128]{1,0:T(8,128)S(1)} collective-permute-done((f32[128,128]{1,0:T(8,128)S(1)}, f32[128,128]{1,0:T(8,128)S(1)}, u32[]{:S(2)}, u32[]{:S(2)}) %collective-permute-start.6) | collective-permute-done | bytes 65568 | tf_op jit(solution)/shard_map/ppermute | solution.py:476
  28.8 0.0 collective-permute-done.5
  28.8 1.6 %collective-permute-start.7 = (f32[136,128]{1,0:T(8,128)S(1)}, f32[136,128]{1,0:T(8,128)S(1)}, u32[]{:S(2)}, u32[]{:S(2)}) collective-permute-start(f32[136,128]{1,0:T(8,128)S(1)} %add.39), channel_id=1, source_target_pairs={{0,8},{1,9},{2,10},{3,11},{4,12},{5,13},{6,14},{7,15},{8,0},{9,1},... | collective-permute-start | bytes 208904 | tf_op jit(solution)/shard_map/ppermute | solution.py:476
  30.5 0.9 %collective-permute-start.8 = (f32[128,128]{1,0:T(8,128)S(1)}, f32[128,128]{1,0:T(8,128)S(1)}, u32[]{:S(2)}, u32[]{:S(2)}) collective-permute-start(f32[128,128]{1,0:T(8,128)S(1)} %select_add_fusion.3), channel_id=1, source_target_pairs={{0,16},{1,17},{2,18},{3,19},{4,20},{5,21},{6,22},{7,23},{8,24},{9,... | collective-permute-start | bytes 196616 | tf_op jit(solution)/shard_map/ppermute | solution.py:476
  31.4 4.9 %collective-permute-done.8 = f32[128,128]{1,0:T(8,128)S(1)} collective-permute-done((f32[128,128]{1,0:T(8,128)S(1)}, f32[128,128]{1,0:T(8,128)S(1)}, u32[]{:S(2)}, u32[]{:S(2)}) %collective-permute-start.8) | collective-permute-done | bytes 65568 | tf_op jit(solution)/shard_map/ppermute | solution.py:476
  36.3 0.0 collective-permute-done.7
  36.4 0.0 copy-start.1
  36.4 0.6 collective-permute-start.9
  37.0 0.2 collective-permute-start.10
  37.2 4.2 %collective-permute-done.10 = f32[128,128]{1,0:T(8,128)S(1)} collective-permute-done((f32[128,128]{1,0:T(8,128)S(1)}, f32[128,128]{1,0:T(8,128)S(1)}, u32[]{:S(2)}, u32[]{:S(2)}) %collective-permute-start.10) | collective-permute-done | bytes 65568 | tf_op jit(solution)/shard_map/ppermute | solution.py:476
  41.3 0.1 collective-permute-done.9
  41.5 0.1 collective-permute-start.12
  41.7 1.4 %collective-permute-start.11 = (f32[256,128]{1,0:T(8,128)S(1)}, f32[256,128]{1,0:T(8,128)S(1)}, u32[]{:S(2)}, u32[]{:S(2)}) collective-permute-start(f32[256,128]{1,0:T(8,128)S(1)} %pad_maximum_fusion.6), channel_id=1, source_target_pairs={{0,4},{1,5},{2,6},{3,7},{4,0},{5,1},{6,2},{7,3},{8,12},{9,13},{10,... | collective-permute-start | bytes 393224 | tf_op jit(solution)/shard_map/ppermute | solution.py:476
  43.1 0.1 collective-permute-done.12
  43.2 0.1 broadcast_select_fusion.1
  43.3 0.0 copy-done.1
  43.3 3.3 %level_first.1 = (f32[128,128]{1,0:T(8,128)S(1)}, f32[128,128]{1,0:T(8,128)S(1)}, f32[128,128]{1,0:T(8,128)S(1)}, f32[8,256]{1,0:T(8,128)S(1)}, f32[256,128]{1,0:T(8,128)S(1)}) custom-call(f32[1040,128]{1,0:T(8,128)S(1)} %pad_maximum_fusion.gram_ref.terms, f32[2,256,256]{2,1,0:T(8,128)S(1)} %copy-done.1), custom_call_target="tpu_custom_call" | custom-call | flops 5000000000 | bytes 262144 | tf_op jit(solution)/shard_map/level_first/pallas_call | solution.py:321
  46.6 1.4 %level_middle.1.swept = f32[128,128]{1,0:T(8,128)S(1)} custom-call(f32[128,128]{1,0:T(8,128)S(1)} %get-tuple-element.81.rest), custom_call_target="tpu_custom_call" | custom-call | flops 2500000000 | bytes 262144 | tf_op jit(solution)/shard_map/level_middle/pallas_call | solution.py:321
  48.0 0.0 collective-permute-done.11
  48.1 0.2 collective-permute-start.13
  48.3 2.1 %level_second.1.inverse = f32[256,256]{1,0:T(8,128)S(1)} custom-call(f32[128,128]{1,0:T(8,128)S(1)} %get-tuple-element.85.first, f32[128,128]{1,0:T(8,128)S(1)} %get-tuple-element.86.across, f32[128,128]{1,0:T(8,128)S(1)} %level_middle.1.swept, f32[8,256]{1,0:T(8,128)S(1)} %get-tuple-element.88.row, f32[256,128]{1,0:T(8,128)S(1)} %get-tuple-element.89.col), custom_call_target="tpu_custom_call" | custom-call | flops 2500000000 | bytes 262144 | tf_op jit(solution)/shard_map/level_second/pallas_call | solution.py:321
  50.3 1.1 %panel_solve.1 = (f32[256,256]{1,0:T(8,128)S(1)}, f32[264,128]{1,0:T(8,128)S(1)}) custom-call(f32[256,256]{1,0:T(8,128)S(1)} %level_second.1.inverse, f32[1040,128]{1,0:T(8,128)S(1)} %pad_maximum_fusion.gram_ref.terms), custom_call_target="tpu_custom_call" | custom-call | bytes 262144 | tf_op jit(solution)/shard_map/panel_solve/pallas_call | solution.py:321
  51.4 1.6 %collective-permute-start.15 = (f32[264,128]{1,0:T(8,128)S(1)}, f32[264,128]{1,0:T(8,128)S(1)}, u32[]{:S(2)}, u32[]{:S(2)}) collective-permute-start(f32[264,128]{1,0:T(8,128)S(1)} %get-tuple-element.98), channel_id=1, source_target_pairs={{0,2},{1,3},{2,0},{3,1},{4,6},{5,7},{6,4},{7,5},{8,10},{9,11},{10,... | collective-permute-start | bytes 405512 | tf_op jit(solution)/shard_map/ppermute | solution.py:476
  53.0 0.0 collective-permute-done.13
  53.1 0.0 copy-start.2
  53.1 3.4 %panel.1 = (f32[2048,256]{1,0:T(8,128)}, f32[2048,256]{1,0:T(8,128)S(1)}, bf16[2048,256]{1,0:T(8,128)(2,1)S(1)}, bf16[2048,256]{1,0:T(8,128)(2,1)S(1)}, f32[512,128]{1,0:T(8,128)S(1)}) custom-call(f32[2048,256]{1,0:T(8,128)S(1)} %get-tuple-element.58.b2, f32[2048,256]{1,0:T(8,128)S(1)} %get-tuple-element.59.b1, f32[2048,256]{1,0:T(8,128)S(1)} %copy-done, ...), custom_call_target="tpu_custom_call" | custom-call | flops 2147483648 | bytes 6291456 | tf_op jit(solution)/shard_map/panel/pallas_call | solution.py:463
  56.5 0.6 collective-permute-start.14
  57.1 0.2 collective-permute-done.15
  57.4 0.0 copy-done.2
  57.4 3.3 %root_first.1 = (f32[128,128]{1,0:T(8,128)S(1)}, f32[128,128]{1,0:T(8,128)S(1)}, f32[128,128]{1,0:T(8,128)S(1)}, f32[8,256]{1,0:T(8,128)S(1)}, f32[256,128]{1,0:T(8,128)S(1)}) custom-call(f32[264,128]{1,0:T(8,128)S(1)} %add.42.gram_ref, f32[1,256,256]{2,1,0:T(8,128)S(1)} %bitcast.1), custom_call_target="tpu_custom_call" | custom-call | flops 5000000000 | bytes 262144 | tf_op jit(solution)/shard_map/root_first/pallas_call | solution.py:321
  60.7 1.4 %root_middle.1.swept = f32[128,128]{1,0:T(8,128)S(1)} custom-call(f32[128,128]{1,0:T(8,128)S(1)} %get-tuple-element.102.rest), custom_call_target="tpu_custom_call" | custom-call | flops 2500000000 | bytes 262144 | tf_op jit(solution)/shard_map/root_middle/pallas_call | solution.py:321
  62.1 0.0 collective-permute-done.14
  62.2 0.1 collective-permute-start.16
  62.2 2.1 %root_second.1.inverse = f32[256,256]{1,0:T(8,128)S(1)} custom-call(f32[128,128]{1,0:T(8,128)S(1)} %get-tuple-element.105.first, f32[128,128]{1,0:T(8,128)S(1)} %get-tuple-element.106.across, f32[128,128]{1,0:T(8,128)S(1)} %root_middle.1.swept, f32[8,256]{1,0:T(8,128)S(1)} %get-tuple-element.108.row, f32[256,128]{1,0:T(8,128)S(1)} %get-tuple-element.109.col), custom_call_target="tpu_custom_call" | custom-call | flops 2500000000 | bytes 262144 | tf_op jit(solution)/shard_map/root_second/pallas_call | solution.py:321
  64.3 0.0 collective-permute-done.16
  64.4 2.4 %field.1 = f32[2048,256]{1,0:T(8,128)} custom-call(f32[2048,256]{1,0:T(8,128)S(1)} %get-tuple-element.94.level, bf16[2048,256]{1,0:T(8,128)(2,1)S(1)} %get-tuple-element.95.high, bf16[2048,256]{1,0:T(8,128)(2,1)S(1)} %get-tuple-element.96.low, f32[256,256]{1,0:T(8,128)S(1)} %root_second.1.inverse, f32[512,128]{1,0:T(8,128)S(1)} %pad_maximum_fusion.4.side), custom_call_target="tpu_custom_call" | custom-call | flops 805306368 | bytes 6291456 | tf_op jit(solution)/shard_map/field/pallas_call | solution.py:463
  (30 shorter events, 0.6 us)
Async XLA Ops:
  0.6 5.0 %copy-start = (f32[2048,256]{1,0:T(8,128)S(1)}, f32[2048,256]{1,0:T(8,128)}, u32[]{:S(2)}) copy-start(f32[2048,256]{1,0:T(8,128)} %sources.3) | copy-start | bytes 6291460
  5.1 2.7 %collective-permute-start = (f32[520,128]{1,0:T(8,128)S(1)}, f32[520,128]{1,0:T(8,128)S(1)}, u32[]{:S(2)}, u32[]{:S(2)}) collective-permute-start(f32[520,128]{1,0:T(8,128)S(1)} %get-tuple-element.63), channel_id=1, source_target_pairs={{0,1},{1,0},{2,3},{3,2},{4,5},{5,4},{6,7},{7,6},{8,9},{9,8},{10,11... | collective-permute-start | bytes 798728 | tf_op jit(solution)/shard_map/ppermute | solution.py:476
  7.8 7.0 %collective-permute-start.2 = (f32[512,128]{1,0:T(8,128)S(1)}, f32[512,128]{1,0:T(8,128)S(1)}, u32[]{:S(2)}, u32[]{:S(2)}) collective-permute-start(f32[512,128]{1,0:T(8,128)S(1)} %get-tuple-element.66), channel_id=1, source_target_pairs={{0,1},{1,0},{2,3},{3,2},{4,5},{5,4},{6,7},{7,6},{8,9},{9,8},{10,11... | collective-permute-start | bytes 786440 | tf_op jit(solution)/shard_map/ppermute | solution.py:476
  8.0 6.8 %collective-permute-start.1 = (f32[264,128]{1,0:T(8,128)S(1)}, f32[264,128]{1,0:T(8,128)S(1)}, u32[]{:S(2)}, u32[]{:S(2)}) collective-permute-start(f32[264,128]{1,0:T(8,128)S(1)} %slice_select_fusion.1), channel_id=1, source_target_pairs={{0,4},{1,5},{2,6},{3,7},{4,0},{5,1},{6,2},{7,3},{8,12},{9,13},{10,... | collective-permute-start | bytes 405512 | tf_op jit(solution)/shard_map/ppermute | solution.py:476
  14.8 6.2 %collective-permute-start.4 = (f32[256,128]{1,0:T(8,128)S(1)}, f32[256,128]{1,0:T(8,128)S(1)}, u32[]{:S(2)}, u32[]{:S(2)}) collective-permute-start(f32[256,128]{1,0:T(8,128)S(1)} %slice_select_fusion.2), channel_id=1, source_target_pairs={{0,4},{1,5},{2,6},{3,7},{4,0},{5,1},{6,2},{7,3},{8,12},{9,13},{10,... | collective-permute-start | bytes 393224 | tf_op jit(solution)/shard_map/ppermute | solution.py:476
  16.7 4.4 %collective-permute-start.3 = (f32[136,128]{1,0:T(8,128)S(1)}, f32[136,128]{1,0:T(8,128)S(1)}, u32[]{:S(2)}, u32[]{:S(2)}) collective-permute-start(f32[136,128]{1,0:T(8,128)S(1)} %slice_select_fusion.4), channel_id=1, source_target_pairs={{0,8},{1,9},{2,10},{3,11},{4,12},{5,13},{6,14},{7,15},{8,0},{9,1},... | collective-permute-start | bytes 208904 | tf_op jit(solution)/shard_map/ppermute | solution.py:476
  21.1 7.7 %collective-permute-start.5 = (f32[136,128]{1,0:T(8,128)S(1)}, f32[136,128]{1,0:T(8,128)S(1)}, u32[]{:S(2)}, u32[]{:S(2)}) collective-permute-start(f32[136,128]{1,0:T(8,128)S(1)} %select_add_fusion.2), channel_id=1, source_target_pairs={{0,16},{1,17},{2,18},{3,19},{4,20},{5,21},{6,22},{7,23},{8,24},{9,... | collective-permute-start | bytes 208904 | tf_op jit(solution)/shard_map/ppermute | solution.py:476
  23.8 5.0 %collective-permute-start.6 = (f32[128,128]{1,0:T(8,128)S(1)}, f32[128,128]{1,0:T(8,128)S(1)}, u32[]{:S(2)}, u32[]{:S(2)}) collective-permute-start(f32[128,128]{1,0:T(8,128)S(1)} %slice_select_fusion.5), channel_id=1, source_target_pairs={{0,8},{1,9},{2,10},{3,11},{4,12},{5,13},{6,14},{7,15},{8,0},{9,1},... | collective-permute-start | bytes 196616 | tf_op jit(solution)/shard_map/ppermute | solution.py:476
  28.8 7.5 %collective-permute-start.7 = (f32[136,128]{1,0:T(8,128)S(1)}, f32[136,128]{1,0:T(8,128)S(1)}, u32[]{:S(2)}, u32[]{:S(2)}) collective-permute-start(f32[136,128]{1,0:T(8,128)S(1)} %add.39), channel_id=1, source_target_pairs={{0,8},{1,9},{2,10},{3,11},{4,12},{5,13},{6,14},{7,15},{8,0},{9,1},... | collective-permute-start | bytes 208904 | tf_op jit(solution)/shard_map/ppermute | solution.py:476
  30.5 5.8 %collective-permute-start.8 = (f32[128,128]{1,0:T(8,128)S(1)}, f32[128,128]{1,0:T(8,128)S(1)}, u32[]{:S(2)}, u32[]{:S(2)}) collective-permute-start(f32[128,128]{1,0:T(8,128)S(1)} %select_add_fusion.3), channel_id=1, source_target_pairs={{0,16},{1,17},{2,18},{3,19},{4,20},{5,21},{6,22},{7,23},{8,24},{9,... | collective-permute-start | bytes 196616 | tf_op jit(solution)/shard_map/ppermute | solution.py:476
  36.4 6.9 %copy-start.1 = (f32[2,256,256]{2,1,0:T(8,128)S(1)}, f32[2,256,256]{2,1,0:T(8,128)}, u32[]{:S(2)}) copy-start(f32[2,256,256]{2,1,0:T(8,128)} %coupling.1) | copy-start | bytes 1572868
  36.4 5.1 %collective-permute-start.9 = (f32[264,128]{1,0:T(8,128)S(1)}, f32[264,128]{1,0:T(8,128)S(1)}, u32[]{:S(2)}, u32[]{:S(2)}) collective-permute-start(f32[264,128]{1,0:T(8,128)S(1)} %pad_maximum_fusion.5), channel_id=1, source_target_pairs={{0,4},{1,5},{2,6},{3,7},{4,0},{5,1},{6,2},{7,3},{8,12},{9,13},{10,... | collective-permute-start | bytes 405512 | tf_op jit(solution)/shard_map/ppermute | solution.py:476
  37.0 4.3 %collective-permute-start.10 = (f32[128,128]{1,0:T(8,128)S(1)}, f32[128,128]{1,0:T(8,128)S(1)}, u32[]{:S(2)}, u32[]{:S(2)}) collective-permute-start(f32[128,128]{1,0:T(8,128)S(1)} %add.41), channel_id=1, source_target_pairs={{0,8},{1,9},{2,10},{3,11},{4,12},{5,13},{6,14},{7,15},{8,0},{9,1},... | collective-permute-start | bytes 196616 | tf_op jit(solution)/shard_map/ppermute | solution.py:476
  41.5 1.6 %collective-permute-start.12 = (f32[520,128]{1,0:T(8,128)S(1)}, f32[520,128]{1,0:T(8,128)S(1)}, u32[]{:S(2)}, u32[]{:S(2)}) collective-permute-start(f32[520,128]{1,0:T(8,128)S(1)} %pad_maximum_fusion.2), channel_id=1, source_target_pairs={{0,1},{1,0},{2,3},{3,2},{4,5},{5,4},{6,7},{7,6},{8,9},{9,8},{10,11... | collective-permute-start | bytes 798728 | tf_op jit(solution)/shard_map/ppermute | solution.py:476
  41.7 6.3 %collective-permute-start.11 = (f32[256,128]{1,0:T(8,128)S(1)}, f32[256,128]{1,0:T(8,128)S(1)}, u32[]{:S(2)}, u32[]{:S(2)}) collective-permute-start(f32[256,128]{1,0:T(8,128)S(1)} %pad_maximum_fusion.6), channel_id=1, source_target_pairs={{0,4},{1,5},{2,6},{3,7},{4,0},{5,1},{6,2},{7,3},{8,12},{9,13},{10,... | collective-permute-start | bytes 393224 | tf_op jit(solution)/shard_map/ppermute | solution.py:476
  48.1 5.0 %collective-permute-start.13 = (f32[512,128]{1,0:T(8,128)S(1)}, f32[512,128]{1,0:T(8,128)S(1)}, u32[]{:S(2)}, u32[]{:S(2)}) collective-permute-start(f32[512,128]{1,0:T(8,128)S(1)} %pad_maximum_fusion.3), channel_id=1, source_target_pairs={{0,1},{1,0},{2,3},{3,2},{4,5},{5,4},{6,7},{7,6},{8,9},{9,8},{10,11... | collective-permute-start | bytes 786440 | tf_op jit(solution)/shard_map/ppermute | solution.py:476
  51.4 5.9 %collective-permute-start.15 = (f32[264,128]{1,0:T(8,128)S(1)}, f32[264,128]{1,0:T(8,128)S(1)}, u32[]{:S(2)}, u32[]{:S(2)}) collective-permute-start(f32[264,128]{1,0:T(8,128)S(1)} %get-tuple-element.98), channel_id=1, source_target_pairs={{0,2},{1,3},{2,0},{3,1},{4,6},{5,7},{6,4},{7,5},{8,10},{9,11},{10,... | collective-permute-start | bytes 405512 | tf_op jit(solution)/shard_map/ppermute | solution.py:476
  53.1 4.2 %copy-start.2 = (f32[256,256]{1,0:T(8,128)S(1)}, f32[256,256]{1,0:T(8,128)}, u32[]{:S(2)}) copy-start(f32[256,256]{1,0:T(8,128)} %param.9) | copy-start | bytes 786436
  56.5 5.6 %collective-permute-start.14 = (f32[256,128]{1,0:T(8,128)S(1)}, f32[256,128]{1,0:T(8,128)S(1)}, u32[]{:S(2)}, u32[]{:S(2)}) collective-permute-start(f32[256,128]{1,0:T(8,128)S(1)} %slice_select_fusion), channel_id=1, source_target_pairs={{0,2},{1,3},{2,0},{3,1},{4,6},{5,7},{6,4},{7,5},{8,10},{9,11},{10,... | collective-permute-start | bytes 393224 | tf_op jit(solution)/shard_map/ppermute | solution.py:476
  62.2 2.2 %collective-permute-start.16 = (f32[256,128]{1,0:T(8,128)S(1)}, f32[256,128]{1,0:T(8,128)S(1)}, u32[]{:S(2)}, u32[]{:S(2)}) collective-permute-start(f32[256,128]{1,0:T(8,128)S(1)} %add.43), channel_id=1, source_target_pairs={{0,1},{1,0},{2,3},{3,2},{4,5},{5,4},{6,7},{7,6},{8,9},{9,8},{10,11... | collective-permute-start | bytes 393224 | tf_op jit(solution)/shard_map/ppermute | solution.py:476
